TPU v7x, 32 devices: a whole 2x2x4 slice. The times are simulated.
32 devices in a mesh: parts: 2 (over y), dp: 4 (over z), tp: 4 (over x, core).
Axes of the slice: x: 2, y: 2, z: 4, core: 2. Of those that a mesh axis runs over, the one named last changes fastest.
Arguments:
- memory_hidden: bfloat16 [512, 5120], P(('parts', 'dp'), 'tp'), parts along dimension 0, may hold values from -6 to 6
- kv_weight: bfloat16 [2, 5120, 1024], P(None, None, 'tp'), may hold values from -0.078125 to 0.078125
- kv_bias: bfloat16 [2, 1024], P(None, 'tp'), may hold values from -3 to 3
- memory_sections: int32 [512], P('parts'), parts along dimension 0, may hold values from 0 to 3, never falling along the last dimension, each value on 1 to 128 neighbouring positions
- group_sections: int32 [8], P(('parts', 'dp')), parts along dimension 0, may hold values from 0 to 3
- queries: bfloat16 [64, 5120], P(('parts', 'dp'), 'tp'), parts along dimension 0, may hold values from -130 to 130
- new_keys: bfloat16 [64, 1024], P(('parts', 'dp'), 'tp'), parts along dimension 0, may hold values from -5 to 5
- new_values: bfloat16 [64, 1024], P(('parts', 'dp'), 'tp'), parts along dimension 0, may hold values from -5 to 5
- cache_keys: bfloat16 [32, 512, 1024], P(('parts', 'dp'), None, 'tp'), parts along dimension 0, may hold values from -5 to 5
- cache_values: bfloat16 [32, 512, 1024], P(('parts', 'dp'), None, 'tp'), parts along dimension 0, may hold values from -5 to 5
- cache_lengths: int32 [32], P(('parts', 'dp')), parts along dimension 0, may hold values from 2 to 512, as said below
- out_weight: bfloat16 [5120, 5120], P('tp', 'dp'), may hold values from -1.25 to 1.25
Outputs:
- output: bfloat16 [64, 5120], P(('parts', 'tp'), 'dp'), parts along dimension 0
There are 2 independent parts, one for each index of `parts`. A program takes and returns all parts, laid end to end along the dimension named above; an argument that names none is the same for every part. Nothing has to cross between parts.
Inputs may be any that keep to these rules, and one draw needn't show every extreme that they name: `memory_sections`: memory rows are grouped by section in order; every section holds at least one row. `cache_lengths`: some request has all 512 slots live.
All inputs are finite; a program needn't handle non-finite values.
Results may differ from a plain program's by a relative error of at most 0.0054.
Values may be sent and summed in bfloat16 or wider, within the bound.
No kernel may reach another device: no remote copies, remote signals or barrier semaphores. Data moves between devices by JAX's collectives and lax.ppermute only.
A program may use at most 64 MiB of HBM per device.

v0:
```python
import functools

import jax
import jax.numpy as jnp
from jax import lax
from jax.experimental import pallas as pl
from jax.experimental.pallas import tpu as pltpu
from jax.sharding import PartitionSpec as P

D = 5120
HQ = 40
KVH = 8
HD = 128
NEW = 2
PER_HEAD = HQ // KVH
INV = 1.0 / HD**0.5

masked_score = -1e30
bf16 = jnp.bfloat16
COVER = 1 << 36
PCOVER = 1 << 30
f32 = jnp.float32

TOP, TOTAL, SECTION = 0, 3, 5
STATS = 16


def nt(a, b):
    return lax.dot_general(a, b, (((1,), (1,)), ((), ())), preferred_element_type=f32)


def nn(a, b):
    return jnp.dot(a, b, preferred_element_type=f32)


def spread(blocks):
    zeros = jnp.zeros_like(blocks[0])
    rows = [
        jnp.concatenate([b if i == j else zeros for i in range(len(blocks))], axis=1)
        if len(blocks) > 1
        else b
        for j, b in enumerate(blocks)
    ]
    return jnp.concatenate(rows, axis=0)


def split(x, pieces):
    out = []
    for _ in range(pieces):
        piece = x.astype(bf16).astype(f32)
        out.append(piece)
        x = x - piece
    return out


def eye(rows, cols):
    row = lax.broadcasted_iota(jnp.int32, (rows, cols), 0)
    return (row == lax.broadcasted_iota(jnp.int32, (rows, cols), 1)).astype(f32).astype(bf16)


def up(n, to):
    return -(-n // to) * to


def cache_kernel(lens_ref, group_ref, q_ref, nk_ref, nv_ref, ck_ref, cv_ref, after, out_ref):
    requests, slots, cols = ck_ref.shape
    heads = cols // HD
    tokens = requests * NEW
    per = PER_HEAD * tokens
    rows = heads * per
    row = lax.broadcasted_iota(jnp.int32, (rows, 1), 0)
    request = lax.rem(lax.div(row, NEW), requests)
    token = lax.rem(row, NEW)
    q = q_ref[...].astype(f32)
    blocks = []
    for j in range(heads):
        parts = [q[:, (j * PER_HEAD + g) * HD : (j * PER_HEAD + g + 1) * HD] for g in range(PER_HEAD)]
        blocks.append(jnp.concatenate(parts, axis=0))
    out_ref[0:rows, :] = jnp.concatenate(blocks, axis=0).astype(bf16)
    qs = spread(blocks).astype(bf16)
    fresh = lax.broadcasted_iota(jnp.int32, (rows, tokens), 1)
    seen = (lax.div(fresh, NEW) == request) & (lax.rem(fresh, NEW) <= token)
    s_new = jnp.where(seen, nt(qs, nk_ref[...]) * INV, masked_score)
    limit = jnp.full((rows, 1), lens_ref[0], jnp.int32)
    for r in range(1, requests):
        limit = jnp.where(request == r, lens_ref[r], limit)
    live = lax.broadcasted_iota(jnp.int32, (rows, slots), 1) < limit
    s = nt(qs, ck_ref[0])
    for r in range(1, requests):
        s = jnp.where(request == r, nt(qs, ck_ref[r]), s)
    s = jnp.where(live, s * INV, masked_score)

    top = jnp.maximum(jnp.max(s, axis=1, keepdims=True), jnp.max(s_new, axis=1, keepdims=True))
    p = jnp.where(live, jnp.exp(s - top), 0.0)
    p_new = jnp.where(seen, jnp.exp(s_new - top), 0.0)
    total = jnp.sum(p, axis=1, keepdims=True) + jnp.sum(p_new, axis=1, keepdims=True)
    p = p.astype(bf16)
    acc = nn(p, cv_ref[0])
    for r in range(1, requests):
        acc = jnp.where(request == r, nn(p, cv_ref[r]), acc)
    acc = acc + nn(p_new.astype(bf16).astype(f32), nv_ref[...].astype(f32))
    mine = jnp.concatenate([acc[j * per : (j + 1) * per, j * HD : (j + 1) * HD] for j in range(heads)], axis=0)
    seg = up(rows, 16)
    out_ref[seg : seg + rows, :] = (mine / total).astype(bf16)

    lane = lax.broadcasted_iota(jnp.int32, (rows, HD), 1)
    stats = jnp.where(lane == SECTION, group_ref[0].astype(f32), 0.0)
    for i, piece in enumerate(split(top, 3)):
        stats = jnp.where(lane == TOP + i, piece, stats)
    for i, piece in enumerate(split(total, 2)):
        stats = jnp.where(lane == TOTAL + i, piece, stats)
    if rows < HD:
        stats = jnp.concatenate([stats, jnp.zeros((HD - rows, HD), f32)], axis=0)
    out_ref[2 * seg : 2 * seg + STATS, :] = nt(eye(STATS, HD), stats.astype(bf16)).astype(bf16)


def project_kernel(bits, first, last, *refs):
    count = len(bits)
    pieces, w_ref, refs = refs[:count], refs[count], refs[count + 1 :]
    rows, depth = pieces[0].shape
    me = lax.axis_index("tp")
    if first:
        acc, squares = [None, None], None
    else:
        acc = [refs[0][s * rows : (s + 1) * rows, :] for s in range(2)]
        squares = refs[1][:, 0:1]
        refs = refs[2:]
    for k, piece in zip(bits, pieces):
        h = piece[...]
        wide = h.astype(f32)
        square = jnp.sum(wide * wide, axis=1, keepdims=True)
        squares = square if squares is None else squares + square
        at = pl.multiple_of((me ^ k) * depth, depth)
        for s in range(2):
            term = nn(h, w_ref[s, pl.ds(at, depth), :])
            acc[s] = term if acc[s] is None else acc[s] + term
    if not last:
        for s in range(2):
            refs[0][s * rows : (s + 1) * rows, :] = acc[s]
        refs[1][...] = jnp.broadcast_to(squares, refs[1].shape)
        return
    b_ref, out_ref = refs
    scale = lax.rsqrt(squares / D + 1e-06)
    for s in range(2):
        bias = b_ref[s : s + 1, :].astype(f32)
        out_ref[s * rows : (s + 1) * rows, :] = (acc[s] * scale + bias).astype(bf16)


def prepare_kernel(heads, *refs):
    parts, (section_ref, q_ref, bias_ref, old_ref, stats_ref) = refs[:-5], refs[-5:]
    groups = len(parts)
    seg = (parts[0].shape[0] - STATS) // 2
    rows = q_ref.shape[0] // groups
    per = rows // heads
    blocks = [part[0:rows, :].astype(f32) for part in parts]
    q_ref[...] = jnp.concatenate(
        [spread([b[j * per : (j + 1) * per, :] for j in range(heads)]) for b in blocks], axis=0
    ).astype(bf16)
    stats = nt(
        eye(rows, HD), jnp.concatenate([part[2 * seg : 2 * seg + STATS, :] for part in parts], axis=0)
    )

    def column(at, pieces):
        columns = []
        for k in range(groups):
            c = k * STATS + at
            columns.append(sum([stats[:, c + i : c + i + 1] for i in range(pieces)]))
        return jnp.concatenate(columns, axis=0)

    top, total = column(TOP, 3), column(TOTAL, 2)
    bias_ref[...] = jnp.where(column(SECTION, 1) == section_ref[...].astype(f32), 0.0, masked_score)
    old = jnp.concatenate([part[seg : seg + rows, :] for part in parts], axis=0).astype(f32)
    old_ref[...] = old * total
    lane = lax.broadcasted_iota(jnp.int32, stats_ref.shape, 1)
    stats_ref[...] = jnp.where(lane == 0, top, total)


def attend_kernel(groups, shares, *refs):
    kvs, (q_ref, bias_ref, old_ref, stats_ref, w_ref) = refs[:groups], refs[groups : groups + 5]
    outs = refs[groups + 5 : groups + 5 + shares]
    k_ref, v_ref, attended_ref, sums_ref = refs[groups + 5 + shares :]
    me_dp, me_tp = lax.axis_index("dp"), lax.axis_index("tp")
    memory = kvs[0].shape[0] // 2
    heads = kvs[0].shape[1] // HD
    tokens = attended_ref.shape[0] // groups
    per = PER_HEAD * tokens
    rows = heads * per
    for k, kv in enumerate(kvs):
        first = pl.multiple_of((me_dp ^ k) * memory, memory)
        k_ref[pl.ds(first, memory), :] = kv[0:memory, :].astype(k_ref.dtype)
        v_ref[pl.ds(first, memory), :] = kv[memory : 2 * memory, :].astype(v_ref.dtype)
    s = nt(q_ref[...], k_ref[...].astype(bf16)) * INV + bias_ref[...]
    old_top, old_total = stats_ref[:, 0:1], stats_ref[:, 1:2]
    top = jnp.maximum(jnp.max(s, axis=1, keepdims=True), old_top)
    p = jnp.exp(s - top)
    shrink = jnp.exp(old_top - top)
    total = jnp.sum(p, axis=1, keepdims=True) + shrink * old_total
    acc = nn(p.astype(bf16), v_ref[...].astype(bf16))
    for k in range(groups):
        at = pl.multiple_of((me_dp ^ k) * tokens, tokens)
        for j in range(heads):
            a = k * rows + j * per
            block = acc[a : a + per, j * HD : (j + 1) * HD] + old_ref[a : a + per, :] * shrink[a : a + per]
            block = block / total[a : a + per]
            for g in range(PER_HEAD):
                c = (j * PER_HEAD + g) * HD
                attended_ref[pl.ds(at, tokens), c : c + HD] = block[g * tokens : (g + 1) * tokens, :]
    sums_ref[...] = nn(attended_ref[...].astype(bf16), w_ref[...])
    share = sums_ref.shape[0] // shares
    for k, out in enumerate(outs):
        at = pl.multiple_of((me_tp ^ k) * share, share)
        out[...] = sums_ref[pl.ds(at, share), :].astype(out.dtype)


SMEM = pl.BlockSpec(memory_space=pltpu.SMEM)
VMEM = pl.BlockSpec(memory_space=pltpu.VMEM)
ANY = pl.BlockSpec(memory_space=pl.ANY)
HBM = pl.BlockSpec(memory_space=pltpu.HBM)
PARAMS = pltpu.CompilerParams(vmem_limit_bytes=24 * 1024 * 1024)


def call(kernel, in_specs, out_shape, scratch, flops, bytes_accessed):
    return pl.pallas_call(
        kernel,
        in_specs=in_specs,
        out_shape=out_shape,
        out_specs=jax.tree.map(lambda _: VMEM, out_shape),
        scratch_shapes=scratch,
        compiler_params=PARAMS,
        cost_estimate=pl.CostEstimate(flops=flops, bytes_accessed=bytes_accessed, transcendentals=0),
    )


def in_hbm(*arrays):
    return [pltpu.with_memory_space_constraint(x, pltpu.HBM) for x in arrays]


def permute(x, axis, bits):
    return lax.ppermute(x, axis, [(i, i ^ bits) for i in range(lax.axis_size(axis))])


def others(x, axis):
    return [x] + [permute(x, axis, bits) for bits in range(1, lax.axis_size(axis))]


def passed_on(x, axis):
    n = lax.axis_size(axis)
    held = {0: x}
    bit = n // 2
    while bit:
        for bits in sorted(held):
            held[bits | bit] = permute(held[bits], axis, bit)
        bit //= 2
    return [held[bits] for bits in range(n)]


def body(
    memory_hidden,
    kv_weight,
    kv_bias,
    memory_sections,
    group_sections,
    queries,
    new_keys,
    new_values,
    cache_keys,
    cache_values,
    cache_lengths,
    out_weight,
):
    groups, shares = lax.axis_size("dp"), lax.axis_size("tp")
    memory, depth = memory_hidden.shape
    requests, slots, cols = cache_keys.shape
    tokens = requests * NEW
    rows = (cols // HD) * PER_HEAD * tokens
    every = memory_sections.shape[0]

    hidden = passed_on(memory_hidden, "tp")
    opened = call(
        lambda *refs: None,
        [ANY],
        jax.ShapeDtypeStruct((8, HD), f32),
        [],
        COVER,
        0,
    )(hidden[1])
    part = call(
        cache_kernel,
        [SMEM] * 2 + [VMEM] * 5 + [ANY],
        pltpu.VMEM((2 * up(rows, 16) + STATS, HD), bf16),
        [],
        4 * rows * slots * cols * requests,
        4 * requests * slots * cols,
    )(cache_lengths, group_sections, queries, new_keys, new_values, cache_keys, cache_values, opened)
    parts = others(part, "dp")
    near, far = list(range(shares - 1)), [shares - 1]
    partial = call(
        functools.partial(project_kernel, near, True, False),
        [VMEM] * (len(near) + 1),
        [pltpu.VMEM((2 * memory, cols), f32), pltpu.VMEM((memory, HD), f32)],
        [],
        COVER,
        4 * D * cols,
    )(*[hidden[k] for k in near], kv_weight)
    kv = call(
        functools.partial(project_kernel, far, False, True),
        [VMEM] * 5,
        pltpu.VMEM((2 * memory, cols), bf16),
        [],
        4 * memory * D * cols // shares,
        4 * D * cols // shares,
    )(hidden[far[0]], kv_weight, *partial, kv_bias)
    kvs = others(kv, "dp")
    prepared = call(
        functools.partial(prepare_kernel, cols // HD),
        [VMEM] * (groups + 1),
        [
            pltpu.VMEM((groups * rows, cols), bf16),
            pltpu.VMEM((groups * rows, every), f32),
            pltpu.VMEM((groups * rows, HD), f32),
            pltpu.VMEM((groups * rows, HD), f32),
        ],
        [],
        PCOVER,
        0,
    )(*parts, memory_sections.reshape(1, every))

    out_rows, out_cols = groups * tokens, out_weight.shape[1]
    share = out_rows // shares
    held = bf16 if memory % 16 == 0 else f32
    pieces = call(
        functools.partial(attend_kernel, groups, shares),
        [VMEM] * (groups + 5),
        [pltpu.VMEM((share, out_cols), f32 if k == 0 else bf16) for k in range(shares)],
        [
            pltpu.VMEM((every, cols), held),
            pltpu.VMEM((every, cols), held),
            pltpu.VMEM((out_rows, out_weight.shape[0]), f32),
            pltpu.VMEM((out_rows, out_cols), f32),
        ],
        2 * out_rows * out_weight.size,
        2 * out_weight.size,
    )(*kvs, *prepared, out_weight)
    summed = pieces[0]
    for bits in range(1, shares):
        summed = summed + permute(pieces[bits], "tp", bits).astype(f32)
    return summed.astype(bf16)


def solution(mesh):
    return jax.shard_map(
        body,
        mesh=mesh,
        in_specs=(
            P(("parts", "dp"), "tp"),
            P(None, None, "tp"),
            P(None, "tp"),
            P("parts"),
            P(("parts", "dp")),
            P(("parts", "dp"), "tp"),
            P(("parts", "dp"), "tp"),
            P(("parts", "dp"), "tp"),
            P(("parts", "dp"), None, "tp"),
            P(("parts", "dp"), None, "tp"),
            P(("parts", "dp")),
            P("tp", "dp"),
        ),
        out_specs=P(("parts", "tp"), "dp"),
        check_vma=False,
    )
```

profile of v0, /device:TPU:0, one launch (start us, length us, event | category | flops | bytes accessed | tf_op | source)
XLA Modules:
  0.0 28.6 jit_solution(9939572607389784844)
XLA Ops:
  0.0 0.5 %collective-permute-start.2 = (bf16[64,1280]{1,0:T(8,128)(2,1)}, bf16[64,1280]{1,0:T(8,128)(2,1)S(1)}, u32[]{:S(2)}, u32[]{:S(2)}) collective-permute-start(bf16[64,1280]{1,0:T(8,128)(2,1)} %refs_0_.1), channel_id=1, source_target_pairs={{0,1},{1,0},{2,3},{3,2},{4,5},{5,4},{6,7},{7,6},{8,9},{9,8},{10,11... | collective-permute-start | bytes 491528 | tf_op jit(solution)/shard_map/ppermute | solution.py:239
  0.5 2.5 %collective-permute-start = (bf16[64,1280]{1,0:T(8,128)(2,1)}, bf16[64,1280]{1,0:T(8,128)(2,1)S(1)}, u32[]{:S(2)}, u32[]{:S(2)}) collective-permute-start(bf16[64,1280]{1,0:T(8,128)(2,1)} %refs_0_.1), channel_id=1, source_target_pairs={{0,2},{1,3},{2,0},{3,1},{4,6},{5,7},{6,4},{7,5},{8,10},{9,11},{10,... | collective-permute-start | bytes 491528 | tf_op jit(solution)/shard_map/ppermute | solution.py:239
  3.7 0.0 copy-start.1
  3.8 0.0 copy-start.2
  3.8 0.0 copy-start.3
  3.8 0.0 copy-start.4
  3.8 0.0 copy-start.5
  3.8 0.0 copy-start.7
  3.8 0.0 slice-start.1
  3.8 0.0 copy-start.8
  3.8 0.0 collective-permute-done.2.refs_1_.refs_0_
  3.8 1.3 %copy-done.1 = bf16[4,512,256]{2,1,0:T(8,128)(2,1)S(1)} copy-done((bf16[4,512,256]{2,1,0:T(8,128)(2,1)S(1)}, bf16[4,512,256]{2,1,0:T(8,128)(2,1)}, u32[]{:S(2)}) %copy-start.1) | copy-done | bytes 1048600
  5.1 0.3 %copy-done.2 = bf16[4,512,256]{2,1,0:T(8,128)(2,1)S(1)} copy-done((bf16[4,512,256]{2,1,0:T(8,128)(2,1)S(1)}, bf16[4,512,256]{2,1,0:T(8,128)(2,1)}, u32[]{:S(2)}) %copy-start.2) | copy-done | bytes 1048600
  5.4 0.0 copy-done.3
  5.5 0.0 copy-done.4
  5.5 0.0 copy-done.5
  5.5 0.0 copy-done.7
  5.5 1.4 %shard_map.121.refs_0_ = bf16[176,128]{1,0:T(8,128)(2,1)S(1)} custom-call(s32[4]{0:T(128)S(1)} %copy-done.7, s32[1]{0:T(128)S(6)} %copy.13.group_ref, bf16[8,1280]{1,0:T(8,128)(2,1)S(1)} %copy-done.3, bf16[8,256]{1,0:T(8,128)(2,1)S(1)} %copy-done.4, bf16[8,256]{1,0:T(8,128)(2,1)S(1)} %copy-done.5, bf16[4,512,256]{2,1,0:T(8,128)(2,1)S(1)} %copy-done.1, ...), custom_call_target="tpu_custom_call" | custom-call | flops 167772160 | bytes 2097152 | tf_op jit(solution)/shard_map/pallas_call | solution.py:287
  6.8 0.0 copy-start.6
  6.9 3.7 %collective-permute-start.8 = (bf16[176,128]{1,0:T(8,128)(2,1)S(1)}, bf16[176,128]{1,0:T(8,128)(2,1)S(1)}, u32[]{:S(2)}, u32[]{:S(2)}) collective-permute-start(bf16[176,128]{1,0:T(8,128)(2,1)S(1)} %shard_map.121.refs_0_), channel_id=1, source_target_pairs={{0,12},{4,8},{8,4},{12,0},{1,13},{5,9},{9,5},{13,1},{2,14},{6,10},... | collective-permute-start | bytes 135176 | tf_op jit(solution)/shard_map/ppermute | solution.py:239
  10.5 0.0 collective-permute-start.7
  10.5 0.8 %collective-permute-start.6 = (bf16[176,128]{1,0:T(8,128)(2,1)S(1)}, bf16[176,128]{1,0:T(8,128)(2,1)S(1)}, u32[]{:S(2)}, u32[]{:S(2)}) collective-permute-start(bf16[176,128]{1,0:T(8,128)(2,1)S(1)} %shard_map.121.refs_0_), channel_id=1, source_target_pairs={{0,4},{4,0},{8,12},{12,8},{1,5},{5,1},{9,13},{13,9},{2,6},{6,2},{1... | collective-permute-start | bytes 135176 | tf_op jit(solution)/shard_map/ppermute | solution.py:239
  11.3 0.0 collective-permute-done.refs_2_
  11.3 0.0 collective-permute-start.1
  11.3 0.0 slice-done
  11.4 0.8 %shard_map.118 = (f32[128,256]{1,0:T(8,128)S(1)}, f32[64,128]{1,0:T(8,128)S(1)}) custom-call(bf16[64,1280]{1,0:T(8,128)(2,1)S(1)} %copy-done.8, bf16[64,1280]{1,0:T(8,128)(2,1)S(1)} %collective-permute-done.2.refs_1_.refs_0_, bf16[64,1280]{1,0:T(8,128)(2,1)S(1)} %collective-permute-done.refs_2_, bf16[2,5120,256]{2,1,0:T(8,128)(2,1)S(1)} %bitcast.2), custom_call_target="tpu_custom_call" | custom-call | flops 68719476736 | bytes 5242880 | tf_op jit(solution)/shard_map/pallas_call | solution.py:297
  12.2 0.0 copy-start
  12.2 0.5 %collective-permute-done.1.refs_0_ = bf16[64,1280]{1,0:T(8,128)(2,1)S(1)} collective-permute-done((bf16[64,1280]{1,0:T(8,128)(2,1)S(1)}, bf16[64,1280]{1,0:T(8,128)(2,1)S(1)}, u32[]{:S(2)}, u32[]{:S(2)}) %collective-permute-start.1) | collective-permute-done | bytes 163872 | tf_op jit(solution)/shard_map/ppermute | solution.py:239
  12.7 0.4 %shard_map.119.refs_0_ = bf16[128,256]{1,0:T(8,128)(2,1)S(1)} custom-call(bf16[64,1280]{1,0:T(8,128)(2,1)S(1)} %collective-permute-done.1.refs_0_, bf16[2,5120,256]{2,1,0:T(8,128)(2,1)S(1)} %bitcast.2, f32[128,256]{1,0:T(8,128)S(1)} %get-tuple-element.15.refs_2_, f32[64,128]{1,0:T(8,128)S(1)} %get-tuple-element.16.refs_3_, bf16[2,256]{1,0:T(2,128)(2,1)S(1)} %copy-done.6), custom_call_target="tpu_custom_call" | custom-call | flops 83886080 | bytes 1310720 | tf_op jit(solution)/shard_map/pallas_call | solution.py:305
  13.1 3.7 %collective-permute-start.5 = (bf16[128,256]{1,0:T(8,128)(2,1)S(1)}, bf16[128,256]{1,0:T(8,128)(2,1)S(1)}, u32[]{:S(2)}, u32[]{:S(2)}) collective-permute-start(bf16[128,256]{1,0:T(8,128)(2,1)S(1)} %shard_map.119.refs_0_), channel_id=1, source_target_pairs={{0,12},{4,8},{8,4},{12,0},{1,13},{5,9},{9,5},{13,1},{2,14},{6,10},... | collective-permute-start | bytes 196616 | tf_op jit(solution)/shard_map/ppermute | solution.py:239
  16.8 0.0 collective-permute-start.4
  16.8 0.0 collective-permute-done.8.refs_3_
  16.8 0.8 %collective-permute-start.3 = (bf16[128,256]{1,0:T(8,128)(2,1)S(1)}, bf16[128,256]{1,0:T(8,128)(2,1)S(1)}, u32[]{:S(2)}, u32[]{:S(2)}) collective-permute-start(bf16[128,256]{1,0:T(8,128)(2,1)S(1)} %shard_map.119.refs_0_), channel_id=1, source_target_pairs={{0,4},{4,0},{8,12},{12,8},{1,5},{5,1},{9,13},{13,9},{2,6},{6,2},{1... | collective-permute-start | bytes 196616 | tf_op jit(solution)/shard_map/ppermute | solution.py:239
  17.5 0.0 collective-permute-done.7.refs_2_
  17.6 0.0 collective-permute-done.6.refs_1_
  17.6 0.0 copy-done.9
  17.6 0.5 %shard_map.122 = (bf16[320,256]{1,0:T(8,128)(2,1)S(1)}, f32[320,256]{1,0:T(8,128)S(1)}, f32[320,128]{1,0:T(8,128)S(1)}, f32[320,128]{1,0:T(8,128)S(1)}) custom-call(bf16[176,128]{1,0:T(8,128)(2,1)S(1)} %shard_map.121.refs_0_, bf16[176,128]{1,0:T(8,128)(2,1)S(1)} %collective-permute-done.6.refs_1_, bf16[176,128]{1,0:T(8,128)(2,1)S(1)} %collective-permute-done.7.refs_2_, ...), custom_call_target="tpu_custom_call" | custom-call | flops 1073741824 | tf_op jit(solution)/shard_map/pallas_call | solution.py:314
  18.0 1.8 %collective-permute-done.5.refs_3_ = bf16[128,256]{1,0:T(8,128)(2,1)S(1)} collective-permute-done((bf16[128,256]{1,0:T(8,128)(2,1)S(1)}, bf16[128,256]{1,0:T(8,128)(2,1)S(1)}, u32[]{:S(2)}, u32[]{:S(2)}) %collective-permute-start.5) | collective-permute-done | bytes 65568 | tf_op jit(solution)/shard_map/ppermute | solution.py:239
  19.8 2.6 %collective-permute-done.4.refs_2_ = bf16[128,256]{1,0:T(8,128)(2,1)S(1)} collective-permute-done((bf16[128,256]{1,0:T(8,128)(2,1)S(1)}, bf16[128,256]{1,0:T(8,128)(2,1)S(1)}, u32[]{:S(2)}, u32[]{:S(2)}) %collective-permute-start.4) | collective-permute-done | bytes 65568 | tf_op jit(solution)/shard_map/ppermute | solution.py:239
  22.4 0.0 collective-permute-done.3.refs_1_
  22.4 1.4 %shard_map.123 = (f32[8,1280]{1,0:T(8,128)S(1)}, bf16[8,1280]{1,0:T(8,128)(2,1)S(1)}, bf16[8,1280]{1,0:T(8,128)(2,1)S(1)}, bf16[8,1280]{1,0:T(8,128)(2,1)S(1)}) custom-call(bf16[128,256]{1,0:T(8,128)(2,1)S(1)} %shard_map.119.refs_0_, bf16[128,256]{1,0:T(8,128)(2,1)S(1)} %collective-permute-done.3.refs_1_, ...), custom_call_target="tpu_custom_call" | custom-call | flops 104857600 | bytes 3276800 | tf_op jit(solution)/shard_map/pallas_call | solution.py:331
  23.9 0.1 collective-permute-start.9
  23.9 0.6 %collective-permute-start.10 = (bf16[8,1280]{1,0:T(8,128)(2,1)S(1)}, bf16[8,1280]{1,0:T(8,128)(2,1)S(1)}, u32[]{:S(2)}, u32[]{:S(2)}) collective-permute-start(bf16[8,1280]{1,0:T(8,128)(2,1)S(1)} %get-tuple-element.23), channel_id=1, source_target_pairs={{0,2},{1,3},{2,0},{3,1},{4,6},{5,7},{6,4},{7,5},{8,10},{9,11},{10,... | collective-permute-start | bytes 61448 | tf_op jit(solution)/shard_map/ppermute | solution.py:239
  24.5 1.3 %collective-permute-start.11 = (bf16[8,1280]{1,0:T(8,128)(2,1)S(1)}, bf16[8,1280]{1,0:T(8,128)(2,1)S(1)}, u32[]{:S(2)}, u32[]{:S(2)}) collective-permute-start(bf16[8,1280]{1,0:T(8,128)(2,1)S(1)} %get-tuple-element.24), channel_id=1, source_target_pairs={{0,3},{1,2},{2,1},{3,0},{4,7},{5,6},{6,5},{7,4},{8,11},{9,10},{10,... | collective-permute-start | bytes 61448 | tf_op jit(solution)/shard_map/ppermute | solution.py:239
  25.8 0.0 collective-permute-done.9
  25.8 2.2 %collective-permute-done.10 = bf16[8,1280]{1,0:T(8,128)(2,1)S(1)} collective-permute-done((bf16[8,1280]{1,0:T(8,128)(2,1)S(1)}, bf16[8,1280]{1,0:T(8,128)(2,1)S(1)}, u32[]{:S(2)}, u32[]{:S(2)}) %collective-permute-start.10) | collective-permute-done | bytes 20512 | tf_op jit(solution)/shard_map/ppermute | solution.py:239
  28.0 0.0 collective-permute-done.11
  28.0 0.6 %add_convert_fusion = bf16[8,1280]{1,0:T(8,128)(2,1)} fusion(bf16[8,1280]{1,0:T(8,128)(2,1)S(1)} %collective-permute-done.11, bf16[8,1280]{1,0:T(8,128)(2,1)S(1)} %collective-permute-done.10, f32[8,1280]{1,0:T(8,128)S(1)} %get-tuple-element.21, bf16[8,1280]{1,0:T(8,128)(2,1)S(1)} %collective-permute-done.9), kind=kLoop, calls=%fused_computation | loop fusion | flops 71680 | bytes 122880 | tf_op jit(solution)/shard_map/convert_element_type | solution.py:347
  (8 shorter events, 0.0 us)
Async XLA Ops:
  0.0 3.8 %collective-permute-start.2 = (bf16[64,1280]{1,0:T(8,128)(2,1)}, bf16[64,1280]{1,0:T(8,128)(2,1)S(1)}, u32[]{:S(2)}, u32[]{:S(2)}) collective-permute-start(bf16[64,1280]{1,0:T(8,128)(2,1)} %refs_0_.1), channel_id=1, source_target_pairs={{0,1},{1,0},{2,3},{3,2},{4,5},{5,4},{6,7},{7,6},{8,9},{9,8},{10,11... | collective-permute-start | bytes 491528 | tf_op jit(solution)/shard_map/ppermute | solution.py:239
  0.5 10.9 %collective-permute-start = (bf16[64,1280]{1,0:T(8,128)(2,1)}, bf16[64,1280]{1,0:T(8,128)(2,1)S(1)}, u32[]{:S(2)}, u32[]{:S(2)}) collective-permute-start(bf16[64,1280]{1,0:T(8,128)(2,1)} %refs_0_.1), channel_id=1, source_target_pairs={{0,2},{1,3},{2,0},{3,1},{4,6},{5,7},{6,4},{7,5},{8,10},{9,11},{10,... | collective-permute-start | bytes 491528 | tf_op jit(solution)/shard_map/ppermute | solution.py:239
  2.9 8.4 %slice-start = ((s8[5242880]{0:T(1024)(128)(4,1)}), s8[4194304]{0:T(1024)(128)(4,1)S(1)}, s32[]{:S(2)}) async-start(s8[5242880]{0:T(1024)(128)(4,1)} %bitcast.1), calls=%async_computation | async-start | bytes 8388608
  3.7 1.4 %copy-start.1 = (bf16[4,512,256]{2,1,0:T(8,128)(2,1)S(1)}, bf16[4,512,256]{2,1,0:T(8,128)(2,1)}, u32[]{:S(2)}) copy-start(bf16[4,512,256]{2,1,0:T(8,128)(2,1)} %ck_ref.1) | copy-start | bytes 3145732
  3.8 1.7 %copy-start.2 = (bf16[4,512,256]{2,1,0:T(8,128)(2,1)S(1)}, bf16[4,512,256]{2,1,0:T(8,128)(2,1)}, u32[]{:S(2)}) copy-start(bf16[4,512,256]{2,1,0:T(8,128)(2,1)} %cv_ref.1) | copy-start | bytes 3145732
  3.8 1.7 %copy-start.3 = (bf16[8,1280]{1,0:T(8,128)(2,1)S(1)}, bf16[8,1280]{1,0:T(8,128)(2,1)}, u32[]{:S(2)}) copy-start(bf16[8,1280]{1,0:T(8,128)(2,1)} %q_ref.1) | copy-start | bytes 61444
  3.8 1.7 %copy-start.4 = (bf16[8,256]{1,0:T(8,128)(2,1)S(1)}, bf16[8,256]{1,0:T(8,128)(2,1)}, u32[]{:S(2)}) copy-start(bf16[8,256]{1,0:T(8,128)(2,1)} %nk_ref.1) | copy-start | bytes 12292
  3.8 1.7 %copy-start.5 = (bf16[8,256]{1,0:T(8,128)(2,1)S(1)}, bf16[8,256]{1,0:T(8,128)(2,1)}, u32[]{:S(2)}) copy-start(bf16[8,256]{1,0:T(8,128)(2,1)} %nv_ref.1) | copy-start | bytes 12292
  3.8 1.7 %copy-start.7 = (s32[4]{0:T(128)S(1)}, s32[4]{0:T(128)}, u32[]{:S(2)}) copy-start(s32[4]{0:T(128)} %lens_ref.1) | copy-start | bytes 52
  3.8 7.5 %slice-start.1 = ((s8[5242880]{0:T(1024)(128)(4,1)}), s8[1048576]{0:T(1024)(128)(4,1)S(1)}, s32[]{:S(2)}) async-start(s8[5242880]{0:T(1024)(128)(4,1)} %bitcast.1), calls=%async_computation.1 | async-start | bytes 2097152
  3.8 7.5 %copy-start.8 = (bf16[64,1280]{1,0:T(8,128)(2,1)S(1)}, bf16[64,1280]{1,0:T(8,128)(2,1)}, u32[]{:S(2)}) copy-start(bf16[64,1280]{1,0:T(8,128)(2,1)} %refs_0_.1) | copy-start | bytes 491524
  6.8 5.9 %copy-start.6 = (bf16[2,256]{1,0:T(2,128)(2,1)S(1)}, bf16[2,256]{1,0:T(2,128)(2,1)}, u32[]{:S(2)}) copy-start(bf16[2,256]{1,0:T(2,128)(2,1)} %refs_4_.1) | copy-start | bytes 3076
  6.9 9.9 %collective-permute-start.8 = (bf16[176,128]{1,0:T(8,128)(2,1)S(1)}, bf16[176,128]{1,0:T(8,128)(2,1)S(1)}, u32[]{:S(2)}, u32[]{:S(2)}) collective-permute-start(bf16[176,128]{1,0:T(8,128)(2,1)S(1)} %shard_map.121.refs_0_), channel_id=1, source_target_pairs={{0,12},{4,8},{8,4},{12,0},{1,13},{5,9},{9,5},{13,1},{2,14},{6,10},... | collective-permute-start | bytes 135176 | tf_op jit(solution)/shard_map/ppermute | solution.py:239
  10.5 7.0 %collective-permute-start.7 = (bf16[176,128]{1,0:T(8,128)(2,1)S(1)}, bf16[176,128]{1,0:T(8,128)(2,1)S(1)}, u32[]{:S(2)}, u32[]{:S(2)}) collective-permute-start(bf16[176,128]{1,0:T(8,128)(2,1)S(1)} %shard_map.121.refs_0_), channel_id=1, source_target_pairs={{0,8},{4,12},{8,0},{12,4},{1,9},{5,13},{9,1},{13,5},{2,10},{6,14},... | collective-permute-start | bytes 135176 | tf_op jit(solution)/shard_map/ppermute | solution.py:239
  10.5 7.0 %collective-permute-start.6 = (bf16[176,128]{1,0:T(8,128)(2,1)S(1)}, bf16[176,128]{1,0:T(8,128)(2,1)S(1)}, u32[]{:S(2)}, u32[]{:S(2)}) collective-permute-start(bf16[176,128]{1,0:T(8,128)(2,1)S(1)} %shard_map.121.refs_0_), channel_id=1, source_target_pairs={{0,4},{4,0},{8,12},{12,8},{1,5},{5,1},{9,13},{13,9},{2,6},{6,2},{1... | collective-permute-start | bytes 135176 | tf_op jit(solution)/shard_map/ppermute | solution.py:239
  11.3 1.4 %collective-permute-start.1 = (bf16[64,1280]{1,0:T(8,128)(2,1)S(1)}, bf16[64,1280]{1,0:T(8,128)(2,1)S(1)}, u32[]{:S(2)}, u32[]{:S(2)}) collective-permute-start(bf16[64,1280]{1,0:T(8,128)(2,1)S(1)} %collective-permute-done.refs_2_), channel_id=1, source_target_pairs={{0,1},{1,0},{2,3},{3,2},{4,5},{5,4},{6,7},{7,6},{8,9},{9,8},{10,11... | collective-permute-start | bytes 491528 | tf_op jit(solution)/shard_map/ppermute | solution.py:239
  12.2 5.4 %copy-start.9 = (s32[256]{0:T(256)S(1)}, s32[256]{0:T(256)}, u32[]{:S(2)}) copy-start(s32[256]{0:T(256)} %param.15) | copy-start | bytes 3076
  12.2 10.2 %copy-start = (bf16[1280,1280]{1,0:T(8,128)(2,1)S(1)}, bf16[1280,1280]{1,0:T(8,128)(2,1)}, u32[]{:S(2)}) copy-start(bf16[1280,1280]{1,0:T(8,128)(2,1)} %refs_8_.1) | copy-start | bytes 9830404
  13.1 6.7 %collective-permute-start.5 = (bf16[128,256]{1,0:T(8,128)(2,1)S(1)}, bf16[128,256]{1,0:T(8,128)(2,1)S(1)}, u32[]{:S(2)}, u32[]{:S(2)}) collective-permute-start(bf16[128,256]{1,0:T(8,128)(2,1)S(1)} %shard_map.119.refs_0_), channel_id=1, source_target_pairs={{0,12},{4,8},{8,4},{12,0},{1,13},{5,9},{9,5},{13,1},{2,14},{6,10},... | collective-permute-start | bytes 196616 | tf_op jit(solution)/shard_map/ppermute | solution.py:239
  16.8 5.7 %collective-permute-start.4 = (bf16[128,256]{1,0:T(8,128)(2,1)S(1)}, bf16[128,256]{1,0:T(8,128)(2,1)S(1)}, u32[]{:S(2)}, u32[]{:S(2)}) collective-permute-start(bf16[128,256]{1,0:T(8,128)(2,1)S(1)} %shard_map.119.refs_0_), channel_id=1, source_target_pairs={{0,8},{4,12},{8,0},{12,4},{1,9},{5,13},{9,1},{13,5},{2,10},{6,14},... | collective-permute-start | bytes 196616 | tf_op jit(solution)/shard_map/ppermute | solution.py:239
  16.8 5.7 %collective-permute-start.3 = (bf16[128,256]{1,0:T(8,128)(2,1)S(1)}, bf16[128,256]{1,0:T(8,128)(2,1)S(1)}, u32[]{:S(2)}, u32[]{:S(2)}) collective-permute-start(bf16[128,256]{1,0:T(8,128)(2,1)S(1)} %shard_map.119.refs_0_), channel_id=1, source_target_pairs={{0,4},{4,0},{8,12},{12,8},{1,5},{5,1},{9,13},{13,9},{2,6},{6,2},{1... | collective-permute-start | bytes 196616 | tf_op jit(solution)/shard_map/ppermute | solution.py:239
  23.9 1.9 %collective-permute-start.9 = (bf16[8,1280]{1,0:T(8,128)(2,1)S(1)}, bf16[8,1280]{1,0:T(8,128)(2,1)S(1)}, u32[]{:S(2)}, u32[]{:S(2)}) collective-permute-start(bf16[8,1280]{1,0:T(8,128)(2,1)S(1)} %get-tuple-element.22), channel_id=1, source_target_pairs={{0,1},{1,0},{2,3},{3,2},{4,5},{5,4},{6,7},{7,6},{8,9},{9,8},{10,11... | collective-permute-start | bytes 61448 | tf_op jit(solution)/shard_map/ppermute | solution.py:239
  23.9 4.0 %collective-permute-start.10 = (bf16[8,1280]{1,0:T(8,128)(2,1)S(1)}, bf16[8,1280]{1,0:T(8,128)(2,1)S(1)}, u32[]{:S(2)}, u32[]{:S(2)}) collective-permute-start(bf16[8,1280]{1,0:T(8,128)(2,1)S(1)} %get-tuple-element.23), channel_id=1, source_target_pairs={{0,2},{1,3},{2,0},{3,1},{4,6},{5,7},{6,4},{7,5},{8,10},{9,11},{10,... | collective-permute-start | bytes 61448 | tf_op jit(solution)/shard_map/ppermute | solution.py:239
  24.5 3.4 %collective-permute-start.11 = (bf16[8,1280]{1,0:T(8,128)(2,1)S(1)}, bf16[8,1280]{1,0:T(8,128)(2,1)S(1)}, u32[]{:S(2)}, u32[]{:S(2)}) collective-permute-start(bf16[8,1280]{1,0:T(8,128)(2,1)S(1)} %get-tuple-element.24), channel_id=1, source_target_pairs={{0,3},{1,2},{2,1},{3,0},{4,7},{5,6},{6,5},{7,4},{8,11},{9,10},{10,... | collective-permute-start | bytes 61448 | tf_op jit(solution)/shard_map/ppermute | solution.py:239
where the time goes:
time: 28.8 us; the launch traced here: 28.6 us
  starting transfers between devices  13.8 us (48%)
  waiting for transfers between devices  7.09 us (25%)
  Pallas kernels  4.48 us (16%)
  local copies, waits for them, and re-layouts  1.65 us (6%)
  between operations  0.98 us (3%)
  other arithmetic  0.62 us (2%)
    ppermute x12, starting transfers between devices, permute(): lax.ppermute(x, axis, [(i, i ^ bits) for i in range(lax.axis_size(axis))])  13.8 us
    ppermute x12, waiting for transfers between devices, permute(): lax.ppermute(x, axis, [(i, i ^ bits) for i in range(lax.axis_size(axis))])  7.09 us
    unnamed x24, local copies, waits for them, and re-layouts  1.65 us
    pallas_call x1, Pallas kernels, body(): call(functools.partial(attend_kernel, groups, shares), [VMEM] * (groups +...  1.42 us
    pallas_call x1, Pallas kernels, body(): call(cache_kernel, [SMEM] * 2 + [VMEM] * 5 + [ANY], pltpu.VMEM((2 * up(ro...  1.38 us
    pallas_call x1, Pallas kernels, body(): call(functools.partial(project_kernel, near, True, False), [VMEM] * (len(...  0.82 us
    convert_element_type x1, other arithmetic, body(): return summed.astype(bf16)  0.62 us
  transfers between devices with their start and end apart: 12, of which 4 were waited for; matrix products, arithmetic and copies ran while one was open for 0% of the time, Pallas kernels for 11%

commit v1 on v0

--- a/solution.py
+++ b/solution.py
@@ -185,8 +185,8 @@
     tokens = attended_ref.shape[0] // groups
     per = PER_HEAD * tokens
     rows = heads * per
-    for k, kv in enumerate(kvs):
-        first = pl.multiple_of((me_dp ^ k) * memory, memory)
+    for bits, kv in zip(relatives(groups), kvs):
+        first = pl.multiple_of((me_dp ^ bits) * memory, memory)
         k_ref[pl.ds(first, memory), :] = kv[0:memory, :].astype(k_ref.dtype)
         v_ref[pl.ds(first, memory), :] = kv[memory : 2 * memory, :].astype(v_ref.dtype)
     s = nt(q_ref[...], k_ref[...].astype(bf16)) * INV + bias_ref[...]
@@ -196,8 +196,8 @@
     shrink = jnp.exp(old_top - top)
     total = jnp.sum(p, axis=1, keepdims=True) + shrink * old_total
     acc = nn(p.astype(bf16), v_ref[...].astype(bf16))
-    for k in range(groups):
-        at = pl.multiple_of((me_dp ^ k) * tokens, tokens)
+    for k, bits in enumerate(relatives(groups)):
+        at = pl.multiple_of((me_dp ^ bits) * tokens, tokens)
         for j in range(heads):
             a = k * rows + j * per
             block = acc[a : a + per, j * HD : (j + 1) * HD] + old_ref[a : a + per, :] * shrink[a : a + per]
@@ -235,12 +235,16 @@
     return [pltpu.with_memory_space_constraint(x, pltpu.HBM) for x in arrays]
 
 
+def relatives(n):
+    return [*range(n // 2), *range(n - 1, n // 2 - 1, -1)]
+
+
 def permute(x, axis, bits):
     return lax.ppermute(x, axis, [(i, i ^ bits) for i in range(lax.axis_size(axis))])
 
 
 def others(x, axis):
-    return [x] + [permute(x, axis, bits) for bits in range(1, lax.axis_size(axis))]
+    return [permute(x, axis, bits) if bits else x for bits in relatives(lax.axis_size(axis))]
 
 
 def passed_on(x, axis):
@@ -275,15 +279,9 @@
     rows = (cols // HD) * PER_HEAD * tokens
     every = memory_sections.shape[0]
 
-    hidden = passed_on(memory_hidden, "tp")
-    opened = call(
-        lambda *refs: None,
-        [ANY],
-        jax.ShapeDtypeStruct((8, HD), f32),
-        [],
-        COVER,
-        0,
-    )(hidden[1])
+    gate = call(lambda *refs: None, [], jax.ShapeDtypeStruct((8, HD), f32), [], COVER, 0)()
+    own, gate = lax.optimization_barrier((memory_hidden, gate))
+    hidden = passed_on(own, "tp")
     part = call(
         cache_kernel,
         [SMEM] * 2 + [VMEM] * 5 + [ANY],
@@ -291,7 +289,7 @@
         [],
         4 * rows * slots * cols * requests,
         4 * requests * slots * cols,
-    )(cache_lengths, group_sections, queries, new_keys, new_values, cache_keys, cache_values, opened)
+    )(cache_lengths, group_sections, queries, new_keys, new_values, cache_keys, cache_values, gate)
     parts = others(part, "dp")
     near, far = list(range(shares - 1)), [shares - 1]
     partial = call(
@@ -342,7 +340,7 @@
         2 * out_weight.size,
     )(*kvs, *prepared, out_weight)
     summed = pieces[0]
-    for bits in range(1, shares):
+    for bits in range(shares - 1, 0, -1):
         summed = summed + permute(pieces[bits], "tp", bits).astype(f32)
     return summed.astype(bf16)
 

time: 28.8 us -> 27.6 us (0.958)
  local copies, waits for them, and re-layouts: 1.65 us -> 0.91 us
  starting transfers between devices: 13.8 us -> 13.3 us
    unnamed x24 -> x22, local copies, waits for them, and re-layouts: 1.65 us -> 0.91 us
    ppermute x12, starting transfers between devices: 13.8 us -> 13.3 us  [permute(): lax.ppermute(x, axis, [(i, i ^ bits) for i in range(lax.axis_size(axis))])]
  transfers between devices with their start and end apart: 12 -> 12, of which waited for: 4 -> 6; matrix products, arithmetic and copies ran while one was open for 0% -> 0% of each run, Pallas kernels for 11% -> 11%
where the time goes in v1:
time: 27.6 us; the launch traced here: 27.4 us
  starting transfers between devices  13.3 us (48%)
  waiting for transfers between devices  7.25 us (26%)
  Pallas kernels  4.48 us (16%)
  local copies, waits for them, and re-layouts  0.91 us (3%)
  between operations  0.84 us (3%)
  other arithmetic  0.62 us (2%)
    ppermute x12, starting transfers between devices, permute(): lax.ppermute(x, axis, [(i, i ^ bits) for i in range(lax.axis_size(axis))])  13.3 us
    ppermute x12, waiting for transfers between devices, permute(): lax.ppermute(x, axis, [(i, i ^ bits) for i in range(lax.axis_size(axis))])  7.25 us
    pallas_call x1, Pallas kernels, body(): call(functools.partial(attend_kernel, groups, shares), [VMEM] * (groups +...  1.42 us
    pallas_call x1, Pallas kernels, body(): call(cache_kernel, [SMEM] * 2 + [VMEM] * 5 + [ANY], pltpu.VMEM((2 * up(ro...  1.38 us
    unnamed x22, local copies, waits for them, and re-layouts  0.91 us
    pallas_call x1, Pallas kernels, body(): call(functools.partial(project_kernel, near, True, False), [VMEM] * (len(...  0.82 us
    convert_element_type x1, other arithmetic, body(): return summed.astype(bf16)  0.62 us
  transfers between devices with their start and end apart: 12, of which 6 were waited for; matrix products, arithmetic and copies ran while one was open for 0% of the time, Pallas kernels for 11%

profile of v1, /device:TPU:0, one launch (start us, length us, event | category | flops | bytes accessed | tf_op | source)
XLA Modules:
  0.0 27.4 jit_solution(10907938074851818952)
XLA Ops:
  0.0 0.0 copy-start.9
  0.0 0.0 copy-start.5
  0.0 0.0 copy-start.4
  0.0 0.0 copy-start
  0.1 0.9 %copy-done.9 = bf16[64,1280]{1,0:T(8,128)(2,1)S(1)} copy-done((bf16[64,1280]{1,0:T(8,128)(2,1)S(1)}, bf16[64,1280]{1,0:T(8,128)(2,1)}, u32[]{:S(2)}) %copy-start.9) | copy-done | bytes 163864
  0.9 2.9 %collective-permute-start = (bf16[64,1280]{1,0:T(8,128)(2,1)S(1)}, bf16[64,1280]{1,0:T(8,128)(2,1)S(1)}, u32[]{:S(2)}, u32[]{:S(2)}) collective-permute-start(bf16[64,1280]{1,0:T(8,128)(2,1)S(1)} %copy-done.9), channel_id=1, source_target_pairs={{0,2},{1,3},{2,0},{3,1},{4,6},{5,7},{6,4},{7,5},{8,10},{9,11},{10,... | collective-permute-start | bytes 491528 | tf_op jit(solution)/shard_map/ppermute | solution.py:243
  3.9 0.0 collective-permute-start.2
  4.5 0.0 copy-done.8
  4.5 0.0 copy-done.3
  4.5 0.0 copy-done.2
  4.5 0.0 copy-done.6
  4.6 0.0 copy-done.5
  4.6 0.0 copy-done.4
  4.6 1.4 %shard_map.121.refs_0_ = bf16[176,128]{1,0:T(8,128)(2,1)S(1)} custom-call(s32[4]{0:T(128)S(1)} %copy-done.8, s32[1]{0:T(128)S(6)} %copy.13.group_ref, bf16[8,1280]{1,0:T(8,128)(2,1)S(1)} %copy-done.4, bf16[8,256]{1,0:T(8,128)(2,1)S(1)} %copy-done.5, bf16[8,256]{1,0:T(8,128)(2,1)S(1)} %copy-done.6, bf16[4,512,256]{2,1,0:T(8,128)(2,1)S(1)} %copy-done.2, ...), custom_call_target="tpu_custom_call" | custom-call | flops 167772160 | bytes 2097152 | tf_op jit(solution)/shard_map/pallas_call | solution.py:285
  6.0 0.0 copy-start.7
  6.0 2.7 %collective-permute-start.8 = (bf16[176,128]{1,0:T(8,128)(2,1)S(1)}, bf16[176,128]{1,0:T(8,128)(2,1)S(1)}, u32[]{:S(2)}, u32[]{:S(2)}) collective-permute-start(bf16[176,128]{1,0:T(8,128)(2,1)S(1)} %shard_map.121.refs_0_), channel_id=1, source_target_pairs={{0,8},{4,12},{8,0},{12,4},{1,9},{5,13},{9,1},{13,5},{2,10},{6,14},... | collective-permute-start | bytes 135176 | tf_op jit(solution)/shard_map/ppermute | solution.py:243
  8.6 1.3 %collective-permute-start.7 = (bf16[176,128]{1,0:T(8,128)(2,1)S(1)}, bf16[176,128]{1,0:T(8,128)(2,1)S(1)}, u32[]{:S(2)}, u32[]{:S(2)}) collective-permute-start(bf16[176,128]{1,0:T(8,128)(2,1)S(1)} %shard_map.121.refs_0_), channel_id=1, source_target_pairs={{0,12},{4,8},{8,4},{12,0},{1,13},{5,9},{9,5},{13,1},{2,14},{6,10},... | collective-permute-start | bytes 135176 | tf_op jit(solution)/shard_map/ppermute | solution.py:243
  10.0 0.2 collective-permute-start.6
  10.2 0.0 collective-permute-done.refs_2_
  10.2 0.0 collective-permute-start.1
  10.2 0.0 collective-permute-done.2.refs_1_
  10.2 0.0 copy-done
  10.2 0.8 %shard_map.119 = (f32[128,256]{1,0:T(8,128)S(1)}, f32[64,128]{1,0:T(8,128)S(1)}) custom-call(bf16[64,1280]{1,0:T(8,128)(2,1)S(1)} %copy-done.9, bf16[64,1280]{1,0:T(8,128)(2,1)S(1)} %collective-permute-done.2.refs_1_, bf16[64,1280]{1,0:T(8,128)(2,1)S(1)} %collective-permute-done.refs_2_, bf16[2,5120,256]{2,1,0:T(8,128)(2,1)S(1)} %copy-done), custom_call_target="tpu_custom_call" | custom-call | flops 68719476736 | bytes 5242880 | tf_op jit(solution)/shard_map/pallas_call | solution.py:295
  11.0 0.0 copy-start.10
  11.1 0.0 copy-start.1
  11.1 0.5 %collective-permute-done.1.refs_0_ = bf16[64,1280]{1,0:T(8,128)(2,1)S(1)} collective-permute-done((bf16[64,1280]{1,0:T(8,128)(2,1)S(1)}, bf16[64,1280]{1,0:T(8,128)(2,1)S(1)}, u32[]{:S(2)}, u32[]{:S(2)}) %collective-permute-start.1) | collective-permute-done | bytes 163872 | tf_op jit(solution)/shard_map/ppermute | solution.py:243
  11.6 0.0 copy-done.7
  11.6 0.4 %shard_map.120.refs_0_ = bf16[128,256]{1,0:T(8,128)(2,1)S(1)} custom-call(bf16[64,1280]{1,0:T(8,128)(2,1)S(1)} %collective-permute-done.1.refs_0_, bf16[2,5120,256]{2,1,0:T(8,128)(2,1)S(1)} %copy-done, f32[128,256]{1,0:T(8,128)S(1)} %get-tuple-element.18.refs_2_, f32[64,128]{1,0:T(8,128)S(1)} %get-tuple-element.19.refs_3_, bf16[2,256]{1,0:T(2,128)(2,1)S(1)} %copy-done.7), custom_call_target="tpu_custom_call" | custom-call | flops 83886080 | bytes 1310720 | tf_op jit(solution)/shard_map/pallas_call | solution.py:303
  12.0 2.9 %collective-permute-start.5 = (bf16[128,256]{1,0:T(8,128)(2,1)S(1)}, bf16[128,256]{1,0:T(8,128)(2,1)S(1)}, u32[]{:S(2)}, u32[]{:S(2)}) collective-permute-start(bf16[128,256]{1,0:T(8,128)(2,1)S(1)} %shard_map.120.refs_0_), channel_id=1, source_target_pairs={{0,8},{4,12},{8,0},{12,4},{1,9},{5,13},{9,1},{13,5},{2,10},{6,14},... | collective-permute-start | bytes 196616 | tf_op jit(solution)/shard_map/ppermute | solution.py:243
  14.9 1.3 %collective-permute-start.4 = (bf16[128,256]{1,0:T(8,128)(2,1)S(1)}, bf16[128,256]{1,0:T(8,128)(2,1)S(1)}, u32[]{:S(2)}, u32[]{:S(2)}) collective-permute-start(bf16[128,256]{1,0:T(8,128)(2,1)S(1)} %shard_map.120.refs_0_), channel_id=1, source_target_pairs={{0,12},{4,8},{8,4},{12,0},{1,13},{5,9},{9,5},{13,1},{2,14},{6,10},... | collective-permute-start | bytes 196616 | tf_op jit(solution)/shard_map/ppermute | solution.py:243
  16.2 0.0 collective-permute-done.8.refs_3_
  16.2 0.0 collective-permute-start.3
  16.2 0.0 collective-permute-done.7.refs_2_
  16.2 0.0 collective-permute-done.6.refs_1_
  16.2 0.0 copy-done.10
  16.2 0.5 %shard_map.122 = (bf16[320,256]{1,0:T(8,128)(2,1)S(1)}, f32[320,256]{1,0:T(8,128)S(1)}, f32[320,128]{1,0:T(8,128)S(1)}, f32[320,128]{1,0:T(8,128)S(1)}) custom-call(bf16[176,128]{1,0:T(8,128)(2,1)S(1)} %shard_map.121.refs_0_, bf16[176,128]{1,0:T(8,128)(2,1)S(1)} %collective-permute-done.6.refs_1_, bf16[176,128]{1,0:T(8,128)(2,1)S(1)} %collective-permute-done.7.refs_2_, ...), custom_call_target="tpu_custom_call" | custom-call | flops 1073741824 | tf_op jit(solution)/shard_map/pallas_call | solution.py:312
  16.7 2.2 %collective-permute-done.5.refs_3_ = bf16[128,256]{1,0:T(8,128)(2,1)S(1)} collective-permute-done((bf16[128,256]{1,0:T(8,128)(2,1)S(1)}, bf16[128,256]{1,0:T(8,128)(2,1)S(1)}, u32[]{:S(2)}, u32[]{:S(2)}) %collective-permute-start.5) | collective-permute-done | bytes 65568 | tf_op jit(solution)/shard_map/ppermute | solution.py:243
  18.9 2.3 %collective-permute-done.4.refs_2_ = bf16[128,256]{1,0:T(8,128)(2,1)S(1)} collective-permute-done((bf16[128,256]{1,0:T(8,128)(2,1)S(1)}, bf16[128,256]{1,0:T(8,128)(2,1)S(1)}, u32[]{:S(2)}, u32[]{:S(2)}) %collective-permute-start.4) | collective-permute-done | bytes 65568 | tf_op jit(solution)/shard_map/ppermute | solution.py:243
  21.3 0.2 collective-permute-done.3.refs_1_
  21.4 0.0 copy-done.1
  21.4 1.4 %shard_map.123 = (f32[8,1280]{1,0:T(8,128)S(1)}, bf16[8,1280]{1,0:T(8,128)(2,1)S(1)}, bf16[8,1280]{1,0:T(8,128)(2,1)S(1)}, bf16[8,1280]{1,0:T(8,128)(2,1)S(1)}) custom-call(bf16[128,256]{1,0:T(8,128)(2,1)S(1)} %shard_map.120.refs_0_, bf16[128,256]{1,0:T(8,128)(2,1)S(1)} %collective-permute-done.3.refs_1_, ...), custom_call_target="tpu_custom_call" | custom-call | flops 104857600 | bytes 3276800 | tf_op jit(solution)/shard_map/pallas_call | solution.py:329
  22.9 0.1 collective-permute-start.9
  22.9 1.3 %collective-permute-start.10 = (bf16[8,1280]{1,0:T(8,128)(2,1)S(1)}, bf16[8,1280]{1,0:T(8,128)(2,1)S(1)}, u32[]{:S(2)}, u32[]{:S(2)}) collective-permute-start(bf16[8,1280]{1,0:T(8,128)(2,1)S(1)} %get-tuple-element.27), channel_id=1, source_target_pairs={{0,2},{1,3},{2,0},{3,1},{4,6},{5,7},{6,4},{7,5},{8,10},{9,11},{10,... | collective-permute-start | bytes 61448 | tf_op jit(solution)/shard_map/ppermute | solution.py:243
  24.3 0.5 %collective-permute-start.11 = (bf16[8,1280]{1,0:T(8,128)(2,1)S(1)}, bf16[8,1280]{1,0:T(8,128)(2,1)S(1)}, u32[]{:S(2)}, u32[]{:S(2)}) collective-permute-start(bf16[8,1280]{1,0:T(8,128)(2,1)S(1)} %get-tuple-element.28), channel_id=1, source_target_pairs={{0,1},{1,0},{2,3},{3,2},{4,5},{5,4},{6,7},{7,6},{8,9},{9,8},{10,11... | collective-permute-start | bytes 61448 | tf_op jit(solution)/shard_map/ppermute | solution.py:243
  24.8 1.4 %collective-permute-done.9 = bf16[8,1280]{1,0:T(8,128)(2,1)S(1)} collective-permute-done((bf16[8,1280]{1,0:T(8,128)(2,1)S(1)}, bf16[8,1280]{1,0:T(8,128)(2,1)S(1)}, u32[]{:S(2)}, u32[]{:S(2)}) %collective-permute-start.9) | collective-permute-done | bytes 20512 | tf_op jit(solution)/shard_map/ppermute | solution.py:243
  26.2 0.6 %collective-permute-done.10 = bf16[8,1280]{1,0:T(8,128)(2,1)S(1)} collective-permute-done((bf16[8,1280]{1,0:T(8,128)(2,1)S(1)}, bf16[8,1280]{1,0:T(8,128)(2,1)S(1)}, u32[]{:S(2)}, u32[]{:S(2)}) %collective-permute-start.10) | collective-permute-done | bytes 20512 | tf_op jit(solution)/shard_map/ppermute | solution.py:243
  26.8 0.0 collective-permute-done.11
  26.8 0.6 %add_convert_fusion = bf16[8,1280]{1,0:T(8,128)(2,1)} fusion(bf16[8,1280]{1,0:T(8,128)(2,1)S(1)} %collective-permute-done.11, bf16[8,1280]{1,0:T(8,128)(2,1)S(1)} %collective-permute-done.10, f32[8,1280]{1,0:T(8,128)S(1)} %get-tuple-element.25, bf16[8,1280]{1,0:T(8,128)(2,1)S(1)} %collective-permute-done.9), kind=kLoop, calls=%fused_computation | loop fusion | flops 71680 | bytes 122880 | tf_op jit(solution)/shard_map/convert_element_type | solution.py:345
  (5 shorter events, 0.0 us)
Async XLA Ops:
  0.0 0.9 %copy-start.9 = (bf16[64,1280]{1,0:T(8,128)(2,1)S(1)}, bf16[64,1280]{1,0:T(8,128)(2,1)}, u32[]{:S(2)}) copy-start(bf16[64,1280]{1,0:T(8,128)(2,1)} %refs_0_) | copy-start | bytes 491524
  0.0 4.5 %copy-start.8 = (s32[4]{0:T(128)S(1)}, s32[4]{0:T(128)}, u32[]{:S(2)}) copy-start(s32[4]{0:T(128)} %lens_ref.1) | copy-start | bytes 52
  0.0 4.5 %copy-start.3 = (bf16[4,512,256]{2,1,0:T(8,128)(2,1)S(1)}, bf16[4,512,256]{2,1,0:T(8,128)(2,1)}, u32[]{:S(2)}) copy-start(bf16[4,512,256]{2,1,0:T(8,128)(2,1)} %cv_ref.1) | copy-start | bytes 3145732
  0.0 4.5 %copy-start.2 = (bf16[4,512,256]{2,1,0:T(8,128)(2,1)S(1)}, bf16[4,512,256]{2,1,0:T(8,128)(2,1)}, u32[]{:S(2)}) copy-start(bf16[4,512,256]{2,1,0:T(8,128)(2,1)} %ck_ref.1) | copy-start | bytes 3145732
  0.0 4.5 %copy-start.6 = (bf16[8,256]{1,0:T(8,128)(2,1)S(1)}, bf16[8,256]{1,0:T(8,128)(2,1)}, u32[]{:S(2)}) copy-start(bf16[8,256]{1,0:T(8,128)(2,1)} %nv_ref.1) | copy-start | bytes 12292
  0.0 4.5 %copy-start.5 = (bf16[8,256]{1,0:T(8,128)(2,1)S(1)}, bf16[8,256]{1,0:T(8,128)(2,1)}, u32[]{:S(2)}) copy-start(bf16[8,256]{1,0:T(8,128)(2,1)} %nk_ref.1) | copy-start | bytes 12292
  0.0 4.5 %copy-start.4 = (bf16[8,1280]{1,0:T(8,128)(2,1)S(1)}, bf16[8,1280]{1,0:T(8,128)(2,1)}, u32[]{:S(2)}) copy-start(bf16[8,1280]{1,0:T(8,128)(2,1)} %q_ref.1) | copy-start | bytes 61444
  0.0 10.2 %copy-start = (bf16[2,5120,256]{2,1,0:T(8,128)(2,1)S(1)}, bf16[2,5120,256]{2,1,0:T(8,128)(2,1)}, u32[]{:S(2)}) copy-start(bf16[2,5120,256]{2,1,0:T(8,128)(2,1)} %refs_1_.1) | copy-start | bytes 15728644
  0.9 9.3 %collective-permute-start = (bf16[64,1280]{1,0:T(8,128)(2,1)S(1)}, bf16[64,1280]{1,0:T(8,128)(2,1)S(1)}, u32[]{:S(2)}, u32[]{:S(2)}) collective-permute-start(bf16[64,1280]{1,0:T(8,128)(2,1)S(1)} %copy-done.9), channel_id=1, source_target_pairs={{0,2},{1,3},{2,0},{3,1},{4,6},{5,7},{6,4},{7,5},{8,10},{9,11},{10,... | collective-permute-start | bytes 491528 | tf_op jit(solution)/shard_map/ppermute | solution.py:243
  3.9 6.4 %collective-permute-start.2 = (bf16[64,1280]{1,0:T(8,128)(2,1)S(1)}, bf16[64,1280]{1,0:T(8,128)(2,1)S(1)}, u32[]{:S(2)}, u32[]{:S(2)}) collective-permute-start(bf16[64,1280]{1,0:T(8,128)(2,1)S(1)} %copy-done.9), channel_id=1, source_target_pairs={{0,1},{1,0},{2,3},{3,2},{4,5},{5,4},{6,7},{7,6},{8,9},{9,8},{10,11... | collective-permute-start | bytes 491528 | tf_op jit(solution)/shard_map/ppermute | solution.py:243
  6.0 5.6 %copy-start.7 = (bf16[2,256]{1,0:T(2,128)(2,1)S(1)}, bf16[2,256]{1,0:T(2,128)(2,1)}, u32[]{:S(2)}) copy-start(bf16[2,256]{1,0:T(2,128)(2,1)} %refs_4_.1) | copy-start | bytes 3076
  6.0 10.2 %collective-permute-start.8 = (bf16[176,128]{1,0:T(8,128)(2,1)S(1)}, bf16[176,128]{1,0:T(8,128)(2,1)S(1)}, u32[]{:S(2)}, u32[]{:S(2)}) collective-permute-start(bf16[176,128]{1,0:T(8,128)(2,1)S(1)} %shard_map.121.refs_0_), channel_id=1, source_target_pairs={{0,8},{4,12},{8,0},{12,4},{1,9},{5,13},{9,1},{13,5},{2,10},{6,14},... | collective-permute-start | bytes 135176 | tf_op jit(solution)/shard_map/ppermute | solution.py:243
  8.6 7.6 %collective-permute-start.7 = (bf16[176,128]{1,0:T(8,128)(2,1)S(1)}, bf16[176,128]{1,0:T(8,128)(2,1)S(1)}, u32[]{:S(2)}, u32[]{:S(2)}) collective-permute-start(bf16[176,128]{1,0:T(8,128)(2,1)S(1)} %shard_map.121.refs_0_), channel_id=1, source_target_pairs={{0,12},{4,8},{8,4},{12,0},{1,13},{5,9},{9,5},{13,1},{2,14},{6,10},... | collective-permute-start | bytes 135176 | tf_op jit(solution)/shard_map/ppermute | solution.py:243
  10.0 6.2 %collective-permute-start.6 = (bf16[176,128]{1,0:T(8,128)(2,1)S(1)}, bf16[176,128]{1,0:T(8,128)(2,1)S(1)}, u32[]{:S(2)}, u32[]{:S(2)}) collective-permute-start(bf16[176,128]{1,0:T(8,128)(2,1)S(1)} %shard_map.121.refs_0_), channel_id=1, source_target_pairs={{0,4},{4,0},{8,12},{12,8},{1,5},{5,1},{9,13},{13,9},{2,6},{6,2},{1... | collective-permute-start | bytes 135176 | tf_op jit(solution)/shard_map/ppermute | solution.py:243
  10.2 1.4 %collective-permute-start.1 = (bf16[64,1280]{1,0:T(8,128)(2,1)S(1)}, bf16[64,1280]{1,0:T(8,128)(2,1)S(1)}, u32[]{:S(2)}, u32[]{:S(2)}) collective-permute-start(bf16[64,1280]{1,0:T(8,128)(2,1)S(1)} %collective-permute-done.refs_2_), channel_id=1, source_target_pairs={{0,1},{1,0},{2,3},{3,2},{4,5},{5,4},{6,7},{7,6},{8,9},{9,8},{10,11... | collective-permute-start | bytes 491528 | tf_op jit(solution)/shard_map/ppermute | solution.py:243
  11.0 5.2 %copy-start.10 = (s32[256]{0:T(256)S(1)}, s32[256]{0:T(256)}, u32[]{:S(2)}) copy-start(s32[256]{0:T(256)} %param.15) | copy-start | bytes 3076
  11.1 10.4 %copy-start.1 = (bf16[1280,1280]{1,0:T(8,128)(2,1)S(1)}, bf16[1280,1280]{1,0:T(8,128)(2,1)}, u32[]{:S(2)}) copy-start(bf16[1280,1280]{1,0:T(8,128)(2,1)} %refs_8_.1) | copy-start | bytes 9830404
  12.0 6.9 %collective-permute-start.5 = (bf16[128,256]{1,0:T(8,128)(2,1)S(1)}, bf16[128,256]{1,0:T(8,128)(2,1)S(1)}, u32[]{:S(2)}, u32[]{:S(2)}) collective-permute-start(bf16[128,256]{1,0:T(8,128)(2,1)S(1)} %shard_map.120.refs_0_), channel_id=1, source_target_pairs={{0,8},{4,12},{8,0},{12,4},{1,9},{5,13},{9,1},{13,5},{2,10},{6,14},... | collective-permute-start | bytes 196616 | tf_op jit(solution)/shard_map/ppermute | solution.py:243
  14.9 6.4 %collective-permute-start.4 = (bf16[128,256]{1,0:T(8,128)(2,1)S(1)}, bf16[128,256]{1,0:T(8,128)(2,1)S(1)}, u32[]{:S(2)}, u32[]{:S(2)}) collective-permute-start(bf16[128,256]{1,0:T(8,128)(2,1)S(1)} %shard_map.120.refs_0_), channel_id=1, source_target_pairs={{0,12},{4,8},{8,4},{12,0},{1,13},{5,9},{9,5},{13,1},{2,14},{6,10},... | collective-permute-start | bytes 196616 | tf_op jit(solution)/shard_map/ppermute | solution.py:243
  16.2 5.2 %collective-permute-start.3 = (bf16[128,256]{1,0:T(8,128)(2,1)S(1)}, bf16[128,256]{1,0:T(8,128)(2,1)S(1)}, u32[]{:S(2)}, u32[]{:S(2)}) collective-permute-start(bf16[128,256]{1,0:T(8,128)(2,1)S(1)} %shard_map.120.refs_0_), channel_id=1, source_target_pairs={{0,4},{4,0},{8,12},{12,8},{1,5},{5,1},{9,13},{13,9},{2,6},{6,2},{1... | collective-permute-start | bytes 196616 | tf_op jit(solution)/shard_map/ppermute | solution.py:243
  22.9 3.3 %collective-permute-start.9 = (bf16[8,1280]{1,0:T(8,128)(2,1)S(1)}, bf16[8,1280]{1,0:T(8,128)(2,1)S(1)}, u32[]{:S(2)}, u32[]{:S(2)}) collective-permute-start(bf16[8,1280]{1,0:T(8,128)(2,1)S(1)} %get-tuple-element.26), channel_id=1, source_target_pairs={{0,3},{1,2},{2,1},{3,0},{4,7},{5,6},{6,5},{7,4},{8,11},{9,10},{10,... | collective-permute-start | bytes 61448 | tf_op jit(solution)/shard_map/ppermute | solution.py:243
  22.9 3.8 %collective-permute-start.10 = (bf16[8,1280]{1,0:T(8,128)(2,1)S(1)}, bf16[8,1280]{1,0:T(8,128)(2,1)S(1)}, u32[]{:S(2)}, u32[]{:S(2)}) collective-permute-start(bf16[8,1280]{1,0:T(8,128)(2,1)S(1)} %get-tuple-element.27), channel_id=1, source_target_pairs={{0,2},{1,3},{2,0},{3,1},{4,6},{5,7},{6,4},{7,5},{8,10},{9,11},{10,... | collective-permute-start | bytes 61448 | tf_op jit(solution)/shard_map/ppermute | solution.py:243
  24.3 2.5 %collective-permute-start.11 = (bf16[8,1280]{1,0:T(8,128)(2,1)S(1)}, bf16[8,1280]{1,0:T(8,128)(2,1)S(1)}, u32[]{:S(2)}, u32[]{:S(2)}) collective-permute-start(bf16[8,1280]{1,0:T(8,128)(2,1)S(1)} %get-tuple-element.28), channel_id=1, source_target_pairs={{0,1},{1,0},{2,3},{3,2},{4,5},{5,4},{6,7},{7,6},{8,9},{9,8},{10,11... | collective-permute-start | bytes 61448 | tf_op jit(solution)/shard_map/ppermute | solution.py:243

commit v2 on v1

--- a/solution.py
+++ b/solution.py
@@ -18,7 +18,7 @@
 masked_score = -1e30
 bf16 = jnp.bfloat16
 COVER = 1 << 36
-PCOVER = 1 << 30
+PCOVER = 1 << 10
 f32 = jnp.float32
 
 TOP, TOTAL, SECTION = 0, 3, 5
@@ -62,7 +62,11 @@
     return -(-n // to) * to
 
 
-def cache_kernel(lens_ref, group_ref, q_ref, nk_ref, nv_ref, ck_ref, cv_ref, after, out_ref):
+def open_kernel(group_ref, after, out_ref):
+    out_ref[...] = jnp.full(out_ref.shape, group_ref[0].astype(f32))
+
+
+def cache_kernel(lens_ref, section_ref, q_ref, nk_ref, nv_ref, ck_ref, cv_ref, out_ref):
     requests, slots, cols = ck_ref.shape
     heads = cols // HD
     tokens = requests * NEW
@@ -104,7 +108,7 @@
     out_ref[seg : seg + rows, :] = (mine / total).astype(bf16)
 
     lane = lax.broadcasted_iota(jnp.int32, (rows, HD), 1)
-    stats = jnp.where(lane == SECTION, group_ref[0].astype(f32), 0.0)
+    stats = jnp.where(lane == SECTION, section_ref[0:1, :], 0.0)
     for i, piece in enumerate(split(top, 3)):
         stats = jnp.where(lane == TOP + i, piece, stats)
     for i, piece in enumerate(split(total, 2)):
@@ -219,13 +223,14 @@
 PARAMS = pltpu.CompilerParams(vmem_limit_bytes=24 * 1024 * 1024)
 
 
-def call(kernel, in_specs, out_shape, scratch, flops, bytes_accessed):
+def call(kernel, in_specs, out_shape, scratch, flops, bytes_accessed, aliases={}):
     return pl.pallas_call(
         kernel,
         in_specs=in_specs,
         out_shape=out_shape,
         out_specs=jax.tree.map(lambda _: VMEM, out_shape),
         scratch_shapes=scratch,
+        input_output_aliases=aliases,
         compiler_params=PARAMS,
         cost_estimate=pl.CostEstimate(flops=flops, bytes_accessed=bytes_accessed, transcendentals=0),
     )
@@ -236,7 +241,7 @@
 
 
 def relatives(n):
-    return [*range(n // 2), *range(n - 1, n // 2 - 1, -1)]
+    return [0, *range(n // 2, n), *range(1, n // 2)]
 
 
 def permute(x, axis, bits):
@@ -280,17 +285,20 @@
     every = memory_sections.shape[0]
 
     gate = call(lambda *refs: None, [], jax.ShapeDtypeStruct((8, HD), f32), [], COVER, 0)()
-    own, gate = lax.optimization_barrier((memory_hidden, gate))
+    group, gate = lax.optimization_barrier((group_sections, gate))
+    section = call(open_kernel, [SMEM, ANY], pltpu.VMEM((8, HD), f32), [], 1 << 10, 0)(group, gate)
+    own, section = lax.optimization_barrier((memory_hidden, section))
     hidden = passed_on(own, "tp")
     part = call(
         cache_kernel,
-        [SMEM] * 2 + [VMEM] * 5 + [ANY],
+        [SMEM] + [VMEM] * 6,
         pltpu.VMEM((2 * up(rows, 16) + STATS, HD), bf16),
         [],
         4 * rows * slots * cols * requests,
         4 * requests * slots * cols,
-    )(cache_lengths, group_sections, queries, new_keys, new_values, cache_keys, cache_values, gate)
-    parts = others(part, "dp")
+    )(cache_lengths, section, queries, new_keys, new_values, cache_keys, cache_values)
+    part_far = permute(part, "dp", groups // 2)
+    part_near = {bits: permute(part, "dp", bits) for bits in range(1, groups // 2)}
     near, far = list(range(shares - 1)), [shares - 1]
     partial = call(
         functools.partial(project_kernel, near, True, False),
@@ -309,6 +317,19 @@
         4 * D * cols // shares,
     )(hidden[far[0]], kv_weight, *partial, kv_bias)
     kvs = others(kv, "dp")
+    part_far = call(
+        lambda x, after, out: None,
+        [VMEM, ANY],
+        pltpu.VMEM(part.shape, bf16),
+        [],
+        COVER,
+        0,
+        {0: 0},
+    )(part_far, kv)
+    parts = {0: part, **part_near}
+    for bits in range(groups // 2):
+        parts[groups // 2 + bits] = permute(part_far, "dp", bits) if bits else part_far
+    parts = [parts[bits] for bits in relatives(groups)]
     prepared = call(
         functools.partial(prepare_kernel, cols // HD),
         [VMEM] * (groups + 1),

time: 27.6 us -> 28.4 us (1.029)
  starting transfers between devices: 13.3 us -> 14.3 us
  local copies, waits for them, and re-layouts: 0.91 us -> 0.1 us
  waiting for transfers between devices: 7.25 us -> 7.65 us
    ppermute x12, starting transfers between devices: 13.3 us -> 14.3 us  [permute(): lax.ppermute(x, axis, [(i, i ^ bits) for i in range(lax.axis_size(axis))])]
    unnamed x22, local copies, waits for them, and re-layouts: 0.91 us -> 0.1 us
    ppermute x12, waiting for transfers between devices: 7.25 us -> 7.65 us  [permute(): lax.ppermute(x, axis, [(i, i ^ bits) for i in range(lax.axis_size(axis))])]
    pallas_call x1 -> x3, Pallas kernels: 1.38 us -> 1.38 us  [the longest x1 1.38 us: body(): call(cache_kernel, [SMEM] + [VMEM] * 6, pltpu.VMEM((2 * up(rows, 16) + ST...]
  transfers between devices with their start and end apart: 12 -> 12, of which waited for: 6 -> 4; matrix products, arithmetic and copies ran while one was open for 0% -> 0% of each run, Pallas kernels for 11% -> 11%
where the time goes in v2:
time: 28.4 us; the launch traced here: 28.2 us
  starting transfers between devices  14.3 us (50%)
  waiting for transfers between devices  7.65 us (27%)
  Pallas kernels  4.48 us (16%)
  between operations  0.98 us (3%)
  other arithmetic  0.62 us (2%)
    ppermute x12, starting transfers between devices, permute(): lax.ppermute(x, axis, [(i, i ^ bits) for i in range(lax.axis_size(axis))])  14.3 us
    ppermute x12, waiting for transfers between devices, permute(): lax.ppermute(x, axis, [(i, i ^ bits) for i in range(lax.axis_size(axis))])  7.65 us
    pallas_call x1, Pallas kernels, body(): call(functools.partial(attend_kernel, groups, shares), [VMEM] * (groups +...  1.43 us
    pallas_call x1, Pallas kernels, body(): call(cache_kernel, [SMEM] + [VMEM] * 6, pltpu.VMEM((2 * up(rows, 16) + ST...  1.38 us
    pallas_call x1, Pallas kernels, body(): call(functools.partial(project_kernel, near, True, False), [VMEM] * (len(...  0.82 us
    convert_element_type x1, other arithmetic, body(): return summed.astype(bf16)  0.62 us
  transfers between devices with their start and end apart: 12, of which 4 were waited for; matrix products, arithmetic and copies ran while one was open for 0% of the time, Pallas kernels for 11%

profile of v2, /device:TPU:0, one launch (start us, length us, event | category | flops | bytes accessed | tf_op | source)
XLA Modules:
  0.0 28.2 jit_solution(5602776629953126752)
XLA Ops:
  0.0 0.0 copy-start.10
  0.0 0.0 copy-start.4
  0.0 0.0 copy-start.3
  0.0 0.0 copy-start.9
  0.0 0.0 copy-start
  0.9 0.1 copy-done.10
  0.9 3.0 %collective-permute-start = (bf16[64,1280]{1,0:T(8,128)(2,1)S(1)}, bf16[64,1280]{1,0:T(8,128)(2,1)S(1)}, u32[]{:S(2)}, u32[]{:S(2)}) collective-permute-start(bf16[64,1280]{1,0:T(8,128)(2,1)S(1)} %copy-done.10), channel_id=1, source_target_pairs={{0,2},{1,3},{2,0},{3,1},{4,6},{5,7},{6,4},{7,5},{8,10},{9,11},{10,... | collective-permute-start | bytes 491528 | tf_op jit(solution)/shard_map/ppermute | solution.py:248
  3.9 0.0 collective-permute-start.2
  3.9 0.0 copy-done.4
  3.9 0.0 copy-done.5
  3.9 0.0 copy-done.6
  3.9 0.0 copy-done.2
  3.9 0.0 copy-done.3
  3.9 0.0 copy-done.9
  3.9 1.4 %shard_map.122.refs_0_ = bf16[176,128]{1,0:T(8,128)(2,1)S(1)} custom-call(s32[4]{0:T(128)S(1)} %copy-done.9, f32[8,128]{1,0:T(8,128)S(1)} %shard_map.119.section_ref, bf16[8,1280]{1,0:T(8,128)(2,1)S(1)} %copy-done.4, bf16[8,256]{1,0:T(8,128)(2,1)S(1)} %copy-done.5, bf16[8,256]{1,0:T(8,128)(2,1)S(1)} %copy-done.6, bf16[4,512,256]{2,1,0:T(8,128)(2,1)S(1)} %copy-done.2, ...), custom_call_target="tpu_custom_call" | custom-call | flops 167772160 | bytes 2097152 | tf_op jit(solution)/shard_map/pallas_call | solution.py:292
  5.3 0.0 copy-start.7
  5.3 2.7 %collective-permute-start.6 = (bf16[176,128]{1,0:T(8,128)(2,1)S(1)}, bf16[176,128]{1,0:T(8,128)(2,1)S(1)}, u32[]{:S(2)}, u32[]{:S(2)}) collective-permute-start(bf16[176,128]{1,0:T(8,128)(2,1)S(1)} %shard_map.122.refs_0_), channel_id=1, source_target_pairs={{0,8},{4,12},{8,0},{12,4},{1,9},{5,13},{9,1},{13,5},{2,10},{6,14},... | collective-permute-start | bytes 135176 | tf_op jit(solution)/shard_map/ppermute | solution.py:248
  8.0 1.6 %collective-permute-start.8 = (bf16[176,128]{1,0:T(8,128)(2,1)S(1)}, bf16[176,128]{1,0:T(8,128)(2,1)S(1)}, u32[]{:S(2)}, u32[]{:S(2)}) collective-permute-start(bf16[176,128]{1,0:T(8,128)(2,1)S(1)} %shard_map.122.refs_0_), channel_id=1, source_target_pairs={{0,4},{4,0},{8,12},{12,8},{1,5},{5,1},{9,13},{13,9},{2,6},{6,2},{1... | collective-permute-start | bytes 135176 | tf_op jit(solution)/shard_map/ppermute | solution.py:248
  9.6 0.0 collective-permute-done.refs_2_
  9.6 0.0 collective-permute-start.1
  9.6 0.0 collective-permute-done.2.refs_1_
  9.6 0.0 copy-done
  9.6 0.8 %shard_map.120 = (f32[128,256]{1,0:T(8,128)S(1)}, f32[64,128]{1,0:T(8,128)S(1)}) custom-call(bf16[64,1280]{1,0:T(8,128)(2,1)S(1)} %copy-done.10, bf16[64,1280]{1,0:T(8,128)(2,1)S(1)} %collective-permute-done.2.refs_1_, bf16[64,1280]{1,0:T(8,128)(2,1)S(1)} %collective-permute-done.refs_2_, bf16[2,5120,256]{2,1,0:T(8,128)(2,1)S(1)} %copy-done), custom_call_target="tpu_custom_call" | custom-call | flops 68719476736 | bytes 5242880 | tf_op jit(solution)/shard_map/pallas_call | solution.py:303
  10.4 0.6 %collective-permute-done.1.refs_0_ = bf16[64,1280]{1,0:T(8,128)(2,1)S(1)} collective-permute-done((bf16[64,1280]{1,0:T(8,128)(2,1)S(1)}, bf16[64,1280]{1,0:T(8,128)(2,1)S(1)}, u32[]{:S(2)}, u32[]{:S(2)}) %collective-permute-start.1) | collective-permute-done | bytes 163872 | tf_op jit(solution)/shard_map/ppermute | solution.py:248
  11.0 0.0 copy-done.7
  11.0 0.4 %shard_map.121.after.refs_0_ = bf16[128,256]{1,0:T(8,128)(2,1)S(1)} custom-call(bf16[64,1280]{1,0:T(8,128)(2,1)S(1)} %collective-permute-done.1.refs_0_, bf16[2,5120,256]{2,1,0:T(8,128)(2,1)S(1)} %copy-done, f32[128,256]{1,0:T(8,128)S(1)} %get-tuple-element.22.refs_2_, f32[64,128]{1,0:T(8,128)S(1)} %get-tuple-element.23.refs_3_, bf16[2,256]{1,0:T(2,128)(2,1)S(1)} %copy-done.7), custom_call_target="tpu_custom_call" | custom-call | flops 83886080 | bytes 1310720 | tf_op jit(solution)/shard_map/pallas_call | solution.py:311
  11.4 0.0 copy-start.1
  11.4 1.4 %collective-permute-start.3 = (bf16[128,256]{1,0:T(8,128)(2,1)S(1)}, bf16[128,256]{1,0:T(8,128)(2,1)S(1)}, u32[]{:S(2)}, u32[]{:S(2)}) collective-permute-start(bf16[128,256]{1,0:T(8,128)(2,1)S(1)} %shard_map.121.after.refs_0_), channel_id=1, source_target_pairs={{0,8},{4,12},{8,0},{12,4},{1,9},{5,13},{9,1},{13,5},{2,10},{6,14},... | collective-permute-start | bytes 196616 | tf_op jit(solution)/shard_map/ppermute | solution.py:248
  12.8 1.5 %collective-permute-start.4 = (bf16[128,256]{1,0:T(8,128)(2,1)S(1)}, bf16[128,256]{1,0:T(8,128)(2,1)S(1)}, u32[]{:S(2)}, u32[]{:S(2)}) collective-permute-start(bf16[128,256]{1,0:T(8,128)(2,1)S(1)} %shard_map.121.after.refs_0_), channel_id=1, source_target_pairs={{0,12},{4,8},{8,4},{12,0},{1,13},{5,9},{9,5},{13,1},{2,14},{6,10},... | collective-permute-start | bytes 196616 | tf_op jit(solution)/shard_map/ppermute | solution.py:248
  14.2 0.7 %collective-permute-start.5 = (bf16[128,256]{1,0:T(8,128)(2,1)S(1)}, bf16[128,256]{1,0:T(8,128)(2,1)S(1)}, u32[]{:S(2)}, u32[]{:S(2)}) collective-permute-start(bf16[128,256]{1,0:T(8,128)(2,1)S(1)} %shard_map.121.after.refs_0_), channel_id=1, source_target_pairs={{0,4},{4,0},{8,12},{12,8},{1,5},{5,1},{9,13},{13,9},{2,6},{6,2},{1... | collective-permute-start | bytes 196616 | tf_op jit(solution)/shard_map/ppermute | solution.py:248
  14.9 0.0 collective-permute-done.6.x
  14.9 1.3 %collective-permute-start.7 = (bf16[176,128]{1,0:T(8,128)(2,1)S(1)}, bf16[176,128]{1,0:T(8,128)(2,1)S(1)}, u32[]{:S(2)}, u32[]{:S(2)}) collective-permute-start(bf16[176,128]{1,0:T(8,128)(2,1)S(1)} %shard_map.123.refs_1_), channel_id=1, source_target_pairs={{0,4},{4,0},{8,12},{12,8},{1,5},{5,1},{9,13},{13,9},{2,6},{6,2},{1... | collective-permute-start | bytes 135176 | tf_op jit(solution)/shard_map/ppermute | solution.py:248
  16.3 0.0 collective-permute-done.8.refs_3_
  16.3 5.2 %collective-permute-done.7.refs_2_ = bf16[176,128]{1,0:T(8,128)(2,1)S(1)} collective-permute-done((bf16[176,128]{1,0:T(8,128)(2,1)S(1)}, bf16[176,128]{1,0:T(8,128)(2,1)S(1)}, u32[]{:S(2)}, u32[]{:S(2)}) %collective-permute-start.7) | collective-permute-done | bytes 45088 | tf_op jit(solution)/shard_map/ppermute | solution.py:248
  21.5 0.0 copy-done.8
  21.5 0.5 %shard_map.124 = (bf16[320,256]{1,0:T(8,128)(2,1)S(1)}, f32[320,256]{1,0:T(8,128)S(1)}, f32[320,128]{1,0:T(8,128)S(1)}, f32[320,128]{1,0:T(8,128)S(1)}) custom-call(bf16[176,128]{1,0:T(8,128)(2,1)S(1)} %shard_map.122.refs_0_, bf16[176,128]{1,0:T(8,128)(2,1)S(1)} %shard_map.123.refs_1_, bf16[176,128]{1,0:T(8,128)(2,1)S(1)} %collective-permute-done.7.refs_2_, ...), custom_call_target="tpu_custom_call" | custom-call | flops 1024 | tf_op jit(solution)/shard_map/pallas_call | solution.py:333
  22.0 0.0 collective-permute-done.3.refs_1_
  22.0 0.0 collective-permute-done.4.refs_2_
  22.0 0.0 collective-permute-done.5.refs_3_
  22.0 0.0 copy-done.1
  22.0 1.4 %shard_map.125 = (f32[8,1280]{1,0:T(8,128)S(1)}, bf16[8,1280]{1,0:T(8,128)(2,1)S(1)}, bf16[8,1280]{1,0:T(8,128)(2,1)S(1)}, bf16[8,1280]{1,0:T(8,128)(2,1)S(1)}) custom-call(bf16[128,256]{1,0:T(8,128)(2,1)S(1)} %shard_map.121.after.refs_0_, bf16[128,256]{1,0:T(8,128)(2,1)S(1)} %collective-permute-done.3.refs_1_, ...), custom_call_target="tpu_custom_call" | custom-call | flops 104857600 | bytes 3276800 | tf_op jit(solution)/shard_map/pallas_call | solution.py:350
  23.4 0.9 %collective-permute-start.10 = (bf16[8,1280]{1,0:T(8,128)(2,1)S(1)}, bf16[8,1280]{1,0:T(8,128)(2,1)S(1)}, u32[]{:S(2)}, u32[]{:S(2)}) collective-permute-start(bf16[8,1280]{1,0:T(8,128)(2,1)S(1)} %get-tuple-element.31), channel_id=1, source_target_pairs={{0,2},{1,3},{2,0},{3,1},{4,6},{5,7},{6,4},{7,5},{8,10},{9,11},{10,... | collective-permute-start | bytes 61448 | tf_op jit(solution)/shard_map/ppermute | solution.py:248
  24.3 0.0 collective-permute-start.11
  24.3 1.3 %collective-permute-start.9 = (bf16[8,1280]{1,0:T(8,128)(2,1)S(1)}, bf16[8,1280]{1,0:T(8,128)(2,1)S(1)}, u32[]{:S(2)}, u32[]{:S(2)}) collective-permute-start(bf16[8,1280]{1,0:T(8,128)(2,1)S(1)} %get-tuple-element.30), channel_id=1, source_target_pairs={{0,3},{1,2},{2,1},{3,0},{4,7},{5,6},{6,5},{7,4},{8,11},{9,10},{10,... | collective-permute-start | bytes 61448 | tf_op jit(solution)/shard_map/ppermute | solution.py:248
  25.6 1.6 %collective-permute-done.10 = bf16[8,1280]{1,0:T(8,128)(2,1)S(1)} collective-permute-done((bf16[8,1280]{1,0:T(8,128)(2,1)S(1)}, bf16[8,1280]{1,0:T(8,128)(2,1)S(1)}, u32[]{:S(2)}, u32[]{:S(2)}) %collective-permute-start.10) | collective-permute-done | bytes 20512 | tf_op jit(solution)/shard_map/ppermute | solution.py:248
  27.3 0.0 collective-permute-done.11
  27.3 0.2 collective-permute-done.9
  27.5 0.6 %add_convert_fusion = bf16[8,1280]{1,0:T(8,128)(2,1)} fusion(bf16[8,1280]{1,0:T(8,128)(2,1)S(1)} %collective-permute-done.11, bf16[8,1280]{1,0:T(8,128)(2,1)S(1)} %collective-permute-done.10, f32[8,1280]{1,0:T(8,128)S(1)} %get-tuple-element.29, bf16[8,1280]{1,0:T(8,128)(2,1)S(1)} %collective-permute-done.9), kind=kLoop, calls=%fused_computation | loop fusion | flops 71680 | bytes 122880 | tf_op jit(solution)/shard_map/convert_element_type | solution.py:366
  (7 shorter events, 0.0 us)
Async XLA Ops:
  0.0 0.9 %copy-start.10 = (bf16[64,1280]{1,0:T(8,128)(2,1)S(1)}, bf16[64,1280]{1,0:T(8,128)(2,1)}, u32[]{:S(2)}) copy-start(bf16[64,1280]{1,0:T(8,128)(2,1)} %refs_0_) | copy-start | bytes 491524
  0.0 3.9 %copy-start.4 = (bf16[8,1280]{1,0:T(8,128)(2,1)S(1)}, bf16[8,1280]{1,0:T(8,128)(2,1)}, u32[]{:S(2)}) copy-start(bf16[8,1280]{1,0:T(8,128)(2,1)} %q_ref.1) | copy-start | bytes 61444
  0.0 3.9 %copy-start.5 = (bf16[8,256]{1,0:T(8,128)(2,1)S(1)}, bf16[8,256]{1,0:T(8,128)(2,1)}, u32[]{:S(2)}) copy-start(bf16[8,256]{1,0:T(8,128)(2,1)} %nk_ref.1) | copy-start | bytes 12292
  0.0 3.9 %copy-start.6 = (bf16[8,256]{1,0:T(8,128)(2,1)S(1)}, bf16[8,256]{1,0:T(8,128)(2,1)}, u32[]{:S(2)}) copy-start(bf16[8,256]{1,0:T(8,128)(2,1)} %nv_ref.1) | copy-start | bytes 12292
  0.0 3.9 %copy-start.2 = (bf16[4,512,256]{2,1,0:T(8,128)(2,1)S(1)}, bf16[4,512,256]{2,1,0:T(8,128)(2,1)}, u32[]{:S(2)}) copy-start(bf16[4,512,256]{2,1,0:T(8,128)(2,1)} %ck_ref.1) | copy-start | bytes 3145732
  0.0 3.9 %copy-start.3 = (bf16[4,512,256]{2,1,0:T(8,128)(2,1)S(1)}, bf16[4,512,256]{2,1,0:T(8,128)(2,1)}, u32[]{:S(2)}) copy-start(bf16[4,512,256]{2,1,0:T(8,128)(2,1)} %cv_ref.1) | copy-start | bytes 3145732
  0.0 3.9 %copy-start.9 = (s32[4]{0:T(128)S(1)}, s32[4]{0:T(128)}, u32[]{:S(2)}) copy-start(s32[4]{0:T(128)} %lens_ref.1) | copy-start | bytes 52
  0.0 9.5 %copy-start = (bf16[2,5120,256]{2,1,0:T(8,128)(2,1)S(1)}, bf16[2,5120,256]{2,1,0:T(8,128)(2,1)}, u32[]{:S(2)}) copy-start(bf16[2,5120,256]{2,1,0:T(8,128)(2,1)} %refs_1_.1) | copy-start | bytes 15728644
  0.9 8.7 %collective-permute-start = (bf16[64,1280]{1,0:T(8,128)(2,1)S(1)}, bf16[64,1280]{1,0:T(8,128)(2,1)S(1)}, u32[]{:S(2)}, u32[]{:S(2)}) collective-permute-start(bf16[64,1280]{1,0:T(8,128)(2,1)S(1)} %copy-done.10), channel_id=1, source_target_pairs={{0,2},{1,3},{2,0},{3,1},{4,6},{5,7},{6,4},{7,5},{8,10},{9,11},{10,... | collective-permute-start | bytes 491528 | tf_op jit(solution)/shard_map/ppermute | solution.py:248
  3.9 5.7 %collective-permute-start.2 = (bf16[64,1280]{1,0:T(8,128)(2,1)S(1)}, bf16[64,1280]{1,0:T(8,128)(2,1)S(1)}, u32[]{:S(2)}, u32[]{:S(2)}) collective-permute-start(bf16[64,1280]{1,0:T(8,128)(2,1)S(1)} %copy-done.10), channel_id=1, source_target_pairs={{0,1},{1,0},{2,3},{3,2},{4,5},{5,4},{6,7},{7,6},{8,9},{9,8},{10,11... | collective-permute-start | bytes 491528 | tf_op jit(solution)/shard_map/ppermute | solution.py:248
  5.3 5.6 %copy-start.7 = (bf16[2,256]{1,0:T(2,128)(2,1)S(1)}, bf16[2,256]{1,0:T(2,128)(2,1)}, u32[]{:S(2)}) copy-start(bf16[2,256]{1,0:T(2,128)(2,1)} %refs_4_.1) | copy-start | bytes 3076
  5.3 9.6 %collective-permute-start.6 = (bf16[176,128]{1,0:T(8,128)(2,1)S(1)}, bf16[176,128]{1,0:T(8,128)(2,1)S(1)}, u32[]{:S(2)}, u32[]{:S(2)}) collective-permute-start(bf16[176,128]{1,0:T(8,128)(2,1)S(1)} %shard_map.122.refs_0_), channel_id=1, source_target_pairs={{0,8},{4,12},{8,0},{12,4},{1,9},{5,13},{9,1},{13,5},{2,10},{6,14},... | collective-permute-start | bytes 135176 | tf_op jit(solution)/shard_map/ppermute | solution.py:248
  8.0 8.3 %collective-permute-start.8 = (bf16[176,128]{1,0:T(8,128)(2,1)S(1)}, bf16[176,128]{1,0:T(8,128)(2,1)S(1)}, u32[]{:S(2)}, u32[]{:S(2)}) collective-permute-start(bf16[176,128]{1,0:T(8,128)(2,1)S(1)} %shard_map.122.refs_0_), channel_id=1, source_target_pairs={{0,4},{4,0},{8,12},{12,8},{1,5},{5,1},{9,13},{13,9},{2,6},{6,2},{1... | collective-permute-start | bytes 135176 | tf_op jit(solution)/shard_map/ppermute | solution.py:248
  9.6 1.4 %collective-permute-start.1 = (bf16[64,1280]{1,0:T(8,128)(2,1)S(1)}, bf16[64,1280]{1,0:T(8,128)(2,1)S(1)}, u32[]{:S(2)}, u32[]{:S(2)}) collective-permute-start(bf16[64,1280]{1,0:T(8,128)(2,1)S(1)} %collective-permute-done.refs_2_), channel_id=1, source_target_pairs={{0,1},{1,0},{2,3},{3,2},{4,5},{5,4},{6,7},{7,6},{8,9},{9,8},{10,11... | collective-permute-start | bytes 491528 | tf_op jit(solution)/shard_map/ppermute | solution.py:248
  11.4 10.1 %copy-start.8 = (s32[256]{0:T(256)S(1)}, s32[256]{0:T(256)}, u32[]{:S(2)}) copy-start(s32[256]{0:T(256)} %param.15) | copy-start | bytes 3076
  11.4 10.6 %copy-start.1 = (bf16[1280,1280]{1,0:T(8,128)(2,1)S(1)}, bf16[1280,1280]{1,0:T(8,128)(2,1)}, u32[]{:S(2)}) copy-start(bf16[1280,1280]{1,0:T(8,128)(2,1)} %refs_8_.1) | copy-start | bytes 9830404
  11.4 10.6 %collective-permute-start.3 = (bf16[128,256]{1,0:T(8,128)(2,1)S(1)}, bf16[128,256]{1,0:T(8,128)(2,1)S(1)}, u32[]{:S(2)}, u32[]{:S(2)}) collective-permute-start(bf16[128,256]{1,0:T(8,128)(2,1)S(1)} %shard_map.121.after.refs_0_), channel_id=1, source_target_pairs={{0,8},{4,12},{8,0},{12,4},{1,9},{5,13},{9,1},{13,5},{2,10},{6,14},... | collective-permute-start | bytes 196616 | tf_op jit(solution)/shard_map/ppermute | solution.py:248
  12.8 9.2 %collective-permute-start.4 = (bf16[128,256]{1,0:T(8,128)(2,1)S(1)}, bf16[128,256]{1,0:T(8,128)(2,1)S(1)}, u32[]{:S(2)}, u32[]{:S(2)}) collective-permute-start(bf16[128,256]{1,0:T(8,128)(2,1)S(1)} %shard_map.121.after.refs_0_), channel_id=1, source_target_pairs={{0,12},{4,8},{8,4},{12,0},{1,13},{5,9},{9,5},{13,1},{2,14},{6,10},... | collective-permute-start | bytes 196616 | tf_op jit(solution)/shard_map/ppermute | solution.py:248
  14.2 7.7 %collective-permute-start.5 = (bf16[128,256]{1,0:T(8,128)(2,1)S(1)}, bf16[128,256]{1,0:T(8,128)(2,1)S(1)}, u32[]{:S(2)}, u32[]{:S(2)}) collective-permute-start(bf16[128,256]{1,0:T(8,128)(2,1)S(1)} %shard_map.121.after.refs_0_), channel_id=1, source_target_pairs={{0,4},{4,0},{8,12},{12,8},{1,5},{5,1},{9,13},{13,9},{2,6},{6,2},{1... | collective-permute-start | bytes 196616 | tf_op jit(solution)/shard_map/ppermute | solution.py:248
  14.9 6.5 %collective-permute-start.7 = (bf16[176,128]{1,0:T(8,128)(2,1)S(1)}, bf16[176,128]{1,0:T(8,128)(2,1)S(1)}, u32[]{:S(2)}, u32[]{:S(2)}) collective-permute-start(bf16[176,128]{1,0:T(8,128)(2,1)S(1)} %shard_map.123.refs_1_), channel_id=1, source_target_pairs={{0,4},{4,0},{8,12},{12,8},{1,5},{5,1},{9,13},{13,9},{2,6},{6,2},{1... | collective-permute-start | bytes 135176 | tf_op jit(solution)/shard_map/ppermute | solution.py:248
  23.4 3.8 %collective-permute-start.10 = (bf16[8,1280]{1,0:T(8,128)(2,1)S(1)}, bf16[8,1280]{1,0:T(8,128)(2,1)S(1)}, u32[]{:S(2)}, u32[]{:S(2)}) collective-permute-start(bf16[8,1280]{1,0:T(8,128)(2,1)S(1)} %get-tuple-element.31), channel_id=1, source_target_pairs={{0,2},{1,3},{2,0},{3,1},{4,6},{5,7},{6,4},{7,5},{8,10},{9,11},{10,... | collective-permute-start | bytes 61448 | tf_op jit(solution)/shard_map/ppermute | solution.py:248
  24.3 3.0 %collective-permute-start.11 = (bf16[8,1280]{1,0:T(8,128)(2,1)S(1)}, bf16[8,1280]{1,0:T(8,128)(2,1)S(1)}, u32[]{:S(2)}, u32[]{:S(2)}) collective-permute-start(bf16[8,1280]{1,0:T(8,128)(2,1)S(1)} %get-tuple-element.32), channel_id=1, source_target_pairs={{0,1},{1,0},{2,3},{3,2},{4,5},{5,4},{6,7},{7,6},{8,9},{9,8},{10,11... | collective-permute-start | bytes 61448 | tf_op jit(solution)/shard_map/ppermute | solution.py:248
  24.3 3.2 %collective-permute-start.9 = (bf16[8,1280]{1,0:T(8,128)(2,1)S(1)}, bf16[8,1280]{1,0:T(8,128)(2,1)S(1)}, u32[]{:S(2)}, u32[]{:S(2)}) collective-permute-start(bf16[8,1280]{1,0:T(8,128)(2,1)S(1)} %get-tuple-element.30), channel_id=1, source_target_pairs={{0,3},{1,2},{2,1},{3,0},{4,7},{5,6},{6,5},{7,4},{8,11},{9,10},{10,... | collective-permute-start | bytes 61448 | tf_op jit(solution)/shard_map/ppermute | solution.py:248

commit v3 on v1

--- a/solution.py
+++ b/solution.py
@@ -62,7 +62,11 @@
     return -(-n // to) * to
 
 
-def cache_kernel(lens_ref, group_ref, q_ref, nk_ref, nv_ref, ck_ref, cv_ref, after, out_ref):
+def open_kernel(group_ref, after, out_ref):
+    out_ref[...] = jnp.full(out_ref.shape, group_ref[0].astype(f32))
+
+
+def cache_kernel(lens_ref, section_ref, q_ref, nk_ref, nv_ref, ck_ref, cv_ref, out_ref):
     requests, slots, cols = ck_ref.shape
     heads = cols // HD
     tokens = requests * NEW
@@ -104,7 +108,7 @@
     out_ref[seg : seg + rows, :] = (mine / total).astype(bf16)
 
     lane = lax.broadcasted_iota(jnp.int32, (rows, HD), 1)
-    stats = jnp.where(lane == SECTION, group_ref[0].astype(f32), 0.0)
+    stats = jnp.where(lane == SECTION, section_ref[0:1, :], 0.0)
     for i, piece in enumerate(split(top, 3)):
         stats = jnp.where(lane == TOP + i, piece, stats)
     for i, piece in enumerate(split(total, 2)):
@@ -139,18 +143,29 @@
             refs[0][s * rows : (s + 1) * rows, :] = acc[s]
         refs[1][...] = jnp.broadcast_to(squares, refs[1].shape)
         return
-    b_ref, out_ref = refs
+    b_ref, *_, far_ref, out_ref, packed_ref = refs
     scale = lax.rsqrt(squares / D + 1e-06)
     for s in range(2):
         bias = b_ref[s : s + 1, :].astype(f32)
-        out_ref[s * rows : (s + 1) * rows, :] = (acc[s] * scale + bias).astype(bf16)
+        out = (acc[s] * scale + bias).astype(bf16)
+        out_ref[s * rows : (s + 1) * rows, :] = out
+        packed_ref[s * rows : (s + 1) * rows, :] = out
+    heads = packed_ref.shape[1] // HD
+    folded = far_ref.shape[0] // heads
+    for j in range(heads):
+        packed_ref[2 * rows :, j * HD : (j + 1) * HD] = far_ref[j * folded : (j + 1) * folded, :]
 
 
 def prepare_kernel(heads, *refs):
-    parts, (section_ref, q_ref, bias_ref, old_ref, stats_ref) = refs[:-5], refs[-5:]
+    parts, (section_ref, q_ref, bias_ref, old_ref, stats_ref) = list(refs[:-5]), refs[-5:]
     groups = len(parts)
-    seg = (parts[0].shape[0] - STATS) // 2
+    folded = parts[0].shape[0] // heads
+    for k in range(groups // 2 + 1, groups):
+        kv = parts[k]
+        at = kv.shape[0] - folded
+        parts[k] = jnp.concatenate([kv[at:, j * HD : (j + 1) * HD] for j in range(heads)], axis=0)
     rows = q_ref.shape[0] // groups
+    seg = up(rows, 16)
     per = rows // heads
     blocks = [part[0:rows, :].astype(f32) for part in parts]
     q_ref[...] = jnp.concatenate(
@@ -180,12 +195,12 @@
     outs = refs[groups + 5 : groups + 5 + shares]
     k_ref, v_ref, attended_ref, sums_ref = refs[groups + 5 + shares :]
     me_dp, me_tp = lax.axis_index("dp"), lax.axis_index("tp")
-    memory = kvs[0].shape[0] // 2
+    memory = k_ref.shape[0] // groups
     heads = kvs[0].shape[1] // HD
     tokens = attended_ref.shape[0] // groups
     per = PER_HEAD * tokens
     rows = heads * per
-    for bits, kv in zip(relatives(groups), kvs):
+    for bits, kv in enumerate(kvs):
         first = pl.multiple_of((me_dp ^ bits) * memory, memory)
         k_ref[pl.ds(first, memory), :] = kv[0:memory, :].astype(k_ref.dtype)
         v_ref[pl.ds(first, memory), :] = kv[memory : 2 * memory, :].astype(v_ref.dtype)
@@ -196,8 +211,8 @@
     shrink = jnp.exp(old_top - top)
     total = jnp.sum(p, axis=1, keepdims=True) + shrink * old_total
     acc = nn(p.astype(bf16), v_ref[...].astype(bf16))
-    for k, bits in enumerate(relatives(groups)):
-        at = pl.multiple_of((me_dp ^ bits) * tokens, tokens)
+    for k in range(groups):
+        at = pl.multiple_of((me_dp ^ k) * tokens, tokens)
         for j in range(heads):
             a = k * rows + j * per
             block = acc[a : a + per, j * HD : (j + 1) * HD] + old_ref[a : a + per, :] * shrink[a : a + per]
@@ -235,25 +250,18 @@
     return [pltpu.with_memory_space_constraint(x, pltpu.HBM) for x in arrays]
 
 
-def relatives(n):
-    return [*range(n // 2), *range(n - 1, n // 2 - 1, -1)]
-
-
 def permute(x, axis, bits):
     return lax.ppermute(x, axis, [(i, i ^ bits) for i in range(lax.axis_size(axis))])
 
 
-def others(x, axis):
-    return [permute(x, axis, bits) if bits else x for bits in relatives(lax.axis_size(axis))]
-
-
-def passed_on(x, axis):
+def passed_on(x, near, axis):
     n = lax.axis_size(axis)
     held = {0: x}
     bit = n // 2
     while bit:
         for bits in sorted(held):
             held[bits | bit] = permute(held[bits], axis, bit)
+        held[0] = near
         bit //= 2
     return [held[bits] for bits in range(n)]
 
@@ -280,17 +288,23 @@
     every = memory_sections.shape[0]
 
     gate = call(lambda *refs: None, [], jax.ShapeDtypeStruct((8, HD), f32), [], COVER, 0)()
-    own, gate = lax.optimization_barrier((memory_hidden, gate))
-    hidden = passed_on(own, "tp")
+    group, gate = lax.optimization_barrier((group_sections, gate))
+    section = call(open_kernel, [SMEM, ANY], pltpu.VMEM((8, HD), f32), [], 1 << 10, 0)(group, gate)
+    own, section = lax.optimization_barrier((memory_hidden, section))
+    heads = cols // HD
+    height = up(2 * up(rows, 16) + STATS, 16 * heads)
     part = call(
         cache_kernel,
-        [SMEM] * 2 + [VMEM] * 5 + [ANY],
-        pltpu.VMEM((2 * up(rows, 16) + STATS, HD), bf16),
+        [SMEM] + [VMEM] * 6,
+        pltpu.VMEM((height, HD), bf16),
         [],
         4 * rows * slots * cols * requests,
         4 * requests * slots * cols,
-    )(cache_lengths, group_sections, queries, new_keys, new_values, cache_keys, cache_values, gate)
-    parts = others(part, "dp")
+    )(cache_lengths, section, queries, new_keys, new_values, cache_keys, cache_values)
+    own_later, part = lax.optimization_barrier((own, part))
+    hidden = passed_on(own, own_later, "tp")
+    part_far = permute(part, "dp", groups // 2)
+    part_near = {bits: permute(part, "dp", bits) for bits in range(1, groups // 2)}
     near, far = list(range(shares - 1)), [shares - 1]
     partial = call(
         functools.partial(project_kernel, near, True, False),
@@ -300,17 +314,23 @@
         COVER,
         4 * D * cols,
     )(*[hidden[k] for k in near], kv_weight)
-    kv = call(
+    kv, packed = call(
         functools.partial(project_kernel, far, False, True),
-        [VMEM] * 5,
-        pltpu.VMEM((2 * memory, cols), bf16),
+        [VMEM] * 5 + [ANY] * len(part_near) + [VMEM],
+        [
+            pltpu.VMEM((2 * memory, cols), bf16),
+            pltpu.VMEM((2 * memory + height // heads, cols), bf16),
+        ],
         [],
         4 * memory * D * cols // shares,
         4 * D * cols // shares,
-    )(hidden[far[0]], kv_weight, *partial, kv_bias)
-    kvs = others(kv, "dp")
+    )(hidden[far[0]], kv_weight, *partial, kv_bias, *part_near.values(), part_far)
+    half = range(1, groups // 2)
+    near_kvs = [permute(packed, "dp", bits) for bits in half]
+    kvs = [kv, *near_kvs, *[permute(kv, "dp", groups // 2 + bits) for bits in range(groups // 2)]]
+    parts = [part, *[part_near[bits] for bits in half], part_far, *near_kvs]
     prepared = call(
-        functools.partial(prepare_kernel, cols // HD),
+        functools.partial(prepare_kernel, heads),
         [VMEM] * (groups + 1),
         [
             pltpu.VMEM((groups * rows, cols), bf16),

time: 27.6 us -> 29.5 us (1.069)
  waiting for transfers between devices: 7.25 us -> 9.28 us
  local copies, waits for them, and re-layouts: 0.91 us -> 0.1 us
  starting transfers between devices: 13.3 us -> 13.9 us
    ppermute x12 -> x11, waiting for transfers between devices: 7.25 us -> 9.28 us  [permute(): lax.ppermute(x, axis, [(i, i ^ bits) for i in range(lax.axis_size(axis))])]
    unnamed x22, local copies, waits for them, and re-layouts: 0.91 us -> 0.1 us
    ppermute x12 -> x11, starting transfers between devices: 13.3 us -> 13.9 us  [permute(): lax.ppermute(x, axis, [(i, i ^ bits) for i in range(lax.axis_size(axis))])]
    pallas_call x3 -> x4, Pallas kernels: 2.23 us -> 2.23 us  [the longest x1 1.38 us: body(): call(cache_kernel, [SMEM] + [VMEM] * 6, pltpu.VMEM((height, HD), bf16), [...]
  transfers between devices with their start and end apart: 12 -> 11, of which waited for: 6 -> 6; matrix products, arithmetic and copies ran while one was open for 0% -> 0% of each run, Pallas kernels for 11% -> 9%
where the time goes in v3:
time: 29.5 us; the launch traced here: 29.4 us
  starting transfers between devices  13.9 us (47%)
  waiting for transfers between devices  9.28 us (31%)
  Pallas kernels  4.48 us (15%)
  between operations  0.95 us (3%)
  other arithmetic  0.62 us (2%)
    ppermute x11, starting transfers between devices, permute(): lax.ppermute(x, axis, [(i, i ^ bits) for i in range(lax.axis_size(axis))])  13.9 us
    ppermute x11, waiting for transfers between devices, permute(): lax.ppermute(x, axis, [(i, i ^ bits) for i in range(lax.axis_size(axis))])  9.28 us
    pallas_call x1, Pallas kernels, body(): call(functools.partial(attend_kernel, groups, shares), [VMEM] * (groups +...  1.42 us
    pallas_call x1, Pallas kernels, body(): call(cache_kernel, [SMEM] + [VMEM] * 6, pltpu.VMEM((height, HD), bf16), [...  1.38 us
    pallas_call x1, Pallas kernels, body(): call(functools.partial(project_kernel, near, True, False), [VMEM] * (len(...  0.82 us
    convert_element_type x1, other arithmetic, body(): return summed.astype(bf16)  0.62 us
  transfers between devices with their start and end apart: 11, of which 6 were waited for; matrix products, arithmetic and copies ran while one was open for 0% of the time, Pallas kernels for 9%

profile of v3, /device:TPU:0, one launch (start us, length us, event | category | flops | bytes accessed | tf_op | source)
XLA Modules:
  0.0 29.4 jit_solution(12736336815924713221)
XLA Ops:
  0.0 0.0 copy-start.9
  0.0 0.0 copy-start.4
  0.0 0.0 copy-start.6
  0.0 0.0 copy-start.2
  0.0 0.0 copy-start.3
  0.0 0.0 copy-start.8
  0.0 0.0 copy-start
  0.9 0.1 copy-done.9
  0.9 3.0 %collective-permute-start = (bf16[64,1280]{1,0:T(8,128)(2,1)S(1)}, bf16[64,1280]{1,0:T(8,128)(2,1)S(1)}, u32[]{:S(2)}, u32[]{:S(2)}) collective-permute-start(bf16[64,1280]{1,0:T(8,128)(2,1)S(1)} %copy-done.9), channel_id=1, source_target_pairs={{0,2},{1,3},{2,0},{3,1},{4,6},{5,7},{6,4},{7,5},{8,10},{9,11},{10,... | collective-permute-start | bytes 491528 | tf_op jit(solution)/shard_map/ppermute | solution.py:254
  3.9 0.0 copy-done.4
  3.9 0.0 copy-done.5
  3.9 0.0 copy-done.6
  3.9 0.0 copy-done.2
  3.9 0.0 copy-done.3
  3.9 0.0 copy-done.8
  3.9 1.4 %shard_map.120.refs_0_ = bf16[192,128]{1,0:T(8,128)(2,1)S(1)} custom-call(s32[4]{0:T(128)S(1)} %copy-done.8, f32[8,128]{1,0:T(8,128)S(1)} %shard_map.119.section_ref, bf16[8,1280]{1,0:T(8,128)(2,1)S(1)} %copy-done.4, bf16[8,256]{1,0:T(8,128)(2,1)S(1)} %copy-done.5, bf16[8,256]{1,0:T(8,128)(2,1)S(1)} %copy-done.6, bf16[4,512,256]{2,1,0:T(8,128)(2,1)S(1)} %copy-done.2, ...), custom_call_target="tpu_custom_call" | custom-call | flops 167772160 | bytes 2097152 | tf_op jit(solution)/shard_map/pallas_call | solution.py:296
  5.3 0.0 copy-start.7
  5.3 0.1 collective-permute-start.2
  5.4 1.6 %collective-permute-start.3 = (bf16[192,128]{1,0:T(8,128)(2,1)S(1)}, bf16[192,128]{1,0:T(8,128)(2,1)S(1)}, u32[]{:S(2)}, u32[]{:S(2)}) collective-permute-start(bf16[192,128]{1,0:T(8,128)(2,1)S(1)} %shard_map.120.refs_0_), channel_id=1, source_target_pairs={{0,4},{4,0},{8,12},{12,8},{1,5},{5,1},{9,13},{13,9},{2,6},{6,2},{1... | collective-permute-start | bytes 147464 | tf_op jit(solution)/shard_map/ppermute | solution.py:254
  7.0 2.6 %collective-permute-start.4 = (bf16[192,128]{1,0:T(8,128)(2,1)S(1)}, bf16[192,128]{1,0:T(8,128)(2,1)S(1)}, u32[]{:S(2)}, u32[]{:S(2)}) collective-permute-start(bf16[192,128]{1,0:T(8,128)(2,1)S(1)} %shard_map.120.refs_0_), channel_id=1, source_target_pairs={{0,8},{4,12},{8,0},{12,4},{1,9},{5,13},{9,1},{13,5},{2,10},{6,14},... | collective-permute-start | bytes 147464 | tf_op jit(solution)/shard_map/ppermute | solution.py:254
  9.6 0.0 collective-permute-done.refs_2_
  9.6 0.0 collective-permute-start.1
  9.6 0.0 collective-permute-done.2.refs_1_
  9.6 0.0 copy-done
  9.7 0.8 %shard_map.121 = (f32[128,256]{1,0:T(8,128)S(1)}, f32[64,128]{1,0:T(8,128)S(1)}) custom-call(bf16[64,1280]{1,0:T(8,128)(2,1)S(1)} %copy-done.9, bf16[64,1280]{1,0:T(8,128)(2,1)S(1)} %collective-permute-done.2.refs_1_, bf16[64,1280]{1,0:T(8,128)(2,1)S(1)} %collective-permute-done.refs_2_, bf16[2,5120,256]{2,1,0:T(8,128)(2,1)S(1)} %copy-done), custom_call_target="tpu_custom_call" | custom-call | flops 68719476736 | bytes 5242880 | tf_op jit(solution)/shard_map/pallas_call | solution.py:309
  10.5 0.0 copy-start.1
  10.5 0.0 collective-permute-done.3.refs_5_.refs_1_
  10.5 2.4 %collective-permute-done.4.refs_6_.refs_2_ = bf16[192,128]{1,0:T(8,128)(2,1)S(1)} collective-permute-done((bf16[192,128]{1,0:T(8,128)(2,1)S(1)}, bf16[192,128]{1,0:T(8,128)(2,1)S(1)}, u32[]{:S(2)}, u32[]{:S(2)}) %collective-permute-start.4) | collective-permute-done | bytes 49184 | tf_op jit(solution)/shard_map/ppermute | solution.py:254
  12.9 0.0 collective-permute-done.1.refs_0_
  12.9 0.0 copy-done.7
  12.9 0.4 %shard_map.122 = (bf16[128,256]{1,0:T(8,128)(2,1)S(1)}, bf16[224,256]{1,0:T(8,128)(2,1)S(1)}) custom-call(bf16[64,1280]{1,0:T(8,128)(2,1)S(1)} %collective-permute-done.1.refs_0_, bf16[2,5120,256]{2,1,0:T(8,128)(2,1)S(1)} %copy-done, f32[128,256]{1,0:T(8,128)S(1)} %get-tuple-element.28.refs_2_, f32[64,128]{1,0:T(8,128)S(1)} %get-tuple-element.29.refs_3_, ...), custom_call_target="tpu_custom_call" | custom-call | flops 83886080 | bytes 1310720 | tf_op jit(solution)/shard_map/pallas_call | solution.py:317
  13.3 0.5 %collective-permute-start.5 = (bf16[224,256]{1,0:T(8,128)(2,1)S(1)}, bf16[224,256]{1,0:T(8,128)(2,1)S(1)}, u32[]{:S(2)}, u32[]{:S(2)}) collective-permute-start(bf16[224,256]{1,0:T(8,128)(2,1)S(1)} %get-tuple-element.32), channel_id=1, source_target_pairs={{0,4},{4,0},{8,12},{12,8},{1,5},{5,1},{9,13},{13,9},{2,6},{6,2},{1... | collective-permute-start | bytes 344072 | tf_op jit(solution)/shard_map/ppermute | solution.py:254
  13.7 2.8 %collective-permute-start.6 = (bf16[128,256]{1,0:T(8,128)(2,1)S(1)}, bf16[128,256]{1,0:T(8,128)(2,1)S(1)}, u32[]{:S(2)}, u32[]{:S(2)}) collective-permute-start(bf16[128,256]{1,0:T(8,128)(2,1)S(1)} %get-tuple-element.31.refs_0_), channel_id=1, source_target_pairs={{0,8},{4,12},{8,0},{12,4},{1,9},{5,13},{9,1},{13,5},{2,10},{6,14},... | collective-permute-start | bytes 196616 | tf_op jit(solution)/shard_map/ppermute | solution.py:254
  16.6 1.2 %collective-permute-start.7 = (bf16[128,256]{1,0:T(8,128)(2,1)S(1)}, bf16[128,256]{1,0:T(8,128)(2,1)S(1)}, u32[]{:S(2)}, u32[]{:S(2)}) collective-permute-start(bf16[128,256]{1,0:T(8,128)(2,1)S(1)} %get-tuple-element.31.refs_0_), channel_id=1, source_target_pairs={{0,12},{4,8},{8,4},{12,0},{1,13},{5,9},{9,5},{13,1},{2,14},{6,10},... | collective-permute-start | bytes 196616 | tf_op jit(solution)/shard_map/ppermute | solution.py:254
  17.7 1.3 %collective-permute-done.5.refs_3_.refs_1_ = bf16[224,256]{1,0:T(8,128)(2,1)S(1)} collective-permute-done((bf16[224,256]{1,0:T(8,128)(2,1)S(1)}, bf16[224,256]{1,0:T(8,128)(2,1)S(1)}, u32[]{:S(2)}, u32[]{:S(2)}) %collective-permute-start.5) | collective-permute-done | bytes 114720 | tf_op jit(solution)/shard_map/ppermute | solution.py:254
  19.0 0.0 copy-done.10
  19.0 0.5 %shard_map.123 = (bf16[320,256]{1,0:T(8,128)(2,1)S(1)}, f32[320,256]{1,0:T(8,128)S(1)}, f32[320,128]{1,0:T(8,128)S(1)}, f32[320,128]{1,0:T(8,128)S(1)}) custom-call(bf16[192,128]{1,0:T(8,128)(2,1)S(1)} %shard_map.120.refs_0_, bf16[192,128]{1,0:T(8,128)(2,1)S(1)} %collective-permute-done.3.refs_5_.refs_1_, ...), custom_call_target="tpu_custom_call" | custom-call | flops 1073741824 | tf_op jit(solution)/shard_map/pallas_call | solution.py:332
  19.5 1.5 %collective-permute-done.6.refs_2_ = bf16[128,256]{1,0:T(8,128)(2,1)S(1)} collective-permute-done((bf16[128,256]{1,0:T(8,128)(2,1)S(1)}, bf16[128,256]{1,0:T(8,128)(2,1)S(1)}, u32[]{:S(2)}, u32[]{:S(2)}) %collective-permute-start.6) | collective-permute-done | bytes 65568 | tf_op jit(solution)/shard_map/ppermute | solution.py:254
  21.0 1.7 %collective-permute-done.7.refs_3_ = bf16[128,256]{1,0:T(8,128)(2,1)S(1)} collective-permute-done((bf16[128,256]{1,0:T(8,128)(2,1)S(1)}, bf16[128,256]{1,0:T(8,128)(2,1)S(1)}, u32[]{:S(2)}, u32[]{:S(2)}) %collective-permute-start.7) | collective-permute-done | bytes 65568 | tf_op jit(solution)/shard_map/ppermute | solution.py:254
  22.6 0.0 copy-done.1
  22.6 1.4 %shard_map.124 = (f32[8,1280]{1,0:T(8,128)S(1)}, bf16[8,1280]{1,0:T(8,128)(2,1)S(1)}, bf16[8,1280]{1,0:T(8,128)(2,1)S(1)}, bf16[8,1280]{1,0:T(8,128)(2,1)S(1)}) custom-call(bf16[128,256]{1,0:T(8,128)(2,1)S(1)} %get-tuple-element.31.refs_0_, bf16[224,256]{1,0:T(8,128)(2,1)S(1)} %collective-permute-done.5.refs_3_.refs_1_, ...), custom_call_target="tpu_custom_call" | custom-call | flops 104857600 | bytes 3276800 | tf_op jit(solution)/shard_map/pallas_call | solution.py:349
  24.1 0.1 collective-permute-start.10
  24.1 0.8 %collective-permute-start.8 = (bf16[8,1280]{1,0:T(8,128)(2,1)S(1)}, bf16[8,1280]{1,0:T(8,128)(2,1)S(1)}, u32[]{:S(2)}, u32[]{:S(2)}) collective-permute-start(bf16[8,1280]{1,0:T(8,128)(2,1)S(1)} %get-tuple-element.38), channel_id=1, source_target_pairs={{0,3},{1,2},{2,1},{3,0},{4,7},{5,6},{6,5},{7,4},{8,11},{9,10},{10,... | collective-permute-start | bytes 61448 | tf_op jit(solution)/shard_map/ppermute | solution.py:254
  25.0 1.3 %collective-permute-start.9 = (bf16[8,1280]{1,0:T(8,128)(2,1)S(1)}, bf16[8,1280]{1,0:T(8,128)(2,1)S(1)}, u32[]{:S(2)}, u32[]{:S(2)}) collective-permute-start(bf16[8,1280]{1,0:T(8,128)(2,1)S(1)} %get-tuple-element.39), channel_id=1, source_target_pairs={{0,2},{1,3},{2,0},{3,1},{4,6},{5,7},{6,4},{7,5},{8,10},{9,11},{10,... | collective-permute-start | bytes 61448 | tf_op jit(solution)/shard_map/ppermute | solution.py:254
  26.3 0.0 collective-permute-done.10
  26.3 1.1 %collective-permute-done.8 = bf16[8,1280]{1,0:T(8,128)(2,1)S(1)} collective-permute-done((bf16[8,1280]{1,0:T(8,128)(2,1)S(1)}, bf16[8,1280]{1,0:T(8,128)(2,1)S(1)}, u32[]{:S(2)}, u32[]{:S(2)}) %collective-permute-start.8) | collective-permute-done | bytes 20512 | tf_op jit(solution)/shard_map/ppermute | solution.py:254
  27.4 1.3 %collective-permute-done.9 = bf16[8,1280]{1,0:T(8,128)(2,1)S(1)} collective-permute-done((bf16[8,1280]{1,0:T(8,128)(2,1)S(1)}, bf16[8,1280]{1,0:T(8,128)(2,1)S(1)}, u32[]{:S(2)}, u32[]{:S(2)}) %collective-permute-start.9) | collective-permute-done | bytes 20512 | tf_op jit(solution)/shard_map/ppermute | solution.py:254
  28.7 0.6 %add_convert_fusion = bf16[8,1280]{1,0:T(8,128)(2,1)} fusion(bf16[8,1280]{1,0:T(8,128)(2,1)S(1)} %collective-permute-done.10, bf16[8,1280]{1,0:T(8,128)(2,1)S(1)} %collective-permute-done.9, f32[8,1280]{1,0:T(8,128)S(1)} %get-tuple-element.37, bf16[8,1280]{1,0:T(8,128)(2,1)S(1)} %collective-permute-done.8), kind=kLoop, calls=%fused_computation | loop fusion | flops 71680 | bytes 122880 | tf_op jit(solution)/shard_map/convert_element_type | solution.py:365
  (4 shorter events, 0.0 us)
Async XLA Ops:
  0.0 0.9 %copy-start.9 = (bf16[64,1280]{1,0:T(8,128)(2,1)S(1)}, bf16[64,1280]{1,0:T(8,128)(2,1)}, u32[]{:S(2)}) copy-start(bf16[64,1280]{1,0:T(8,128)(2,1)} %refs_0_) | copy-start | bytes 491524
  0.0 3.9 %copy-start.4 = (bf16[8,1280]{1,0:T(8,128)(2,1)S(1)}, bf16[8,1280]{1,0:T(8,128)(2,1)}, u32[]{:S(2)}) copy-start(bf16[8,1280]{1,0:T(8,128)(2,1)} %q_ref.1) | copy-start | bytes 61444
  0.0 3.9 %copy-start.5 = (bf16[8,256]{1,0:T(8,128)(2,1)S(1)}, bf16[8,256]{1,0:T(8,128)(2,1)}, u32[]{:S(2)}) copy-start(bf16[8,256]{1,0:T(8,128)(2,1)} %nk_ref.1) | copy-start | bytes 12292
  0.0 3.9 %copy-start.6 = (bf16[8,256]{1,0:T(8,128)(2,1)S(1)}, bf16[8,256]{1,0:T(8,128)(2,1)}, u32[]{:S(2)}) copy-start(bf16[8,256]{1,0:T(8,128)(2,1)} %nv_ref.1) | copy-start | bytes 12292
  0.0 3.9 %copy-start.2 = (bf16[4,512,256]{2,1,0:T(8,128)(2,1)S(1)}, bf16[4,512,256]{2,1,0:T(8,128)(2,1)}, u32[]{:S(2)}) copy-start(bf16[4,512,256]{2,1,0:T(8,128)(2,1)} %ck_ref.1) | copy-start | bytes 3145732
  0.0 3.9 %copy-start.3 = (bf16[4,512,256]{2,1,0:T(8,128)(2,1)S(1)}, bf16[4,512,256]{2,1,0:T(8,128)(2,1)}, u32[]{:S(2)}) copy-start(bf16[4,512,256]{2,1,0:T(8,128)(2,1)} %cv_ref.1) | copy-start | bytes 3145732
  0.0 3.9 %copy-start.8 = (s32[4]{0:T(128)S(1)}, s32[4]{0:T(128)}, u32[]{:S(2)}) copy-start(s32[4]{0:T(128)} %lens_ref.1) | copy-start | bytes 52
  0.0 9.6 %copy-start = (bf16[2,5120,256]{2,1,0:T(8,128)(2,1)S(1)}, bf16[2,5120,256]{2,1,0:T(8,128)(2,1)}, u32[]{:S(2)}) copy-start(bf16[2,5120,256]{2,1,0:T(8,128)(2,1)} %refs_1_.1) | copy-start | bytes 15728644
  0.9 8.7 %collective-permute-start = (bf16[64,1280]{1,0:T(8,128)(2,1)S(1)}, bf16[64,1280]{1,0:T(8,128)(2,1)S(1)}, u32[]{:S(2)}, u32[]{:S(2)}) collective-permute-start(bf16[64,1280]{1,0:T(8,128)(2,1)S(1)} %copy-done.9), channel_id=1, source_target_pairs={{0,2},{1,3},{2,0},{3,1},{4,6},{5,7},{6,4},{7,5},{8,10},{9,11},{10,... | collective-permute-start | bytes 491528 | tf_op jit(solution)/shard_map/ppermute | solution.py:254
  5.3 7.6 %copy-start.7 = (bf16[2,256]{1,0:T(2,128)(2,1)S(1)}, bf16[2,256]{1,0:T(2,128)(2,1)}, u32[]{:S(2)}) copy-start(bf16[2,256]{1,0:T(2,128)(2,1)} %refs_4_.1) | copy-start | bytes 3076
  5.3 4.3 %collective-permute-start.2 = (bf16[64,1280]{1,0:T(8,128)(2,1)S(1)}, bf16[64,1280]{1,0:T(8,128)(2,1)S(1)}, u32[]{:S(2)}, u32[]{:S(2)}) collective-permute-start(bf16[64,1280]{1,0:T(8,128)(2,1)S(1)} %copy-done.9), channel_id=1, source_target_pairs={{0,1},{1,0},{2,3},{3,2},{4,5},{5,4},{6,7},{7,6},{8,9},{9,8},{10,11... | collective-permute-start | bytes 491528 | tf_op jit(solution)/shard_map/ppermute | solution.py:254
  5.4 5.1 %collective-permute-start.3 = (bf16[192,128]{1,0:T(8,128)(2,1)S(1)}, bf16[192,128]{1,0:T(8,128)(2,1)S(1)}, u32[]{:S(2)}, u32[]{:S(2)}) collective-permute-start(bf16[192,128]{1,0:T(8,128)(2,1)S(1)} %shard_map.120.refs_0_), channel_id=1, source_target_pairs={{0,4},{4,0},{8,12},{12,8},{1,5},{5,1},{9,13},{13,9},{2,6},{6,2},{1... | collective-permute-start | bytes 147464 | tf_op jit(solution)/shard_map/ppermute | solution.py:254
  7.0 5.9 %collective-permute-start.4 = (bf16[192,128]{1,0:T(8,128)(2,1)S(1)}, bf16[192,128]{1,0:T(8,128)(2,1)S(1)}, u32[]{:S(2)}, u32[]{:S(2)}) collective-permute-start(bf16[192,128]{1,0:T(8,128)(2,1)S(1)} %shard_map.120.refs_0_), channel_id=1, source_target_pairs={{0,8},{4,12},{8,0},{12,4},{1,9},{5,13},{9,1},{13,5},{2,10},{6,14},... | collective-permute-start | bytes 147464 | tf_op jit(solution)/shard_map/ppermute | solution.py:254
  9.6 3.3 %collective-permute-start.1 = (bf16[64,1280]{1,0:T(8,128)(2,1)S(1)}, bf16[64,1280]{1,0:T(8,128)(2,1)S(1)}, u32[]{:S(2)}, u32[]{:S(2)}) collective-permute-start(bf16[64,1280]{1,0:T(8,128)(2,1)S(1)} %collective-permute-done.refs_2_), channel_id=1, source_target_pairs={{0,1},{1,0},{2,3},{3,2},{4,5},{5,4},{6,7},{7,6},{8,9},{9,8},{10,11... | collective-permute-start | bytes 491528 | tf_op jit(solution)/shard_map/ppermute | solution.py:254
  10.5 8.5 %copy-start.10 = (s32[256]{0:T(256)S(1)}, s32[256]{0:T(256)}, u32[]{:S(2)}) copy-start(s32[256]{0:T(256)} %param.15) | copy-start | bytes 3076
  10.5 12.2 %copy-start.1 = (bf16[1280,1280]{1,0:T(8,128)(2,1)S(1)}, bf16[1280,1280]{1,0:T(8,128)(2,1)}, u32[]{:S(2)}) copy-start(bf16[1280,1280]{1,0:T(8,128)(2,1)} %refs_8_.1) | copy-start | bytes 9830404
  13.3 5.7 %collective-permute-start.5 = (bf16[224,256]{1,0:T(8,128)(2,1)S(1)}, bf16[224,256]{1,0:T(8,128)(2,1)S(1)}, u32[]{:S(2)}, u32[]{:S(2)}) collective-permute-start(bf16[224,256]{1,0:T(8,128)(2,1)S(1)} %get-tuple-element.32), channel_id=1, source_target_pairs={{0,4},{4,0},{8,12},{12,8},{1,5},{5,1},{9,13},{13,9},{2,6},{6,2},{1... | collective-permute-start | bytes 344072 | tf_op jit(solution)/shard_map/ppermute | solution.py:254
  13.7 7.2 %collective-permute-start.6 = (bf16[128,256]{1,0:T(8,128)(2,1)S(1)}, bf16[128,256]{1,0:T(8,128)(2,1)S(1)}, u32[]{:S(2)}, u32[]{:S(2)}) collective-permute-start(bf16[128,256]{1,0:T(8,128)(2,1)S(1)} %get-tuple-element.31.refs_0_), channel_id=1, source_target_pairs={{0,8},{4,12},{8,0},{12,4},{1,9},{5,13},{9,1},{13,5},{2,10},{6,14},... | collective-permute-start | bytes 196616 | tf_op jit(solution)/shard_map/ppermute | solution.py:254
  16.6 6.1 %collective-permute-start.7 = (bf16[128,256]{1,0:T(8,128)(2,1)S(1)}, bf16[128,256]{1,0:T(8,128)(2,1)S(1)}, u32[]{:S(2)}, u32[]{:S(2)}) collective-permute-start(bf16[128,256]{1,0:T(8,128)(2,1)S(1)} %get-tuple-element.31.refs_0_), channel_id=1, source_target_pairs={{0,12},{4,8},{8,4},{12,0},{1,13},{5,9},{9,5},{13,1},{2,14},{6,10},... | collective-permute-start | bytes 196616 | tf_op jit(solution)/shard_map/ppermute | solution.py:254
  24.1 2.2 %collective-permute-start.10 = (bf16[8,1280]{1,0:T(8,128)(2,1)S(1)}, bf16[8,1280]{1,0:T(8,128)(2,1)S(1)}, u32[]{:S(2)}, u32[]{:S(2)}) collective-permute-start(bf16[8,1280]{1,0:T(8,128)(2,1)S(1)} %get-tuple-element.40), channel_id=1, source_target_pairs={{0,1},{1,0},{2,3},{3,2},{4,5},{5,4},{6,7},{7,6},{8,9},{9,8},{10,11... | collective-permute-start | bytes 61448 | tf_op jit(solution)/shard_map/ppermute | solution.py:254
  24.1 3.3 %collective-permute-start.8 = (bf16[8,1280]{1,0:T(8,128)(2,1)S(1)}, bf16[8,1280]{1,0:T(8,128)(2,1)S(1)}, u32[]{:S(2)}, u32[]{:S(2)}) collective-permute-start(bf16[8,1280]{1,0:T(8,128)(2,1)S(1)} %get-tuple-element.38), channel_id=1, source_target_pairs={{0,3},{1,2},{2,1},{3,0},{4,7},{5,6},{6,5},{7,4},{8,11},{9,10},{10,... | collective-permute-start | bytes 61448 | tf_op jit(solution)/shard_map/ppermute | solution.py:254
  25.0 3.8 %collective-permute-start.9 = (bf16[8,1280]{1,0:T(8,128)(2,1)S(1)}, bf16[8,1280]{1,0:T(8,128)(2,1)S(1)}, u32[]{:S(2)}, u32[]{:S(2)}) collective-permute-start(bf16[8,1280]{1,0:T(8,128)(2,1)S(1)} %get-tuple-element.39), channel_id=1, source_target_pairs={{0,2},{1,3},{2,0},{3,1},{4,6},{5,7},{6,4},{7,5},{8,10},{9,11},{10,... | collective-permute-start | bytes 61448 | tf_op jit(solution)/shard_map/ppermute | solution.py:254

commit v4 on v2

--- a/solution.py
+++ b/solution.py
@@ -150,8 +150,14 @@
         out_ref[s * rows : (s + 1) * rows, :] = (acc[s] * scale + bias).astype(bf16)
 
 
+def pair_kernel(near_ref, far_ref, after, out_ref):
+    out_ref[0] = near_ref[...]
+    out_ref[1] = far_ref[...]
+
+
 def prepare_kernel(heads, *refs):
-    parts, (section_ref, q_ref, bias_ref, old_ref, stats_ref) = refs[:-5], refs[-5:]
+    pairs, (section_ref, q_ref, bias_ref, old_ref, stats_ref) = refs[:-5], refs[-5:]
+    parts = [pair.at[i] for i in range(2) for pair in pairs]
     groups = len(parts)
     seg = (parts[0].shape[0] - STATS) // 2
     rows = q_ref.shape[0] // groups
@@ -189,7 +195,7 @@
     tokens = attended_ref.shape[0] // groups
     per = PER_HEAD * tokens
     rows = heads * per
-    for bits, kv in zip(relatives(groups), kvs):
+    for bits, kv in enumerate(kvs):
         first = pl.multiple_of((me_dp ^ bits) * memory, memory)
         k_ref[pl.ds(first, memory), :] = kv[0:memory, :].astype(k_ref.dtype)
         v_ref[pl.ds(first, memory), :] = kv[memory : 2 * memory, :].astype(v_ref.dtype)
@@ -200,8 +206,8 @@
     shrink = jnp.exp(old_top - top)
     total = jnp.sum(p, axis=1, keepdims=True) + shrink * old_total
     acc = nn(p.astype(bf16), v_ref[...].astype(bf16))
-    for k, bits in enumerate(relatives(groups)):
-        at = pl.multiple_of((me_dp ^ bits) * tokens, tokens)
+    for k in range(groups):
+        at = pl.multiple_of((me_dp ^ k) * tokens, tokens)
         for j in range(heads):
             a = k * rows + j * per
             block = acc[a : a + per, j * HD : (j + 1) * HD] + old_ref[a : a + per, :] * shrink[a : a + per]
@@ -223,14 +229,13 @@
 PARAMS = pltpu.CompilerParams(vmem_limit_bytes=24 * 1024 * 1024)
 
 
-def call(kernel, in_specs, out_shape, scratch, flops, bytes_accessed, aliases={}):
+def call(kernel, in_specs, out_shape, scratch, flops, bytes_accessed):
     return pl.pallas_call(
         kernel,
         in_specs=in_specs,
         out_shape=out_shape,
         out_specs=jax.tree.map(lambda _: VMEM, out_shape),
         scratch_shapes=scratch,
-        input_output_aliases=aliases,
         compiler_params=PARAMS,
         cost_estimate=pl.CostEstimate(flops=flops, bytes_accessed=bytes_accessed, transcendentals=0),
     )
@@ -240,25 +245,18 @@
     return [pltpu.with_memory_space_constraint(x, pltpu.HBM) for x in arrays]
 
 
-def relatives(n):
-    return [0, *range(n // 2, n), *range(1, n // 2)]
-
-
 def permute(x, axis, bits):
     return lax.ppermute(x, axis, [(i, i ^ bits) for i in range(lax.axis_size(axis))])
 
 
-def others(x, axis):
-    return [permute(x, axis, bits) if bits else x for bits in relatives(lax.axis_size(axis))]
-
-
-def passed_on(x, axis):
+def passed_on(x, near, axis):
     n = lax.axis_size(axis)
     held = {0: x}
     bit = n // 2
     while bit:
         for bits in sorted(held):
             held[bits | bit] = permute(held[bits], axis, bit)
+        held[0] = near
         bit //= 2
     return [held[bits] for bits in range(n)]
 
@@ -288,7 +286,6 @@
     group, gate = lax.optimization_barrier((group_sections, gate))
     section = call(open_kernel, [SMEM, ANY], pltpu.VMEM((8, HD), f32), [], 1 << 10, 0)(group, gate)
     own, section = lax.optimization_barrier((memory_hidden, section))
-    hidden = passed_on(own, "tp")
     part = call(
         cache_kernel,
         [SMEM] + [VMEM] * 6,
@@ -297,8 +294,9 @@
         4 * rows * slots * cols * requests,
         4 * requests * slots * cols,
     )(cache_lengths, section, queries, new_keys, new_values, cache_keys, cache_values)
+    own_later, part = lax.optimization_barrier((own, part))
+    hidden = passed_on(own, own_later, "tp")
     part_far = permute(part, "dp", groups // 2)
-    part_near = {bits: permute(part, "dp", bits) for bits in range(1, groups // 2)}
     near, far = list(range(shares - 1)), [shares - 1]
     partial = call(
         functools.partial(project_kernel, near, True, False),
@@ -316,23 +314,22 @@
         4 * memory * D * cols // shares,
         4 * D * cols // shares,
     )(hidden[far[0]], kv_weight, *partial, kv_bias)
-    kvs = others(kv, "dp")
-    part_far = call(
-        lambda x, after, out: None,
-        [VMEM, ANY],
-        pltpu.VMEM(part.shape, bf16),
+    kv_far = permute(kv, "dp", groups // 2)
+    pair = call(
+        pair_kernel,
+        [VMEM, VMEM, ANY],
+        pltpu.VMEM((2,) + part.shape, bf16),
         [],
         COVER,
         0,
-        {0: 0},
-    )(part_far, kv)
-    parts = {0: part, **part_near}
-    for bits in range(groups // 2):
-        parts[groups // 2 + bits] = permute(part_far, "dp", bits) if bits else part_far
-    parts = [parts[bits] for bits in relatives(groups)]
+    )(part, part_far, kv)
+    kv_on, _ = lax.optimization_barrier((kv_far, pair))
+    half = range(1, groups // 2)
+    pairs = [pair, *[permute(pair, "dp", bits) for bits in half]]
+    kvs = [kv, *[permute(kv, "dp", bits) for bits in half], kv_far, *[permute(kv_on, "dp", bits) for bits in half]]
     prepared = call(
         functools.partial(prepare_kernel, cols // HD),
-        [VMEM] * (groups + 1),
+        [VMEM] * (groups // 2 + 1),
         [
             pltpu.VMEM((groups * rows, cols), bf16),
             pltpu.VMEM((groups * rows, every), f32),
@@ -342,7 +339,7 @@
         [],
         PCOVER,
         0,
-    )(*parts, memory_sections.reshape(1, every))
+    )(*pairs, memory_sections.reshape(1, every))
 
     out_rows, out_cols = groups * tokens, out_weight.shape[1]
     share = out_rows // shares

time: 28.4 us -> 28.4 us (level)
    ppermute x12 -> x11, waiting for transfers between devices: 7.65 us -> 7.82 us  [permute(): lax.ppermute(x, axis, [(i, i ^ bits) for i in range(lax.axis_size(axis))])]
    ppermute x12 -> x11, starting transfers between devices: 14.3 us -> 14.3 us  [permute(): lax.ppermute(x, axis, [(i, i ^ bits) for i in range(lax.axis_size(axis))])]
  transfers between devices with their start and end apart: 12 -> 11, of which waited for: 4 -> 7; matrix products, arithmetic and copies ran while one was open for 0% -> 0% of each run, Pallas kernels for 11% -> 11%
where the time goes in v4:
time: 28.4 us; the launch traced here: 28.3 us
  starting transfers between devices  14.3 us (50%)
  waiting for transfers between devices  7.82 us (28%)
  Pallas kernels  4.49 us (16%)
  between operations  0.94 us (3%)
  other arithmetic  0.62 us (2%)
    ppermute x11, starting transfers between devices, permute(): lax.ppermute(x, axis, [(i, i ^ bits) for i in range(lax.axis_size(axis))])  14.3 us
    ppermute x11, waiting for transfers between devices, permute(): lax.ppermute(x, axis, [(i, i ^ bits) for i in range(lax.axis_size(axis))])  7.82 us
    pallas_call x1, Pallas kernels, body(): call(functools.partial(attend_kernel, groups, shares), [VMEM] * (groups +...  1.43 us
    pallas_call x1, Pallas kernels, body(): call(cache_kernel, [SMEM] + [VMEM] * 6, pltpu.VMEM((2 * up(rows, 16) + ST...  1.38 us
    pallas_call x1, Pallas kernels, body(): call(functools.partial(project_kernel, near, True, False), [VMEM] * (len(...  0.82 us
    convert_element_type x1, other arithmetic, body(): return summed.astype(bf16)  0.62 us
  transfers between devices with their start and end apart: 11, of which 7 were waited for; matrix products, arithmetic and copies ran while one was open for 0% of the time, Pallas kernels for 11%

profile of v4, /device:TPU:0, one launch (start us, length us, event | category | flops | bytes accessed | tf_op | source)
XLA Modules:
  0.0 28.3 jit_solution(13597931627473103568)
XLA Ops:
  0.0 0.0 copy-start.10
  0.0 0.0 copy-start.4
  0.0 0.0 copy-start.5
  0.0 0.0 copy-start.6
  0.0 0.0 copy-start.3
  0.0 0.0 copy-start.9
  0.0 0.0 copy-start
  0.9 0.1 copy-done.10
  0.9 3.0 %collective-permute-start = (bf16[64,1280]{1,0:T(8,128)(2,1)S(1)}, bf16[64,1280]{1,0:T(8,128)(2,1)S(1)}, u32[]{:S(2)}, u32[]{:S(2)}) collective-permute-start(bf16[64,1280]{1,0:T(8,128)(2,1)S(1)} %copy-done.10), channel_id=1, source_target_pairs={{0,2},{1,3},{2,0},{3,1},{4,6},{5,7},{6,4},{7,5},{8,10},{9,11},{10,... | collective-permute-start | bytes 491528 | tf_op jit(solution)/shard_map/ppermute | solution.py:249
  3.9 0.0 copy-done.4
  3.9 0.0 copy-done.5
  3.9 0.0 copy-done.6
  3.9 0.0 copy-done.2
  3.9 0.0 copy-done.3
  3.9 0.0 copy-done.9
  3.9 1.4 %shard_map.120.near_ref = bf16[176,128]{1,0:T(8,128)(2,1)S(1)} custom-call(s32[4]{0:T(128)S(1)} %copy-done.9, f32[8,128]{1,0:T(8,128)S(1)} %shard_map.119.section_ref, bf16[8,1280]{1,0:T(8,128)(2,1)S(1)} %copy-done.4, bf16[8,256]{1,0:T(8,128)(2,1)S(1)} %copy-done.5, bf16[8,256]{1,0:T(8,128)(2,1)S(1)} %copy-done.6, bf16[4,512,256]{2,1,0:T(8,128)(2,1)S(1)} %copy-done.2, ...), custom_call_target="tpu_custom_call" | custom-call | flops 167772160 | bytes 2097152 | tf_op jit(solution)/shard_map/pallas_call | solution.py:289
  5.3 0.0 copy-start.7
  5.3 0.1 collective-permute-start.2
  5.4 2.7 %collective-permute-start.5 = (bf16[176,128]{1,0:T(8,128)(2,1)S(1)}, bf16[176,128]{1,0:T(8,128)(2,1)S(1)}, u32[]{:S(2)}, u32[]{:S(2)}) collective-permute-start(bf16[176,128]{1,0:T(8,128)(2,1)S(1)} %shard_map.120.near_ref), channel_id=1, source_target_pairs={{0,8},{4,12},{8,0},{12,4},{1,9},{5,13},{9,1},{13,5},{2,10},{6,14},... | collective-permute-start | bytes 135176 | tf_op jit(solution)/shard_map/ppermute | solution.py:249
  8.1 0.0 collective-permute-done.refs_2_
  8.1 0.1 collective-permute-start.1
  8.2 0.0 collective-permute-done.2.refs_1_
  8.2 0.0 copy-done
  8.2 0.8 %shard_map.121 = (f32[128,256]{1,0:T(8,128)S(1)}, f32[64,128]{1,0:T(8,128)S(1)}) custom-call(bf16[64,1280]{1,0:T(8,128)(2,1)S(1)} %copy-done.10, bf16[64,1280]{1,0:T(8,128)(2,1)S(1)} %collective-permute-done.2.refs_1_, bf16[64,1280]{1,0:T(8,128)(2,1)S(1)} %collective-permute-done.refs_2_, bf16[2,5120,256]{2,1,0:T(8,128)(2,1)S(1)} %copy-done), custom_call_target="tpu_custom_call" | custom-call | flops 68719476736 | bytes 5242880 | tf_op jit(solution)/shard_map/pallas_call | solution.py:301
  9.0 0.4 %collective-permute-done.1.refs_0_ = bf16[64,1280]{1,0:T(8,128)(2,1)S(1)} collective-permute-done((bf16[64,1280]{1,0:T(8,128)(2,1)S(1)}, bf16[64,1280]{1,0:T(8,128)(2,1)S(1)}, u32[]{:S(2)}, u32[]{:S(2)}) %collective-permute-start.1) | collective-permute-done | bytes 163872 | tf_op jit(solution)/shard_map/ppermute | solution.py:249
  9.5 0.0 copy-done.7
  9.5 0.4 %shard_map.122.after.refs_0_ = bf16[128,256]{1,0:T(8,128)(2,1)S(1)} custom-call(bf16[64,1280]{1,0:T(8,128)(2,1)S(1)} %collective-permute-done.1.refs_0_, bf16[2,5120,256]{2,1,0:T(8,128)(2,1)S(1)} %copy-done, f32[128,256]{1,0:T(8,128)S(1)} %get-tuple-element.27.refs_2_, f32[64,128]{1,0:T(8,128)S(1)} %get-tuple-element.28.refs_3_, bf16[2,256]{1,0:T(2,128)(2,1)S(1)} %copy-done.7), custom_call_target="tpu_custom_call" | custom-call | flops 83886080 | bytes 1310720 | tf_op jit(solution)/shard_map/pallas_call | solution.py:309
  9.9 0.0 copy-start.1
  9.9 2.9 %collective-permute-start.4 = (bf16[128,256]{1,0:T(8,128)(2,1)S(1)}, bf16[128,256]{1,0:T(8,128)(2,1)S(1)}, u32[]{:S(2)}, u32[]{:S(2)}) collective-permute-start(bf16[128,256]{1,0:T(8,128)(2,1)S(1)} %shard_map.122.after.refs_0_), channel_id=1, source_target_pairs={{0,8},{4,12},{8,0},{12,4},{1,9},{5,13},{9,1},{13,5},{2,10},{6,14},... | collective-permute-start | bytes 196616 | tf_op jit(solution)/shard_map/ppermute | solution.py:249
  12.8 0.0 collective-permute-done.5.far_ref
  12.8 1.6 %collective-permute-start.7 = (bf16[2,176,128]{2,1,0:T(8,128)(2,1)S(1)}, bf16[2,176,128]{2,1,0:T(8,128)(2,1)S(1)}, u32[]{:S(2)}, u32[]{:S(2)}) collective-permute-start(bf16[2,176,128]{2,1,0:T(8,128)(2,1)S(1)} %shard_map.123.refs_0_), channel_id=1, source_target_pairs={{0,4},{4,0},{8,12},{12,8},{1,5},{5,1},{9,13},{13,9},{2,6},{6,2},{1... | collective-permute-start | bytes 270344 | tf_op jit(solution)/shard_map/ppermute | solution.py:249
  14.4 0.5 %collective-permute-start.3 = (bf16[128,256]{1,0:T(8,128)(2,1)S(1)}, bf16[128,256]{1,0:T(8,128)(2,1)S(1)}, u32[]{:S(2)}, u32[]{:S(2)}) collective-permute-start(bf16[128,256]{1,0:T(8,128)(2,1)S(1)} %shard_map.122.after.refs_0_), channel_id=1, source_target_pairs={{0,4},{4,0},{8,12},{12,8},{1,5},{5,1},{9,13},{13,9},{2,6},{6,2},{1... | collective-permute-start | bytes 196616 | tf_op jit(solution)/shard_map/ppermute | solution.py:249
  14.9 1.3 %collective-permute-done.4.refs_2_ = bf16[128,256]{1,0:T(8,128)(2,1)S(1)} collective-permute-done((bf16[128,256]{1,0:T(8,128)(2,1)S(1)}, bf16[128,256]{1,0:T(8,128)(2,1)S(1)}, u32[]{:S(2)}, u32[]{:S(2)}) %collective-permute-start.4) | collective-permute-done | bytes 65568 | tf_op jit(solution)/shard_map/ppermute | solution.py:249
  16.2 1.3 %collective-permute-start.6 = (bf16[128,256]{1,0:T(8,128)(2,1)S(1)}, bf16[128,256]{1,0:T(8,128)(2,1)S(1)}, u32[]{:S(2)}, u32[]{:S(2)}) collective-permute-start(bf16[128,256]{1,0:T(8,128)(2,1)S(1)} %collective-permute-done.4.refs_2_), channel_id=1, source_target_pairs={{0,4},{4,0},{8,12},{12,8},{1,5},{5,1},{9,13},{13,9},{2,6},{6,2},{1... | collective-permute-start | bytes 196616 | tf_op jit(solution)/shard_map/ppermute | solution.py:249
  17.5 0.7 %collective-permute-done.7.refs_1_ = bf16[2,176,128]{2,1,0:T(8,128)(2,1)S(1)} collective-permute-done((bf16[2,176,128]{2,1,0:T(8,128)(2,1)S(1)}, bf16[2,176,128]{2,1,0:T(8,128)(2,1)S(1)}, u32[]{:S(2)}, u32[]{:S(2)}) %collective-permute-start.7) | collective-permute-done | bytes 90144 | tf_op jit(solution)/shard_map/ppermute | solution.py:249
  18.2 0.0 copy-done.8
  18.2 0.5 %shard_map.124 = (bf16[320,256]{1,0:T(8,128)(2,1)S(1)}, f32[320,256]{1,0:T(8,128)S(1)}, f32[320,128]{1,0:T(8,128)S(1)}, f32[320,128]{1,0:T(8,128)S(1)}) custom-call(bf16[2,176,128]{2,1,0:T(8,128)(2,1)S(1)} %shard_map.123.refs_0_, bf16[2,176,128]{2,1,0:T(8,128)(2,1)S(1)} %collective-permute-done.7.refs_1_, s32[1,256]{1,0:T(1,128)S(1)} %bitcast.1), custom_call_target="tpu_custom_call" | custom-call | flops 1024 | tf_op jit(solution)/shard_map/pallas_call | solution.py:330
  18.7 0.9 %collective-permute-done.3.refs_1_ = bf16[128,256]{1,0:T(8,128)(2,1)S(1)} collective-permute-done((bf16[128,256]{1,0:T(8,128)(2,1)S(1)}, bf16[128,256]{1,0:T(8,128)(2,1)S(1)}, u32[]{:S(2)}, u32[]{:S(2)}) %collective-permute-start.3) | collective-permute-done | bytes 65568 | tf_op jit(solution)/shard_map/ppermute | solution.py:249
  19.6 0.9 %collective-permute-done.6.refs_3_ = bf16[128,256]{1,0:T(8,128)(2,1)S(1)} collective-permute-done((bf16[128,256]{1,0:T(8,128)(2,1)S(1)}, bf16[128,256]{1,0:T(8,128)(2,1)S(1)}, u32[]{:S(2)}, u32[]{:S(2)}) %collective-permute-start.6) | collective-permute-done | bytes 65568 | tf_op jit(solution)/shard_map/ppermute | solution.py:249
  20.5 0.0 copy-done.1
  20.5 1.4 %shard_map.125 = (f32[8,1280]{1,0:T(8,128)S(1)}, bf16[8,1280]{1,0:T(8,128)(2,1)S(1)}, bf16[8,1280]{1,0:T(8,128)(2,1)S(1)}, bf16[8,1280]{1,0:T(8,128)(2,1)S(1)}) custom-call(bf16[128,256]{1,0:T(8,128)(2,1)S(1)} %shard_map.122.after.refs_0_, bf16[128,256]{1,0:T(8,128)(2,1)S(1)} %collective-permute-done.3.refs_1_, ...), custom_call_target="tpu_custom_call" | custom-call | flops 104857600 | bytes 3276800 | tf_op jit(solution)/shard_map/pallas_call | solution.py:347
  21.9 0.1 collective-permute-start.10
  22.0 1.9 %collective-permute-start.8 = (bf16[8,1280]{1,0:T(8,128)(2,1)S(1)}, bf16[8,1280]{1,0:T(8,128)(2,1)S(1)}, u32[]{:S(2)}, u32[]{:S(2)}) collective-permute-start(bf16[8,1280]{1,0:T(8,128)(2,1)S(1)} %get-tuple-element.36), channel_id=1, source_target_pairs={{0,3},{1,2},{2,1},{3,0},{4,7},{5,6},{6,5},{7,4},{8,11},{9,10},{10,... | collective-permute-start | bytes 61448 | tf_op jit(solution)/shard_map/ppermute | solution.py:249
  23.9 0.3 %collective-permute-start.9 = (bf16[8,1280]{1,0:T(8,128)(2,1)S(1)}, bf16[8,1280]{1,0:T(8,128)(2,1)S(1)}, u32[]{:S(2)}, u32[]{:S(2)}) collective-permute-start(bf16[8,1280]{1,0:T(8,128)(2,1)S(1)} %get-tuple-element.37), channel_id=1, source_target_pairs={{0,2},{1,3},{2,0},{3,1},{4,6},{5,7},{6,4},{7,5},{8,10},{9,11},{10,... | collective-permute-start | bytes 61448 | tf_op jit(solution)/shard_map/ppermute | solution.py:249
  24.2 0.0 collective-permute-done.10
  24.2 1.2 %collective-permute-done.8 = bf16[8,1280]{1,0:T(8,128)(2,1)S(1)} collective-permute-done((bf16[8,1280]{1,0:T(8,128)(2,1)S(1)}, bf16[8,1280]{1,0:T(8,128)(2,1)S(1)}, u32[]{:S(2)}, u32[]{:S(2)}) %collective-permute-start.8) | collective-permute-done | bytes 20512 | tf_op jit(solution)/shard_map/ppermute | solution.py:249
  25.4 2.3 %collective-permute-done.9 = bf16[8,1280]{1,0:T(8,128)(2,1)S(1)} collective-permute-done((bf16[8,1280]{1,0:T(8,128)(2,1)S(1)}, bf16[8,1280]{1,0:T(8,128)(2,1)S(1)}, u32[]{:S(2)}, u32[]{:S(2)}) %collective-permute-start.9) | collective-permute-done | bytes 20512 | tf_op jit(solution)/shard_map/ppermute | solution.py:249
  27.7 0.6 %add_convert_fusion = bf16[8,1280]{1,0:T(8,128)(2,1)} fusion(bf16[8,1280]{1,0:T(8,128)(2,1)S(1)} %collective-permute-done.10, bf16[8,1280]{1,0:T(8,128)(2,1)S(1)} %collective-permute-done.9, f32[8,1280]{1,0:T(8,128)S(1)} %get-tuple-element.35, bf16[8,1280]{1,0:T(8,128)(2,1)S(1)} %collective-permute-done.8), kind=kLoop, calls=%fused_computation | loop fusion | flops 71680 | bytes 122880 | tf_op jit(solution)/shard_map/convert_element_type | solution.py:363
  (5 shorter events, 0.0 us)
Async XLA Ops:
  0.0 0.9 %copy-start.10 = (bf16[64,1280]{1,0:T(8,128)(2,1)S(1)}, bf16[64,1280]{1,0:T(8,128)(2,1)}, u32[]{:S(2)}) copy-start(bf16[64,1280]{1,0:T(8,128)(2,1)} %refs_0_) | copy-start | bytes 491524
  0.0 3.9 %copy-start.4 = (bf16[8,1280]{1,0:T(8,128)(2,1)S(1)}, bf16[8,1280]{1,0:T(8,128)(2,1)}, u32[]{:S(2)}) copy-start(bf16[8,1280]{1,0:T(8,128)(2,1)} %q_ref.1) | copy-start | bytes 61444
  0.0 3.9 %copy-start.5 = (bf16[8,256]{1,0:T(8,128)(2,1)S(1)}, bf16[8,256]{1,0:T(8,128)(2,1)}, u32[]{:S(2)}) copy-start(bf16[8,256]{1,0:T(8,128)(2,1)} %nk_ref.1) | copy-start | bytes 12292
  0.0 3.9 %copy-start.6 = (bf16[8,256]{1,0:T(8,128)(2,1)S(1)}, bf16[8,256]{1,0:T(8,128)(2,1)}, u32[]{:S(2)}) copy-start(bf16[8,256]{1,0:T(8,128)(2,1)} %nv_ref.1) | copy-start | bytes 12292
  0.0 3.9 %copy-start.2 = (bf16[4,512,256]{2,1,0:T(8,128)(2,1)S(1)}, bf16[4,512,256]{2,1,0:T(8,128)(2,1)}, u32[]{:S(2)}) copy-start(bf16[4,512,256]{2,1,0:T(8,128)(2,1)} %ck_ref.1) | copy-start | bytes 3145732
  0.0 3.9 %copy-start.3 = (bf16[4,512,256]{2,1,0:T(8,128)(2,1)S(1)}, bf16[4,512,256]{2,1,0:T(8,128)(2,1)}, u32[]{:S(2)}) copy-start(bf16[4,512,256]{2,1,0:T(8,128)(2,1)} %cv_ref.1) | copy-start | bytes 3145732
  0.0 3.9 %copy-start.9 = (s32[4]{0:T(128)S(1)}, s32[4]{0:T(128)}, u32[]{:S(2)}) copy-start(s32[4]{0:T(128)} %lens_ref.1) | copy-start | bytes 52
  0.0 8.2 %copy-start = (bf16[2,5120,256]{2,1,0:T(8,128)(2,1)S(1)}, bf16[2,5120,256]{2,1,0:T(8,128)(2,1)}, u32[]{:S(2)}) copy-start(bf16[2,5120,256]{2,1,0:T(8,128)(2,1)} %refs_1_.1) | copy-start | bytes 15728644
  0.9 7.2 %collective-permute-start = (bf16[64,1280]{1,0:T(8,128)(2,1)S(1)}, bf16[64,1280]{1,0:T(8,128)(2,1)S(1)}, u32[]{:S(2)}, u32[]{:S(2)}) collective-permute-start(bf16[64,1280]{1,0:T(8,128)(2,1)S(1)} %copy-done.10), channel_id=1, source_target_pairs={{0,2},{1,3},{2,0},{3,1},{4,6},{5,7},{6,4},{7,5},{8,10},{9,11},{10,... | collective-permute-start | bytes 491528 | tf_op jit(solution)/shard_map/ppermute | solution.py:249
  5.3 4.2 %copy-start.7 = (bf16[2,256]{1,0:T(2,128)(2,1)S(1)}, bf16[2,256]{1,0:T(2,128)(2,1)}, u32[]{:S(2)}) copy-start(bf16[2,256]{1,0:T(2,128)(2,1)} %refs_4_.1) | copy-start | bytes 3076
  5.3 2.9 %collective-permute-start.2 = (bf16[64,1280]{1,0:T(8,128)(2,1)S(1)}, bf16[64,1280]{1,0:T(8,128)(2,1)S(1)}, u32[]{:S(2)}, u32[]{:S(2)}) collective-permute-start(bf16[64,1280]{1,0:T(8,128)(2,1)S(1)} %copy-done.10), channel_id=1, source_target_pairs={{0,1},{1,0},{2,3},{3,2},{4,5},{5,4},{6,7},{7,6},{8,9},{9,8},{10,11... | collective-permute-start | bytes 491528 | tf_op jit(solution)/shard_map/ppermute | solution.py:249
  5.4 7.4 %collective-permute-start.5 = (bf16[176,128]{1,0:T(8,128)(2,1)S(1)}, bf16[176,128]{1,0:T(8,128)(2,1)S(1)}, u32[]{:S(2)}, u32[]{:S(2)}) collective-permute-start(bf16[176,128]{1,0:T(8,128)(2,1)S(1)} %shard_map.120.near_ref), channel_id=1, source_target_pairs={{0,8},{4,12},{8,0},{12,4},{1,9},{5,13},{9,1},{13,5},{2,10},{6,14},... | collective-permute-start | bytes 135176 | tf_op jit(solution)/shard_map/ppermute | solution.py:249
  8.1 1.4 %collective-permute-start.1 = (bf16[64,1280]{1,0:T(8,128)(2,1)S(1)}, bf16[64,1280]{1,0:T(8,128)(2,1)S(1)}, u32[]{:S(2)}, u32[]{:S(2)}) collective-permute-start(bf16[64,1280]{1,0:T(8,128)(2,1)S(1)} %collective-permute-done.refs_2_), channel_id=1, source_target_pairs={{0,1},{1,0},{2,3},{3,2},{4,5},{5,4},{6,7},{7,6},{8,9},{9,8},{10,11... | collective-permute-start | bytes 491528 | tf_op jit(solution)/shard_map/ppermute | solution.py:249
  9.9 8.3 %copy-start.8 = (s32[256]{0:T(256)S(1)}, s32[256]{0:T(256)}, u32[]{:S(2)}) copy-start(s32[256]{0:T(256)} %param.15) | copy-start | bytes 3076
  9.9 10.6 %copy-start.1 = (bf16[1280,1280]{1,0:T(8,128)(2,1)S(1)}, bf16[1280,1280]{1,0:T(8,128)(2,1)}, u32[]{:S(2)}) copy-start(bf16[1280,1280]{1,0:T(8,128)(2,1)} %refs_8_.1) | copy-start | bytes 9830404
  9.9 6.3 %collective-permute-start.4 = (bf16[128,256]{1,0:T(8,128)(2,1)S(1)}, bf16[128,256]{1,0:T(8,128)(2,1)S(1)}, u32[]{:S(2)}, u32[]{:S(2)}) collective-permute-start(bf16[128,256]{1,0:T(8,128)(2,1)S(1)} %shard_map.122.after.refs_0_), channel_id=1, source_target_pairs={{0,8},{4,12},{8,0},{12,4},{1,9},{5,13},{9,1},{13,5},{2,10},{6,14},... | collective-permute-start | bytes 196616 | tf_op jit(solution)/shard_map/ppermute | solution.py:249
  12.8 5.4 %collective-permute-start.7 = (bf16[2,176,128]{2,1,0:T(8,128)(2,1)S(1)}, bf16[2,176,128]{2,1,0:T(8,128)(2,1)S(1)}, u32[]{:S(2)}, u32[]{:S(2)}) collective-permute-start(bf16[2,176,128]{2,1,0:T(8,128)(2,1)S(1)} %shard_map.123.refs_0_), channel_id=1, source_target_pairs={{0,4},{4,0},{8,12},{12,8},{1,5},{5,1},{9,13},{13,9},{2,6},{6,2},{1... | collective-permute-start | bytes 270344 | tf_op jit(solution)/shard_map/ppermute | solution.py:249
  14.4 5.1 %collective-permute-start.3 = (bf16[128,256]{1,0:T(8,128)(2,1)S(1)}, bf16[128,256]{1,0:T(8,128)(2,1)S(1)}, u32[]{:S(2)}, u32[]{:S(2)}) collective-permute-start(bf16[128,256]{1,0:T(8,128)(2,1)S(1)} %shard_map.122.after.refs_0_), channel_id=1, source_target_pairs={{0,4},{4,0},{8,12},{12,8},{1,5},{5,1},{9,13},{13,9},{2,6},{6,2},{1... | collective-permute-start | bytes 196616 | tf_op jit(solution)/shard_map/ppermute | solution.py:249
  16.2 4.3 %collective-permute-start.6 = (bf16[128,256]{1,0:T(8,128)(2,1)S(1)}, bf16[128,256]{1,0:T(8,128)(2,1)S(1)}, u32[]{:S(2)}, u32[]{:S(2)}) collective-permute-start(bf16[128,256]{1,0:T(8,128)(2,1)S(1)} %collective-permute-done.4.refs_2_), channel_id=1, source_target_pairs={{0,4},{4,0},{8,12},{12,8},{1,5},{5,1},{9,13},{13,9},{2,6},{6,2},{1... | collective-permute-start | bytes 196616 | tf_op jit(solution)/shard_map/ppermute | solution.py:249
  21.9 2.2 %collective-permute-start.10 = (bf16[8,1280]{1,0:T(8,128)(2,1)S(1)}, bf16[8,1280]{1,0:T(8,128)(2,1)S(1)}, u32[]{:S(2)}, u32[]{:S(2)}) collective-permute-start(bf16[8,1280]{1,0:T(8,128)(2,1)S(1)} %get-tuple-element.38), channel_id=1, source_target_pairs={{0,1},{1,0},{2,3},{3,2},{4,5},{5,4},{6,7},{7,6},{8,9},{9,8},{10,11... | collective-permute-start | bytes 61448 | tf_op jit(solution)/shard_map/ppermute | solution.py:249
  22.0 3.3 %collective-permute-start.8 = (bf16[8,1280]{1,0:T(8,128)(2,1)S(1)}, bf16[8,1280]{1,0:T(8,128)(2,1)S(1)}, u32[]{:S(2)}, u32[]{:S(2)}) collective-permute-start(bf16[8,1280]{1,0:T(8,128)(2,1)S(1)} %get-tuple-element.36), channel_id=1, source_target_pairs={{0,3},{1,2},{2,1},{3,0},{4,7},{5,6},{6,5},{7,4},{8,11},{9,10},{10,... | collective-permute-start | bytes 61448 | tf_op jit(solution)/shard_map/ppermute | solution.py:249
  23.9 3.8 %collective-permute-start.9 = (bf16[8,1280]{1,0:T(8,128)(2,1)S(1)}, bf16[8,1280]{1,0:T(8,128)(2,1)S(1)}, u32[]{:S(2)}, u32[]{:S(2)}) collective-permute-start(bf16[8,1280]{1,0:T(8,128)(2,1)S(1)} %get-tuple-element.37), channel_id=1, source_target_pairs={{0,2},{1,3},{2,0},{3,1},{4,6},{5,7},{6,4},{7,5},{8,10},{9,11},{10,... | collective-permute-start | bytes 61448 | tf_op jit(solution)/shard_map/ppermute | solution.py:249

commit v5 on v4

--- a/solution.py
+++ b/solution.py
@@ -143,21 +143,15 @@
             refs[0][s * rows : (s + 1) * rows, :] = acc[s]
         refs[1][...] = jnp.broadcast_to(squares, refs[1].shape)
         return
-    b_ref, out_ref = refs
+    b_ref, *_, out_ref = refs
     scale = lax.rsqrt(squares / D + 1e-06)
     for s in range(2):
         bias = b_ref[s : s + 1, :].astype(f32)
         out_ref[s * rows : (s + 1) * rows, :] = (acc[s] * scale + bias).astype(bf16)
 
 
-def pair_kernel(near_ref, far_ref, after, out_ref):
-    out_ref[0] = near_ref[...]
-    out_ref[1] = far_ref[...]
-
-
 def prepare_kernel(heads, *refs):
-    pairs, (section_ref, q_ref, bias_ref, old_ref, stats_ref) = refs[:-5], refs[-5:]
-    parts = [pair.at[i] for i in range(2) for pair in pairs]
+    parts, (section_ref, q_ref, bias_ref, old_ref, stats_ref) = refs[:-5], refs[-5:]
     groups = len(parts)
     seg = (parts[0].shape[0] - STATS) // 2
     rows = q_ref.shape[0] // groups
@@ -296,7 +290,9 @@
     )(cache_lengths, section, queries, new_keys, new_values, cache_keys, cache_values)
     own_later, part = lax.optimization_barrier((own, part))
     hidden = passed_on(own, own_later, "tp")
+    half = range(1, groups // 2)
     part_far = permute(part, "dp", groups // 2)
+    part_near = [permute(part, "dp", bits) for bits in half]
     near, far = list(range(shares - 1)), [shares - 1]
     partial = call(
         functools.partial(project_kernel, near, True, False),
@@ -308,28 +304,28 @@
     )(*[hidden[k] for k in near], kv_weight)
     kv = call(
         functools.partial(project_kernel, far, False, True),
-        [VMEM] * 5,
+        [VMEM] * 5 + [ANY] * len(part_near),
         pltpu.VMEM((2 * memory, cols), bf16),
         [],
         4 * memory * D * cols // shares,
         4 * D * cols // shares,
-    )(hidden[far[0]], kv_weight, *partial, kv_bias)
+    )(hidden[far[0]], kv_weight, *partial, kv_bias, *part_near)
     kv_far = permute(kv, "dp", groups // 2)
-    pair = call(
-        pair_kernel,
-        [VMEM, VMEM, ANY],
-        pltpu.VMEM((2,) + part.shape, bf16),
-        [],
-        COVER,
-        0,
-    )(part, part_far, kv)
-    kv_on, _ = lax.optimization_barrier((kv_far, pair))
-    half = range(1, groups // 2)
-    pairs = [pair, *[permute(pair, "dp", bits) for bits in half]]
+    part_far = pl.pallas_call(
+        lambda *refs: None,
+        in_specs=[VMEM, ANY],
+        out_shape=pltpu.VMEM(part.shape, bf16),
+        out_specs=VMEM,
+        input_output_aliases={0: 0},
+        compiler_params=PARAMS,
+        cost_estimate=pl.CostEstimate(flops=COVER, bytes_accessed=0, transcendentals=0),
+    )(part_far, kv)
+    parts = [part, *part_near, part_far, *[permute(part_far, "dp", bits) for bits in half]]
+    kv_on, *_ = lax.optimization_barrier((kv_far, *parts[groups // 2 :]))
     kvs = [kv, *[permute(kv, "dp", bits) for bits in half], kv_far, *[permute(kv_on, "dp", bits) for bits in half]]
     prepared = call(
         functools.partial(prepare_kernel, cols // HD),
-        [VMEM] * (groups // 2 + 1),
+        [VMEM] * (groups + 1),
         [
             pltpu.VMEM((groups * rows, cols), bf16),
             pltpu.VMEM((groups * rows, every), f32),
@@ -339,7 +335,7 @@
         [],
         PCOVER,
         0,
-    )(*pairs, memory_sections.reshape(1, every))
+    )(*parts, memory_sections.reshape(1, every))
 
     out_rows, out_cols = groups * tokens, out_weight.shape[1]
     share = out_rows // shares
@@ -358,7 +354,7 @@
         2 * out_weight.size,
     )(*kvs, *prepared, out_weight)
     summed = pieces[0]
-    for bits in range(shares - 1, 0, -1):
+    for bits in [*range(1, shares - 2), *range(shares - 1, shares - 3, -1)]:
         summed = summed + permute(pieces[bits], "tp", bits).astype(f32)
     return summed.astype(bf16)
 

time: 28.4 us -> 29 us (1.021)
  waiting for transfers between devices: 7.82 us -> 9.69 us
  starting transfers between devices: 14.3 us -> 13 us
    ppermute x11 -> x12, waiting for transfers between devices: 7.82 us -> 9.69 us  [permute(): lax.ppermute(x, axis, [(i, i ^ bits) for i in range(lax.axis_size(axis))])]
    ppermute x11 -> x12, starting transfers between devices: 14.3 us -> 13 us  [permute(): lax.ppermute(x, axis, [(i, i ^ bits) for i in range(lax.axis_size(axis))])]
  transfers between devices with their start and end apart: 11 -> 12, of which waited for: 7 -> 6; matrix products, arithmetic and copies ran while one was open for 0% -> 0% of each run, Pallas kernels for 11% -> 11%
where the time goes in v5:
time: 29 us; the launch traced here: 28.9 us
  starting transfers between devices  13 us (45%)
  waiting for transfers between devices  9.69 us (33%)
  Pallas kernels  4.48 us (15%)
  between operations  0.95 us (3%)
  other arithmetic  0.62 us (2%)
    ppermute x12, starting transfers between devices, permute(): lax.ppermute(x, axis, [(i, i ^ bits) for i in range(lax.axis_size(axis))])  13 us
    ppermute x12, waiting for transfers between devices, permute(): lax.ppermute(x, axis, [(i, i ^ bits) for i in range(lax.axis_size(axis))])  9.69 us
    pallas_call x1, Pallas kernels, body(): call(functools.partial(attend_kernel, groups, shares), [VMEM] * (groups +...  1.42 us
    pallas_call x1, Pallas kernels, body(): call(cache_kernel, [SMEM] + [VMEM] * 6, pltpu.VMEM((2 * up(rows, 16) + ST...  1.38 us
    pallas_call x1, Pallas kernels, body(): call(functools.partial(project_kernel, near, True, False), [VMEM] * (len(...  0.82 us
    convert_element_type x1, other arithmetic, body(): return summed.astype(bf16)  0.62 us
  transfers between devices with their start and end apart: 12, of which 6 were waited for; matrix products, arithmetic and copies ran while one was open for 0% of the time, Pallas kernels for 11%

profile of v5, /device:TPU:0, one launch (start us, length us, event | category | flops | bytes accessed | tf_op | source)
XLA Modules:
  0.0 28.9 jit_solution(18193373435196786600)
XLA Ops:
  0.0 0.0 copy-start.10
  0.0 0.0 copy-start.4
  0.0 0.0 copy-start.3
  0.0 0.0 copy-start.9
  0.0 0.0 copy-start
  0.9 0.1 copy-done.10
  0.9 3.0 %collective-permute-start = (bf16[64,1280]{1,0:T(8,128)(2,1)S(1)}, bf16[64,1280]{1,0:T(8,128)(2,1)S(1)}, u32[]{:S(2)}, u32[]{:S(2)}) collective-permute-start(bf16[64,1280]{1,0:T(8,128)(2,1)S(1)} %copy-done.10), channel_id=1, source_target_pairs={{0,2},{1,3},{2,0},{3,1},{4,6},{5,7},{6,4},{7,5},{8,10},{9,11},{10,... | collective-permute-start | bytes 491528 | tf_op jit(solution)/shard_map/ppermute | solution.py:243
  3.9 0.0 copy-done.4
  3.9 0.0 copy-done.5
  3.9 0.0 copy-done.6
  3.9 0.0 copy-done.2
  3.9 0.0 copy-done.3
  3.9 0.0 copy-done.9
  3.9 1.4 %shard_map.120.refs_0_ = bf16[176,128]{1,0:T(8,128)(2,1)S(1)} custom-call(s32[4]{0:T(128)S(1)} %copy-done.9, f32[8,128]{1,0:T(8,128)S(1)} %shard_map.119.section_ref, bf16[8,1280]{1,0:T(8,128)(2,1)S(1)} %copy-done.4, bf16[8,256]{1,0:T(8,128)(2,1)S(1)} %copy-done.5, bf16[8,256]{1,0:T(8,128)(2,1)S(1)} %copy-done.6, bf16[4,512,256]{2,1,0:T(8,128)(2,1)S(1)} %copy-done.2, ...), custom_call_target="tpu_custom_call" | custom-call | flops 167772160 | bytes 2097152 | tf_op jit(solution)/shard_map/pallas_call | solution.py:283
  5.3 0.0 copy-start.8
  5.3 0.1 collective-permute-start.2
  5.4 1.6 %collective-permute-start.3 = (bf16[176,128]{1,0:T(8,128)(2,1)S(1)}, bf16[176,128]{1,0:T(8,128)(2,1)S(1)}, u32[]{:S(2)}, u32[]{:S(2)}) collective-permute-start(bf16[176,128]{1,0:T(8,128)(2,1)S(1)} %shard_map.120.refs_0_), channel_id=1, source_target_pairs={{0,4},{4,0},{8,12},{12,8},{1,5},{5,1},{9,13},{13,9},{2,6},{6,2},{1... | collective-permute-start | bytes 135176 | tf_op jit(solution)/shard_map/ppermute | solution.py:243
  7.0 2.6 %collective-permute-start.6 = (bf16[176,128]{1,0:T(8,128)(2,1)S(1)}, bf16[176,128]{1,0:T(8,128)(2,1)S(1)}, u32[]{:S(2)}, u32[]{:S(2)}) collective-permute-start(bf16[176,128]{1,0:T(8,128)(2,1)S(1)} %shard_map.120.refs_0_), channel_id=1, source_target_pairs={{0,8},{4,12},{8,0},{12,4},{1,9},{5,13},{9,1},{13,5},{2,10},{6,14},... | collective-permute-start | bytes 135176 | tf_op jit(solution)/shard_map/ppermute | solution.py:243
  9.6 0.0 collective-permute-done.refs_2_
  9.6 0.0 collective-permute-start.1
  9.6 0.0 collective-permute-done.2.refs_1_
  9.6 0.0 copy-done
  9.7 0.8 %shard_map.121 = (f32[128,256]{1,0:T(8,128)S(1)}, f32[64,128]{1,0:T(8,128)S(1)}) custom-call(bf16[64,1280]{1,0:T(8,128)(2,1)S(1)} %copy-done.10, bf16[64,1280]{1,0:T(8,128)(2,1)S(1)} %collective-permute-done.2.refs_1_, bf16[64,1280]{1,0:T(8,128)(2,1)S(1)} %collective-permute-done.refs_2_, bf16[2,5120,256]{2,1,0:T(8,128)(2,1)S(1)} %copy-done), custom_call_target="tpu_custom_call" | custom-call | flops 68719476736 | bytes 5242880 | tf_op jit(solution)/shard_map/pallas_call | solution.py:297
  10.5 0.0 collective-permute-done.3.refs_5_.refs_1_
  10.5 0.5 %collective-permute-done.1.refs_0_ = bf16[64,1280]{1,0:T(8,128)(2,1)S(1)} collective-permute-done((bf16[64,1280]{1,0:T(8,128)(2,1)S(1)}, bf16[64,1280]{1,0:T(8,128)(2,1)S(1)}, u32[]{:S(2)}, u32[]{:S(2)}) %collective-permute-start.1) | collective-permute-done | bytes 163872 | tf_op jit(solution)/shard_map/ppermute | solution.py:243
  11.0 0.0 copy-done.8
  11.0 0.4 %shard_map.122.refs_1_.refs_0_ = bf16[128,256]{1,0:T(8,128)(2,1)S(1)} custom-call(bf16[64,1280]{1,0:T(8,128)(2,1)S(1)} %collective-permute-done.1.refs_0_, bf16[2,5120,256]{2,1,0:T(8,128)(2,1)S(1)} %copy-done, f32[128,256]{1,0:T(8,128)S(1)} %get-tuple-element.27.refs_2_, f32[64,128]{1,0:T(8,128)S(1)} %get-tuple-element.28.refs_3_, ...), custom_call_target="tpu_custom_call" | custom-call | flops 83886080 | bytes 1310720 | tf_op jit(solution)/shard_map/pallas_call | solution.py:305
  11.4 0.0 copy-start.1
  11.4 1.5 %collective-permute-start.5 = (bf16[128,256]{1,0:T(8,128)(2,1)S(1)}, bf16[128,256]{1,0:T(8,128)(2,1)S(1)}, u32[]{:S(2)}, u32[]{:S(2)}) collective-permute-start(bf16[128,256]{1,0:T(8,128)(2,1)S(1)} %shard_map.122.refs_1_.refs_0_), channel_id=1, source_target_pairs={{0,8},{4,12},{8,0},{12,4},{1,9},{5,13},{9,1},{13,5},{2,10},{6,14},... | collective-permute-start | bytes 196616 | tf_op jit(solution)/shard_map/ppermute | solution.py:243
  13.0 0.0 collective-permute-done.6.refs_0_
  13.0 1.4 %collective-permute-start.7 = (bf16[176,128]{1,0:T(8,128)(2,1)S(1)}, bf16[176,128]{1,0:T(8,128)(2,1)S(1)}, u32[]{:S(2)}, u32[]{:S(2)}) collective-permute-start(bf16[176,128]{1,0:T(8,128)(2,1)S(1)} %shard_map.123.refs_2_), channel_id=1, source_target_pairs={{0,4},{4,0},{8,12},{12,8},{1,5},{5,1},{9,13},{13,9},{2,6},{6,2},{1... | collective-permute-start | bytes 135176 | tf_op jit(solution)/shard_map/ppermute | solution.py:243
  14.4 0.6 %collective-permute-start.4 = (bf16[128,256]{1,0:T(8,128)(2,1)S(1)}, bf16[128,256]{1,0:T(8,128)(2,1)S(1)}, u32[]{:S(2)}, u32[]{:S(2)}) collective-permute-start(bf16[128,256]{1,0:T(8,128)(2,1)S(1)} %shard_map.122.refs_1_.refs_0_), channel_id=1, source_target_pairs={{0,4},{4,0},{8,12},{12,8},{1,5},{5,1},{9,13},{13,9},{2,6},{6,2},{1... | collective-permute-start | bytes 196616 | tf_op jit(solution)/shard_map/ppermute | solution.py:243
  15.0 3.6 %collective-permute-done.7.refs_3_ = bf16[176,128]{1,0:T(8,128)(2,1)S(1)} collective-permute-done((bf16[176,128]{1,0:T(8,128)(2,1)S(1)}, bf16[176,128]{1,0:T(8,128)(2,1)S(1)}, u32[]{:S(2)}, u32[]{:S(2)}) %collective-permute-start.7) | collective-permute-done | bytes 45088 | tf_op jit(solution)/shard_map/ppermute | solution.py:243
  18.6 0.0 collective-permute-done.5.refs_2_
  18.6 0.3 collective-permute-start.8
  18.9 0.0 copy-done.7
  18.9 0.5 %shard_map.124 = (bf16[320,256]{1,0:T(8,128)(2,1)S(1)}, f32[320,256]{1,0:T(8,128)S(1)}, f32[320,128]{1,0:T(8,128)S(1)}, f32[320,128]{1,0:T(8,128)S(1)}) custom-call(bf16[176,128]{1,0:T(8,128)(2,1)S(1)} %shard_map.120.refs_0_, bf16[176,128]{1,0:T(8,128)(2,1)S(1)} %collective-permute-done.3.refs_5_.refs_1_, bf16[176,128]{1,0:T(8,128)(2,1)S(1)} %shard_map.123.refs_2_, ...), custom_call_target="tpu_custom_call" | custom-call | flops 1024 | tf_op jit(solution)/shard_map/pallas_call | solution.py:326
  19.4 0.2 collective-permute-done.4.refs_1_
  19.6 3.3 %collective-permute-done.8.refs_3_ = bf16[128,256]{1,0:T(8,128)(2,1)S(1)} collective-permute-done((bf16[128,256]{1,0:T(8,128)(2,1)S(1)}, bf16[128,256]{1,0:T(8,128)(2,1)S(1)}, u32[]{:S(2)}, u32[]{:S(2)}) %collective-permute-start.8) | collective-permute-done | bytes 65568 | tf_op jit(solution)/shard_map/ppermute | solution.py:243
  22.9 0.0 copy-done.1
  22.9 1.4 %shard_map.125 = (f32[8,1280]{1,0:T(8,128)S(1)}, bf16[8,1280]{1,0:T(8,128)(2,1)S(1)}, bf16[8,1280]{1,0:T(8,128)(2,1)S(1)}, bf16[8,1280]{1,0:T(8,128)(2,1)S(1)}) custom-call(bf16[128,256]{1,0:T(8,128)(2,1)S(1)} %shard_map.122.refs_1_.refs_0_, bf16[128,256]{1,0:T(8,128)(2,1)S(1)} %collective-permute-done.4.refs_1_, ...), custom_call_target="tpu_custom_call" | custom-call | flops 104857600 | bytes 3276800 | tf_op jit(solution)/shard_map/pallas_call | solution.py:343
  24.3 0.1 collective-permute-start.10
  24.4 0.6 %collective-permute-start.11 = (bf16[8,1280]{1,0:T(8,128)(2,1)S(1)}, bf16[8,1280]{1,0:T(8,128)(2,1)S(1)}, u32[]{:S(2)}, u32[]{:S(2)}) collective-permute-start(bf16[8,1280]{1,0:T(8,128)(2,1)S(1)} %get-tuple-element.38), channel_id=1, source_target_pairs={{0,2},{1,3},{2,0},{3,1},{4,6},{5,7},{6,4},{7,5},{8,10},{9,11},{10,... | collective-permute-start | bytes 61448 | tf_op jit(solution)/shard_map/ppermute | solution.py:243
  25.0 1.3 %collective-permute-start.9 = (bf16[8,1280]{1,0:T(8,128)(2,1)S(1)}, bf16[8,1280]{1,0:T(8,128)(2,1)S(1)}, u32[]{:S(2)}, u32[]{:S(2)}) collective-permute-start(bf16[8,1280]{1,0:T(8,128)(2,1)S(1)} %get-tuple-element.36), channel_id=1, source_target_pairs={{0,1},{1,0},{2,3},{3,2},{4,5},{5,4},{6,7},{7,6},{8,9},{9,8},{10,11... | collective-permute-start | bytes 61448 | tf_op jit(solution)/shard_map/ppermute | solution.py:243
  26.3 1.3 %collective-permute-done.10 = bf16[8,1280]{1,0:T(8,128)(2,1)S(1)} collective-permute-done((bf16[8,1280]{1,0:T(8,128)(2,1)S(1)}, bf16[8,1280]{1,0:T(8,128)(2,1)S(1)}, u32[]{:S(2)}, u32[]{:S(2)}) %collective-permute-start.10) | collective-permute-done | bytes 20512 | tf_op jit(solution)/shard_map/ppermute | solution.py:243
  27.6 0.7 %collective-permute-done.11 = bf16[8,1280]{1,0:T(8,128)(2,1)S(1)} collective-permute-done((bf16[8,1280]{1,0:T(8,128)(2,1)S(1)}, bf16[8,1280]{1,0:T(8,128)(2,1)S(1)}, u32[]{:S(2)}, u32[]{:S(2)}) %collective-permute-start.11) | collective-permute-done | bytes 20512 | tf_op jit(solution)/shard_map/ppermute | solution.py:243
  28.3 0.0 collective-permute-done.9
  28.3 0.6 %add_convert_fusion = bf16[8,1280]{1,0:T(8,128)(2,1)} fusion(bf16[8,1280]{1,0:T(8,128)(2,1)S(1)} %collective-permute-done.11, bf16[8,1280]{1,0:T(8,128)(2,1)S(1)} %collective-permute-done.10, f32[8,1280]{1,0:T(8,128)S(1)} %get-tuple-element.35, bf16[8,1280]{1,0:T(8,128)(2,1)S(1)} %collective-permute-done.9), kind=kLoop, calls=%fused_computation | loop fusion | flops 71680 | bytes 122880 | tf_op jit(solution)/shard_map/convert_element_type | solution.py:359
  (7 shorter events, 0.0 us)
Async XLA Ops:
  0.0 0.9 %copy-start.10 = (bf16[64,1280]{1,0:T(8,128)(2,1)S(1)}, bf16[64,1280]{1,0:T(8,128)(2,1)}, u32[]{:S(2)}) copy-start(bf16[64,1280]{1,0:T(8,128)(2,1)} %refs_0_) | copy-start | bytes 491524
  0.0 3.9 %copy-start.4 = (bf16[8,1280]{1,0:T(8,128)(2,1)S(1)}, bf16[8,1280]{1,0:T(8,128)(2,1)}, u32[]{:S(2)}) copy-start(bf16[8,1280]{1,0:T(8,128)(2,1)} %q_ref.1) | copy-start | bytes 61444
  0.0 3.9 %copy-start.5 = (bf16[8,256]{1,0:T(8,128)(2,1)S(1)}, bf16[8,256]{1,0:T(8,128)(2,1)}, u32[]{:S(2)}) copy-start(bf16[8,256]{1,0:T(8,128)(2,1)} %nk_ref.1) | copy-start | bytes 12292
  0.0 3.9 %copy-start.6 = (bf16[8,256]{1,0:T(8,128)(2,1)S(1)}, bf16[8,256]{1,0:T(8,128)(2,1)}, u32[]{:S(2)}) copy-start(bf16[8,256]{1,0:T(8,128)(2,1)} %nv_ref.1) | copy-start | bytes 12292
  0.0 3.9 %copy-start.2 = (bf16[4,512,256]{2,1,0:T(8,128)(2,1)S(1)}, bf16[4,512,256]{2,1,0:T(8,128)(2,1)}, u32[]{:S(2)}) copy-start(bf16[4,512,256]{2,1,0:T(8,128)(2,1)} %ck_ref.1) | copy-start | bytes 3145732
  0.0 3.9 %copy-start.3 = (bf16[4,512,256]{2,1,0:T(8,128)(2,1)S(1)}, bf16[4,512,256]{2,1,0:T(8,128)(2,1)}, u32[]{:S(2)}) copy-start(bf16[4,512,256]{2,1,0:T(8,128)(2,1)} %cv_ref.1) | copy-start | bytes 3145732
  0.0 3.9 %copy-start.9 = (s32[4]{0:T(128)S(1)}, s32[4]{0:T(128)}, u32[]{:S(2)}) copy-start(s32[4]{0:T(128)} %lens_ref.1) | copy-start | bytes 52
  0.0 9.6 %copy-start = (bf16[2,5120,256]{2,1,0:T(8,128)(2,1)S(1)}, bf16[2,5120,256]{2,1,0:T(8,128)(2,1)}, u32[]{:S(2)}) copy-start(bf16[2,5120,256]{2,1,0:T(8,128)(2,1)} %refs_1_.1) | copy-start | bytes 15728644
  0.9 8.7 %collective-permute-start = (bf16[64,1280]{1,0:T(8,128)(2,1)S(1)}, bf16[64,1280]{1,0:T(8,128)(2,1)S(1)}, u32[]{:S(2)}, u32[]{:S(2)}) collective-permute-start(bf16[64,1280]{1,0:T(8,128)(2,1)S(1)} %copy-done.10), channel_id=1, source_target_pairs={{0,2},{1,3},{2,0},{3,1},{4,6},{5,7},{6,4},{7,5},{8,10},{9,11},{10,... | collective-permute-start | bytes 491528 | tf_op jit(solution)/shard_map/ppermute | solution.py:243
  5.3 5.7 %copy-start.8 = (bf16[2,256]{1,0:T(2,128)(2,1)S(1)}, bf16[2,256]{1,0:T(2,128)(2,1)}, u32[]{:S(2)}) copy-start(bf16[2,256]{1,0:T(2,128)(2,1)} %refs_4_.1) | copy-start | bytes 3076
  5.3 4.3 %collective-permute-start.2 = (bf16[64,1280]{1,0:T(8,128)(2,1)S(1)}, bf16[64,1280]{1,0:T(8,128)(2,1)S(1)}, u32[]{:S(2)}, u32[]{:S(2)}) collective-permute-start(bf16[64,1280]{1,0:T(8,128)(2,1)S(1)} %copy-done.10), channel_id=1, source_target_pairs={{0,1},{1,0},{2,3},{3,2},{4,5},{5,4},{6,7},{7,6},{8,9},{9,8},{10,11... | collective-permute-start | bytes 491528 | tf_op jit(solution)/shard_map/ppermute | solution.py:243
  5.4 5.1 %collective-permute-start.3 = (bf16[176,128]{1,0:T(8,128)(2,1)S(1)}, bf16[176,128]{1,0:T(8,128)(2,1)S(1)}, u32[]{:S(2)}, u32[]{:S(2)}) collective-permute-start(bf16[176,128]{1,0:T(8,128)(2,1)S(1)} %shard_map.120.refs_0_), channel_id=1, source_target_pairs={{0,4},{4,0},{8,12},{12,8},{1,5},{5,1},{9,13},{13,9},{2,6},{6,2},{1... | collective-permute-start | bytes 135176 | tf_op jit(solution)/shard_map/ppermute | solution.py:243
  7.0 5.9 %collective-permute-start.6 = (bf16[176,128]{1,0:T(8,128)(2,1)S(1)}, bf16[176,128]{1,0:T(8,128)(2,1)S(1)}, u32[]{:S(2)}, u32[]{:S(2)}) collective-permute-start(bf16[176,128]{1,0:T(8,128)(2,1)S(1)} %shard_map.120.refs_0_), channel_id=1, source_target_pairs={{0,8},{4,12},{8,0},{12,4},{1,9},{5,13},{9,1},{13,5},{2,10},{6,14},... | collective-permute-start | bytes 135176 | tf_op jit(solution)/shard_map/ppermute | solution.py:243
  9.6 1.4 %collective-permute-start.1 = (bf16[64,1280]{1,0:T(8,128)(2,1)S(1)}, bf16[64,1280]{1,0:T(8,128)(2,1)S(1)}, u32[]{:S(2)}, u32[]{:S(2)}) collective-permute-start(bf16[64,1280]{1,0:T(8,128)(2,1)S(1)} %collective-permute-done.refs_2_), channel_id=1, source_target_pairs={{0,1},{1,0},{2,3},{3,2},{4,5},{5,4},{6,7},{7,6},{8,9},{9,8},{10,11... | collective-permute-start | bytes 491528 | tf_op jit(solution)/shard_map/ppermute | solution.py:243
  11.4 7.5 %copy-start.7 = (s32[256]{0:T(256)S(1)}, s32[256]{0:T(256)}, u32[]{:S(2)}) copy-start(s32[256]{0:T(256)} %param.15) | copy-start | bytes 3076
  11.4 11.5 %copy-start.1 = (bf16[1280,1280]{1,0:T(8,128)(2,1)S(1)}, bf16[1280,1280]{1,0:T(8,128)(2,1)}, u32[]{:S(2)}) copy-start(bf16[1280,1280]{1,0:T(8,128)(2,1)} %refs_8_.1) | copy-start | bytes 9830404
  11.4 7.2 %collective-permute-start.5 = (bf16[128,256]{1,0:T(8,128)(2,1)S(1)}, bf16[128,256]{1,0:T(8,128)(2,1)S(1)}, u32[]{:S(2)}, u32[]{:S(2)}) collective-permute-start(bf16[128,256]{1,0:T(8,128)(2,1)S(1)} %shard_map.122.refs_1_.refs_0_), channel_id=1, source_target_pairs={{0,8},{4,12},{8,0},{12,4},{1,9},{5,13},{9,1},{13,5},{2,10},{6,14},... | collective-permute-start | bytes 196616 | tf_op jit(solution)/shard_map/ppermute | solution.py:243
  13.0 5.6 %collective-permute-start.7 = (bf16[176,128]{1,0:T(8,128)(2,1)S(1)}, bf16[176,128]{1,0:T(8,128)(2,1)S(1)}, u32[]{:S(2)}, u32[]{:S(2)}) collective-permute-start(bf16[176,128]{1,0:T(8,128)(2,1)S(1)} %shard_map.123.refs_2_), channel_id=1, source_target_pairs={{0,4},{4,0},{8,12},{12,8},{1,5},{5,1},{9,13},{13,9},{2,6},{6,2},{1... | collective-permute-start | bytes 135176 | tf_op jit(solution)/shard_map/ppermute | solution.py:243
  14.4 5.2 %collective-permute-start.4 = (bf16[128,256]{1,0:T(8,128)(2,1)S(1)}, bf16[128,256]{1,0:T(8,128)(2,1)S(1)}, u32[]{:S(2)}, u32[]{:S(2)}) collective-permute-start(bf16[128,256]{1,0:T(8,128)(2,1)S(1)} %shard_map.122.refs_1_.refs_0_), channel_id=1, source_target_pairs={{0,4},{4,0},{8,12},{12,8},{1,5},{5,1},{9,13},{13,9},{2,6},{6,2},{1... | collective-permute-start | bytes 196616 | tf_op jit(solution)/shard_map/ppermute | solution.py:243
  18.6 4.3 %collective-permute-start.8 = (bf16[128,256]{1,0:T(8,128)(2,1)S(1)}, bf16[128,256]{1,0:T(8,128)(2,1)S(1)}, u32[]{:S(2)}, u32[]{:S(2)}) collective-permute-start(bf16[128,256]{1,0:T(8,128)(2,1)S(1)} %collective-permute-done.5.refs_2_), channel_id=1, source_target_pairs={{0,4},{4,0},{8,12},{12,8},{1,5},{5,1},{9,13},{13,9},{2,6},{6,2},{1... | collective-permute-start | bytes 196616 | tf_op jit(solution)/shard_map/ppermute | solution.py:243
  24.3 3.3 %collective-permute-start.10 = (bf16[8,1280]{1,0:T(8,128)(2,1)S(1)}, bf16[8,1280]{1,0:T(8,128)(2,1)S(1)}, u32[]{:S(2)}, u32[]{:S(2)}) collective-permute-start(bf16[8,1280]{1,0:T(8,128)(2,1)S(1)} %get-tuple-element.37), channel_id=1, source_target_pairs={{0,3},{1,2},{2,1},{3,0},{4,7},{5,6},{6,5},{7,4},{8,11},{9,10},{10,... | collective-permute-start | bytes 61448 | tf_op jit(solution)/shard_map/ppermute | solution.py:243
  24.4 3.8 %collective-permute-start.11 = (bf16[8,1280]{1,0:T(8,128)(2,1)S(1)}, bf16[8,1280]{1,0:T(8,128)(2,1)S(1)}, u32[]{:S(2)}, u32[]{:S(2)}) collective-permute-start(bf16[8,1280]{1,0:T(8,128)(2,1)S(1)} %get-tuple-element.38), channel_id=1, source_target_pairs={{0,2},{1,3},{2,0},{3,1},{4,6},{5,7},{6,4},{7,5},{8,10},{9,11},{10,... | collective-permute-start | bytes 61448 | tf_op jit(solution)/shard_map/ppermute | solution.py:243
  25.0 3.3 %collective-permute-start.9 = (bf16[8,1280]{1,0:T(8,128)(2,1)S(1)}, bf16[8,1280]{1,0:T(8,128)(2,1)S(1)}, u32[]{:S(2)}, u32[]{:S(2)}) collective-permute-start(bf16[8,1280]{1,0:T(8,128)(2,1)S(1)} %get-tuple-element.36), channel_id=1, source_target_pairs={{0,1},{1,0},{2,3},{3,2},{4,5},{5,4},{6,7},{7,6},{8,9},{9,8},{10,11... | collective-permute-start | bytes 61448 | tf_op jit(solution)/shard_map/ppermute | solution.py:243

commit v6 on v4

--- a/solution.py
+++ b/solution.py
@@ -358,7 +358,7 @@
         2 * out_weight.size,
     )(*kvs, *prepared, out_weight)
     summed = pieces[0]
-    for bits in range(shares - 1, 0, -1):
+    for bits in [*range(shares - 2, 0, -1), shares - 1]:
         summed = summed + permute(pieces[bits], "tp", bits).astype(f32)
     return summed.astype(bf16)
 

time: 28.4 us -> 27 us (0.951)
  waiting for transfers between devices: 7.82 us -> 6.68 us
    ppermute x11, waiting for transfers between devices: 7.82 us -> 6.68 us  [permute(): lax.ppermute(x, axis, [(i, i ^ bits) for i in range(lax.axis_size(axis))])]
where the time goes in v6:
time: 27 us; the launch traced here: 26.9 us
  starting transfers between devices  14.1 us (52%)
  waiting for transfers between devices  6.68 us (25%)
  Pallas kernels  4.49 us (17%)
  between operations  0.93 us (3%)
  other arithmetic  0.62 us (2%)
    ppermute x11, starting transfers between devices, permute(): lax.ppermute(x, axis, [(i, i ^ bits) for i in range(lax.axis_size(axis))])  14.1 us
    ppermute x11, waiting for transfers between devices, permute(): lax.ppermute(x, axis, [(i, i ^ bits) for i in range(lax.axis_size(axis))])  6.68 us
    pallas_call x1, Pallas kernels, body(): call(functools.partial(attend_kernel, groups, shares), [VMEM] * (groups +...  1.43 us
    pallas_call x1, Pallas kernels, body(): call(cache_kernel, [SMEM] + [VMEM] * 6, pltpu.VMEM((2 * up(rows, 16) + ST...  1.38 us
    pallas_call x1, Pallas kernels, body(): call(functools.partial(project_kernel, near, True, False), [VMEM] * (len(...  0.82 us
    convert_element_type x1, other arithmetic, body(): return summed.astype(bf16)  0.62 us
  transfers between devices with their start and end apart: 11, of which 7 were waited for; matrix products, arithmetic and copies ran while one was open for 0% of the time, Pallas kernels for 11%

profile of v6, /device:TPU:0, one launch (start us, length us, event | category | flops | bytes accessed | tf_op | source)
XLA Modules:
  0.0 26.9 jit_solution(13550471993893126969)
XLA Ops:
  0.0 0.0 copy-start.10
  0.0 0.0 copy-start.4
  0.0 0.0 copy-start.5
  0.0 0.0 copy-start.6
  0.0 0.0 copy-start.3
  0.0 0.0 copy-start.9
  0.0 0.0 copy-start
  0.9 0.1 copy-done.10
  0.9 3.0 %collective-permute-start = (bf16[64,1280]{1,0:T(8,128)(2,1)S(1)}, bf16[64,1280]{1,0:T(8,128)(2,1)S(1)}, u32[]{:S(2)}, u32[]{:S(2)}) collective-permute-start(bf16[64,1280]{1,0:T(8,128)(2,1)S(1)} %copy-done.10), channel_id=1, source_target_pairs={{0,2},{1,3},{2,0},{3,1},{4,6},{5,7},{6,4},{7,5},{8,10},{9,11},{10,... | collective-permute-start | bytes 491528 | tf_op jit(solution)/shard_map/ppermute | solution.py:249
  3.9 0.0 copy-done.4
  3.9 0.0 copy-done.5
  3.9 0.0 copy-done.6
  3.9 0.0 copy-done.2
  3.9 0.0 copy-done.3
  3.9 0.0 copy-done.9
  3.9 1.4 %shard_map.120.near_ref = bf16[176,128]{1,0:T(8,128)(2,1)S(1)} custom-call(s32[4]{0:T(128)S(1)} %copy-done.9, f32[8,128]{1,0:T(8,128)S(1)} %shard_map.119.section_ref, bf16[8,1280]{1,0:T(8,128)(2,1)S(1)} %copy-done.4, bf16[8,256]{1,0:T(8,128)(2,1)S(1)} %copy-done.5, bf16[8,256]{1,0:T(8,128)(2,1)S(1)} %copy-done.6, bf16[4,512,256]{2,1,0:T(8,128)(2,1)S(1)} %copy-done.2, ...), custom_call_target="tpu_custom_call" | custom-call | flops 167772160 | bytes 2097152 | tf_op jit(solution)/shard_map/pallas_call | solution.py:289
  5.3 0.0 copy-start.7
  5.3 0.1 collective-permute-start.2
  5.4 2.7 %collective-permute-start.5 = (bf16[176,128]{1,0:T(8,128)(2,1)S(1)}, bf16[176,128]{1,0:T(8,128)(2,1)S(1)}, u32[]{:S(2)}, u32[]{:S(2)}) collective-permute-start(bf16[176,128]{1,0:T(8,128)(2,1)S(1)} %shard_map.120.near_ref), channel_id=1, source_target_pairs={{0,8},{4,12},{8,0},{12,4},{1,9},{5,13},{9,1},{13,5},{2,10},{6,14},... | collective-permute-start | bytes 135176 | tf_op jit(solution)/shard_map/ppermute | solution.py:249
  8.1 0.0 collective-permute-done.refs_2_
  8.1 0.1 collective-permute-start.1
  8.2 0.0 collective-permute-done.2.refs_1_
  8.2 0.0 copy-done
  8.2 0.8 %shard_map.121 = (f32[128,256]{1,0:T(8,128)S(1)}, f32[64,128]{1,0:T(8,128)S(1)}) custom-call(bf16[64,1280]{1,0:T(8,128)(2,1)S(1)} %copy-done.10, bf16[64,1280]{1,0:T(8,128)(2,1)S(1)} %collective-permute-done.2.refs_1_, bf16[64,1280]{1,0:T(8,128)(2,1)S(1)} %collective-permute-done.refs_2_, bf16[2,5120,256]{2,1,0:T(8,128)(2,1)S(1)} %copy-done), custom_call_target="tpu_custom_call" | custom-call | flops 68719476736 | bytes 5242880 | tf_op jit(solution)/shard_map/pallas_call | solution.py:301
  9.0 0.4 %collective-permute-done.1.refs_0_ = bf16[64,1280]{1,0:T(8,128)(2,1)S(1)} collective-permute-done((bf16[64,1280]{1,0:T(8,128)(2,1)S(1)}, bf16[64,1280]{1,0:T(8,128)(2,1)S(1)}, u32[]{:S(2)}, u32[]{:S(2)}) %collective-permute-start.1) | collective-permute-done | bytes 163872 | tf_op jit(solution)/shard_map/ppermute | solution.py:249
  9.5 0.0 copy-done.7
  9.5 0.4 %shard_map.122.after.refs_0_ = bf16[128,256]{1,0:T(8,128)(2,1)S(1)} custom-call(bf16[64,1280]{1,0:T(8,128)(2,1)S(1)} %collective-permute-done.1.refs_0_, bf16[2,5120,256]{2,1,0:T(8,128)(2,1)S(1)} %copy-done, f32[128,256]{1,0:T(8,128)S(1)} %get-tuple-element.27.refs_2_, f32[64,128]{1,0:T(8,128)S(1)} %get-tuple-element.28.refs_3_, bf16[2,256]{1,0:T(2,128)(2,1)S(1)} %copy-done.7), custom_call_target="tpu_custom_call" | custom-call | flops 83886080 | bytes 1310720 | tf_op jit(solution)/shard_map/pallas_call | solution.py:309
  9.9 0.0 copy-start.1
  9.9 2.9 %collective-permute-start.4 = (bf16[128,256]{1,0:T(8,128)(2,1)S(1)}, bf16[128,256]{1,0:T(8,128)(2,1)S(1)}, u32[]{:S(2)}, u32[]{:S(2)}) collective-permute-start(bf16[128,256]{1,0:T(8,128)(2,1)S(1)} %shard_map.122.after.refs_0_), channel_id=1, source_target_pairs={{0,8},{4,12},{8,0},{12,4},{1,9},{5,13},{9,1},{13,5},{2,10},{6,14},... | collective-permute-start | bytes 196616 | tf_op jit(solution)/shard_map/ppermute | solution.py:249
  12.8 0.0 collective-permute-done.5.far_ref
  12.8 1.6 %collective-permute-start.7 = (bf16[2,176,128]{2,1,0:T(8,128)(2,1)S(1)}, bf16[2,176,128]{2,1,0:T(8,128)(2,1)S(1)}, u32[]{:S(2)}, u32[]{:S(2)}) collective-permute-start(bf16[2,176,128]{2,1,0:T(8,128)(2,1)S(1)} %shard_map.123.refs_0_), channel_id=1, source_target_pairs={{0,4},{4,0},{8,12},{12,8},{1,5},{5,1},{9,13},{13,9},{2,6},{6,2},{1... | collective-permute-start | bytes 270344 | tf_op jit(solution)/shard_map/ppermute | solution.py:249
  14.4 0.5 %collective-permute-start.3 = (bf16[128,256]{1,0:T(8,128)(2,1)S(1)}, bf16[128,256]{1,0:T(8,128)(2,1)S(1)}, u32[]{:S(2)}, u32[]{:S(2)}) collective-permute-start(bf16[128,256]{1,0:T(8,128)(2,1)S(1)} %shard_map.122.after.refs_0_), channel_id=1, source_target_pairs={{0,4},{4,0},{8,12},{12,8},{1,5},{5,1},{9,13},{13,9},{2,6},{6,2},{1... | collective-permute-start | bytes 196616 | tf_op jit(solution)/shard_map/ppermute | solution.py:249
  14.9 1.3 %collective-permute-done.4.refs_2_ = bf16[128,256]{1,0:T(8,128)(2,1)S(1)} collective-permute-done((bf16[128,256]{1,0:T(8,128)(2,1)S(1)}, bf16[128,256]{1,0:T(8,128)(2,1)S(1)}, u32[]{:S(2)}, u32[]{:S(2)}) %collective-permute-start.4) | collective-permute-done | bytes 65568 | tf_op jit(solution)/shard_map/ppermute | solution.py:249
  16.2 1.3 %collective-permute-start.6 = (bf16[128,256]{1,0:T(8,128)(2,1)S(1)}, bf16[128,256]{1,0:T(8,128)(2,1)S(1)}, u32[]{:S(2)}, u32[]{:S(2)}) collective-permute-start(bf16[128,256]{1,0:T(8,128)(2,1)S(1)} %collective-permute-done.4.refs_2_), channel_id=1, source_target_pairs={{0,4},{4,0},{8,12},{12,8},{1,5},{5,1},{9,13},{13,9},{2,6},{6,2},{1... | collective-permute-start | bytes 196616 | tf_op jit(solution)/shard_map/ppermute | solution.py:249
  17.5 0.7 %collective-permute-done.7.refs_1_ = bf16[2,176,128]{2,1,0:T(8,128)(2,1)S(1)} collective-permute-done((bf16[2,176,128]{2,1,0:T(8,128)(2,1)S(1)}, bf16[2,176,128]{2,1,0:T(8,128)(2,1)S(1)}, u32[]{:S(2)}, u32[]{:S(2)}) %collective-permute-start.7) | collective-permute-done | bytes 90144 | tf_op jit(solution)/shard_map/ppermute | solution.py:249
  18.2 0.0 copy-done.8
  18.2 0.5 %shard_map.124 = (bf16[320,256]{1,0:T(8,128)(2,1)S(1)}, f32[320,256]{1,0:T(8,128)S(1)}, f32[320,128]{1,0:T(8,128)S(1)}, f32[320,128]{1,0:T(8,128)S(1)}) custom-call(bf16[2,176,128]{2,1,0:T(8,128)(2,1)S(1)} %shard_map.123.refs_0_, bf16[2,176,128]{2,1,0:T(8,128)(2,1)S(1)} %collective-permute-done.7.refs_1_, s32[1,256]{1,0:T(1,128)S(1)} %bitcast.1), custom_call_target="tpu_custom_call" | custom-call | flops 1024 | tf_op jit(solution)/shard_map/pallas_call | solution.py:330
  18.7 0.9 %collective-permute-done.3.refs_1_ = bf16[128,256]{1,0:T(8,128)(2,1)S(1)} collective-permute-done((bf16[128,256]{1,0:T(8,128)(2,1)S(1)}, bf16[128,256]{1,0:T(8,128)(2,1)S(1)}, u32[]{:S(2)}, u32[]{:S(2)}) %collective-permute-start.3) | collective-permute-done | bytes 65568 | tf_op jit(solution)/shard_map/ppermute | solution.py:249
  19.6 0.9 %collective-permute-done.6.refs_3_ = bf16[128,256]{1,0:T(8,128)(2,1)S(1)} collective-permute-done((bf16[128,256]{1,0:T(8,128)(2,1)S(1)}, bf16[128,256]{1,0:T(8,128)(2,1)S(1)}, u32[]{:S(2)}, u32[]{:S(2)}) %collective-permute-start.6) | collective-permute-done | bytes 65568 | tf_op jit(solution)/shard_map/ppermute | solution.py:249
  20.5 0.0 copy-done.1
  20.5 1.4 %shard_map.125 = (f32[8,1280]{1,0:T(8,128)S(1)}, bf16[8,1280]{1,0:T(8,128)(2,1)S(1)}, bf16[8,1280]{1,0:T(8,128)(2,1)S(1)}, bf16[8,1280]{1,0:T(8,128)(2,1)S(1)}) custom-call(bf16[128,256]{1,0:T(8,128)(2,1)S(1)} %shard_map.122.after.refs_0_, bf16[128,256]{1,0:T(8,128)(2,1)S(1)} %collective-permute-done.3.refs_1_, ...), custom_call_target="tpu_custom_call" | custom-call | flops 104857600 | bytes 3276800 | tf_op jit(solution)/shard_map/pallas_call | solution.py:347
  21.9 0.5 %collective-permute-start.10 = (bf16[8,1280]{1,0:T(8,128)(2,1)S(1)}, bf16[8,1280]{1,0:T(8,128)(2,1)S(1)}, u32[]{:S(2)}, u32[]{:S(2)}) collective-permute-start(bf16[8,1280]{1,0:T(8,128)(2,1)S(1)} %get-tuple-element.38), channel_id=1, source_target_pairs={{0,3},{1,2},{2,1},{3,0},{4,7},{5,6},{6,5},{7,4},{8,11},{9,10},{10,... | collective-permute-start | bytes 61448 | tf_op jit(solution)/shard_map/ppermute | solution.py:249
  22.5 1.4 %collective-permute-start.8 = (bf16[8,1280]{1,0:T(8,128)(2,1)S(1)}, bf16[8,1280]{1,0:T(8,128)(2,1)S(1)}, u32[]{:S(2)}, u32[]{:S(2)}) collective-permute-start(bf16[8,1280]{1,0:T(8,128)(2,1)S(1)} %get-tuple-element.36), channel_id=1, source_target_pairs={{0,2},{1,3},{2,0},{3,1},{4,6},{5,7},{6,4},{7,5},{8,10},{9,11},{10,... | collective-permute-start | bytes 61448 | tf_op jit(solution)/shard_map/ppermute | solution.py:249
  23.8 0.1 collective-permute-start.9
  23.9 1.3 %collective-permute-done.10 = bf16[8,1280]{1,0:T(8,128)(2,1)S(1)} collective-permute-done((bf16[8,1280]{1,0:T(8,128)(2,1)S(1)}, bf16[8,1280]{1,0:T(8,128)(2,1)S(1)}, u32[]{:S(2)}, u32[]{:S(2)}) %collective-permute-start.10) | collective-permute-done | bytes 20512 | tf_op jit(solution)/shard_map/ppermute | solution.py:249
  25.2 1.0 %collective-permute-done.8 = bf16[8,1280]{1,0:T(8,128)(2,1)S(1)} collective-permute-done((bf16[8,1280]{1,0:T(8,128)(2,1)S(1)}, bf16[8,1280]{1,0:T(8,128)(2,1)S(1)}, u32[]{:S(2)}, u32[]{:S(2)}) %collective-permute-start.8) | collective-permute-done | bytes 20512 | tf_op jit(solution)/shard_map/ppermute | solution.py:249
  26.3 0.0 collective-permute-done.9
  26.3 0.6 %add_convert_fusion = bf16[8,1280]{1,0:T(8,128)(2,1)} fusion(bf16[8,1280]{1,0:T(8,128)(2,1)S(1)} %collective-permute-done.10, bf16[8,1280]{1,0:T(8,128)(2,1)S(1)} %collective-permute-done.9, f32[8,1280]{1,0:T(8,128)S(1)} %get-tuple-element.35, bf16[8,1280]{1,0:T(8,128)(2,1)S(1)} %collective-permute-done.8), kind=kLoop, calls=%fused_computation | loop fusion | flops 71680 | bytes 122880 | tf_op jit(solution)/shard_map/convert_element_type | solution.py:363
  (5 shorter events, 0.0 us)
Async XLA Ops:
  0.0 0.9 %copy-start.10 = (bf16[64,1280]{1,0:T(8,128)(2,1)S(1)}, bf16[64,1280]{1,0:T(8,128)(2,1)}, u32[]{:S(2)}) copy-start(bf16[64,1280]{1,0:T(8,128)(2,1)} %refs_0_) | copy-start | bytes 491524
  0.0 3.9 %copy-start.4 = (bf16[8,1280]{1,0:T(8,128)(2,1)S(1)}, bf16[8,1280]{1,0:T(8,128)(2,1)}, u32[]{:S(2)}) copy-start(bf16[8,1280]{1,0:T(8,128)(2,1)} %q_ref.1) | copy-start | bytes 61444
  0.0 3.9 %copy-start.5 = (bf16[8,256]{1,0:T(8,128)(2,1)S(1)}, bf16[8,256]{1,0:T(8,128)(2,1)}, u32[]{:S(2)}) copy-start(bf16[8,256]{1,0:T(8,128)(2,1)} %nk_ref.1) | copy-start | bytes 12292
  0.0 3.9 %copy-start.6 = (bf16[8,256]{1,0:T(8,128)(2,1)S(1)}, bf16[8,256]{1,0:T(8,128)(2,1)}, u32[]{:S(2)}) copy-start(bf16[8,256]{1,0:T(8,128)(2,1)} %nv_ref.1) | copy-start | bytes 12292
  0.0 3.9 %copy-start.2 = (bf16[4,512,256]{2,1,0:T(8,128)(2,1)S(1)}, bf16[4,512,256]{2,1,0:T(8,128)(2,1)}, u32[]{:S(2)}) copy-start(bf16[4,512,256]{2,1,0:T(8,128)(2,1)} %ck_ref.1) | copy-start | bytes 3145732
  0.0 3.9 %copy-start.3 = (bf16[4,512,256]{2,1,0:T(8,128)(2,1)S(1)}, bf16[4,512,256]{2,1,0:T(8,128)(2,1)}, u32[]{:S(2)}) copy-start(bf16[4,512,256]{2,1,0:T(8,128)(2,1)} %cv_ref.1) | copy-start | bytes 3145732
  0.0 3.9 %copy-start.9 = (s32[4]{0:T(128)S(1)}, s32[4]{0:T(128)}, u32[]{:S(2)}) copy-start(s32[4]{0:T(128)} %lens_ref.1) | copy-start | bytes 52
  0.0 8.2 %copy-start = (bf16[2,5120,256]{2,1,0:T(8,128)(2,1)S(1)}, bf16[2,5120,256]{2,1,0:T(8,128)(2,1)}, u32[]{:S(2)}) copy-start(bf16[2,5120,256]{2,1,0:T(8,128)(2,1)} %refs_1_.1) | copy-start | bytes 15728644
  0.9 7.2 %collective-permute-start = (bf16[64,1280]{1,0:T(8,128)(2,1)S(1)}, bf16[64,1280]{1,0:T(8,128)(2,1)S(1)}, u32[]{:S(2)}, u32[]{:S(2)}) collective-permute-start(bf16[64,1280]{1,0:T(8,128)(2,1)S(1)} %copy-done.10), channel_id=1, source_target_pairs={{0,2},{1,3},{2,0},{3,1},{4,6},{5,7},{6,4},{7,5},{8,10},{9,11},{10,... | collective-permute-start | bytes 491528 | tf_op jit(solution)/shard_map/ppermute | solution.py:249
  5.3 4.2 %copy-start.7 = (bf16[2,256]{1,0:T(2,128)(2,1)S(1)}, bf16[2,256]{1,0:T(2,128)(2,1)}, u32[]{:S(2)}) copy-start(bf16[2,256]{1,0:T(2,128)(2,1)} %refs_4_.1) | copy-start | bytes 3076
  5.3 2.9 %collective-permute-start.2 = (bf16[64,1280]{1,0:T(8,128)(2,1)S(1)}, bf16[64,1280]{1,0:T(8,128)(2,1)S(1)}, u32[]{:S(2)}, u32[]{:S(2)}) collective-permute-start(bf16[64,1280]{1,0:T(8,128)(2,1)S(1)} %copy-done.10), channel_id=1, source_target_pairs={{0,1},{1,0},{2,3},{3,2},{4,5},{5,4},{6,7},{7,6},{8,9},{9,8},{10,11... | collective-permute-start | bytes 491528 | tf_op jit(solution)/shard_map/ppermute | solution.py:249
  5.4 7.4 %collective-permute-start.5 = (bf16[176,128]{1,0:T(8,128)(2,1)S(1)}, bf16[176,128]{1,0:T(8,128)(2,1)S(1)}, u32[]{:S(2)}, u32[]{:S(2)}) collective-permute-start(bf16[176,128]{1,0:T(8,128)(2,1)S(1)} %shard_map.120.near_ref), channel_id=1, source_target_pairs={{0,8},{4,12},{8,0},{12,4},{1,9},{5,13},{9,1},{13,5},{2,10},{6,14},... | collective-permute-start | bytes 135176 | tf_op jit(solution)/shard_map/ppermute | solution.py:249
  8.1 1.4 %collective-permute-start.1 = (bf16[64,1280]{1,0:T(8,128)(2,1)S(1)}, bf16[64,1280]{1,0:T(8,128)(2,1)S(1)}, u32[]{:S(2)}, u32[]{:S(2)}) collective-permute-start(bf16[64,1280]{1,0:T(8,128)(2,1)S(1)} %collective-permute-done.refs_2_), channel_id=1, source_target_pairs={{0,1},{1,0},{2,3},{3,2},{4,5},{5,4},{6,7},{7,6},{8,9},{9,8},{10,11... | collective-permute-start | bytes 491528 | tf_op jit(solution)/shard_map/ppermute | solution.py:249
  9.9 8.3 %copy-start.8 = (s32[256]{0:T(256)S(1)}, s32[256]{0:T(256)}, u32[]{:S(2)}) copy-start(s32[256]{0:T(256)} %param.15) | copy-start | bytes 3076
  9.9 10.6 %copy-start.1 = (bf16[1280,1280]{1,0:T(8,128)(2,1)S(1)}, bf16[1280,1280]{1,0:T(8,128)(2,1)}, u32[]{:S(2)}) copy-start(bf16[1280,1280]{1,0:T(8,128)(2,1)} %refs_8_.1) | copy-start | bytes 9830404
  9.9 6.3 %collective-permute-start.4 = (bf16[128,256]{1,0:T(8,128)(2,1)S(1)}, bf16[128,256]{1,0:T(8,128)(2,1)S(1)}, u32[]{:S(2)}, u32[]{:S(2)}) collective-permute-start(bf16[128,256]{1,0:T(8,128)(2,1)S(1)} %shard_map.122.after.refs_0_), channel_id=1, source_target_pairs={{0,8},{4,12},{8,0},{12,4},{1,9},{5,13},{9,1},{13,5},{2,10},{6,14},... | collective-permute-start | bytes 196616 | tf_op jit(solution)/shard_map/ppermute | solution.py:249
  12.8 5.4 %collective-permute-start.7 = (bf16[2,176,128]{2,1,0:T(8,128)(2,1)S(1)}, bf16[2,176,128]{2,1,0:T(8,128)(2,1)S(1)}, u32[]{:S(2)}, u32[]{:S(2)}) collective-permute-start(bf16[2,176,128]{2,1,0:T(8,128)(2,1)S(1)} %shard_map.123.refs_0_), channel_id=1, source_target_pairs={{0,4},{4,0},{8,12},{12,8},{1,5},{5,1},{9,13},{13,9},{2,6},{6,2},{1... | collective-permute-start | bytes 270344 | tf_op jit(solution)/shard_map/ppermute | solution.py:249
  14.4 5.1 %collective-permute-start.3 = (bf16[128,256]{1,0:T(8,128)(2,1)S(1)}, bf16[128,256]{1,0:T(8,128)(2,1)S(1)}, u32[]{:S(2)}, u32[]{:S(2)}) collective-permute-start(bf16[128,256]{1,0:T(8,128)(2,1)S(1)} %shard_map.122.after.refs_0_), channel_id=1, source_target_pairs={{0,4},{4,0},{8,12},{12,8},{1,5},{5,1},{9,13},{13,9},{2,6},{6,2},{1... | collective-permute-start | bytes 196616 | tf_op jit(solution)/shard_map/ppermute | solution.py:249
  16.2 4.3 %collective-permute-start.6 = (bf16[128,256]{1,0:T(8,128)(2,1)S(1)}, bf16[128,256]{1,0:T(8,128)(2,1)S(1)}, u32[]{:S(2)}, u32[]{:S(2)}) collective-permute-start(bf16[128,256]{1,0:T(8,128)(2,1)S(1)} %collective-permute-done.4.refs_2_), channel_id=1, source_target_pairs={{0,4},{4,0},{8,12},{12,8},{1,5},{5,1},{9,13},{13,9},{2,6},{6,2},{1... | collective-permute-start | bytes 196616 | tf_op jit(solution)/shard_map/ppermute | solution.py:249
  21.9 3.3 %collective-permute-start.10 = (bf16[8,1280]{1,0:T(8,128)(2,1)S(1)}, bf16[8,1280]{1,0:T(8,128)(2,1)S(1)}, u32[]{:S(2)}, u32[]{:S(2)}) collective-permute-start(bf16[8,1280]{1,0:T(8,128)(2,1)S(1)} %get-tuple-element.38), channel_id=1, source_target_pairs={{0,3},{1,2},{2,1},{3,0},{4,7},{5,6},{6,5},{7,4},{8,11},{9,10},{10,... | collective-permute-start | bytes 61448 | tf_op jit(solution)/shard_map/ppermute | solution.py:249
  22.5 3.8 %collective-permute-start.8 = (bf16[8,1280]{1,0:T(8,128)(2,1)S(1)}, bf16[8,1280]{1,0:T(8,128)(2,1)S(1)}, u32[]{:S(2)}, u32[]{:S(2)}) collective-permute-start(bf16[8,1280]{1,0:T(8,128)(2,1)S(1)} %get-tuple-element.36), channel_id=1, source_target_pairs={{0,2},{1,3},{2,0},{3,1},{4,6},{5,7},{6,4},{7,5},{8,10},{9,11},{10,... | collective-permute-start | bytes 61448 | tf_op jit(solution)/shard_map/ppermute | solution.py:249
  23.8 2.4 %collective-permute-start.9 = (bf16[8,1280]{1,0:T(8,128)(2,1)S(1)}, bf16[8,1280]{1,0:T(8,128)(2,1)S(1)}, u32[]{:S(2)}, u32[]{:S(2)}) collective-permute-start(bf16[8,1280]{1,0:T(8,128)(2,1)S(1)} %get-tuple-element.37), channel_id=1, source_target_pairs={{0,1},{1,0},{2,3},{3,2},{4,5},{5,4},{6,7},{7,6},{8,9},{9,8},{10,11... | collective-permute-start | bytes 61448 | tf_op jit(solution)/shard_map/ppermute | solution.py:249

commit v7 on v5

--- a/solution.py
+++ b/solution.py
@@ -18,7 +18,6 @@
 masked_score = -1e30
 bf16 = jnp.bfloat16
 COVER = 1 << 36
-PCOVER = 1 << 10
 f32 = jnp.float32
 
 TOP, TOTAL, SECTION = 0, 3, 5
@@ -143,7 +142,7 @@
             refs[0][s * rows : (s + 1) * rows, :] = acc[s]
         refs[1][...] = jnp.broadcast_to(squares, refs[1].shape)
         return
-    b_ref, *_, out_ref = refs
+    b_ref, out_ref = refs
     scale = lax.rsqrt(squares / D + 1e-06)
     for s in range(2):
         bias = b_ref[s : s + 1, :].astype(f32)
@@ -290,9 +289,7 @@
     )(cache_lengths, section, queries, new_keys, new_values, cache_keys, cache_values)
     own_later, part = lax.optimization_barrier((own, part))
     hidden = passed_on(own, own_later, "tp")
-    half = range(1, groups // 2)
-    part_far = permute(part, "dp", groups // 2)
-    part_near = [permute(part, "dp", bits) for bits in half]
+    parts = [permute(part, "dp", bits) if bits else part for bits in range(groups)]
     near, far = list(range(shares - 1)), [shares - 1]
     partial = call(
         functools.partial(project_kernel, near, True, False),
@@ -304,25 +301,13 @@
     )(*[hidden[k] for k in near], kv_weight)
     kv = call(
         functools.partial(project_kernel, far, False, True),
-        [VMEM] * 5 + [ANY] * len(part_near),
+        [VMEM] * 5,
         pltpu.VMEM((2 * memory, cols), bf16),
         [],
         4 * memory * D * cols // shares,
         4 * D * cols // shares,
-    )(hidden[far[0]], kv_weight, *partial, kv_bias, *part_near)
+    )(hidden[far[0]], kv_weight, *partial, kv_bias)
     kv_far = permute(kv, "dp", groups // 2)
-    part_far = pl.pallas_call(
-        lambda *refs: None,
-        in_specs=[VMEM, ANY],
-        out_shape=pltpu.VMEM(part.shape, bf16),
-        out_specs=VMEM,
-        input_output_aliases={0: 0},
-        compiler_params=PARAMS,
-        cost_estimate=pl.CostEstimate(flops=COVER, bytes_accessed=0, transcendentals=0),
-    )(part_far, kv)
-    parts = [part, *part_near, part_far, *[permute(part_far, "dp", bits) for bits in half]]
-    kv_on, *_ = lax.optimization_barrier((kv_far, *parts[groups // 2 :]))
-    kvs = [kv, *[permute(kv, "dp", bits) for bits in half], kv_far, *[permute(kv_on, "dp", bits) for bits in half]]
     prepared = call(
         functools.partial(prepare_kernel, cols // HD),
         [VMEM] * (groups + 1),
@@ -333,9 +318,12 @@
             pltpu.VMEM((groups * rows, HD), f32),
         ],
         [],
-        PCOVER,
+        COVER,
         0,
     )(*parts, memory_sections.reshape(1, every))
+    half = range(1, groups // 2)
+    kv_on, *_ = lax.optimization_barrier((kv_far, *prepared))
+    kvs = [kv, *[permute(kv, "dp", bits) for bits in half], kv_far, *[permute(kv_on, "dp", bits) for bits in half]]
 
     out_rows, out_cols = groups * tokens, out_weight.shape[1]
     share = out_rows // shares

time: 29 us -> 28.8 us (level)
  starting transfers between devices: 13 us -> 11.6 us
  waiting for transfers between devices: 9.69 us -> 10.9 us
    ppermute x12, starting transfers between devices: 13 us -> 11.6 us  [permute(): lax.ppermute(x, axis, [(i, i ^ bits) for i in range(lax.axis_size(axis))])]
    ppermute x12, waiting for transfers between devices: 9.69 us -> 10.9 us  [permute(): lax.ppermute(x, axis, [(i, i ^ bits) for i in range(lax.axis_size(axis))])]
  transfers between devices with their start and end apart: 12 -> 12, of which waited for: 6 -> 7; matrix products, arithmetic and copies ran while one was open for 0% -> 0% of each run, Pallas kernels for 11% -> 11%
where the time goes in v7:
time: 28.8 us; the launch traced here: 28.6 us
  starting transfers between devices  11.6 us (40%)
  waiting for transfers between devices  10.9 us (38%)
  Pallas kernels  4.47 us (16%)
  between operations  0.94 us (3%)
  other arithmetic  0.62 us (2%)
    ppermute x12, starting transfers between devices, permute(): lax.ppermute(x, axis, [(i, i ^ bits) for i in range(lax.axis_size(axis))])  11.6 us
    ppermute x12, waiting for transfers between devices, permute(): lax.ppermute(x, axis, [(i, i ^ bits) for i in range(lax.axis_size(axis))])  10.9 us
    pallas_call x1, Pallas kernels, body(): call(functools.partial(attend_kernel, groups, shares), [VMEM] * (groups +...  1.42 us
    pallas_call x1, Pallas kernels, body(): call(cache_kernel, [SMEM] + [VMEM] * 6, pltpu.VMEM((2 * up(rows, 16) + ST...  1.38 us
    pallas_call x1, Pallas kernels, body(): call(functools.partial(project_kernel, near, True, False), [VMEM] * (len(...  0.82 us
    convert_element_type x1, other arithmetic, body(): return summed.astype(bf16)  0.62 us
  transfers between devices with their start and end apart: 12, of which 7 were waited for; matrix products, arithmetic and copies ran while one was open for 0% of the time, Pallas kernels for 11%

profile of v7, /device:TPU:0, one launch (start us, length us, event | category | flops | bytes accessed | tf_op | source)
XLA Modules:
  0.0 28.6 jit_solution(3710445677357791713)
XLA Ops:
  0.0 0.0 copy-start.9
  0.0 0.0 copy-start.4
  0.0 0.0 copy-start.5
  0.0 0.0 copy-start.3
  0.0 0.0 copy-start.8
  0.0 0.0 copy-start
  0.9 0.1 copy-done.9
  0.9 3.0 %collective-permute-start = (bf16[64,1280]{1,0:T(8,128)(2,1)S(1)}, bf16[64,1280]{1,0:T(8,128)(2,1)S(1)}, u32[]{:S(2)}, u32[]{:S(2)}) collective-permute-start(bf16[64,1280]{1,0:T(8,128)(2,1)S(1)} %copy-done.9), channel_id=1, source_target_pairs={{0,2},{1,3},{2,0},{3,1},{4,6},{5,7},{6,4},{7,5},{8,10},{9,11},{10,... | collective-permute-start | bytes 491528 | tf_op jit(solution)/shard_map/ppermute | solution.py:242
  3.9 0.0 copy-done.4
  3.9 0.0 copy-done.5
  3.9 0.0 copy-done.6
  3.9 0.0 copy-done.2
  3.9 0.0 copy-done.3
  3.9 0.0 copy-done.8
  3.9 1.4 %shard_map.120.refs_0_ = bf16[176,128]{1,0:T(8,128)(2,1)S(1)} custom-call(s32[4]{0:T(128)S(1)} %copy-done.8, f32[8,128]{1,0:T(8,128)S(1)} %shard_map.119.section_ref, bf16[8,1280]{1,0:T(8,128)(2,1)S(1)} %copy-done.4, bf16[8,256]{1,0:T(8,128)(2,1)S(1)} %copy-done.5, bf16[8,256]{1,0:T(8,128)(2,1)S(1)} %copy-done.6, bf16[4,512,256]{2,1,0:T(8,128)(2,1)S(1)} %copy-done.2, ...), custom_call_target="tpu_custom_call" | custom-call | flops 167772160 | bytes 2097152 | tf_op jit(solution)/shard_map/pallas_call | solution.py:282
  5.3 0.0 copy-start.7
  5.3 0.1 collective-permute-start.2
  5.4 1.6 %collective-permute-start.5 = (bf16[176,128]{1,0:T(8,128)(2,1)S(1)}, bf16[176,128]{1,0:T(8,128)(2,1)S(1)}, u32[]{:S(2)}, u32[]{:S(2)}) collective-permute-start(bf16[176,128]{1,0:T(8,128)(2,1)S(1)} %shard_map.120.refs_0_), channel_id=1, source_target_pairs={{0,4},{4,0},{8,12},{12,8},{1,5},{5,1},{9,13},{13,9},{2,6},{6,2},{1... | collective-permute-start | bytes 135176 | tf_op jit(solution)/shard_map/ppermute | solution.py:242
  7.0 2.6 %collective-permute-start.6 = (bf16[176,128]{1,0:T(8,128)(2,1)S(1)}, bf16[176,128]{1,0:T(8,128)(2,1)S(1)}, u32[]{:S(2)}, u32[]{:S(2)}) collective-permute-start(bf16[176,128]{1,0:T(8,128)(2,1)S(1)} %shard_map.120.refs_0_), channel_id=1, source_target_pairs={{0,8},{4,12},{8,0},{12,4},{1,9},{5,13},{9,1},{13,5},{2,10},{6,14},... | collective-permute-start | bytes 135176 | tf_op jit(solution)/shard_map/ppermute | solution.py:242
  9.6 0.2 collective-permute-start.7
  9.9 0.0 collective-permute-done.refs_2_
  9.9 0.0 collective-permute-start.1
  9.9 0.0 collective-permute-done.2.refs_1_
  9.9 0.0 copy-done
  9.9 0.8 %shard_map.121 = (f32[128,256]{1,0:T(8,128)S(1)}, f32[64,128]{1,0:T(8,128)S(1)}) custom-call(bf16[64,1280]{1,0:T(8,128)(2,1)S(1)} %copy-done.9, bf16[64,1280]{1,0:T(8,128)(2,1)S(1)} %collective-permute-done.2.refs_1_, bf16[64,1280]{1,0:T(8,128)(2,1)S(1)} %collective-permute-done.refs_2_, bf16[2,5120,256]{2,1,0:T(8,128)(2,1)S(1)} %copy-done), custom_call_target="tpu_custom_call" | custom-call | flops 68719476736 | bytes 5242880 | tf_op jit(solution)/shard_map/pallas_call | solution.py:294
  10.7 0.6 %collective-permute-done.1.refs_0_ = bf16[64,1280]{1,0:T(8,128)(2,1)S(1)} collective-permute-done((bf16[64,1280]{1,0:T(8,128)(2,1)S(1)}, bf16[64,1280]{1,0:T(8,128)(2,1)S(1)}, u32[]{:S(2)}, u32[]{:S(2)}) %collective-permute-start.1) | collective-permute-done | bytes 163872 | tf_op jit(solution)/shard_map/ppermute | solution.py:242
  11.3 0.0 copy-done.7
  11.3 0.4 %shard_map.122.refs_0_ = bf16[128,256]{1,0:T(8,128)(2,1)S(1)} custom-call(bf16[64,1280]{1,0:T(8,128)(2,1)S(1)} %collective-permute-done.1.refs_0_, bf16[2,5120,256]{2,1,0:T(8,128)(2,1)S(1)} %copy-done, f32[128,256]{1,0:T(8,128)S(1)} %get-tuple-element.27.refs_2_, f32[64,128]{1,0:T(8,128)S(1)} %get-tuple-element.28.refs_3_, bf16[2,256]{1,0:T(2,128)(2,1)S(1)} %copy-done.7), custom_call_target="tpu_custom_call" | custom-call | flops 83886080 | bytes 1310720 | tf_op jit(solution)/shard_map/pallas_call | solution.py:302
  11.6 1.8 %collective-permute-start.4 = (bf16[128,256]{1,0:T(8,128)(2,1)S(1)}, bf16[128,256]{1,0:T(8,128)(2,1)S(1)}, u32[]{:S(2)}, u32[]{:S(2)}) collective-permute-start(bf16[128,256]{1,0:T(8,128)(2,1)S(1)} %shard_map.122.refs_0_), channel_id=1, source_target_pairs={{0,8},{4,12},{8,0},{12,4},{1,9},{5,13},{9,1},{13,5},{2,10},{6,14},... | collective-permute-start | bytes 196616 | tf_op jit(solution)/shard_map/ppermute | solution.py:242
  13.4 0.0 collective-permute-done.5.refs_1_
  13.4 0.0 collective-permute-done.6.refs_2_
  13.4 2.1 %collective-permute-done.7.refs_3_ = bf16[176,128]{1,0:T(8,128)(2,1)S(1)} collective-permute-done((bf16[176,128]{1,0:T(8,128)(2,1)S(1)}, bf16[176,128]{1,0:T(8,128)(2,1)S(1)}, u32[]{:S(2)}, u32[]{:S(2)}) %collective-permute-start.7) | collective-permute-done | bytes 45088 | tf_op jit(solution)/shard_map/ppermute | solution.py:242
  15.5 0.0 copy-done.10
  15.5 0.5 %shard_map.123 = (bf16[320,256]{1,0:T(8,128)(2,1)S(1)}, f32[320,256]{1,0:T(8,128)S(1)}, f32[320,128]{1,0:T(8,128)S(1)}, f32[320,128]{1,0:T(8,128)S(1)}) custom-call(bf16[176,128]{1,0:T(8,128)(2,1)S(1)} %shard_map.120.refs_0_, bf16[176,128]{1,0:T(8,128)(2,1)S(1)} %collective-permute-done.5.refs_1_, bf16[176,128]{1,0:T(8,128)(2,1)S(1)} %collective-permute-done.6.refs_2_, ...), custom_call_target="tpu_custom_call" | custom-call | flops 68719476736 | tf_op jit(solution)/shard_map/pallas_call | solution.py:311
  16.0 0.5 %collective-permute-start.3 = (bf16[128,256]{1,0:T(8,128)(2,1)S(1)}, bf16[128,256]{1,0:T(8,128)(2,1)S(1)}, u32[]{:S(2)}, u32[]{:S(2)}) collective-permute-start(bf16[128,256]{1,0:T(8,128)(2,1)S(1)} %shard_map.122.refs_0_), channel_id=1, source_target_pairs={{0,4},{4,0},{8,12},{12,8},{1,5},{5,1},{9,13},{13,9},{2,6},{6,2},{1... | collective-permute-start | bytes 196616 | tf_op jit(solution)/shard_map/ppermute | solution.py:242
  16.4 2.0 %collective-permute-done.4.refs_2_ = bf16[128,256]{1,0:T(8,128)(2,1)S(1)} collective-permute-done((bf16[128,256]{1,0:T(8,128)(2,1)S(1)}, bf16[128,256]{1,0:T(8,128)(2,1)S(1)}, u32[]{:S(2)}, u32[]{:S(2)}) %collective-permute-start.4) | collective-permute-done | bytes 65568 | tf_op jit(solution)/shard_map/ppermute | solution.py:242
  18.4 0.0 collective-permute-start.8
  18.4 1.9 %collective-permute-done.3.refs_1_ = bf16[128,256]{1,0:T(8,128)(2,1)S(1)} collective-permute-done((bf16[128,256]{1,0:T(8,128)(2,1)S(1)}, bf16[128,256]{1,0:T(8,128)(2,1)S(1)}, u32[]{:S(2)}, u32[]{:S(2)}) %collective-permute-start.3) | collective-permute-done | bytes 65568 | tf_op jit(solution)/shard_map/ppermute | solution.py:242
  20.3 2.3 %collective-permute-done.8.refs_3_ = bf16[128,256]{1,0:T(8,128)(2,1)S(1)} collective-permute-done((bf16[128,256]{1,0:T(8,128)(2,1)S(1)}, bf16[128,256]{1,0:T(8,128)(2,1)S(1)}, u32[]{:S(2)}, u32[]{:S(2)}) %collective-permute-start.8) | collective-permute-done | bytes 65568 | tf_op jit(solution)/shard_map/ppermute | solution.py:242
  22.7 0.0 copy-done.1
  22.7 1.4 %shard_map.124 = (f32[8,1280]{1,0:T(8,128)S(1)}, bf16[8,1280]{1,0:T(8,128)(2,1)S(1)}, bf16[8,1280]{1,0:T(8,128)(2,1)S(1)}, bf16[8,1280]{1,0:T(8,128)(2,1)S(1)}) custom-call(bf16[128,256]{1,0:T(8,128)(2,1)S(1)} %shard_map.122.refs_0_, bf16[128,256]{1,0:T(8,128)(2,1)S(1)} %collective-permute-done.3.refs_1_, ...), custom_call_target="tpu_custom_call" | custom-call | flops 104857600 | bytes 3276800 | tf_op jit(solution)/shard_map/pallas_call | solution.py:331
  24.1 0.1 collective-permute-start.10
  24.2 0.8 %collective-permute-start.11 = (bf16[8,1280]{1,0:T(8,128)(2,1)S(1)}, bf16[8,1280]{1,0:T(8,128)(2,1)S(1)}, u32[]{:S(2)}, u32[]{:S(2)}) collective-permute-start(bf16[8,1280]{1,0:T(8,128)(2,1)S(1)} %get-tuple-element.38), channel_id=1, source_target_pairs={{0,2},{1,3},{2,0},{3,1},{4,6},{5,7},{6,4},{7,5},{8,10},{9,11},{10,... | collective-permute-start | bytes 61448 | tf_op jit(solution)/shard_map/ppermute | solution.py:242
  24.9 1.1 %collective-permute-start.9 = (bf16[8,1280]{1,0:T(8,128)(2,1)S(1)}, bf16[8,1280]{1,0:T(8,128)(2,1)S(1)}, u32[]{:S(2)}, u32[]{:S(2)}) collective-permute-start(bf16[8,1280]{1,0:T(8,128)(2,1)S(1)} %get-tuple-element.36), channel_id=1, source_target_pairs={{0,1},{1,0},{2,3},{3,2},{4,5},{5,4},{6,7},{7,6},{8,9},{9,8},{10,11... | collective-permute-start | bytes 61448 | tf_op jit(solution)/shard_map/ppermute | solution.py:242
  26.0 1.3 %collective-permute-done.10 = bf16[8,1280]{1,0:T(8,128)(2,1)S(1)} collective-permute-done((bf16[8,1280]{1,0:T(8,128)(2,1)S(1)}, bf16[8,1280]{1,0:T(8,128)(2,1)S(1)}, u32[]{:S(2)}, u32[]{:S(2)}) %collective-permute-start.10) | collective-permute-done | bytes 20512 | tf_op jit(solution)/shard_map/ppermute | solution.py:242
  27.4 0.7 %collective-permute-done.11 = bf16[8,1280]{1,0:T(8,128)(2,1)S(1)} collective-permute-done((bf16[8,1280]{1,0:T(8,128)(2,1)S(1)}, bf16[8,1280]{1,0:T(8,128)(2,1)S(1)}, u32[]{:S(2)}, u32[]{:S(2)}) %collective-permute-start.11) | collective-permute-done | bytes 20512 | tf_op jit(solution)/shard_map/ppermute | solution.py:242
  28.0 0.0 collective-permute-done.9
  28.0 0.6 %add_convert_fusion = bf16[8,1280]{1,0:T(8,128)(2,1)} fusion(bf16[8,1280]{1,0:T(8,128)(2,1)S(1)} %collective-permute-done.11, bf16[8,1280]{1,0:T(8,128)(2,1)S(1)} %collective-permute-done.10, f32[8,1280]{1,0:T(8,128)S(1)} %get-tuple-element.35, bf16[8,1280]{1,0:T(8,128)(2,1)S(1)} %collective-permute-done.9), kind=kLoop, calls=%fused_computation | loop fusion | flops 71680 | bytes 122880 | tf_op jit(solution)/shard_map/convert_element_type | solution.py:347
  (6 shorter events, 0.0 us)
Async XLA Ops:
  0.0 0.9 %copy-start.9 = (bf16[64,1280]{1,0:T(8,128)(2,1)S(1)}, bf16[64,1280]{1,0:T(8,128)(2,1)}, u32[]{:S(2)}) copy-start(bf16[64,1280]{1,0:T(8,128)(2,1)} %refs_0_) | copy-start | bytes 491524
  0.0 3.9 %copy-start.4 = (bf16[8,1280]{1,0:T(8,128)(2,1)S(1)}, bf16[8,1280]{1,0:T(8,128)(2,1)}, u32[]{:S(2)}) copy-start(bf16[8,1280]{1,0:T(8,128)(2,1)} %q_ref.1) | copy-start | bytes 61444
  0.0 3.9 %copy-start.5 = (bf16[8,256]{1,0:T(8,128)(2,1)S(1)}, bf16[8,256]{1,0:T(8,128)(2,1)}, u32[]{:S(2)}) copy-start(bf16[8,256]{1,0:T(8,128)(2,1)} %nk_ref.1) | copy-start | bytes 12292
  0.0 3.9 %copy-start.6 = (bf16[8,256]{1,0:T(8,128)(2,1)S(1)}, bf16[8,256]{1,0:T(8,128)(2,1)}, u32[]{:S(2)}) copy-start(bf16[8,256]{1,0:T(8,128)(2,1)} %nv_ref.1) | copy-start | bytes 12292
  0.0 3.9 %copy-start.2 = (bf16[4,512,256]{2,1,0:T(8,128)(2,1)S(1)}, bf16[4,512,256]{2,1,0:T(8,128)(2,1)}, u32[]{:S(2)}) copy-start(bf16[4,512,256]{2,1,0:T(8,128)(2,1)} %ck_ref.1) | copy-start | bytes 3145732
  0.0 3.9 %copy-start.3 = (bf16[4,512,256]{2,1,0:T(8,128)(2,1)S(1)}, bf16[4,512,256]{2,1,0:T(8,128)(2,1)}, u32[]{:S(2)}) copy-start(bf16[4,512,256]{2,1,0:T(8,128)(2,1)} %cv_ref.1) | copy-start | bytes 3145732
  0.0 3.9 %copy-start.8 = (s32[4]{0:T(128)S(1)}, s32[4]{0:T(128)}, u32[]{:S(2)}) copy-start(s32[4]{0:T(128)} %lens_ref.1) | copy-start | bytes 52
  0.0 9.8 %copy-start = (bf16[2,5120,256]{2,1,0:T(8,128)(2,1)S(1)}, bf16[2,5120,256]{2,1,0:T(8,128)(2,1)}, u32[]{:S(2)}) copy-start(bf16[2,5120,256]{2,1,0:T(8,128)(2,1)} %refs_1_.1) | copy-start | bytes 15728644
  0.9 8.9 %collective-permute-start = (bf16[64,1280]{1,0:T(8,128)(2,1)S(1)}, bf16[64,1280]{1,0:T(8,128)(2,1)S(1)}, u32[]{:S(2)}, u32[]{:S(2)}) collective-permute-start(bf16[64,1280]{1,0:T(8,128)(2,1)S(1)} %copy-done.9), channel_id=1, source_target_pairs={{0,2},{1,3},{2,0},{3,1},{4,6},{5,7},{6,4},{7,5},{8,10},{9,11},{10,... | collective-permute-start | bytes 491528 | tf_op jit(solution)/shard_map/ppermute | solution.py:242
  5.3 5.9 %copy-start.7 = (bf16[2,256]{1,0:T(2,128)(2,1)S(1)}, bf16[2,256]{1,0:T(2,128)(2,1)}, u32[]{:S(2)}) copy-start(bf16[2,256]{1,0:T(2,128)(2,1)} %refs_4_.1) | copy-start | bytes 3076
  5.3 4.5 %collective-permute-start.2 = (bf16[64,1280]{1,0:T(8,128)(2,1)S(1)}, bf16[64,1280]{1,0:T(8,128)(2,1)S(1)}, u32[]{:S(2)}, u32[]{:S(2)}) collective-permute-start(bf16[64,1280]{1,0:T(8,128)(2,1)S(1)} %copy-done.9), channel_id=1, source_target_pairs={{0,1},{1,0},{2,3},{3,2},{4,5},{5,4},{6,7},{7,6},{8,9},{9,8},{10,11... | collective-permute-start | bytes 491528 | tf_op jit(solution)/shard_map/ppermute | solution.py:242
  5.4 8.0 %collective-permute-start.5 = (bf16[176,128]{1,0:T(8,128)(2,1)S(1)}, bf16[176,128]{1,0:T(8,128)(2,1)S(1)}, u32[]{:S(2)}, u32[]{:S(2)}) collective-permute-start(bf16[176,128]{1,0:T(8,128)(2,1)S(1)} %shard_map.120.refs_0_), channel_id=1, source_target_pairs={{0,4},{4,0},{8,12},{12,8},{1,5},{5,1},{9,13},{13,9},{2,6},{6,2},{1... | collective-permute-start | bytes 135176 | tf_op jit(solution)/shard_map/ppermute | solution.py:242
  7.0 6.3 %collective-permute-start.6 = (bf16[176,128]{1,0:T(8,128)(2,1)S(1)}, bf16[176,128]{1,0:T(8,128)(2,1)S(1)}, u32[]{:S(2)}, u32[]{:S(2)}) collective-permute-start(bf16[176,128]{1,0:T(8,128)(2,1)S(1)} %shard_map.120.refs_0_), channel_id=1, source_target_pairs={{0,8},{4,12},{8,0},{12,4},{1,9},{5,13},{9,1},{13,5},{2,10},{6,14},... | collective-permute-start | bytes 135176 | tf_op jit(solution)/shard_map/ppermute | solution.py:242
  9.6 5.9 %collective-permute-start.7 = (bf16[176,128]{1,0:T(8,128)(2,1)S(1)}, bf16[176,128]{1,0:T(8,128)(2,1)S(1)}, u32[]{:S(2)}, u32[]{:S(2)}) collective-permute-start(bf16[176,128]{1,0:T(8,128)(2,1)S(1)} %shard_map.120.refs_0_), channel_id=1, source_target_pairs={{0,12},{4,8},{8,4},{12,0},{1,13},{5,9},{9,5},{13,1},{2,14},{6,10},... | collective-permute-start | bytes 135176 | tf_op jit(solution)/shard_map/ppermute | solution.py:242
  9.9 1.4 %collective-permute-start.1 = (bf16[64,1280]{1,0:T(8,128)(2,1)S(1)}, bf16[64,1280]{1,0:T(8,128)(2,1)S(1)}, u32[]{:S(2)}, u32[]{:S(2)}) collective-permute-start(bf16[64,1280]{1,0:T(8,128)(2,1)S(1)} %collective-permute-done.refs_2_), channel_id=1, source_target_pairs={{0,1},{1,0},{2,3},{3,2},{4,5},{5,4},{6,7},{7,6},{8,9},{9,8},{10,11... | collective-permute-start | bytes 491528 | tf_op jit(solution)/shard_map/ppermute | solution.py:242
  10.7 4.8 %copy-start.10 = (s32[256]{0:T(256)S(1)}, s32[256]{0:T(256)}, u32[]{:S(2)}) copy-start(s32[256]{0:T(256)} %param.15) | copy-start | bytes 3076
  11.6 6.8 %collective-permute-start.4 = (bf16[128,256]{1,0:T(8,128)(2,1)S(1)}, bf16[128,256]{1,0:T(8,128)(2,1)S(1)}, u32[]{:S(2)}, u32[]{:S(2)}) collective-permute-start(bf16[128,256]{1,0:T(8,128)(2,1)S(1)} %shard_map.122.refs_0_), channel_id=1, source_target_pairs={{0,8},{4,12},{8,0},{12,4},{1,9},{5,13},{9,1},{13,5},{2,10},{6,14},... | collective-permute-start | bytes 196616 | tf_op jit(solution)/shard_map/ppermute | solution.py:242
  15.5 7.2 %copy-start.1 = (bf16[1280,1280]{1,0:T(8,128)(2,1)S(1)}, bf16[1280,1280]{1,0:T(8,128)(2,1)}, u32[]{:S(2)}) copy-start(bf16[1280,1280]{1,0:T(8,128)(2,1)} %refs_8_.1) | copy-start | bytes 9830404
  16.0 4.4 %collective-permute-start.3 = (bf16[128,256]{1,0:T(8,128)(2,1)S(1)}, bf16[128,256]{1,0:T(8,128)(2,1)S(1)}, u32[]{:S(2)}, u32[]{:S(2)}) collective-permute-start(bf16[128,256]{1,0:T(8,128)(2,1)S(1)} %shard_map.122.refs_0_), channel_id=1, source_target_pairs={{0,4},{4,0},{8,12},{12,8},{1,5},{5,1},{9,13},{13,9},{2,6},{6,2},{1... | collective-permute-start | bytes 196616 | tf_op jit(solution)/shard_map/ppermute | solution.py:242
  18.4 4.3 %collective-permute-start.8 = (bf16[128,256]{1,0:T(8,128)(2,1)S(1)}, bf16[128,256]{1,0:T(8,128)(2,1)S(1)}, u32[]{:S(2)}, u32[]{:S(2)}) collective-permute-start(bf16[128,256]{1,0:T(8,128)(2,1)S(1)} %collective-permute-done.4.refs_2_), channel_id=1, source_target_pairs={{0,4},{4,0},{8,12},{12,8},{1,5},{5,1},{9,13},{13,9},{2,6},{6,2},{1... | collective-permute-start | bytes 196616 | tf_op jit(solution)/shard_map/ppermute | solution.py:242
  24.1 3.3 %collective-permute-start.10 = (bf16[8,1280]{1,0:T(8,128)(2,1)S(1)}, bf16[8,1280]{1,0:T(8,128)(2,1)S(1)}, u32[]{:S(2)}, u32[]{:S(2)}) collective-permute-start(bf16[8,1280]{1,0:T(8,128)(2,1)S(1)} %get-tuple-element.37), channel_id=1, source_target_pairs={{0,3},{1,2},{2,1},{3,0},{4,7},{5,6},{6,5},{7,4},{8,11},{9,10},{10,... | collective-permute-start | bytes 61448 | tf_op jit(solution)/shard_map/ppermute | solution.py:242
  24.2 3.8 %collective-permute-start.11 = (bf16[8,1280]{1,0:T(8,128)(2,1)S(1)}, bf16[8,1280]{1,0:T(8,128)(2,1)S(1)}, u32[]{:S(2)}, u32[]{:S(2)}) collective-permute-start(bf16[8,1280]{1,0:T(8,128)(2,1)S(1)} %get-tuple-element.38), channel_id=1, source_target_pairs={{0,2},{1,3},{2,0},{3,1},{4,6},{5,7},{6,4},{7,5},{8,10},{9,11},{10,... | collective-permute-start | bytes 61448 | tf_op jit(solution)/shard_map/ppermute | solution.py:242
  24.9 3.1 %collective-permute-start.9 = (bf16[8,1280]{1,0:T(8,128)(2,1)S(1)}, bf16[8,1280]{1,0:T(8,128)(2,1)S(1)}, u32[]{:S(2)}, u32[]{:S(2)}) collective-permute-start(bf16[8,1280]{1,0:T(8,128)(2,1)S(1)} %get-tuple-element.36), channel_id=1, source_target_pairs={{0,1},{1,0},{2,3},{3,2},{4,5},{5,4},{6,7},{7,6},{8,9},{9,8},{10,11... | collective-permute-start | bytes 61448 | tf_op jit(solution)/shard_map/ppermute | solution.py:242

commit v8 on v7

--- a/solution.py
+++ b/solution.py
@@ -18,6 +18,7 @@
 masked_score = -1e30
 bf16 = jnp.bfloat16
 COVER = 1 << 36
+PCOVER = 1 << 10
 f32 = jnp.float32
 
 TOP, TOTAL, SECTION = 0, 3, 5
@@ -149,11 +150,25 @@
         out_ref[s * rows : (s + 1) * rows, :] = (acc[s] * scale + bias).astype(bf16)
 
 
+def pack_kernel(kv_ref, part_ref, *refs):
+    out_ref = refs[-1]
+    rows, heads = kv_ref.shape[0], kv_ref.shape[1] // HD
+    folded = part_ref.shape[0] // heads
+    out_ref[0:rows, :] = kv_ref[...]
+    for j in range(heads):
+        out_ref[rows:, j * HD : (j + 1) * HD] = part_ref[j * folded : (j + 1) * folded, :]
+
+
 def prepare_kernel(heads, *refs):
-    parts, (section_ref, q_ref, bias_ref, old_ref, stats_ref) = refs[:-5], refs[-5:]
+    parts, (section_ref, q_ref, bias_ref, old_ref, stats_ref) = list(refs[:-5]), refs[-5:]
     groups = len(parts)
-    seg = (parts[0].shape[0] - STATS) // 2
+    folded = parts[0].shape[0] // heads
+    for k in range(groups // 2 + 1, groups):
+        packed = parts[k]
+        at = packed.shape[0] - folded
+        parts[k] = jnp.concatenate([packed[at:, j * HD : (j + 1) * HD] for j in range(heads)], axis=0)
     rows = q_ref.shape[0] // groups
+    seg = up(rows, 16)
     per = rows // heads
     blocks = [part[0:rows, :].astype(f32) for part in parts]
     q_ref[...] = jnp.concatenate(
@@ -183,7 +198,7 @@
     outs = refs[groups + 5 : groups + 5 + shares]
     k_ref, v_ref, attended_ref, sums_ref = refs[groups + 5 + shares :]
     me_dp, me_tp = lax.axis_index("dp"), lax.axis_index("tp")
-    memory = kvs[0].shape[0] // 2
+    memory = k_ref.shape[0] // groups
     heads = kvs[0].shape[1] // HD
     tokens = attended_ref.shape[0] // groups
     per = PER_HEAD * tokens
@@ -279,17 +294,21 @@
     group, gate = lax.optimization_barrier((group_sections, gate))
     section = call(open_kernel, [SMEM, ANY], pltpu.VMEM((8, HD), f32), [], 1 << 10, 0)(group, gate)
     own, section = lax.optimization_barrier((memory_hidden, section))
+    heads = cols // HD
+    height = up(2 * up(rows, 16) + STATS, 16 * heads)
     part = call(
         cache_kernel,
         [SMEM] + [VMEM] * 6,
-        pltpu.VMEM((2 * up(rows, 16) + STATS, HD), bf16),
+        pltpu.VMEM((height, HD), bf16),
         [],
         4 * rows * slots * cols * requests,
         4 * requests * slots * cols,
     )(cache_lengths, section, queries, new_keys, new_values, cache_keys, cache_values)
     own_later, part = lax.optimization_barrier((own, part))
     hidden = passed_on(own, own_later, "tp")
-    parts = [permute(part, "dp", bits) if bits else part for bits in range(groups)]
+    half = range(1, groups // 2)
+    part_far = permute(part, "dp", groups // 2)
+    part_near = [permute(part, "dp", bits) for bits in half]
     near, far = list(range(shares - 1)), [shares - 1]
     partial = call(
         functools.partial(project_kernel, near, True, False),
@@ -308,8 +327,20 @@
         4 * D * cols // shares,
     )(hidden[far[0]], kv_weight, *partial, kv_bias)
     kv_far = permute(kv, "dp", groups // 2)
+    packed = call(
+        pack_kernel,
+        [VMEM, VMEM] + [ANY] * len(part_near),
+        pltpu.VMEM((2 * memory + height // heads, cols), bf16),
+        [],
+        COVER,
+        0,
+    )(kv, part_far, *part_near)
+    kv_on, _ = lax.optimization_barrier((kv_far, packed))
+    near = [permute(packed, "dp", bits) for bits in half]
+    parts = [part, *part_near, part_far, *near]
+    kvs = [kv, *near, kv_far, *[permute(kv_on, "dp", bits) for bits in half]]
     prepared = call(
-        functools.partial(prepare_kernel, cols // HD),
+        functools.partial(prepare_kernel, heads),
         [VMEM] * (groups + 1),
         [
             pltpu.VMEM((groups * rows, cols), bf16),
@@ -318,12 +349,9 @@
             pltpu.VMEM((groups * rows, HD), f32),
         ],
         [],
-        COVER,
+        PCOVER,
         0,
     )(*parts, memory_sections.reshape(1, every))
-    half = range(1, groups // 2)
-    kv_on, *_ = lax.optimization_barrier((kv_far, *prepared))
-    kvs = [kv, *[permute(kv, "dp", bits) for bits in half], kv_far, *[permute(kv_on, "dp", bits) for bits in half]]
 
     out_rows, out_cols = groups * tokens, out_weight.shape[1]
     share = out_rows // shares
@@ -342,7 +370,7 @@
         2 * out_weight.size,
     )(*kvs, *prepared, out_weight)
     summed = pieces[0]
-    for bits in [*range(1, shares - 2), *range(shares - 1, shares - 3, -1)]:
+    for bits in [*range(shares - 2, 0, -1), shares - 1]:
         summed = summed + permute(pieces[bits], "tp", bits).astype(f32)
     return summed.astype(bf16)
 

time: 28.8 us -> 28.3 us (0.983)
  waiting for transfers between devices: 10.9 us -> 9.83 us
  starting transfers between devices: 11.6 us -> 12.2 us
    ppermute x12 -> x11, waiting for transfers between devices: 10.9 us -> 9.83 us  [permute(): lax.ppermute(x, axis, [(i, i ^ bits) for i in range(lax.axis_size(axis))])]
    ppermute x12 -> x11, starting transfers between devices: 11.6 us -> 12.2 us  [permute(): lax.ppermute(x, axis, [(i, i ^ bits) for i in range(lax.axis_size(axis))])]
    pallas_call x2 -> x3, Pallas kernels: 1.85 us -> 1.86 us  [the longest x1 1.38 us: body(): call(cache_kernel, [SMEM] + [VMEM] * 6, pltpu.VMEM((height, HD), bf16), [...]
  transfers between devices with their start and end apart: 12 -> 11, of which waited for: 7 -> 6; matrix products, arithmetic and copies ran while one was open for 0% -> 0% of each run, Pallas kernels for 11% -> 11%
where the time goes in v8:
time: 28.3 us; the launch traced here: 28.2 us
  starting transfers between devices  12.2 us (43%)
  waiting for transfers between devices  9.83 us (35%)
  Pallas kernels  4.49 us (16%)
  between operations  0.95 us (3%)
  other arithmetic  0.62 us (2%)
    ppermute x11, starting transfers between devices, permute(): lax.ppermute(x, axis, [(i, i ^ bits) for i in range(lax.axis_size(axis))])  12.2 us
    ppermute x11, waiting for transfers between devices, permute(): lax.ppermute(x, axis, [(i, i ^ bits) for i in range(lax.axis_size(axis))])  9.83 us
    pallas_call x1, Pallas kernels, body(): call(functools.partial(attend_kernel, groups, shares), [VMEM] * (groups +...  1.42 us
    pallas_call x1, Pallas kernels, body(): call(cache_kernel, [SMEM] + [VMEM] * 6, pltpu.VMEM((height, HD), bf16), [...  1.38 us
    pallas_call x1, Pallas kernels, body(): call(functools.partial(project_kernel, near, True, False), [VMEM] * (len(...  0.82 us
    convert_element_type x1, other arithmetic, body(): return summed.astype(bf16)  0.62 us
  transfers between devices with their start and end apart: 11, of which 6 were waited for; matrix products, arithmetic and copies ran while one was open for 0% of the time, Pallas kernels for 11%

profile of v8, /device:TPU:0, one launch (start us, length us, event | category | flops | bytes accessed | tf_op | source)
XLA Modules:
  0.0 28.2 jit_solution(16714933331819234734)
XLA Ops:
  0.0 0.0 copy-start.10
  0.0 0.0 copy-start.5
  0.0 0.0 copy-start.6
  0.0 0.0 copy-start.2
  0.0 0.0 copy-start.3
  0.0 0.0 copy-start.9
  0.0 0.0 copy-start
  0.9 0.1 copy-done.10
  0.9 3.0 %collective-permute-start = (bf16[64,1280]{1,0:T(8,128)(2,1)S(1)}, bf16[64,1280]{1,0:T(8,128)(2,1)S(1)}, u32[]{:S(2)}, u32[]{:S(2)}) collective-permute-start(bf16[64,1280]{1,0:T(8,128)(2,1)S(1)} %copy-done.10), channel_id=1, source_target_pairs={{0,2},{1,3},{2,0},{3,1},{4,6},{5,7},{6,4},{7,5},{8,10},{9,11},{10,... | collective-permute-start | bytes 491528 | tf_op jit(solution)/shard_map/ppermute | solution.py:257
  3.9 0.0 copy-done.4
  3.9 0.0 copy-done.5
  3.9 0.0 copy-done.6
  3.9 0.0 copy-done.2
  3.9 0.0 copy-done.3
  3.9 0.0 copy-done.9
  3.9 1.4 %shard_map.120.refs_0_ = bf16[192,128]{1,0:T(8,128)(2,1)S(1)} custom-call(s32[4]{0:T(128)S(1)} %copy-done.9, f32[8,128]{1,0:T(8,128)S(1)} %shard_map.119.section_ref, bf16[8,1280]{1,0:T(8,128)(2,1)S(1)} %copy-done.4, bf16[8,256]{1,0:T(8,128)(2,1)S(1)} %copy-done.5, bf16[8,256]{1,0:T(8,128)(2,1)S(1)} %copy-done.6, bf16[4,512,256]{2,1,0:T(8,128)(2,1)S(1)} %copy-done.2, ...), custom_call_target="tpu_custom_call" | custom-call | flops 167772160 | bytes 2097152 | tf_op jit(solution)/shard_map/pallas_call | solution.py:299
  5.3 0.0 copy-start.7
  5.3 0.1 collective-permute-start.2
  5.4 2.7 %collective-permute-start.3 = (bf16[192,128]{1,0:T(8,128)(2,1)S(1)}, bf16[192,128]{1,0:T(8,128)(2,1)S(1)}, u32[]{:S(2)}, u32[]{:S(2)}) collective-permute-start(bf16[192,128]{1,0:T(8,128)(2,1)S(1)} %shard_map.120.refs_0_), channel_id=1, source_target_pairs={{0,8},{4,12},{8,0},{12,4},{1,9},{5,13},{9,1},{13,5},{2,10},{6,14},... | collective-permute-start | bytes 147464 | tf_op jit(solution)/shard_map/ppermute | solution.py:257
  8.1 1.6 %collective-permute-start.4 = (bf16[192,128]{1,0:T(8,128)(2,1)S(1)}, bf16[192,128]{1,0:T(8,128)(2,1)S(1)}, u32[]{:S(2)}, u32[]{:S(2)}) collective-permute-start(bf16[192,128]{1,0:T(8,128)(2,1)S(1)} %shard_map.120.refs_0_), channel_id=1, source_target_pairs={{0,4},{4,0},{8,12},{12,8},{1,5},{5,1},{9,13},{13,9},{2,6},{6,2},{1... | collective-permute-start | bytes 147464 | tf_op jit(solution)/shard_map/ppermute | solution.py:257
  9.6 0.0 collective-permute-done.refs_2_
  9.6 0.0 collective-permute-start.1
  9.6 0.0 collective-permute-done.2.refs_1_
  9.6 0.0 copy-done
  9.7 0.8 %shard_map.121 = (f32[128,256]{1,0:T(8,128)S(1)}, f32[64,128]{1,0:T(8,128)S(1)}) custom-call(bf16[64,1280]{1,0:T(8,128)(2,1)S(1)} %copy-done.10, bf16[64,1280]{1,0:T(8,128)(2,1)S(1)} %collective-permute-done.2.refs_1_, bf16[64,1280]{1,0:T(8,128)(2,1)S(1)} %collective-permute-done.refs_2_, bf16[2,5120,256]{2,1,0:T(8,128)(2,1)S(1)} %copy-done), custom_call_target="tpu_custom_call" | custom-call | flops 68719476736 | bytes 5242880 | tf_op jit(solution)/shard_map/pallas_call | solution.py:313
  10.5 0.6 %collective-permute-done.1.refs_0_ = bf16[64,1280]{1,0:T(8,128)(2,1)S(1)} collective-permute-done((bf16[64,1280]{1,0:T(8,128)(2,1)S(1)}, bf16[64,1280]{1,0:T(8,128)(2,1)S(1)}, u32[]{:S(2)}, u32[]{:S(2)}) %collective-permute-start.1) | collective-permute-done | bytes 163872 | tf_op jit(solution)/shard_map/ppermute | solution.py:257
  11.0 0.0 copy-done.7
  11.0 0.4 %shard_map.122.kv_ref.refs_0_ = bf16[128,256]{1,0:T(8,128)(2,1)S(1)} custom-call(bf16[64,1280]{1,0:T(8,128)(2,1)S(1)} %collective-permute-done.1.refs_0_, bf16[2,5120,256]{2,1,0:T(8,128)(2,1)S(1)} %copy-done, f32[128,256]{1,0:T(8,128)S(1)} %get-tuple-element.27.refs_2_, f32[64,128]{1,0:T(8,128)S(1)} %get-tuple-element.28.refs_3_, bf16[2,256]{1,0:T(2,128)(2,1)S(1)} %copy-done.7), custom_call_target="tpu_custom_call" | custom-call | flops 83886080 | bytes 1310720 | tf_op jit(solution)/shard_map/pallas_call | solution.py:321
  11.4 0.0 copy-start.1
  11.4 1.4 %collective-permute-start.6 = (bf16[128,256]{1,0:T(8,128)(2,1)S(1)}, bf16[128,256]{1,0:T(8,128)(2,1)S(1)}, u32[]{:S(2)}, u32[]{:S(2)}) collective-permute-start(bf16[128,256]{1,0:T(8,128)(2,1)S(1)} %shard_map.122.kv_ref.refs_0_), channel_id=1, source_target_pairs={{0,8},{4,12},{8,0},{12,4},{1,9},{5,13},{9,1},{13,5},{2,10},{6,14},... | collective-permute-start | bytes 196616 | tf_op jit(solution)/shard_map/ppermute | solution.py:257
  12.8 0.0 collective-permute-done.3.part_ref.refs_2_
  12.8 0.0 collective-permute-done.4.refs_0_.refs_1_
  12.8 1.6 %collective-permute-start.5 = (bf16[224,256]{1,0:T(8,128)(2,1)S(1)}, bf16[224,256]{1,0:T(8,128)(2,1)S(1)}, u32[]{:S(2)}, u32[]{:S(2)}) collective-permute-start(bf16[224,256]{1,0:T(8,128)(2,1)S(1)} %shard_map.123), channel_id=1, source_target_pairs={{0,4},{4,0},{8,12},{12,8},{1,5},{5,1},{9,13},{13,9},{2,6},{6,2},{1... | collective-permute-start | bytes 344072 | tf_op jit(solution)/shard_map/ppermute | solution.py:257
  14.5 3.4 %collective-permute-done.6.refs_2_ = bf16[128,256]{1,0:T(8,128)(2,1)S(1)} collective-permute-done((bf16[128,256]{1,0:T(8,128)(2,1)S(1)}, bf16[128,256]{1,0:T(8,128)(2,1)S(1)}, u32[]{:S(2)}, u32[]{:S(2)}) %collective-permute-start.6) | collective-permute-done | bytes 65568 | tf_op jit(solution)/shard_map/ppermute | solution.py:257
  17.9 0.0 collective-permute-start.7
  17.9 1.3 %collective-permute-done.5.refs_3_.refs_1_ = bf16[224,256]{1,0:T(8,128)(2,1)S(1)} collective-permute-done((bf16[224,256]{1,0:T(8,128)(2,1)S(1)}, bf16[224,256]{1,0:T(8,128)(2,1)S(1)}, u32[]{:S(2)}, u32[]{:S(2)}) %collective-permute-start.5) | collective-permute-done | bytes 114720 | tf_op jit(solution)/shard_map/ppermute | solution.py:257
  19.2 0.0 copy-done.8
  19.2 0.5 %shard_map.124 = (bf16[320,256]{1,0:T(8,128)(2,1)S(1)}, f32[320,256]{1,0:T(8,128)S(1)}, f32[320,128]{1,0:T(8,128)S(1)}, f32[320,128]{1,0:T(8,128)S(1)}) custom-call(bf16[192,128]{1,0:T(8,128)(2,1)S(1)} %shard_map.120.refs_0_, bf16[192,128]{1,0:T(8,128)(2,1)S(1)} %collective-permute-done.4.refs_0_.refs_1_, ...), custom_call_target="tpu_custom_call" | custom-call | flops 1024 | tf_op jit(solution)/shard_map/pallas_call | solution.py:342
  19.7 2.5 %collective-permute-done.7.refs_3_ = bf16[128,256]{1,0:T(8,128)(2,1)S(1)} collective-permute-done((bf16[128,256]{1,0:T(8,128)(2,1)S(1)}, bf16[128,256]{1,0:T(8,128)(2,1)S(1)}, u32[]{:S(2)}, u32[]{:S(2)}) %collective-permute-start.7) | collective-permute-done | bytes 65568 | tf_op jit(solution)/shard_map/ppermute | solution.py:257
  22.1 0.0 copy-done.1
  22.2 1.4 %shard_map.125 = (f32[8,1280]{1,0:T(8,128)S(1)}, bf16[8,1280]{1,0:T(8,128)(2,1)S(1)}, bf16[8,1280]{1,0:T(8,128)(2,1)S(1)}, bf16[8,1280]{1,0:T(8,128)(2,1)S(1)}) custom-call(bf16[128,256]{1,0:T(8,128)(2,1)S(1)} %shard_map.122.kv_ref.refs_0_, bf16[224,256]{1,0:T(8,128)(2,1)S(1)} %collective-permute-done.5.refs_3_.refs_1_, ...), custom_call_target="tpu_custom_call" | custom-call | flops 104857600 | bytes 3276800 | tf_op jit(solution)/shard_map/pallas_call | solution.py:359
  23.6 0.1 collective-permute-start.10
  23.7 0.8 %collective-permute-start.8 = (bf16[8,1280]{1,0:T(8,128)(2,1)S(1)}, bf16[8,1280]{1,0:T(8,128)(2,1)S(1)}, u32[]{:S(2)}, u32[]{:S(2)}) collective-permute-start(bf16[8,1280]{1,0:T(8,128)(2,1)S(1)} %get-tuple-element.36), channel_id=1, source_target_pairs={{0,2},{1,3},{2,0},{3,1},{4,6},{5,7},{6,4},{7,5},{8,10},{9,11},{10,... | collective-permute-start | bytes 61448 | tf_op jit(solution)/shard_map/ppermute | solution.py:257
  24.5 1.0 %collective-permute-start.9 = (bf16[8,1280]{1,0:T(8,128)(2,1)S(1)}, bf16[8,1280]{1,0:T(8,128)(2,1)S(1)}, u32[]{:S(2)}, u32[]{:S(2)}) collective-permute-start(bf16[8,1280]{1,0:T(8,128)(2,1)S(1)} %get-tuple-element.37), channel_id=1, source_target_pairs={{0,1},{1,0},{2,3},{3,2},{4,5},{5,4},{6,7},{7,6},{8,9},{9,8},{10,11... | collective-permute-start | bytes 61448 | tf_op jit(solution)/shard_map/ppermute | solution.py:257
  25.5 1.3 %collective-permute-done.10 = bf16[8,1280]{1,0:T(8,128)(2,1)S(1)} collective-permute-done((bf16[8,1280]{1,0:T(8,128)(2,1)S(1)}, bf16[8,1280]{1,0:T(8,128)(2,1)S(1)}, u32[]{:S(2)}, u32[]{:S(2)}) %collective-permute-start.10) | collective-permute-done | bytes 20512 | tf_op jit(solution)/shard_map/ppermute | solution.py:257
  26.9 0.7 %collective-permute-done.8 = bf16[8,1280]{1,0:T(8,128)(2,1)S(1)} collective-permute-done((bf16[8,1280]{1,0:T(8,128)(2,1)S(1)}, bf16[8,1280]{1,0:T(8,128)(2,1)S(1)}, u32[]{:S(2)}, u32[]{:S(2)}) %collective-permute-start.8) | collective-permute-done | bytes 20512 | tf_op jit(solution)/shard_map/ppermute | solution.py:257
  27.6 0.0 collective-permute-done.9
  27.6 0.6 %add_convert_fusion = bf16[8,1280]{1,0:T(8,128)(2,1)} fusion(bf16[8,1280]{1,0:T(8,128)(2,1)S(1)} %collective-permute-done.10, bf16[8,1280]{1,0:T(8,128)(2,1)S(1)} %collective-permute-done.9, f32[8,1280]{1,0:T(8,128)S(1)} %get-tuple-element.35, bf16[8,1280]{1,0:T(8,128)(2,1)S(1)} %collective-permute-done.8), kind=kLoop, calls=%fused_computation | loop fusion | flops 71680 | bytes 122880 | tf_op jit(solution)/shard_map/convert_element_type | solution.py:375
  (5 shorter events, 0.0 us)
Async XLA Ops:
  0.0 0.9 %copy-start.10 = (bf16[64,1280]{1,0:T(8,128)(2,1)S(1)}, bf16[64,1280]{1,0:T(8,128)(2,1)}, u32[]{:S(2)}) copy-start(bf16[64,1280]{1,0:T(8,128)(2,1)} %refs_0_) | copy-start | bytes 491524
  0.0 3.9 %copy-start.4 = (bf16[8,1280]{1,0:T(8,128)(2,1)S(1)}, bf16[8,1280]{1,0:T(8,128)(2,1)}, u32[]{:S(2)}) copy-start(bf16[8,1280]{1,0:T(8,128)(2,1)} %q_ref.1) | copy-start | bytes 61444
  0.0 3.9 %copy-start.5 = (bf16[8,256]{1,0:T(8,128)(2,1)S(1)}, bf16[8,256]{1,0:T(8,128)(2,1)}, u32[]{:S(2)}) copy-start(bf16[8,256]{1,0:T(8,128)(2,1)} %nk_ref.1) | copy-start | bytes 12292
  0.0 3.9 %copy-start.6 = (bf16[8,256]{1,0:T(8,128)(2,1)S(1)}, bf16[8,256]{1,0:T(8,128)(2,1)}, u32[]{:S(2)}) copy-start(bf16[8,256]{1,0:T(8,128)(2,1)} %nv_ref.1) | copy-start | bytes 12292
  0.0 3.9 %copy-start.2 = (bf16[4,512,256]{2,1,0:T(8,128)(2,1)S(1)}, bf16[4,512,256]{2,1,0:T(8,128)(2,1)}, u32[]{:S(2)}) copy-start(bf16[4,512,256]{2,1,0:T(8,128)(2,1)} %ck_ref.1) | copy-start | bytes 3145732
  0.0 3.9 %copy-start.3 = (bf16[4,512,256]{2,1,0:T(8,128)(2,1)S(1)}, bf16[4,512,256]{2,1,0:T(8,128)(2,1)}, u32[]{:S(2)}) copy-start(bf16[4,512,256]{2,1,0:T(8,128)(2,1)} %cv_ref.1) | copy-start | bytes 3145732
  0.0 3.9 %copy-start.9 = (s32[4]{0:T(128)S(1)}, s32[4]{0:T(128)}, u32[]{:S(2)}) copy-start(s32[4]{0:T(128)} %lens_ref.1) | copy-start | bytes 52
  0.0 9.6 %copy-start = (bf16[2,5120,256]{2,1,0:T(8,128)(2,1)S(1)}, bf16[2,5120,256]{2,1,0:T(8,128)(2,1)}, u32[]{:S(2)}) copy-start(bf16[2,5120,256]{2,1,0:T(8,128)(2,1)} %refs_1_.1) | copy-start | bytes 15728644
  0.9 8.7 %collective-permute-start = (bf16[64,1280]{1,0:T(8,128)(2,1)S(1)}, bf16[64,1280]{1,0:T(8,128)(2,1)S(1)}, u32[]{:S(2)}, u32[]{:S(2)}) collective-permute-start(bf16[64,1280]{1,0:T(8,128)(2,1)S(1)} %copy-done.10), channel_id=1, source_target_pairs={{0,2},{1,3},{2,0},{3,1},{4,6},{5,7},{6,4},{7,5},{8,10},{9,11},{10,... | collective-permute-start | bytes 491528 | tf_op jit(solution)/shard_map/ppermute | solution.py:257
  5.3 5.7 %copy-start.7 = (bf16[2,256]{1,0:T(2,128)(2,1)S(1)}, bf16[2,256]{1,0:T(2,128)(2,1)}, u32[]{:S(2)}) copy-start(bf16[2,256]{1,0:T(2,128)(2,1)} %refs_4_.1) | copy-start | bytes 3076
  5.3 4.3 %collective-permute-start.2 = (bf16[64,1280]{1,0:T(8,128)(2,1)S(1)}, bf16[64,1280]{1,0:T(8,128)(2,1)S(1)}, u32[]{:S(2)}, u32[]{:S(2)}) collective-permute-start(bf16[64,1280]{1,0:T(8,128)(2,1)S(1)} %copy-done.10), channel_id=1, source_target_pairs={{0,1},{1,0},{2,3},{3,2},{4,5},{5,4},{6,7},{7,6},{8,9},{9,8},{10,11... | collective-permute-start | bytes 491528 | tf_op jit(solution)/shard_map/ppermute | solution.py:257
  5.4 7.4 %collective-permute-start.3 = (bf16[192,128]{1,0:T(8,128)(2,1)S(1)}, bf16[192,128]{1,0:T(8,128)(2,1)S(1)}, u32[]{:S(2)}, u32[]{:S(2)}) collective-permute-start(bf16[192,128]{1,0:T(8,128)(2,1)S(1)} %shard_map.120.refs_0_), channel_id=1, source_target_pairs={{0,8},{4,12},{8,0},{12,4},{1,9},{5,13},{9,1},{13,5},{2,10},{6,14},... | collective-permute-start | bytes 147464 | tf_op jit(solution)/shard_map/ppermute | solution.py:257
  8.1 4.7 %collective-permute-start.4 = (bf16[192,128]{1,0:T(8,128)(2,1)S(1)}, bf16[192,128]{1,0:T(8,128)(2,1)S(1)}, u32[]{:S(2)}, u32[]{:S(2)}) collective-permute-start(bf16[192,128]{1,0:T(8,128)(2,1)S(1)} %shard_map.120.refs_0_), channel_id=1, source_target_pairs={{0,4},{4,0},{8,12},{12,8},{1,5},{5,1},{9,13},{13,9},{2,6},{6,2},{1... | collective-permute-start | bytes 147464 | tf_op jit(solution)/shard_map/ppermute | solution.py:257
  9.6 1.4 %collective-permute-start.1 = (bf16[64,1280]{1,0:T(8,128)(2,1)S(1)}, bf16[64,1280]{1,0:T(8,128)(2,1)S(1)}, u32[]{:S(2)}, u32[]{:S(2)}) collective-permute-start(bf16[64,1280]{1,0:T(8,128)(2,1)S(1)} %collective-permute-done.refs_2_), channel_id=1, source_target_pairs={{0,1},{1,0},{2,3},{3,2},{4,5},{5,4},{6,7},{7,6},{8,9},{9,8},{10,11... | collective-permute-start | bytes 491528 | tf_op jit(solution)/shard_map/ppermute | solution.py:257
  11.4 7.8 %copy-start.8 = (s32[256]{0:T(256)S(1)}, s32[256]{0:T(256)}, u32[]{:S(2)}) copy-start(s32[256]{0:T(256)} %param.15) | copy-start | bytes 3076
  11.4 10.7 %copy-start.1 = (bf16[1280,1280]{1,0:T(8,128)(2,1)S(1)}, bf16[1280,1280]{1,0:T(8,128)(2,1)}, u32[]{:S(2)}) copy-start(bf16[1280,1280]{1,0:T(8,128)(2,1)} %refs_8_.1) | copy-start | bytes 9830404
  11.4 6.5 %collective-permute-start.6 = (bf16[128,256]{1,0:T(8,128)(2,1)S(1)}, bf16[128,256]{1,0:T(8,128)(2,1)S(1)}, u32[]{:S(2)}, u32[]{:S(2)}) collective-permute-start(bf16[128,256]{1,0:T(8,128)(2,1)S(1)} %shard_map.122.kv_ref.refs_0_), channel_id=1, source_target_pairs={{0,8},{4,12},{8,0},{12,4},{1,9},{5,13},{9,1},{13,5},{2,10},{6,14},... | collective-permute-start | bytes 196616 | tf_op jit(solution)/shard_map/ppermute | solution.py:257
  12.8 6.4 %collective-permute-start.5 = (bf16[224,256]{1,0:T(8,128)(2,1)S(1)}, bf16[224,256]{1,0:T(8,128)(2,1)S(1)}, u32[]{:S(2)}, u32[]{:S(2)}) collective-permute-start(bf16[224,256]{1,0:T(8,128)(2,1)S(1)} %shard_map.123), channel_id=1, source_target_pairs={{0,4},{4,0},{8,12},{12,8},{1,5},{5,1},{9,13},{13,9},{2,6},{6,2},{1... | collective-permute-start | bytes 344072 | tf_op jit(solution)/shard_map/ppermute | solution.py:257
  17.9 4.3 %collective-permute-start.7 = (bf16[128,256]{1,0:T(8,128)(2,1)S(1)}, bf16[128,256]{1,0:T(8,128)(2,1)S(1)}, u32[]{:S(2)}, u32[]{:S(2)}) collective-permute-start(bf16[128,256]{1,0:T(8,128)(2,1)S(1)} %collective-permute-done.6.refs_2_), channel_id=1, source_target_pairs={{0,4},{4,0},{8,12},{12,8},{1,5},{5,1},{9,13},{13,9},{2,6},{6,2},{1... | collective-permute-start | bytes 196616 | tf_op jit(solution)/shard_map/ppermute | solution.py:257
  23.6 3.3 %collective-permute-start.10 = (bf16[8,1280]{1,0:T(8,128)(2,1)S(1)}, bf16[8,1280]{1,0:T(8,128)(2,1)S(1)}, u32[]{:S(2)}, u32[]{:S(2)}) collective-permute-start(bf16[8,1280]{1,0:T(8,128)(2,1)S(1)} %get-tuple-element.38), channel_id=1, source_target_pairs={{0,3},{1,2},{2,1},{3,0},{4,7},{5,6},{6,5},{7,4},{8,11},{9,10},{10,... | collective-permute-start | bytes 61448 | tf_op jit(solution)/shard_map/ppermute | solution.py:257
  23.7 3.9 %collective-permute-start.8 = (bf16[8,1280]{1,0:T(8,128)(2,1)S(1)}, bf16[8,1280]{1,0:T(8,128)(2,1)S(1)}, u32[]{:S(2)}, u32[]{:S(2)}) collective-permute-start(bf16[8,1280]{1,0:T(8,128)(2,1)S(1)} %get-tuple-element.36), channel_id=1, source_target_pairs={{0,2},{1,3},{2,0},{3,1},{4,6},{5,7},{6,4},{7,5},{8,10},{9,11},{10,... | collective-permute-start | bytes 61448 | tf_op jit(solution)/shard_map/ppermute | solution.py:257
  24.5 3.1 %collective-permute-start.9 = (bf16[8,1280]{1,0:T(8,128)(2,1)S(1)}, bf16[8,1280]{1,0:T(8,128)(2,1)S(1)}, u32[]{:S(2)}, u32[]{:S(2)}) collective-permute-start(bf16[8,1280]{1,0:T(8,128)(2,1)S(1)} %get-tuple-element.37), channel_id=1, source_target_pairs={{0,1},{1,0},{2,3},{3,2},{4,5},{5,4},{6,7},{7,6},{8,9},{9,8},{10,11... | collective-permute-start | bytes 61448 | tf_op jit(solution)/shard_map/ppermute | solution.py:257

commit v9 on v6

--- a/solution.py
+++ b/solution.py
@@ -295,7 +295,7 @@
         4 * requests * slots * cols,
     )(cache_lengths, section, queries, new_keys, new_values, cache_keys, cache_values)
     own_later, part = lax.optimization_barrier((own, part))
-    hidden = passed_on(own, own_later, "tp")
+    hidden = passed_on(memory_hidden, own_later, "tp")
     part_far = permute(part, "dp", groups // 2)
     near, far = list(range(shares - 1)), [shares - 1]
     partial = call(

time: 27 us -> 27.2 us (level)
  waiting for transfers between devices: 6.68 us -> 8.17 us
  starting transfers between devices: 14.1 us -> 12.9 us
    ppermute x11, waiting for transfers between devices: 6.68 us -> 8.17 us  [permute(): lax.ppermute(x, axis, [(i, i ^ bits) for i in range(lax.axis_size(axis))])]
    ppermute x11, starting transfers between devices: 14.1 us -> 12.9 us  [permute(): lax.ppermute(x, axis, [(i, i ^ bits) for i in range(lax.axis_size(axis))])]
where the time goes in v9:
time: 27.2 us; the launch traced here: 27.1 us
  starting transfers between devices  12.9 us (47%)
  waiting for transfers between devices  8.17 us (30%)
  Pallas kernels  4.48 us (16%)
  between operations  0.82 us (3%)
  other arithmetic  0.62 us (2%)
    ppermute x11, starting transfers between devices, permute(): lax.ppermute(x, axis, [(i, i ^ bits) for i in range(lax.axis_size(axis))])  12.9 us
    ppermute x11, waiting for transfers between devices, permute(): lax.ppermute(x, axis, [(i, i ^ bits) for i in range(lax.axis_size(axis))])  8.17 us
    pallas_call x1, Pallas kernels, body(): call(functools.partial(attend_kernel, groups, shares), [VMEM] * (groups +...  1.42 us
    pallas_call x1, Pallas kernels, body(): call(cache_kernel, [SMEM] + [VMEM] * 6, pltpu.VMEM((2 * up(rows, 16) + ST...  1.38 us
    pallas_call x1, Pallas kernels, body(): call(functools.partial(project_kernel, near, True, False), [VMEM] * (len(...  0.81 us
    convert_element_type x1, other arithmetic, body(): return summed.astype(bf16)  0.62 us
  transfers between devices with their start and end apart: 11, of which 7 were waited for; matrix products, arithmetic and copies ran while one was open for 0% of the time, Pallas kernels for 11%

profile of v9, /device:TPU:0, one launch (start us, length us, event | category | flops | bytes accessed | tf_op | source)
XLA Modules:
  0.0 27.1 jit_solution(5891634244930892855)
XLA Ops:
  0.0 0.0 copy-start.4
  0.0 0.0 copy-start.5
  0.0 0.0 copy-start.6
  0.0 0.0 copy-start.2
  0.0 0.0 copy-start.3
  0.0 0.0 copy-start.9
  0.0 0.0 copy-start
  0.0 3.0 %collective-permute-start = (bf16[64,1280]{1,0:T(8,128)(2,1)}, bf16[64,1280]{1,0:T(8,128)(2,1)S(1)}, u32[]{:S(2)}, u32[]{:S(2)}) collective-permute-start(bf16[64,1280]{1,0:T(8,128)(2,1)} %refs_0_), channel_id=1, source_target_pairs={{0,2},{1,3},{2,0},{3,1},{4,6},{5,7},{6,4},{7,5},{8,10},{9,11},{10,... | collective-permute-start | bytes 491528 | tf_op jit(solution)/shard_map/ppermute | solution.py:249
  3.7 0.0 copy-done.4
  3.7 0.0 copy-done.5
  3.7 0.0 copy-done.6
  3.8 0.0 copy-done.2
  3.8 0.0 copy-done.3
  3.8 0.0 copy-done.9
  3.8 1.4 %shard_map.120.near_ref = bf16[176,128]{1,0:T(8,128)(2,1)S(1)} custom-call(s32[4]{0:T(128)S(1)} %copy-done.9, f32[8,128]{1,0:T(8,128)S(1)} %shard_map.119.section_ref, bf16[8,1280]{1,0:T(8,128)(2,1)S(1)} %copy-done.4, bf16[8,256]{1,0:T(8,128)(2,1)S(1)} %copy-done.5, bf16[8,256]{1,0:T(8,128)(2,1)S(1)} %copy-done.6, bf16[4,512,256]{2,1,0:T(8,128)(2,1)S(1)} %copy-done.2, ...), custom_call_target="tpu_custom_call" | custom-call | flops 167772160 | bytes 2097152 | tf_op jit(solution)/shard_map/pallas_call | solution.py:289
  5.2 0.0 copy-done.10
  5.2 0.0 copy-start.7
  5.2 0.1 collective-permute-start.2
  5.3 3.1 %collective-permute-start.5 = (bf16[176,128]{1,0:T(8,128)(2,1)S(1)}, bf16[176,128]{1,0:T(8,128)(2,1)S(1)}, u32[]{:S(2)}, u32[]{:S(2)}) collective-permute-start(bf16[176,128]{1,0:T(8,128)(2,1)S(1)} %shard_map.120.near_ref), channel_id=1, source_target_pairs={{0,8},{4,12},{8,0},{12,4},{1,9},{5,13},{9,1},{13,5},{2,10},{6,14},... | collective-permute-start | bytes 135176 | tf_op jit(solution)/shard_map/ppermute | solution.py:249
  8.4 0.0 collective-permute-done.refs_2_
  8.4 0.2 collective-permute-start.1
  8.5 0.0 collective-permute-done.2.refs_1_
  8.5 0.0 copy-done
  8.6 0.8 %shard_map.121 = (f32[128,256]{1,0:T(8,128)S(1)}, f32[64,128]{1,0:T(8,128)S(1)}) custom-call(bf16[64,1280]{1,0:T(8,128)(2,1)S(1)} %copy-done.10, bf16[64,1280]{1,0:T(8,128)(2,1)S(1)} %collective-permute-done.2.refs_1_, bf16[64,1280]{1,0:T(8,128)(2,1)S(1)} %collective-permute-done.refs_2_, bf16[2,5120,256]{2,1,0:T(8,128)(2,1)S(1)} %copy-done), custom_call_target="tpu_custom_call" | custom-call | flops 68719476736 | bytes 5242880 | tf_op jit(solution)/shard_map/pallas_call | solution.py:301
  9.4 0.4 %collective-permute-done.1.refs_0_ = bf16[64,1280]{1,0:T(8,128)(2,1)S(1)} collective-permute-done((bf16[64,1280]{1,0:T(8,128)(2,1)S(1)}, bf16[64,1280]{1,0:T(8,128)(2,1)S(1)}, u32[]{:S(2)}, u32[]{:S(2)}) %collective-permute-start.1) | collective-permute-done | bytes 163872 | tf_op jit(solution)/shard_map/ppermute | solution.py:249
  9.8 0.0 copy-done.7
  9.8 0.4 %shard_map.122.after.refs_0_ = bf16[128,256]{1,0:T(8,128)(2,1)S(1)} custom-call(bf16[64,1280]{1,0:T(8,128)(2,1)S(1)} %collective-permute-done.1.refs_0_, bf16[2,5120,256]{2,1,0:T(8,128)(2,1)S(1)} %copy-done, f32[128,256]{1,0:T(8,128)S(1)} %get-tuple-element.27.refs_2_, f32[64,128]{1,0:T(8,128)S(1)} %get-tuple-element.28.refs_3_, bf16[2,256]{1,0:T(2,128)(2,1)S(1)} %copy-done.7), custom_call_target="tpu_custom_call" | custom-call | flops 83886080 | bytes 1310720 | tf_op jit(solution)/shard_map/pallas_call | solution.py:309
  10.2 0.0 copy-start.1
  10.2 2.0 %collective-permute-start.4 = (bf16[128,256]{1,0:T(8,128)(2,1)S(1)}, bf16[128,256]{1,0:T(8,128)(2,1)S(1)}, u32[]{:S(2)}, u32[]{:S(2)}) collective-permute-start(bf16[128,256]{1,0:T(8,128)(2,1)S(1)} %shard_map.122.after.refs_0_), channel_id=1, source_target_pairs={{0,8},{4,12},{8,0},{12,4},{1,9},{5,13},{9,1},{13,5},{2,10},{6,14},... | collective-permute-start | bytes 196616 | tf_op jit(solution)/shard_map/ppermute | solution.py:249
  12.2 0.0 collective-permute-done.5.far_ref
  12.2 1.6 %collective-permute-start.7 = (bf16[2,176,128]{2,1,0:T(8,128)(2,1)S(1)}, bf16[2,176,128]{2,1,0:T(8,128)(2,1)S(1)}, u32[]{:S(2)}, u32[]{:S(2)}) collective-permute-start(bf16[2,176,128]{2,1,0:T(8,128)(2,1)S(1)} %shard_map.123.refs_0_), channel_id=1, source_target_pairs={{0,4},{4,0},{8,12},{12,8},{1,5},{5,1},{9,13},{13,9},{2,6},{6,2},{1... | collective-permute-start | bytes 270344 | tf_op jit(solution)/shard_map/ppermute | solution.py:249
  13.8 0.4 %collective-permute-start.3 = (bf16[128,256]{1,0:T(8,128)(2,1)S(1)}, bf16[128,256]{1,0:T(8,128)(2,1)S(1)}, u32[]{:S(2)}, u32[]{:S(2)}) collective-permute-start(bf16[128,256]{1,0:T(8,128)(2,1)S(1)} %shard_map.122.after.refs_0_), channel_id=1, source_target_pairs={{0,4},{4,0},{8,12},{12,8},{1,5},{5,1},{9,13},{13,9},{2,6},{6,2},{1... | collective-permute-start | bytes 196616 | tf_op jit(solution)/shard_map/ppermute | solution.py:249
  14.3 2.5 %collective-permute-done.4.refs_2_ = bf16[128,256]{1,0:T(8,128)(2,1)S(1)} collective-permute-done((bf16[128,256]{1,0:T(8,128)(2,1)S(1)}, bf16[128,256]{1,0:T(8,128)(2,1)S(1)}, u32[]{:S(2)}, u32[]{:S(2)}) %collective-permute-start.4) | collective-permute-done | bytes 65568 | tf_op jit(solution)/shard_map/ppermute | solution.py:249
  16.8 0.6 %collective-permute-start.6 = (bf16[128,256]{1,0:T(8,128)(2,1)S(1)}, bf16[128,256]{1,0:T(8,128)(2,1)S(1)}, u32[]{:S(2)}, u32[]{:S(2)}) collective-permute-start(bf16[128,256]{1,0:T(8,128)(2,1)S(1)} %collective-permute-done.4.refs_2_), channel_id=1, source_target_pairs={{0,4},{4,0},{8,12},{12,8},{1,5},{5,1},{9,13},{13,9},{2,6},{6,2},{1... | collective-permute-start | bytes 196616 | tf_op jit(solution)/shard_map/ppermute | solution.py:249
  17.4 0.8 %collective-permute-done.7.refs_1_ = bf16[2,176,128]{2,1,0:T(8,128)(2,1)S(1)} collective-permute-done((bf16[2,176,128]{2,1,0:T(8,128)(2,1)S(1)}, bf16[2,176,128]{2,1,0:T(8,128)(2,1)S(1)}, u32[]{:S(2)}, u32[]{:S(2)}) %collective-permute-start.7) | collective-permute-done | bytes 90144 | tf_op jit(solution)/shard_map/ppermute | solution.py:249
  18.1 0.0 copy-done.8
  18.1 0.5 %shard_map.124 = (bf16[320,256]{1,0:T(8,128)(2,1)S(1)}, f32[320,256]{1,0:T(8,128)S(1)}, f32[320,128]{1,0:T(8,128)S(1)}, f32[320,128]{1,0:T(8,128)S(1)}) custom-call(bf16[2,176,128]{2,1,0:T(8,128)(2,1)S(1)} %shard_map.123.refs_0_, bf16[2,176,128]{2,1,0:T(8,128)(2,1)S(1)} %collective-permute-done.7.refs_1_, s32[1,256]{1,0:T(1,128)S(1)} %bitcast.1), custom_call_target="tpu_custom_call" | custom-call | flops 1024 | tf_op jit(solution)/shard_map/pallas_call | solution.py:330
  18.6 0.8 %collective-permute-done.3.refs_1_ = bf16[128,256]{1,0:T(8,128)(2,1)S(1)} collective-permute-done((bf16[128,256]{1,0:T(8,128)(2,1)S(1)}, bf16[128,256]{1,0:T(8,128)(2,1)S(1)}, u32[]{:S(2)}, u32[]{:S(2)}) %collective-permute-start.3) | collective-permute-done | bytes 65568 | tf_op jit(solution)/shard_map/ppermute | solution.py:249
  19.4 1.6 %collective-permute-done.6.refs_3_ = bf16[128,256]{1,0:T(8,128)(2,1)S(1)} collective-permute-done((bf16[128,256]{1,0:T(8,128)(2,1)S(1)}, bf16[128,256]{1,0:T(8,128)(2,1)S(1)}, u32[]{:S(2)}, u32[]{:S(2)}) %collective-permute-start.6) | collective-permute-done | bytes 65568 | tf_op jit(solution)/shard_map/ppermute | solution.py:249
  21.1 0.0 copy-done.1
  21.1 1.4 %shard_map.125 = (f32[8,1280]{1,0:T(8,128)S(1)}, bf16[8,1280]{1,0:T(8,128)(2,1)S(1)}, bf16[8,1280]{1,0:T(8,128)(2,1)S(1)}, bf16[8,1280]{1,0:T(8,128)(2,1)S(1)}) custom-call(bf16[128,256]{1,0:T(8,128)(2,1)S(1)} %shard_map.122.after.refs_0_, bf16[128,256]{1,0:T(8,128)(2,1)S(1)} %collective-permute-done.3.refs_1_, ...), custom_call_target="tpu_custom_call" | custom-call | flops 104857600 | bytes 3276800 | tf_op jit(solution)/shard_map/pallas_call | solution.py:347
  22.5 0.1 collective-permute-start.10
  22.6 0.7 %collective-permute-start.8 = (bf16[8,1280]{1,0:T(8,128)(2,1)S(1)}, bf16[8,1280]{1,0:T(8,128)(2,1)S(1)}, u32[]{:S(2)}, u32[]{:S(2)}) collective-permute-start(bf16[8,1280]{1,0:T(8,128)(2,1)S(1)} %get-tuple-element.36), channel_id=1, source_target_pairs={{0,2},{1,3},{2,0},{3,1},{4,6},{5,7},{6,4},{7,5},{8,10},{9,11},{10,... | collective-permute-start | bytes 61448 | tf_op jit(solution)/shard_map/ppermute | solution.py:249
  23.2 1.2 %collective-permute-start.9 = (bf16[8,1280]{1,0:T(8,128)(2,1)S(1)}, bf16[8,1280]{1,0:T(8,128)(2,1)S(1)}, u32[]{:S(2)}, u32[]{:S(2)}) collective-permute-start(bf16[8,1280]{1,0:T(8,128)(2,1)S(1)} %get-tuple-element.37), channel_id=1, source_target_pairs={{0,1},{1,0},{2,3},{3,2},{4,5},{5,4},{6,7},{7,6},{8,9},{9,8},{10,11... | collective-permute-start | bytes 61448 | tf_op jit(solution)/shard_map/ppermute | solution.py:249
  24.4 1.3 %collective-permute-done.10 = bf16[8,1280]{1,0:T(8,128)(2,1)S(1)} collective-permute-done((bf16[8,1280]{1,0:T(8,128)(2,1)S(1)}, bf16[8,1280]{1,0:T(8,128)(2,1)S(1)}, u32[]{:S(2)}, u32[]{:S(2)}) %collective-permute-start.10) | collective-permute-done | bytes 20512 | tf_op jit(solution)/shard_map/ppermute | solution.py:249
  25.8 0.7 %collective-permute-done.8 = bf16[8,1280]{1,0:T(8,128)(2,1)S(1)} collective-permute-done((bf16[8,1280]{1,0:T(8,128)(2,1)S(1)}, bf16[8,1280]{1,0:T(8,128)(2,1)S(1)}, u32[]{:S(2)}, u32[]{:S(2)}) %collective-permute-start.8) | collective-permute-done | bytes 20512 | tf_op jit(solution)/shard_map/ppermute | solution.py:249
  26.4 0.0 collective-permute-done.9
  26.4 0.6 %add_convert_fusion = bf16[8,1280]{1,0:T(8,128)(2,1)} fusion(bf16[8,1280]{1,0:T(8,128)(2,1)S(1)} %collective-permute-done.10, bf16[8,1280]{1,0:T(8,128)(2,1)S(1)} %collective-permute-done.9, f32[8,1280]{1,0:T(8,128)S(1)} %get-tuple-element.35, bf16[8,1280]{1,0:T(8,128)(2,1)S(1)} %collective-permute-done.8), kind=kLoop, calls=%fused_computation | loop fusion | flops 71680 | bytes 122880 | tf_op jit(solution)/shard_map/convert_element_type | solution.py:363
  (5 shorter events, 0.0 us)
Async XLA Ops:
  0.0 5.2 %copy-start.10 = (bf16[64,1280]{1,0:T(8,128)(2,1)S(1)}, bf16[64,1280]{1,0:T(8,128)(2,1)}, u32[]{:S(2)}) copy-start(bf16[64,1280]{1,0:T(8,128)(2,1)} %refs_0_) | copy-start | bytes 491524
  0.0 3.7 %copy-start.4 = (bf16[8,1280]{1,0:T(8,128)(2,1)S(1)}, bf16[8,1280]{1,0:T(8,128)(2,1)}, u32[]{:S(2)}) copy-start(bf16[8,1280]{1,0:T(8,128)(2,1)} %q_ref.1) | copy-start | bytes 61444
  0.0 3.7 %copy-start.5 = (bf16[8,256]{1,0:T(8,128)(2,1)S(1)}, bf16[8,256]{1,0:T(8,128)(2,1)}, u32[]{:S(2)}) copy-start(bf16[8,256]{1,0:T(8,128)(2,1)} %nk_ref.1) | copy-start | bytes 12292
  0.0 3.7 %copy-start.6 = (bf16[8,256]{1,0:T(8,128)(2,1)S(1)}, bf16[8,256]{1,0:T(8,128)(2,1)}, u32[]{:S(2)}) copy-start(bf16[8,256]{1,0:T(8,128)(2,1)} %nv_ref.1) | copy-start | bytes 12292
  0.0 3.8 %copy-start.2 = (bf16[4,512,256]{2,1,0:T(8,128)(2,1)S(1)}, bf16[4,512,256]{2,1,0:T(8,128)(2,1)}, u32[]{:S(2)}) copy-start(bf16[4,512,256]{2,1,0:T(8,128)(2,1)} %ck_ref.1) | copy-start | bytes 3145732
  0.0 3.8 %copy-start.3 = (bf16[4,512,256]{2,1,0:T(8,128)(2,1)S(1)}, bf16[4,512,256]{2,1,0:T(8,128)(2,1)}, u32[]{:S(2)}) copy-start(bf16[4,512,256]{2,1,0:T(8,128)(2,1)} %cv_ref.1) | copy-start | bytes 3145732
  0.0 3.8 %copy-start.9 = (s32[4]{0:T(128)S(1)}, s32[4]{0:T(128)}, u32[]{:S(2)}) copy-start(s32[4]{0:T(128)} %lens_ref.1) | copy-start | bytes 52
  0.0 8.5 %copy-start = (bf16[2,5120,256]{2,1,0:T(8,128)(2,1)S(1)}, bf16[2,5120,256]{2,1,0:T(8,128)(2,1)}, u32[]{:S(2)}) copy-start(bf16[2,5120,256]{2,1,0:T(8,128)(2,1)} %refs_1_.1) | copy-start | bytes 15728644
  0.0 8.3 %collective-permute-start = (bf16[64,1280]{1,0:T(8,128)(2,1)}, bf16[64,1280]{1,0:T(8,128)(2,1)S(1)}, u32[]{:S(2)}, u32[]{:S(2)}) collective-permute-start(bf16[64,1280]{1,0:T(8,128)(2,1)} %refs_0_), channel_id=1, source_target_pairs={{0,2},{1,3},{2,0},{3,1},{4,6},{5,7},{6,4},{7,5},{8,10},{9,11},{10,... | collective-permute-start | bytes 491528 | tf_op jit(solution)/shard_map/ppermute | solution.py:249
  5.2 4.6 %copy-start.7 = (bf16[2,256]{1,0:T(2,128)(2,1)S(1)}, bf16[2,256]{1,0:T(2,128)(2,1)}, u32[]{:S(2)}) copy-start(bf16[2,256]{1,0:T(2,128)(2,1)} %refs_4_.1) | copy-start | bytes 3076
  5.2 3.4 %collective-permute-start.2 = (bf16[64,1280]{1,0:T(8,128)(2,1)S(1)}, bf16[64,1280]{1,0:T(8,128)(2,1)S(1)}, u32[]{:S(2)}, u32[]{:S(2)}) collective-permute-start(bf16[64,1280]{1,0:T(8,128)(2,1)S(1)} %copy-done.10), channel_id=1, source_target_pairs={{0,1},{1,0},{2,3},{3,2},{4,5},{5,4},{6,7},{7,6},{8,9},{9,8},{10,11... | collective-permute-start | bytes 491528 | tf_op jit(solution)/shard_map/ppermute | solution.py:249
  5.3 6.9 %collective-permute-start.5 = (bf16[176,128]{1,0:T(8,128)(2,1)S(1)}, bf16[176,128]{1,0:T(8,128)(2,1)S(1)}, u32[]{:S(2)}, u32[]{:S(2)}) collective-permute-start(bf16[176,128]{1,0:T(8,128)(2,1)S(1)} %shard_map.120.near_ref), channel_id=1, source_target_pairs={{0,8},{4,12},{8,0},{12,4},{1,9},{5,13},{9,1},{13,5},{2,10},{6,14},... | collective-permute-start | bytes 135176 | tf_op jit(solution)/shard_map/ppermute | solution.py:249
  8.4 1.4 %collective-permute-start.1 = (bf16[64,1280]{1,0:T(8,128)(2,1)S(1)}, bf16[64,1280]{1,0:T(8,128)(2,1)S(1)}, u32[]{:S(2)}, u32[]{:S(2)}) collective-permute-start(bf16[64,1280]{1,0:T(8,128)(2,1)S(1)} %collective-permute-done.refs_2_), channel_id=1, source_target_pairs={{0,1},{1,0},{2,3},{3,2},{4,5},{5,4},{6,7},{7,6},{8,9},{9,8},{10,11... | collective-permute-start | bytes 491528 | tf_op jit(solution)/shard_map/ppermute | solution.py:249
  10.2 8.0 %copy-start.8 = (s32[256]{0:T(256)S(1)}, s32[256]{0:T(256)}, u32[]{:S(2)}) copy-start(s32[256]{0:T(256)} %param.15) | copy-start | bytes 3076
  10.2 10.9 %copy-start.1 = (bf16[1280,1280]{1,0:T(8,128)(2,1)S(1)}, bf16[1280,1280]{1,0:T(8,128)(2,1)}, u32[]{:S(2)}) copy-start(bf16[1280,1280]{1,0:T(8,128)(2,1)} %refs_8_.1) | copy-start | bytes 9830404
  10.2 6.6 %collective-permute-start.4 = (bf16[128,256]{1,0:T(8,128)(2,1)S(1)}, bf16[128,256]{1,0:T(8,128)(2,1)S(1)}, u32[]{:S(2)}, u32[]{:S(2)}) collective-permute-start(bf16[128,256]{1,0:T(8,128)(2,1)S(1)} %shard_map.122.after.refs_0_), channel_id=1, source_target_pairs={{0,8},{4,12},{8,0},{12,4},{1,9},{5,13},{9,1},{13,5},{2,10},{6,14},... | collective-permute-start | bytes 196616 | tf_op jit(solution)/shard_map/ppermute | solution.py:249
  12.2 6.0 %collective-permute-start.7 = (bf16[2,176,128]{2,1,0:T(8,128)(2,1)S(1)}, bf16[2,176,128]{2,1,0:T(8,128)(2,1)S(1)}, u32[]{:S(2)}, u32[]{:S(2)}) collective-permute-start(bf16[2,176,128]{2,1,0:T(8,128)(2,1)S(1)} %shard_map.123.refs_0_), channel_id=1, source_target_pairs={{0,4},{4,0},{8,12},{12,8},{1,5},{5,1},{9,13},{13,9},{2,6},{6,2},{1... | collective-permute-start | bytes 270344 | tf_op jit(solution)/shard_map/ppermute | solution.py:249
  13.8 5.6 %collective-permute-start.3 = (bf16[128,256]{1,0:T(8,128)(2,1)S(1)}, bf16[128,256]{1,0:T(8,128)(2,1)S(1)}, u32[]{:S(2)}, u32[]{:S(2)}) collective-permute-start(bf16[128,256]{1,0:T(8,128)(2,1)S(1)} %shard_map.122.after.refs_0_), channel_id=1, source_target_pairs={{0,4},{4,0},{8,12},{12,8},{1,5},{5,1},{9,13},{13,9},{2,6},{6,2},{1... | collective-permute-start | bytes 196616 | tf_op jit(solution)/shard_map/ppermute | solution.py:249
  16.8 4.3 %collective-permute-start.6 = (bf16[128,256]{1,0:T(8,128)(2,1)S(1)}, bf16[128,256]{1,0:T(8,128)(2,1)S(1)}, u32[]{:S(2)}, u32[]{:S(2)}) collective-permute-start(bf16[128,256]{1,0:T(8,128)(2,1)S(1)} %collective-permute-done.4.refs_2_), channel_id=1, source_target_pairs={{0,4},{4,0},{8,12},{12,8},{1,5},{5,1},{9,13},{13,9},{2,6},{6,2},{1... | collective-permute-start | bytes 196616 | tf_op jit(solution)/shard_map/ppermute | solution.py:249
  22.5 3.3 %collective-permute-start.10 = (bf16[8,1280]{1,0:T(8,128)(2,1)S(1)}, bf16[8,1280]{1,0:T(8,128)(2,1)S(1)}, u32[]{:S(2)}, u32[]{:S(2)}) collective-permute-start(bf16[8,1280]{1,0:T(8,128)(2,1)S(1)} %get-tuple-element.38), channel_id=1, source_target_pairs={{0,3},{1,2},{2,1},{3,0},{4,7},{5,6},{6,5},{7,4},{8,11},{9,10},{10,... | collective-permute-start | bytes 61448 | tf_op jit(solution)/shard_map/ppermute | solution.py:249
  22.6 3.8 %collective-permute-start.8 = (bf16[8,1280]{1,0:T(8,128)(2,1)S(1)}, bf16[8,1280]{1,0:T(8,128)(2,1)S(1)}, u32[]{:S(2)}, u32[]{:S(2)}) collective-permute-start(bf16[8,1280]{1,0:T(8,128)(2,1)S(1)} %get-tuple-element.36), channel_id=1, source_target_pairs={{0,2},{1,3},{2,0},{3,1},{4,6},{5,7},{6,4},{7,5},{8,10},{9,11},{10,... | collective-permute-start | bytes 61448 | tf_op jit(solution)/shard_map/ppermute | solution.py:249
  23.2 3.2 %collective-permute-start.9 = (bf16[8,1280]{1,0:T(8,128)(2,1)S(1)}, bf16[8,1280]{1,0:T(8,128)(2,1)S(1)}, u32[]{:S(2)}, u32[]{:S(2)}) collective-permute-start(bf16[8,1280]{1,0:T(8,128)(2,1)S(1)} %get-tuple-element.37), channel_id=1, source_target_pairs={{0,1},{1,0},{2,3},{3,2},{4,5},{5,4},{6,7},{7,6},{8,9},{9,8},{10,11... | collective-permute-start | bytes 61448 | tf_op jit(solution)/shard_map/ppermute | solution.py:249

commit v10 on v8

--- a/solution.py
+++ b/solution.py
@@ -305,10 +305,9 @@
         4 * requests * slots * cols,
     )(cache_lengths, section, queries, new_keys, new_values, cache_keys, cache_values)
     own_later, part = lax.optimization_barrier((own, part))
-    hidden = passed_on(own, own_later, "tp")
+    hidden = passed_on(memory_hidden, own_later, "tp")
     half = range(1, groups // 2)
     part_far = permute(part, "dp", groups // 2)
-    part_near = [permute(part, "dp", bits) for bits in half]
     near, far = list(range(shares - 1)), [shares - 1]
     partial = call(
         functools.partial(project_kernel, near, True, False),
@@ -318,6 +317,8 @@
         COVER,
         4 * D * cols,
     )(*[hidden[k] for k in near], kv_weight)
+    part_later, *_ = lax.optimization_barrier((part, *partial))
+    part_near = [permute(part_later, "dp", bits) for bits in half]
     kv = call(
         functools.partial(project_kernel, far, False, True),
         [VMEM] * 5,

time: 28.3 us -> 28.4 us (level)
  starting transfers between devices: 12.2 us -> 13.4 us
  waiting for transfers between devices: 9.83 us -> 8.9 us
    ppermute x11, starting transfers between devices: 12.2 us -> 13.4 us  [permute(): lax.ppermute(x, axis, [(i, i ^ bits) for i in range(lax.axis_size(axis))])]
    ppermute x11, waiting for transfers between devices: 9.83 us -> 8.9 us  [permute(): lax.ppermute(x, axis, [(i, i ^ bits) for i in range(lax.axis_size(axis))])]
where the time goes in v10:
time: 28.4 us; the launch traced here: 28.3 us
  starting transfers between devices  13.4 us (47%)
  waiting for transfers between devices  8.9 us (31%)
  Pallas kernels  4.48 us (16%)
  between operations  0.82 us (3%)
  other arithmetic  0.62 us (2%)
    ppermute x11, starting transfers between devices, permute(): lax.ppermute(x, axis, [(i, i ^ bits) for i in range(lax.axis_size(axis))])  13.4 us
    ppermute x11, waiting for transfers between devices, permute(): lax.ppermute(x, axis, [(i, i ^ bits) for i in range(lax.axis_size(axis))])  8.9 us
    pallas_call x1, Pallas kernels, body(): call(functools.partial(attend_kernel, groups, shares), [VMEM] * (groups +...  1.42 us
    pallas_call x1, Pallas kernels, body(): call(cache_kernel, [SMEM] + [VMEM] * 6, pltpu.VMEM((height, HD), bf16), [...  1.38 us
    pallas_call x1, Pallas kernels, body(): call(functools.partial(project_kernel, near, True, False), [VMEM] * (len(...  0.81 us
    convert_element_type x1, other arithmetic, body(): return summed.astype(bf16)  0.62 us
  transfers between devices with their start and end apart: 11, of which 6 were waited for; matrix products, arithmetic and copies ran while one was open for 0% of the time, Pallas kernels for 11%

profile of v10, /device:TPU:0, one launch (start us, length us, event | category | flops | bytes accessed | tf_op | source)
XLA Modules:
  0.0 28.3 jit_solution(17772561438101321320)
XLA Ops:
  0.0 0.0 copy-start.10
  0.0 0.0 copy-start.4
  0.0 0.0 copy-start.5
  0.0 0.0 copy-start.6
  0.0 0.0 copy-start.3
  0.0 0.0 copy-start.9
  0.0 0.0 copy-start
  0.0 3.0 %collective-permute-start = (bf16[64,1280]{1,0:T(8,128)(2,1)}, bf16[64,1280]{1,0:T(8,128)(2,1)S(1)}, u32[]{:S(2)}, u32[]{:S(2)}) collective-permute-start(bf16[64,1280]{1,0:T(8,128)(2,1)} %refs_0_), channel_id=1, source_target_pairs={{0,2},{1,3},{2,0},{3,1},{4,6},{5,7},{6,4},{7,5},{8,10},{9,11},{10,... | collective-permute-start | bytes 491528 | tf_op jit(solution)/shard_map/ppermute | solution.py:257
  3.7 0.0 copy-done.4
  3.7 0.0 copy-done.5
  3.7 0.0 copy-done.6
  3.8 0.0 copy-done.2
  3.8 0.0 copy-done.3
  3.8 0.0 copy-done.9
  3.8 1.4 %shard_map.120.refs_0_ = bf16[192,128]{1,0:T(8,128)(2,1)S(1)} custom-call(s32[4]{0:T(128)S(1)} %copy-done.9, f32[8,128]{1,0:T(8,128)S(1)} %shard_map.119.section_ref, bf16[8,1280]{1,0:T(8,128)(2,1)S(1)} %copy-done.4, bf16[8,256]{1,0:T(8,128)(2,1)S(1)} %copy-done.5, bf16[8,256]{1,0:T(8,128)(2,1)S(1)} %copy-done.6, bf16[4,512,256]{2,1,0:T(8,128)(2,1)S(1)} %copy-done.2, ...), custom_call_target="tpu_custom_call" | custom-call | flops 167772160 | bytes 2097152 | tf_op jit(solution)/shard_map/pallas_call | solution.py:299
  5.2 0.0 copy-done.10
  5.2 0.0 copy-start.7
  5.2 0.1 collective-permute-start.2
  5.3 3.1 %collective-permute-start.3 = (bf16[192,128]{1,0:T(8,128)(2,1)S(1)}, bf16[192,128]{1,0:T(8,128)(2,1)S(1)}, u32[]{:S(2)}, u32[]{:S(2)}) collective-permute-start(bf16[192,128]{1,0:T(8,128)(2,1)S(1)} %shard_map.120.refs_0_), channel_id=1, source_target_pairs={{0,8},{4,12},{8,0},{12,4},{1,9},{5,13},{9,1},{13,5},{2,10},{6,14},... | collective-permute-start | bytes 147464 | tf_op jit(solution)/shard_map/ppermute | solution.py:257
  8.4 0.0 collective-permute-done.refs_2_
  8.4 0.2 collective-permute-start.1
  8.5 0.0 collective-permute-done.2.refs_1_
  8.5 0.0 copy-done
  8.6 0.8 %shard_map.121 = (f32[128,256]{1,0:T(8,128)S(1)}, f32[64,128]{1,0:T(8,128)S(1)}) custom-call(bf16[64,1280]{1,0:T(8,128)(2,1)S(1)} %copy-done.10, bf16[64,1280]{1,0:T(8,128)(2,1)S(1)} %collective-permute-done.2.refs_1_, bf16[64,1280]{1,0:T(8,128)(2,1)S(1)} %collective-permute-done.refs_2_, bf16[2,5120,256]{2,1,0:T(8,128)(2,1)S(1)} %copy-done), custom_call_target="tpu_custom_call" | custom-call | flops 68719476736 | bytes 5242880 | tf_op jit(solution)/shard_map/pallas_call | solution.py:312
  9.4 1.6 %collective-permute-start.4 = (bf16[192,128]{1,0:T(8,128)(2,1)S(1)}, bf16[192,128]{1,0:T(8,128)(2,1)S(1)}, u32[]{:S(2)}, u32[]{:S(2)}) collective-permute-start(bf16[192,128]{1,0:T(8,128)(2,1)S(1)} %shard_map.120.refs_0_), channel_id=1, source_target_pairs={{0,4},{4,0},{8,12},{12,8},{1,5},{5,1},{9,13},{13,9},{2,6},{6,2},{1... | collective-permute-start | bytes 147464 | tf_op jit(solution)/shard_map/ppermute | solution.py:257
  11.0 0.0 collective-permute-done.1.refs_0_
  11.0 0.0 copy-done.7
  11.0 0.4 %shard_map.122.kv_ref.refs_0_ = bf16[128,256]{1,0:T(8,128)(2,1)S(1)} custom-call(bf16[64,1280]{1,0:T(8,128)(2,1)S(1)} %collective-permute-done.1.refs_0_, bf16[2,5120,256]{2,1,0:T(8,128)(2,1)S(1)} %copy-done, f32[128,256]{1,0:T(8,128)S(1)} %get-tuple-element.28.refs_2_, f32[64,128]{1,0:T(8,128)S(1)} %get-tuple-element.29.refs_3_, bf16[2,256]{1,0:T(2,128)(2,1)S(1)} %copy-done.7), custom_call_target="tpu_custom_call" | custom-call | flops 83886080 | bytes 1310720 | tf_op jit(solution)/shard_map/pallas_call | solution.py:322
  11.4 0.0 copy-start.1
  11.4 1.8 %collective-permute-start.6 = (bf16[128,256]{1,0:T(8,128)(2,1)S(1)}, bf16[128,256]{1,0:T(8,128)(2,1)S(1)}, u32[]{:S(2)}, u32[]{:S(2)}) collective-permute-start(bf16[128,256]{1,0:T(8,128)(2,1)S(1)} %shard_map.122.kv_ref.refs_0_), channel_id=1, source_target_pairs={{0,8},{4,12},{8,0},{12,4},{1,9},{5,13},{9,1},{13,5},{2,10},{6,14},... | collective-permute-start | bytes 196616 | tf_op jit(solution)/shard_map/ppermute | solution.py:257
  13.2 0.0 collective-permute-done.3.part_ref.refs_2_
  13.3 0.3 collective-permute-done.4.refs_0_.refs_1_
  13.5 1.6 %collective-permute-start.5 = (bf16[224,256]{1,0:T(8,128)(2,1)S(1)}, bf16[224,256]{1,0:T(8,128)(2,1)S(1)}, u32[]{:S(2)}, u32[]{:S(2)}) collective-permute-start(bf16[224,256]{1,0:T(8,128)(2,1)S(1)} %shard_map.123), channel_id=1, source_target_pairs={{0,4},{4,0},{8,12},{12,8},{1,5},{5,1},{9,13},{13,9},{2,6},{6,2},{1... | collective-permute-start | bytes 344072 | tf_op jit(solution)/shard_map/ppermute | solution.py:257
  15.2 2.7 %collective-permute-done.6.refs_2_ = bf16[128,256]{1,0:T(8,128)(2,1)S(1)} collective-permute-done((bf16[128,256]{1,0:T(8,128)(2,1)S(1)}, bf16[128,256]{1,0:T(8,128)(2,1)S(1)}, u32[]{:S(2)}, u32[]{:S(2)}) %collective-permute-start.6) | collective-permute-done | bytes 65568 | tf_op jit(solution)/shard_map/ppermute | solution.py:257
  17.8 0.0 collective-permute-start.7
  17.8 1.7 %collective-permute-done.5.refs_3_.refs_1_ = bf16[224,256]{1,0:T(8,128)(2,1)S(1)} collective-permute-done((bf16[224,256]{1,0:T(8,128)(2,1)S(1)}, bf16[224,256]{1,0:T(8,128)(2,1)S(1)}, u32[]{:S(2)}, u32[]{:S(2)}) %collective-permute-start.5) | collective-permute-done | bytes 114720 | tf_op jit(solution)/shard_map/ppermute | solution.py:257
  19.5 0.0 copy-done.8
  19.5 0.5 %shard_map.124 = (bf16[320,256]{1,0:T(8,128)(2,1)S(1)}, f32[320,256]{1,0:T(8,128)S(1)}, f32[320,128]{1,0:T(8,128)S(1)}, f32[320,128]{1,0:T(8,128)S(1)}) custom-call(bf16[192,128]{1,0:T(8,128)(2,1)S(1)} %shard_map.120.refs_0_, bf16[192,128]{1,0:T(8,128)(2,1)S(1)} %collective-permute-done.4.refs_0_.refs_1_, ...), custom_call_target="tpu_custom_call" | custom-call | flops 1024 | tf_op jit(solution)/shard_map/pallas_call | solution.py:343
  20.0 2.1 %collective-permute-done.7.refs_3_ = bf16[128,256]{1,0:T(8,128)(2,1)S(1)} collective-permute-done((bf16[128,256]{1,0:T(8,128)(2,1)S(1)}, bf16[128,256]{1,0:T(8,128)(2,1)S(1)}, u32[]{:S(2)}, u32[]{:S(2)}) %collective-permute-start.7) | collective-permute-done | bytes 65568 | tf_op jit(solution)/shard_map/ppermute | solution.py:257
  22.1 0.0 copy-done.1
  22.1 1.4 %shard_map.125 = (f32[8,1280]{1,0:T(8,128)S(1)}, bf16[8,1280]{1,0:T(8,128)(2,1)S(1)}, bf16[8,1280]{1,0:T(8,128)(2,1)S(1)}, bf16[8,1280]{1,0:T(8,128)(2,1)S(1)}) custom-call(bf16[128,256]{1,0:T(8,128)(2,1)S(1)} %shard_map.122.kv_ref.refs_0_, bf16[224,256]{1,0:T(8,128)(2,1)S(1)} %collective-permute-done.5.refs_3_.refs_1_, ...), custom_call_target="tpu_custom_call" | custom-call | flops 104857600 | bytes 3276800 | tf_op jit(solution)/shard_map/pallas_call | solution.py:360
  23.5 0.1 collective-permute-start.10
  23.6 1.0 %collective-permute-start.8 = (bf16[8,1280]{1,0:T(8,128)(2,1)S(1)}, bf16[8,1280]{1,0:T(8,128)(2,1)S(1)}, u32[]{:S(2)}, u32[]{:S(2)}) collective-permute-start(bf16[8,1280]{1,0:T(8,128)(2,1)S(1)} %get-tuple-element.38), channel_id=1, source_target_pairs={{0,2},{1,3},{2,0},{3,1},{4,6},{5,7},{6,4},{7,5},{8,10},{9,11},{10,... | collective-permute-start | bytes 61448 | tf_op jit(solution)/shard_map/ppermute | solution.py:257
  24.6 0.8 %collective-permute-start.9 = (bf16[8,1280]{1,0:T(8,128)(2,1)S(1)}, bf16[8,1280]{1,0:T(8,128)(2,1)S(1)}, u32[]{:S(2)}, u32[]{:S(2)}) collective-permute-start(bf16[8,1280]{1,0:T(8,128)(2,1)S(1)} %get-tuple-element.39), channel_id=1, source_target_pairs={{0,1},{1,0},{2,3},{3,2},{4,5},{5,4},{6,7},{7,6},{8,9},{9,8},{10,11... | collective-permute-start | bytes 61448 | tf_op jit(solution)/shard_map/ppermute | solution.py:257
  25.5 1.3 %collective-permute-done.10 = bf16[8,1280]{1,0:T(8,128)(2,1)S(1)} collective-permute-done((bf16[8,1280]{1,0:T(8,128)(2,1)S(1)}, bf16[8,1280]{1,0:T(8,128)(2,1)S(1)}, u32[]{:S(2)}, u32[]{:S(2)}) %collective-permute-start.10) | collective-permute-done | bytes 20512 | tf_op jit(solution)/shard_map/ppermute | solution.py:257
  26.8 0.8 %collective-permute-done.8 = bf16[8,1280]{1,0:T(8,128)(2,1)S(1)} collective-permute-done((bf16[8,1280]{1,0:T(8,128)(2,1)S(1)}, bf16[8,1280]{1,0:T(8,128)(2,1)S(1)}, u32[]{:S(2)}, u32[]{:S(2)}) %collective-permute-start.8) | collective-permute-done | bytes 20512 | tf_op jit(solution)/shard_map/ppermute | solution.py:257
  27.6 0.0 collective-permute-done.9
  27.6 0.6 %add_convert_fusion = bf16[8,1280]{1,0:T(8,128)(2,1)} fusion(bf16[8,1280]{1,0:T(8,128)(2,1)S(1)} %collective-permute-done.10, bf16[8,1280]{1,0:T(8,128)(2,1)S(1)} %collective-permute-done.9, f32[8,1280]{1,0:T(8,128)S(1)} %get-tuple-element.37, bf16[8,1280]{1,0:T(8,128)(2,1)S(1)} %collective-permute-done.8), kind=kLoop, calls=%fused_computation | loop fusion | flops 71680 | bytes 122880 | tf_op jit(solution)/shard_map/convert_element_type | solution.py:376
  (5 shorter events, 0.0 us)
Async XLA Ops:
  0.0 5.2 %copy-start.10 = (bf16[64,1280]{1,0:T(8,128)(2,1)S(1)}, bf16[64,1280]{1,0:T(8,128)(2,1)}, u32[]{:S(2)}) copy-start(bf16[64,1280]{1,0:T(8,128)(2,1)} %refs_0_) | copy-start | bytes 491524
  0.0 3.7 %copy-start.4 = (bf16[8,1280]{1,0:T(8,128)(2,1)S(1)}, bf16[8,1280]{1,0:T(8,128)(2,1)}, u32[]{:S(2)}) copy-start(bf16[8,1280]{1,0:T(8,128)(2,1)} %q_ref.1) | copy-start | bytes 61444
  0.0 3.7 %copy-start.5 = (bf16[8,256]{1,0:T(8,128)(2,1)S(1)}, bf16[8,256]{1,0:T(8,128)(2,1)}, u32[]{:S(2)}) copy-start(bf16[8,256]{1,0:T(8,128)(2,1)} %nk_ref.1) | copy-start | bytes 12292
  0.0 3.7 %copy-start.6 = (bf16[8,256]{1,0:T(8,128)(2,1)S(1)}, bf16[8,256]{1,0:T(8,128)(2,1)}, u32[]{:S(2)}) copy-start(bf16[8,256]{1,0:T(8,128)(2,1)} %nv_ref.1) | copy-start | bytes 12292
  0.0 3.8 %copy-start.2 = (bf16[4,512,256]{2,1,0:T(8,128)(2,1)S(1)}, bf16[4,512,256]{2,1,0:T(8,128)(2,1)}, u32[]{:S(2)}) copy-start(bf16[4,512,256]{2,1,0:T(8,128)(2,1)} %ck_ref.1) | copy-start | bytes 3145732
  0.0 3.8 %copy-start.3 = (bf16[4,512,256]{2,1,0:T(8,128)(2,1)S(1)}, bf16[4,512,256]{2,1,0:T(8,128)(2,1)}, u32[]{:S(2)}) copy-start(bf16[4,512,256]{2,1,0:T(8,128)(2,1)} %cv_ref.1) | copy-start | bytes 3145732
  0.0 3.8 %copy-start.9 = (s32[4]{0:T(128)S(1)}, s32[4]{0:T(128)}, u32[]{:S(2)}) copy-start(s32[4]{0:T(128)} %lens_ref.1) | copy-start | bytes 52
  0.0 8.5 %copy-start = (bf16[2,5120,256]{2,1,0:T(8,128)(2,1)S(1)}, bf16[2,5120,256]{2,1,0:T(8,128)(2,1)}, u32[]{:S(2)}) copy-start(bf16[2,5120,256]{2,1,0:T(8,128)(2,1)} %refs_1_.1) | copy-start | bytes 15728644
  0.0 8.3 %collective-permute-start = (bf16[64,1280]{1,0:T(8,128)(2,1)}, bf16[64,1280]{1,0:T(8,128)(2,1)S(1)}, u32[]{:S(2)}, u32[]{:S(2)}) collective-permute-start(bf16[64,1280]{1,0:T(8,128)(2,1)} %refs_0_), channel_id=1, source_target_pairs={{0,2},{1,3},{2,0},{3,1},{4,6},{5,7},{6,4},{7,5},{8,10},{9,11},{10,... | collective-permute-start | bytes 491528 | tf_op jit(solution)/shard_map/ppermute | solution.py:257
  5.2 5.8 %copy-start.7 = (bf16[2,256]{1,0:T(2,128)(2,1)S(1)}, bf16[2,256]{1,0:T(2,128)(2,1)}, u32[]{:S(2)}) copy-start(bf16[2,256]{1,0:T(2,128)(2,1)} %refs_4_.1) | copy-start | bytes 3076
  5.2 3.4 %collective-permute-start.2 = (bf16[64,1280]{1,0:T(8,128)(2,1)S(1)}, bf16[64,1280]{1,0:T(8,128)(2,1)S(1)}, u32[]{:S(2)}, u32[]{:S(2)}) collective-permute-start(bf16[64,1280]{1,0:T(8,128)(2,1)S(1)} %copy-done.10), channel_id=1, source_target_pairs={{0,1},{1,0},{2,3},{3,2},{4,5},{5,4},{6,7},{7,6},{8,9},{9,8},{10,11... | collective-permute-start | bytes 491528 | tf_op jit(solution)/shard_map/ppermute | solution.py:257
  5.3 8.0 %collective-permute-start.3 = (bf16[192,128]{1,0:T(8,128)(2,1)S(1)}, bf16[192,128]{1,0:T(8,128)(2,1)S(1)}, u32[]{:S(2)}, u32[]{:S(2)}) collective-permute-start(bf16[192,128]{1,0:T(8,128)(2,1)S(1)} %shard_map.120.refs_0_), channel_id=1, source_target_pairs={{0,8},{4,12},{8,0},{12,4},{1,9},{5,13},{9,1},{13,5},{2,10},{6,14},... | collective-permute-start | bytes 147464 | tf_op jit(solution)/shard_map/ppermute | solution.py:257
  8.4 2.6 %collective-permute-start.1 = (bf16[64,1280]{1,0:T(8,128)(2,1)S(1)}, bf16[64,1280]{1,0:T(8,128)(2,1)S(1)}, u32[]{:S(2)}, u32[]{:S(2)}) collective-permute-start(bf16[64,1280]{1,0:T(8,128)(2,1)S(1)} %collective-permute-done.refs_2_), channel_id=1, source_target_pairs={{0,1},{1,0},{2,3},{3,2},{4,5},{5,4},{6,7},{7,6},{8,9},{9,8},{10,11... | collective-permute-start | bytes 491528 | tf_op jit(solution)/shard_map/ppermute | solution.py:257
  9.4 4.2 %collective-permute-start.4 = (bf16[192,128]{1,0:T(8,128)(2,1)S(1)}, bf16[192,128]{1,0:T(8,128)(2,1)S(1)}, u32[]{:S(2)}, u32[]{:S(2)}) collective-permute-start(bf16[192,128]{1,0:T(8,128)(2,1)S(1)} %shard_map.120.refs_0_), channel_id=1, source_target_pairs={{0,4},{4,0},{8,12},{12,8},{1,5},{5,1},{9,13},{13,9},{2,6},{6,2},{1... | collective-permute-start | bytes 147464 | tf_op jit(solution)/shard_map/ppermute | solution.py:257
  11.4 8.1 %copy-start.8 = (s32[256]{0:T(256)S(1)}, s32[256]{0:T(256)}, u32[]{:S(2)}) copy-start(s32[256]{0:T(256)} %param.15) | copy-start | bytes 3076
  11.4 10.7 %copy-start.1 = (bf16[1280,1280]{1,0:T(8,128)(2,1)S(1)}, bf16[1280,1280]{1,0:T(8,128)(2,1)}, u32[]{:S(2)}) copy-start(bf16[1280,1280]{1,0:T(8,128)(2,1)} %refs_8_.1) | copy-start | bytes 9830404
  11.4 6.4 %collective-permute-start.6 = (bf16[128,256]{1,0:T(8,128)(2,1)S(1)}, bf16[128,256]{1,0:T(8,128)(2,1)S(1)}, u32[]{:S(2)}, u32[]{:S(2)}) collective-permute-start(bf16[128,256]{1,0:T(8,128)(2,1)S(1)} %shard_map.122.kv_ref.refs_0_), channel_id=1, source_target_pairs={{0,8},{4,12},{8,0},{12,4},{1,9},{5,13},{9,1},{13,5},{2,10},{6,14},... | collective-permute-start | bytes 196616 | tf_op jit(solution)/shard_map/ppermute | solution.py:257
  13.5 6.0 %collective-permute-start.5 = (bf16[224,256]{1,0:T(8,128)(2,1)S(1)}, bf16[224,256]{1,0:T(8,128)(2,1)S(1)}, u32[]{:S(2)}, u32[]{:S(2)}) collective-permute-start(bf16[224,256]{1,0:T(8,128)(2,1)S(1)} %shard_map.123), channel_id=1, source_target_pairs={{0,4},{4,0},{8,12},{12,8},{1,5},{5,1},{9,13},{13,9},{2,6},{6,2},{1... | collective-permute-start | bytes 344072 | tf_op jit(solution)/shard_map/ppermute | solution.py:257
  17.8 4.3 %collective-permute-start.7 = (bf16[128,256]{1,0:T(8,128)(2,1)S(1)}, bf16[128,256]{1,0:T(8,128)(2,1)S(1)}, u32[]{:S(2)}, u32[]{:S(2)}) collective-permute-start(bf16[128,256]{1,0:T(8,128)(2,1)S(1)} %collective-permute-done.6.refs_2_), channel_id=1, source_target_pairs={{0,4},{4,0},{8,12},{12,8},{1,5},{5,1},{9,13},{13,9},{2,6},{6,2},{1... | collective-permute-start | bytes 196616 | tf_op jit(solution)/shard_map/ppermute | solution.py:257
  23.5 3.3 %collective-permute-start.10 = (bf16[8,1280]{1,0:T(8,128)(2,1)S(1)}, bf16[8,1280]{1,0:T(8,128)(2,1)S(1)}, u32[]{:S(2)}, u32[]{:S(2)}) collective-permute-start(bf16[8,1280]{1,0:T(8,128)(2,1)S(1)} %get-tuple-element.40), channel_id=1, source_target_pairs={{0,3},{1,2},{2,1},{3,0},{4,7},{5,6},{6,5},{7,4},{8,11},{9,10},{10,... | collective-permute-start | bytes 61448 | tf_op jit(solution)/shard_map/ppermute | solution.py:257
  23.6 4.0 %collective-permute-start.8 = (bf16[8,1280]{1,0:T(8,128)(2,1)S(1)}, bf16[8,1280]{1,0:T(8,128)(2,1)S(1)}, u32[]{:S(2)}, u32[]{:S(2)}) collective-permute-start(bf16[8,1280]{1,0:T(8,128)(2,1)S(1)} %get-tuple-element.38), channel_id=1, source_target_pairs={{0,2},{1,3},{2,0},{3,1},{4,6},{5,7},{6,4},{7,5},{8,10},{9,11},{10,... | collective-permute-start | bytes 61448 | tf_op jit(solution)/shard_map/ppermute | solution.py:257
  24.6 3.0 %collective-permute-start.9 = (bf16[8,1280]{1,0:T(8,128)(2,1)S(1)}, bf16[8,1280]{1,0:T(8,128)(2,1)S(1)}, u32[]{:S(2)}, u32[]{:S(2)}) collective-permute-start(bf16[8,1280]{1,0:T(8,128)(2,1)S(1)} %get-tuple-element.39), channel_id=1, source_target_pairs={{0,1},{1,0},{2,3},{3,2},{4,5},{5,4},{6,7},{7,6},{8,9},{9,8},{10,11... | collective-permute-start | bytes 61448 | tf_op jit(solution)/shard_map/ppermute | solution.py:257

commit v11 on v10

--- a/solution.py
+++ b/solution.py
@@ -150,8 +150,8 @@
         out_ref[s * rows : (s + 1) * rows, :] = (acc[s] * scale + bias).astype(bf16)
 
 
-def pack_kernel(kv_ref, part_ref, *refs):
-    out_ref = refs[-1]
+def pack_kernel(kv_ref, *refs):
+    part_ref, out_ref = refs[-2:]
     rows, heads = kv_ref.shape[0], kv_ref.shape[1] // HD
     folded = part_ref.shape[0] // heads
     out_ref[0:rows, :] = kv_ref[...]
@@ -161,7 +161,9 @@
 
 def prepare_kernel(heads, *refs):
     parts, (section_ref, q_ref, bias_ref, old_ref, stats_ref) = list(refs[:-5]), refs[-5:]
-    groups = len(parts)
+    groups = (len(parts) + 1) * 2 // 3
+    for k in range(1, groups // 2):
+        parts[k] = parts[k][...] + parts.pop(groups // 2)[...]
     folded = parts[0].shape[0] // heads
     for k in range(groups // 2 + 1, groups):
         packed = parts[k]
@@ -253,8 +255,9 @@
     return [pltpu.with_memory_space_constraint(x, pltpu.HBM) for x in arrays]
 
 
-def permute(x, axis, bits):
-    return lax.ppermute(x, axis, [(i, i ^ bits) for i in range(lax.axis_size(axis))])
+def permute(x, axis, bits, among=None):
+    devices = range(lax.axis_size(axis)) if among is None else among
+    return lax.ppermute(x, axis, [(i, i ^ bits) for i in devices])
 
 
 def passed_on(x, near, axis):
@@ -307,7 +310,9 @@
     own_later, part = lax.optimization_barrier((own, part))
     hidden = passed_on(memory_hidden, own_later, "tp")
     half = range(1, groups // 2)
+    lower, upper = range(groups // 2), range(groups // 2, groups)
     part_far = permute(part, "dp", groups // 2)
+    part_near = [permute(part, "dp", bits, lower) for bits in half]
     near, far = list(range(shares - 1)), [shares - 1]
     partial = call(
         functools.partial(project_kernel, near, True, False),
@@ -317,8 +322,6 @@
         COVER,
         4 * D * cols,
     )(*[hidden[k] for k in near], kv_weight)
-    part_later, *_ = lax.optimization_barrier((part, *partial))
-    part_near = [permute(part_later, "dp", bits) for bits in half]
     kv = call(
         functools.partial(project_kernel, far, False, True),
         [VMEM] * 5,
@@ -330,19 +333,21 @@
     kv_far = permute(kv, "dp", groups // 2)
     packed = call(
         pack_kernel,
-        [VMEM, VMEM] + [ANY] * len(part_near),
+        [VMEM] + [ANY] * len(part_near) + [VMEM],
         pltpu.VMEM((2 * memory + height // heads, cols), bf16),
         [],
         COVER,
         0,
-    )(kv, part_far, *part_near)
+    )(kv, *part_near, part_far)
     kv_on, _ = lax.optimization_barrier((kv_far, packed))
     near = [permute(packed, "dp", bits) for bits in half]
-    parts = [part, *part_near, part_far, *near]
+    part_later, _ = lax.optimization_barrier((part, packed))
+    part_late = [permute(part_later, "dp", bits, upper) for bits in half]
+    parts = [part, *part_near, *part_late, part_far, *near]
     kvs = [kv, *near, kv_far, *[permute(kv_on, "dp", bits) for bits in half]]
     prepared = call(
         functools.partial(prepare_kernel, heads),
-        [VMEM] * (groups + 1),
+        [VMEM] * (len(parts) + 1),
         [
             pltpu.VMEM((groups * rows, cols), bf16),
             pltpu.VMEM((groups * rows, every), f32),
@@ -371,7 +376,7 @@
         2 * out_weight.size,
     )(*kvs, *prepared, out_weight)
     summed = pieces[0]
-    for bits in [*range(shares - 2, 0, -1), shares - 1]:
+    for bits in [*range(1, shares - 2), *range(shares - 1, shares - 3, -1)]:
         summed = summed + permute(pieces[bits], "tp", bits).astype(f32)
     return summed.astype(bf16)
 

time: 28.4 us -> 29.8 us (1.049)
  the two profiles are of different devices: /device:TPU:0 before, /device:TPU:21 now
where the time goes in v11:
time: 29.8 us; the launch traced here: 29.7 us
  starting transfers between devices  14.9 us (50%)
  waiting for transfers between devices  8.42 us (28%)
  Pallas kernels  4.48 us (15%)
  between operations  1.19 us (4%)
  other arithmetic  0.62 us (2%)
    ppermute x12, starting transfers between devices, permute(): return lax.ppermute(x, axis, [(i, i ^ bits) for i in devices])  14.9 us
    ppermute x12, waiting for transfers between devices, permute(): return lax.ppermute(x, axis, [(i, i ^ bits) for i in devices])  8.42 us
    pallas_call x1, Pallas kernels, body(): call(functools.partial(attend_kernel, groups, shares), [VMEM] * (groups +...  1.43 us
    pallas_call x1, Pallas kernels, body(): call(cache_kernel, [SMEM] + [VMEM] * 6, pltpu.VMEM((height, HD), bf16), [...  1.37 us
    pallas_call x1, Pallas kernels, body(): call(functools.partial(project_kernel, near, True, False), [VMEM] * (len(...  0.81 us
    convert_element_type x1, other arithmetic, body(): return summed.astype(bf16)  0.62 us
  transfers between devices with their start and end apart: 12, of which 6 were waited for; matrix products, arithmetic and copies ran while one was open for 0% of the time, Pallas kernels for 10%

profile of v11, /device:TPU:21, one launch (start us, length us, event | category | flops | bytes accessed | tf_op | source)
XLA Modules:
  0.0 29.7 jit_solution(8205879158299123583)
XLA Ops:
  0.0 0.0 copy-start.6
  0.0 0.0 copy-start.2
  0.0 0.0 copy-start.3
  0.0 0.0 copy-start.9
  0.0 0.0 copy-start
  0.1 1.3 %collective-permute-start = (bf16[64,1280]{1,0:T(8,128)(2,1)}, bf16[64,1280]{1,0:T(8,128)(2,1)S(1)}, u32[]{:S(2)}, u32[]{:S(2)}) collective-permute-start(bf16[64,1280]{1,0:T(8,128)(2,1)} %refs_0_), channel_id=1, source_target_pairs={{0,2},{1,3},{2,0},{3,1},{4,6},{5,7},{6,4},{7,5},{8,10},{9,11},{10,... | collective-permute-start | bytes 491528 | tf_op jit(solution)/shard_map/ppermute | solution.py:260
  2.3 0.0 copy-done.4
  2.3 0.0 copy-done.5
  2.3 0.0 copy-done.6
  2.4 0.0 copy-done.2
  2.4 0.0 copy-done.3
  2.4 0.0 copy-done.9
  2.4 1.4 %shard_map.120.refs_0_ = bf16[192,128]{1,0:T(8,128)(2,1)S(1)} custom-call(s32[4]{0:T(128)S(1)} %copy-done.9, f32[8,128]{1,0:T(8,128)S(1)} %shard_map.119.section_ref, bf16[8,1280]{1,0:T(8,128)(2,1)S(1)} %copy-done.4, bf16[8,256]{1,0:T(8,128)(2,1)S(1)} %copy-done.5, bf16[8,256]{1,0:T(8,128)(2,1)S(1)} %copy-done.6, bf16[4,512,256]{2,1,0:T(8,128)(2,1)S(1)} %copy-done.2, ...), custom_call_target="tpu_custom_call" | custom-call | flops 167772160 | bytes 2097152 | tf_op jit(solution)/shard_map/pallas_call | solution.py:302
  3.8 0.0 copy-done.10
  3.8 0.0 copy-start.7
  3.8 1.2 %collective-permute-start.2 = (bf16[64,1280]{1,0:T(8,128)(2,1)S(1)}, bf16[64,1280]{1,0:T(8,128)(2,1)S(1)}, u32[]{:S(2)}, u32[]{:S(2)}) collective-permute-start(bf16[64,1280]{1,0:T(8,128)(2,1)S(1)} %copy-done.10), channel_id=1, source_target_pairs={{0,1},{1,0},{2,3},{3,2},{4,5},{5,4},{6,7},{7,6},{8,9},{9,8},{10,11... | collective-permute-start | bytes 491528 | tf_op jit(solution)/shard_map/ppermute | solution.py:260
  4.9 0.7 %collective-permute-start.3 = (bf16[192,128]{1,0:T(8,128)(2,1)S(1)}, bf16[192,128]{1,0:T(8,128)(2,1)S(1)}, u32[]{:S(2)}, u32[]{:S(2)}) collective-permute-start(bf16[192,128]{1,0:T(8,128)(2,1)S(1)} %shard_map.120.refs_0_), channel_id=1, source_target_pairs={{0,4},{4,0},{1,5},{5,1},{2,6},{6,2},{3,7},{7,3},{16,20},{20,16},{1... | collective-permute-start | bytes 147464 | tf_op jit(solution)/shard_map/ppermute | solution.py:260
  5.6 2.7 %collective-permute-start.4 = (bf16[192,128]{1,0:T(8,128)(2,1)S(1)}, bf16[192,128]{1,0:T(8,128)(2,1)S(1)}, u32[]{:S(2)}, u32[]{:S(2)}) collective-permute-start(bf16[192,128]{1,0:T(8,128)(2,1)S(1)} %shard_map.120.refs_0_), channel_id=1, source_target_pairs={{0,8},{4,12},{8,0},{12,4},{1,9},{5,13},{9,1},{13,5},{2,10},{6,14},... | collective-permute-start | bytes 147464 | tf_op jit(solution)/shard_map/ppermute | solution.py:260
  8.3 0.0 collective-permute-done.refs_2_
  8.3 0.6 %collective-permute-start.1 = (bf16[64,1280]{1,0:T(8,128)(2,1)S(1)}, bf16[64,1280]{1,0:T(8,128)(2,1)S(1)}, u32[]{:S(2)}, u32[]{:S(2)}) collective-permute-start(bf16[64,1280]{1,0:T(8,128)(2,1)S(1)} %collective-permute-done.refs_2_), channel_id=1, source_target_pairs={{0,1},{1,0},{2,3},{3,2},{4,5},{5,4},{6,7},{7,6},{8,9},{9,8},{10,11... | collective-permute-start | bytes 491528 | tf_op jit(solution)/shard_map/ppermute | solution.py:260
  8.8 0.0 collective-permute-done.2.refs_1_
  8.8 0.0 copy-done
  8.9 0.8 %shard_map.121 = (f32[128,256]{1,0:T(8,128)S(1)}, f32[64,128]{1,0:T(8,128)S(1)}) custom-call(bf16[64,1280]{1,0:T(8,128)(2,1)S(1)} %copy-done.10, bf16[64,1280]{1,0:T(8,128)(2,1)S(1)} %collective-permute-done.2.refs_1_, bf16[64,1280]{1,0:T(8,128)(2,1)S(1)} %collective-permute-done.refs_2_, bf16[2,5120,256]{2,1,0:T(8,128)(2,1)S(1)} %copy-done), custom_call_target="tpu_custom_call" | custom-call | flops 68719476736 | bytes 5242880 | tf_op jit(solution)/shard_map/pallas_call | solution.py:317
  9.7 0.2 collective-permute-done.1.refs_0_
  9.9 0.0 copy-done.7
  9.9 0.4 %shard_map.122.kv_ref.refs_0_ = bf16[128,256]{1,0:T(8,128)(2,1)S(1)} custom-call(bf16[64,1280]{1,0:T(8,128)(2,1)S(1)} %collective-permute-done.1.refs_0_, bf16[2,5120,256]{2,1,0:T(8,128)(2,1)S(1)} %copy-done, f32[128,256]{1,0:T(8,128)S(1)} %get-tuple-element.28.refs_2_, f32[64,128]{1,0:T(8,128)S(1)} %get-tuple-element.29.refs_3_, bf16[2,256]{1,0:T(2,128)(2,1)S(1)} %copy-done.7), custom_call_target="tpu_custom_call" | custom-call | flops 83886080 | bytes 1310720 | tf_op jit(solution)/shard_map/pallas_call | solution.py:325
  10.3 0.0 copy-start.1
  10.3 0.1 collective-permute-start.6
  10.4 0.0 collective-permute-done.3.refs_0_.refs_1_
  10.4 0.7 %collective-permute-done.4.refs_1_.refs_3_ = bf16[192,128]{1,0:T(8,128)(2,1)S(1)} collective-permute-done((bf16[192,128]{1,0:T(8,128)(2,1)S(1)}, bf16[192,128]{1,0:T(8,128)(2,1)S(1)}, u32[]{:S(2)}, u32[]{:S(2)}) %collective-permute-start.4) | collective-permute-done | bytes 49184 | tf_op jit(solution)/shard_map/ppermute | solution.py:260
  11.1 0.2 collective-permute-start.5
  11.3 3.2 %collective-permute-done.6.refs_2_ = bf16[128,256]{1,0:T(8,128)(2,1)S(1)} collective-permute-done((bf16[128,256]{1,0:T(8,128)(2,1)S(1)}, bf16[128,256]{1,0:T(8,128)(2,1)S(1)}, u32[]{:S(2)}, u32[]{:S(2)}) %collective-permute-start.6) | collective-permute-done | bytes 65568 | tf_op jit(solution)/shard_map/ppermute | solution.py:260
  14.5 0.2 collective-permute-start.7
  14.6 3.2 %collective-permute-start.8 = (bf16[192,128]{1,0:T(8,128)(2,1)S(1)}, bf16[192,128]{1,0:T(8,128)(2,1)S(1)}, u32[]{:S(2)}, u32[]{:S(2)}) collective-permute-start(bf16[192,128]{1,0:T(8,128)(2,1)S(1)} %shard_map.120.refs_0_), channel_id=1, source_target_pairs={{8,12},{12,8},{9,13},{13,9},{10,14},{14,10},{11,15},{15,11},{24,28... | collective-permute-start | bytes 147464 | tf_op jit(solution)/shard_map/ppermute | solution.py:260
  17.9 2.2 %collective-permute-done.8.refs_2_ = bf16[192,128]{1,0:T(8,128)(2,1)S(1)} collective-permute-done((bf16[192,128]{1,0:T(8,128)(2,1)S(1)}, bf16[192,128]{1,0:T(8,128)(2,1)S(1)}, u32[]{:S(2)}, u32[]{:S(2)}) %collective-permute-start.8) | collective-permute-done | bytes 49184 | tf_op jit(solution)/shard_map/ppermute | solution.py:260
  20.0 0.0 collective-permute-done.5.refs_4_.refs_1_
  20.0 0.0 copy-done.8
  20.0 0.5 %shard_map.124 = (bf16[320,256]{1,0:T(8,128)(2,1)S(1)}, f32[320,256]{1,0:T(8,128)S(1)}, f32[320,128]{1,0:T(8,128)S(1)}, f32[320,128]{1,0:T(8,128)S(1)}) custom-call(bf16[192,128]{1,0:T(8,128)(2,1)S(1)} %shard_map.120.refs_0_, bf16[192,128]{1,0:T(8,128)(2,1)S(1)} %collective-permute-done.3.refs_0_.refs_1_, ...), custom_call_target="tpu_custom_call" | custom-call | flops 1024 | tf_op jit(solution)/shard_map/pallas_call | solution.py:348
  20.5 0.0 collective-permute-done.7.refs_3_
  20.5 0.0 copy-done.1
  20.5 1.4 %shard_map.125 = (f32[8,1280]{1,0:T(8,128)S(1)}, bf16[8,1280]{1,0:T(8,128)(2,1)S(1)}, bf16[8,1280]{1,0:T(8,128)(2,1)S(1)}, bf16[8,1280]{1,0:T(8,128)(2,1)S(1)}) custom-call(bf16[128,256]{1,0:T(8,128)(2,1)S(1)} %shard_map.122.kv_ref.refs_0_, bf16[224,256]{1,0:T(8,128)(2,1)S(1)} %collective-permute-done.5.refs_4_.refs_1_, ...), custom_call_target="tpu_custom_call" | custom-call | flops 104857600 | bytes 3276800 | tf_op jit(solution)/shard_map/pallas_call | solution.py:365
  22.0 4.0 %collective-permute-start.10 = (bf16[8,1280]{1,0:T(8,128)(2,1)S(1)}, bf16[8,1280]{1,0:T(8,128)(2,1)S(1)}, u32[]{:S(2)}, u32[]{:S(2)}) collective-permute-start(bf16[8,1280]{1,0:T(8,128)(2,1)S(1)} %get-tuple-element.39), channel_id=1, source_target_pairs={{0,3},{1,2},{2,1},{3,0},{4,7},{5,6},{6,5},{7,4},{8,11},{9,10},{10,... | collective-permute-start | bytes 61448 | tf_op jit(solution)/shard_map/ppermute | solution.py:260
  26.0 0.9 %collective-permute-start.11 = (bf16[8,1280]{1,0:T(8,128)(2,1)S(1)}, bf16[8,1280]{1,0:T(8,128)(2,1)S(1)}, u32[]{:S(2)}, u32[]{:S(2)}) collective-permute-start(bf16[8,1280]{1,0:T(8,128)(2,1)S(1)} %get-tuple-element.40), channel_id=1, source_target_pairs={{0,2},{1,3},{2,0},{3,1},{4,6},{5,7},{6,4},{7,5},{8,10},{9,11},{10,... | collective-permute-start | bytes 61448 | tf_op jit(solution)/shard_map/ppermute | solution.py:260
  26.9 0.0 collective-permute-start.9
  26.9 0.5 %collective-permute-done.10 = bf16[8,1280]{1,0:T(8,128)(2,1)S(1)} collective-permute-done((bf16[8,1280]{1,0:T(8,128)(2,1)S(1)}, bf16[8,1280]{1,0:T(8,128)(2,1)S(1)}, u32[]{:S(2)}, u32[]{:S(2)}) %collective-permute-start.10) | collective-permute-done | bytes 20512 | tf_op jit(solution)/shard_map/ppermute | solution.py:260
  27.5 1.6 %collective-permute-done.11 = bf16[8,1280]{1,0:T(8,128)(2,1)S(1)} collective-permute-done((bf16[8,1280]{1,0:T(8,128)(2,1)S(1)}, bf16[8,1280]{1,0:T(8,128)(2,1)S(1)}, u32[]{:S(2)}, u32[]{:S(2)}) %collective-permute-start.11) | collective-permute-done | bytes 20512 | tf_op jit(solution)/shard_map/ppermute | solution.py:260
  29.0 0.0 collective-permute-done.9
  29.0 0.6 %add_convert_fusion = bf16[8,1280]{1,0:T(8,128)(2,1)} fusion(bf16[8,1280]{1,0:T(8,128)(2,1)S(1)} %collective-permute-done.11, bf16[8,1280]{1,0:T(8,128)(2,1)S(1)} %collective-permute-done.10, f32[8,1280]{1,0:T(8,128)S(1)} %get-tuple-element.37, bf16[8,1280]{1,0:T(8,128)(2,1)S(1)} %collective-permute-done.9), kind=kLoop, calls=%fused_computation | loop fusion | flops 71680 | bytes 122880 | tf_op jit(solution)/shard_map/convert_element_type | solution.py:381
  (7 shorter events, 0.0 us)
Async XLA Ops:
  0.0 3.8 %copy-start.10 = (bf16[64,1280]{1,0:T(8,128)(2,1)S(1)}, bf16[64,1280]{1,0:T(8,128)(2,1)}, u32[]{:S(2)}) copy-start(bf16[64,1280]{1,0:T(8,128)(2,1)} %refs_0_) | copy-start | bytes 491524
  0.0 2.3 %copy-start.4 = (bf16[8,1280]{1,0:T(8,128)(2,1)S(1)}, bf16[8,1280]{1,0:T(8,128)(2,1)}, u32[]{:S(2)}) copy-start(bf16[8,1280]{1,0:T(8,128)(2,1)} %q_ref.1) | copy-start | bytes 61444
  0.0 2.3 %copy-start.5 = (bf16[8,256]{1,0:T(8,128)(2,1)S(1)}, bf16[8,256]{1,0:T(8,128)(2,1)}, u32[]{:S(2)}) copy-start(bf16[8,256]{1,0:T(8,128)(2,1)} %nk_ref.1) | copy-start | bytes 12292
  0.0 2.3 %copy-start.6 = (bf16[8,256]{1,0:T(8,128)(2,1)S(1)}, bf16[8,256]{1,0:T(8,128)(2,1)}, u32[]{:S(2)}) copy-start(bf16[8,256]{1,0:T(8,128)(2,1)} %nv_ref.1) | copy-start | bytes 12292
  0.0 2.3 %copy-start.2 = (bf16[4,512,256]{2,1,0:T(8,128)(2,1)S(1)}, bf16[4,512,256]{2,1,0:T(8,128)(2,1)}, u32[]{:S(2)}) copy-start(bf16[4,512,256]{2,1,0:T(8,128)(2,1)} %ck_ref.1) | copy-start | bytes 3145732
  0.0 2.3 %copy-start.3 = (bf16[4,512,256]{2,1,0:T(8,128)(2,1)S(1)}, bf16[4,512,256]{2,1,0:T(8,128)(2,1)}, u32[]{:S(2)}) copy-start(bf16[4,512,256]{2,1,0:T(8,128)(2,1)} %cv_ref.1) | copy-start | bytes 3145732
  0.0 2.3 %copy-start.9 = (s32[4]{0:T(128)S(1)}, s32[4]{0:T(128)}, u32[]{:S(2)}) copy-start(s32[4]{0:T(128)} %lens_ref.1) | copy-start | bytes 52
  0.0 8.8 %copy-start = (bf16[2,5120,256]{2,1,0:T(8,128)(2,1)S(1)}, bf16[2,5120,256]{2,1,0:T(8,128)(2,1)}, u32[]{:S(2)}) copy-start(bf16[2,5120,256]{2,1,0:T(8,128)(2,1)} %refs_1_.1) | copy-start | bytes 15728644
  0.1 8.2 %collective-permute-start = (bf16[64,1280]{1,0:T(8,128)(2,1)}, bf16[64,1280]{1,0:T(8,128)(2,1)S(1)}, u32[]{:S(2)}, u32[]{:S(2)}) collective-permute-start(bf16[64,1280]{1,0:T(8,128)(2,1)} %refs_0_), channel_id=1, source_target_pairs={{0,2},{1,3},{2,0},{3,1},{4,6},{5,7},{6,4},{7,5},{8,10},{9,11},{10,... | collective-permute-start | bytes 491528 | tf_op jit(solution)/shard_map/ppermute | solution.py:260
  3.8 6.1 %copy-start.7 = (bf16[2,256]{1,0:T(2,128)(2,1)S(1)}, bf16[2,256]{1,0:T(2,128)(2,1)}, u32[]{:S(2)}) copy-start(bf16[2,256]{1,0:T(2,128)(2,1)} %refs_4_.1) | copy-start | bytes 3076
  3.8 5.1 %collective-permute-start.2 = (bf16[64,1280]{1,0:T(8,128)(2,1)S(1)}, bf16[64,1280]{1,0:T(8,128)(2,1)S(1)}, u32[]{:S(2)}, u32[]{:S(2)}) collective-permute-start(bf16[64,1280]{1,0:T(8,128)(2,1)S(1)} %copy-done.10), channel_id=1, source_target_pairs={{0,1},{1,0},{2,3},{3,2},{4,5},{5,4},{6,7},{7,6},{8,9},{9,8},{10,11... | collective-permute-start | bytes 491528 | tf_op jit(solution)/shard_map/ppermute | solution.py:260
  4.9 5.4 %collective-permute-start.3 = (bf16[192,128]{1,0:T(8,128)(2,1)S(1)}, bf16[192,128]{1,0:T(8,128)(2,1)S(1)}, u32[]{:S(2)}, u32[]{:S(2)}) collective-permute-start(bf16[192,128]{1,0:T(8,128)(2,1)S(1)} %shard_map.120.refs_0_), channel_id=1, source_target_pairs={{0,4},{4,0},{1,5},{5,1},{2,6},{6,2},{3,7},{7,3},{16,20},{20,16},{1... | collective-permute-start | bytes 147464 | tf_op jit(solution)/shard_map/ppermute | solution.py:260
  5.6 5.5 %collective-permute-start.4 = (bf16[192,128]{1,0:T(8,128)(2,1)S(1)}, bf16[192,128]{1,0:T(8,128)(2,1)S(1)}, u32[]{:S(2)}, u32[]{:S(2)}) collective-permute-start(bf16[192,128]{1,0:T(8,128)(2,1)S(1)} %shard_map.120.refs_0_), channel_id=1, source_target_pairs={{0,8},{4,12},{8,0},{12,4},{1,9},{5,13},{9,1},{13,5},{2,10},{6,14},... | collective-permute-start | bytes 147464 | tf_op jit(solution)/shard_map/ppermute | solution.py:260
  8.3 1.6 %collective-permute-start.1 = (bf16[64,1280]{1,0:T(8,128)(2,1)S(1)}, bf16[64,1280]{1,0:T(8,128)(2,1)S(1)}, u32[]{:S(2)}, u32[]{:S(2)}) collective-permute-start(bf16[64,1280]{1,0:T(8,128)(2,1)S(1)} %collective-permute-done.refs_2_), channel_id=1, source_target_pairs={{0,1},{1,0},{2,3},{3,2},{4,5},{5,4},{6,7},{7,6},{8,9},{9,8},{10,11... | collective-permute-start | bytes 491528 | tf_op jit(solution)/shard_map/ppermute | solution.py:260
  10.3 9.8 %copy-start.8 = (s32[256]{0:T(256)S(1)}, s32[256]{0:T(256)}, u32[]{:S(2)}) copy-start(s32[256]{0:T(256)} %param.15) | copy-start | bytes 3076
  10.3 10.3 %copy-start.1 = (bf16[1280,1280]{1,0:T(8,128)(2,1)S(1)}, bf16[1280,1280]{1,0:T(8,128)(2,1)}, u32[]{:S(2)}) copy-start(bf16[1280,1280]{1,0:T(8,128)(2,1)} %refs_8_.1) | copy-start | bytes 9830404
  10.3 4.2 %collective-permute-start.6 = (bf16[128,256]{1,0:T(8,128)(2,1)S(1)}, bf16[128,256]{1,0:T(8,128)(2,1)S(1)}, u32[]{:S(2)}, u32[]{:S(2)}) collective-permute-start(bf16[128,256]{1,0:T(8,128)(2,1)S(1)} %shard_map.122.kv_ref.refs_0_), channel_id=1, source_target_pairs={{0,8},{4,12},{8,0},{12,4},{1,9},{5,13},{9,1},{13,5},{2,10},{6,14},... | collective-permute-start | bytes 196616 | tf_op jit(solution)/shard_map/ppermute | solution.py:260
  11.1 8.9 %collective-permute-start.5 = (bf16[224,256]{1,0:T(8,128)(2,1)S(1)}, bf16[224,256]{1,0:T(8,128)(2,1)S(1)}, u32[]{:S(2)}, u32[]{:S(2)}) collective-permute-start(bf16[224,256]{1,0:T(8,128)(2,1)S(1)} %shard_map.123), channel_id=1, source_target_pairs={{0,4},{4,0},{8,12},{12,8},{1,5},{5,1},{9,13},{13,9},{2,6},{6,2},{1... | collective-permute-start | bytes 344072 | tf_op jit(solution)/shard_map/ppermute | solution.py:260
  14.5 6.1 %collective-permute-start.7 = (bf16[128,256]{1,0:T(8,128)(2,1)S(1)}, bf16[128,256]{1,0:T(8,128)(2,1)S(1)}, u32[]{:S(2)}, u32[]{:S(2)}) collective-permute-start(bf16[128,256]{1,0:T(8,128)(2,1)S(1)} %collective-permute-done.6.refs_2_), channel_id=1, source_target_pairs={{0,4},{4,0},{8,12},{12,8},{1,5},{5,1},{9,13},{13,9},{2,6},{6,2},{1... | collective-permute-start | bytes 196616 | tf_op jit(solution)/shard_map/ppermute | solution.py:260
  14.6 5.4 %collective-permute-start.8 = (bf16[192,128]{1,0:T(8,128)(2,1)S(1)}, bf16[192,128]{1,0:T(8,128)(2,1)S(1)}, u32[]{:S(2)}, u32[]{:S(2)}) collective-permute-start(bf16[192,128]{1,0:T(8,128)(2,1)S(1)} %shard_map.120.refs_0_), channel_id=1, source_target_pairs={{8,12},{12,8},{9,13},{13,9},{10,14},{14,10},{11,15},{15,11},{24,28... | collective-permute-start | bytes 147464 | tf_op jit(solution)/shard_map/ppermute | solution.py:260
  22.0 5.5 %collective-permute-start.10 = (bf16[8,1280]{1,0:T(8,128)(2,1)S(1)}, bf16[8,1280]{1,0:T(8,128)(2,1)S(1)}, u32[]{:S(2)}, u32[]{:S(2)}) collective-permute-start(bf16[8,1280]{1,0:T(8,128)(2,1)S(1)} %get-tuple-element.39), channel_id=1, source_target_pairs={{0,3},{1,2},{2,1},{3,0},{4,7},{5,6},{6,5},{7,4},{8,11},{9,10},{10,... | collective-permute-start | bytes 61448 | tf_op jit(solution)/shard_map/ppermute | solution.py:260
  26.0 3.0 %collective-permute-start.11 = (bf16[8,1280]{1,0:T(8,128)(2,1)S(1)}, bf16[8,1280]{1,0:T(8,128)(2,1)S(1)}, u32[]{:S(2)}, u32[]{:S(2)}) collective-permute-start(bf16[8,1280]{1,0:T(8,128)(2,1)S(1)} %get-tuple-element.40), channel_id=1, source_target_pairs={{0,2},{1,3},{2,0},{3,1},{4,6},{5,7},{6,4},{7,5},{8,10},{9,11},{10,... | collective-permute-start | bytes 61448 | tf_op jit(solution)/shard_map/ppermute | solution.py:260
  26.9 2.1 %collective-permute-start.9 = (bf16[8,1280]{1,0:T(8,128)(2,1)S(1)}, bf16[8,1280]{1,0:T(8,128)(2,1)S(1)}, u32[]{:S(2)}, u32[]{:S(2)}) collective-permute-start(bf16[8,1280]{1,0:T(8,128)(2,1)S(1)} %get-tuple-element.38), channel_id=1, source_target_pairs={{0,1},{1,0},{2,3},{3,2},{4,5},{5,4},{6,7},{7,6},{8,9},{9,8},{10,11... | collective-permute-start | bytes 61448 | tf_op jit(solution)/shard_map/ppermute | solution.py:260

commit v12 on v9

--- a/solution.py
+++ b/solution.py
@@ -156,7 +156,7 @@
 
 
 def prepare_kernel(heads, *refs):
-    pairs, (section_ref, q_ref, bias_ref, old_ref, stats_ref) = refs[:-5], refs[-5:]
+    pairs, (section_ref, q_ref, first_bias_ref, last_bias_ref, old_ref, stats_ref) = refs[:-6], refs[-6:]
     parts = [pair.at[i] for i in range(2) for pair in pairs]
     groups = len(parts)
     seg = (parts[0].shape[0] - STATS) // 2
@@ -178,43 +178,74 @@
         return jnp.concatenate(columns, axis=0)
 
     top, total = column(TOP, 3), column(TOTAL, 2)
-    bias_ref[...] = jnp.where(column(SECTION, 1) == section_ref[...].astype(f32), 0.0, masked_score)
+    every = section_ref.shape[1]
+    memory = every // groups
+    sections = jnp.broadcast_to(section_ref[...].astype(f32), (8, every))
+    me = lax.axis_index("dp")
+    ordered = []
+    for k in range(groups):
+        back = lax.rem(every - (me ^ k) * memory, every)
+        ordered.append(pltpu.roll(sections, back, 1)[0:1, 0:memory])
+    first = groups // 2 + 1
+    own_section = column(SECTION, 1)
+    for bias_ref, some in ((first_bias_ref, ordered[:first]), (last_bias_ref, ordered[first:])):
+        same = own_section == jnp.concatenate(some, axis=1)
+        bias_ref[...] = jnp.where(same, 0.0, masked_score)
     old = jnp.concatenate([part[seg : seg + rows, :] for part in parts], axis=0).astype(f32)
     old_ref[...] = old * total
     lane = lax.broadcasted_iota(jnp.int32, stats_ref.shape, 1)
     stats_ref[...] = jnp.where(lane == 0, top, total)
 
 
-def attend_kernel(groups, shares, *refs):
-    kvs, (q_ref, bias_ref, old_ref, stats_ref, w_ref) = refs[:groups], refs[groups : groups + 5]
-    outs = refs[groups + 5 : groups + 5 + shares]
-    k_ref, v_ref, attended_ref, sums_ref = refs[groups + 5 + shares :]
-    me_dp, me_tp = lax.axis_index("dp"), lax.axis_index("tp")
+def stack(blocks):
+    if blocks[0].shape[0] % 16:
+        return jnp.concatenate([b.astype(f32) for b in blocks], axis=0).astype(bf16)
+    return jnp.concatenate(blocks, axis=0)
+
+
+def join(kvs, groups, q_ref, bias_ref, old_ref, stats_ref):
     memory = kvs[0].shape[0] // 2
     heads = kvs[0].shape[1] // HD
-    tokens = attended_ref.shape[0] // groups
-    per = PER_HEAD * tokens
-    rows = heads * per
-    for bits, kv in enumerate(kvs):
-        first = pl.multiple_of((me_dp ^ bits) * memory, memory)
-        k_ref[pl.ds(first, memory), :] = kv[0:memory, :].astype(k_ref.dtype)
-        v_ref[pl.ds(first, memory), :] = kv[memory : 2 * memory, :].astype(v_ref.dtype)
-    s = nt(q_ref[...], k_ref[...].astype(bf16)) * INV + bias_ref[...]
+    per = q_ref.shape[0] // (groups * heads)
+    keys = stack([kv[0:memory, :] for kv in kvs])
+    values = stack([kv[memory : 2 * memory, :] for kv in kvs])
+    s = nt(q_ref[...], keys) * INV + bias_ref[...]
     old_top, old_total = stats_ref[:, 0:1], stats_ref[:, 1:2]
     top = jnp.maximum(jnp.max(s, axis=1, keepdims=True), old_top)
     p = jnp.exp(s - top)
     shrink = jnp.exp(old_top - top)
     total = jnp.sum(p, axis=1, keepdims=True) + shrink * old_total
-    acc = nn(p.astype(bf16), v_ref[...].astype(bf16))
+    acc = nn(p.astype(bf16), values)
+    own_heads = [
+        acc[(k * heads + j) * per : (k * heads + j + 1) * per, j * HD : (j + 1) * HD]
+        for k in range(groups)
+        for j in range(heads)
+    ]
+    return jnp.concatenate(own_heads, axis=0) + old_ref[...] * shrink, top, total
+
+
+def first_attend_kernel(groups, *refs):
+    kvs, (q_ref, bias_ref, old_ref, stats_ref, out_ref, out_stats_ref) = refs[:-6], refs[-6:]
+    acc, top, total = join(kvs, groups, q_ref, bias_ref, old_ref, stats_ref)
+    out_ref[...] = acc
+    lane = lax.broadcasted_iota(jnp.int32, out_stats_ref.shape, 1)
+    out_stats_ref[...] = jnp.where(lane == 0, top, total)
+
+
+def attend_kernel(count, groups, shares, *refs):
+    kvs, (q_ref, bias_ref, old_ref, stats_ref, w_ref) = refs[:count], refs[count : count + 5]
+    outs = refs[count + 5 : count + 5 + shares]
+    attended_ref, sums_ref = refs[count + 5 + shares :]
+    me_dp, me_tp = lax.axis_index("dp"), lax.axis_index("tp")
+    heads = kvs[0].shape[1] // HD
+    tokens = attended_ref.shape[0] // groups
+    acc, _, total = join(kvs, groups, q_ref, bias_ref, old_ref, stats_ref)
+    acc = acc / total
     for k in range(groups):
         at = pl.multiple_of((me_dp ^ k) * tokens, tokens)
-        for j in range(heads):
-            a = k * rows + j * per
-            block = acc[a : a + per, j * HD : (j + 1) * HD] + old_ref[a : a + per, :] * shrink[a : a + per]
-            block = block / total[a : a + per]
-            for g in range(PER_HEAD):
-                c = (j * PER_HEAD + g) * HD
-                attended_ref[pl.ds(at, tokens), c : c + HD] = block[g * tokens : (g + 1) * tokens, :]
+        for c in range(heads * PER_HEAD):
+            row = (k * heads * PER_HEAD + c) * tokens
+            attended_ref[pl.ds(at, tokens), c * HD : (c + 1) * HD] = acc[row : row + tokens, :]
     sums_ref[...] = nn(attended_ref[...].astype(bf16), w_ref[...])
     share = sums_ref.shape[0] // shares
     for k, out in enumerate(outs):
@@ -332,7 +363,8 @@
         [VMEM] * (groups // 2 + 1),
         [
             pltpu.VMEM((groups * rows, cols), bf16),
-            pltpu.VMEM((groups * rows, every), f32),
+            pltpu.VMEM((groups * rows, (groups // 2 + 1) * memory), f32),
+            pltpu.VMEM((groups * rows, (groups // 2 - 1) * memory), f32),
             pltpu.VMEM((groups * rows, HD), f32),
             pltpu.VMEM((groups * rows, HD), f32),
         ],
@@ -343,22 +375,29 @@
 
     out_rows, out_cols = groups * tokens, out_weight.shape[1]
     share = out_rows // shares
-    held = bf16 if memory % 16 == 0 else f32
+    asked, first_bias, last_bias, old, stats = prepared
+    first = groups // 2 + 1
+    old, stats = call(
+        functools.partial(first_attend_kernel, groups),
+        [VMEM] * (first + 4),
+        [pltpu.VMEM(old.shape, f32), pltpu.VMEM(stats.shape, f32)],
+        [],
+        4 * groups * rows * first * memory * cols,
+        4 * old.size,
+    )(*kvs[:first], asked, first_bias, old, stats)
     pieces = call(
-        functools.partial(attend_kernel, groups, shares),
-        [VMEM] * (groups + 5),
+        functools.partial(attend_kernel, groups - first, groups, shares),
+        [VMEM] * (groups - first + 5),
         [pltpu.VMEM((share, out_cols), f32 if k == 0 else bf16) for k in range(shares)],
         [
-            pltpu.VMEM((every, cols), held),
-            pltpu.VMEM((every, cols), held),
             pltpu.VMEM((out_rows, out_weight.shape[0]), f32),
             pltpu.VMEM((out_rows, out_cols), f32),
         ],
         2 * out_rows * out_weight.size,
         2 * out_weight.size,
-    )(*kvs, *prepared, out_weight)
+    )(*kvs[first:], asked, last_bias, old, stats, out_weight)
     summed = pieces[0]
-    for bits in [*range(shares - 2, 0, -1), shares - 1]:
+    for bits in [*range(shares // 2, shares), *range(1, shares // 2)]:
         summed = summed + permute(pieces[bits], "tp", bits).astype(f32)
     return summed.astype(bf16)
 

time: 27.2 us -> 27.7 us (1.018)
  Pallas kernels: 4.48 us -> 5.54 us
  waiting for transfers between devices: 8.17 us -> 7.32 us
  starting transfers between devices: 12.9 us -> 13.2 us
    pallas_call x1 -> x2, Pallas kernels: 1.42 us -> 2.48 us  [the longest x1 1.76 us: body(): call(functools.partial(attend_kernel, groups - first, groups, shares), [V...]
    ppermute x11, waiting for transfers between devices: 8.17 us -> 7.32 us  [permute(): lax.ppermute(x, axis, [(i, i ^ bits) for i in range(lax.axis_size(axis))])]
    ppermute x11, starting transfers between devices: 12.9 us -> 13.2 us  [permute(): lax.ppermute(x, axis, [(i, i ^ bits) for i in range(lax.axis_size(axis))])]
  transfers between devices with their start and end apart: 11 -> 11, of which waited for: 7 -> 6; matrix products, arithmetic and copies ran while one was open for 0% -> 0% of each run, Pallas kernels for 11% -> 14%
where the time goes in v12:
time: 27.7 us; the launch traced here: 27.5 us
  starting transfers between devices  13.2 us (48%)
  waiting for transfers between devices  7.32 us (26%)
  Pallas kernels  5.54 us (20%)
  between operations  0.81 us (3%)
  other arithmetic  0.62 us (2%)
    ppermute x11, starting transfers between devices, permute(): lax.ppermute(x, axis, [(i, i ^ bits) for i in range(lax.axis_size(axis))])  13.2 us
    ppermute x11, waiting for transfers between devices, permute(): lax.ppermute(x, axis, [(i, i ^ bits) for i in range(lax.axis_size(axis))])  7.32 us
    pallas_call x1, Pallas kernels, body(): call(functools.partial(attend_kernel, groups - first, groups, shares), [V...  1.76 us
    pallas_call x1, Pallas kernels, body(): call(cache_kernel, [SMEM] + [VMEM] * 6, pltpu.VMEM((2 * up(rows, 16) + ST...  1.38 us
    pallas_call x1, Pallas kernels, body(): call(functools.partial(project_kernel, near, True, False), [VMEM] * (len(...  0.81 us
    pallas_call x1, Pallas kernels, body(): call(functools.partial(first_attend_kernel, groups), [VMEM] * (first + 4)...  0.72 us
    convert_element_type x1, other arithmetic, body(): return summed.astype(bf16)  0.62 us
  transfers between devices with their start and end apart: 11, of which 6 were waited for; matrix products, arithmetic and copies ran while one was open for 0% of the time, Pallas kernels for 14%

profile of v12, /device:TPU:0, one launch (start us, length us, event | category | flops | bytes accessed | tf_op | source)
XLA Modules:
  0.0 27.5 jit_solution(3983965089173738654)
XLA Ops:
  0.0 0.0 copy-start.10
  0.0 0.0 copy-start.3
  0.0 0.0 copy-start.2
  0.0 0.0 copy-start.5
  0.0 0.0 copy-start.4
  0.0 0.0 copy-start
  0.0 3.0 %collective-permute-start = (bf16[64,1280]{1,0:T(8,128)(2,1)}, bf16[64,1280]{1,0:T(8,128)(2,1)S(1)}, u32[]{:S(2)}, u32[]{:S(2)}) collective-permute-start(bf16[64,1280]{1,0:T(8,128)(2,1)} %refs_0_), channel_id=1, source_target_pairs={{0,2},{1,3},{2,0},{3,1},{4,6},{5,7},{6,4},{7,5},{8,10},{9,11},{10,... | collective-permute-start | bytes 491528 | tf_op jit(solution)/shard_map/ppermute | solution.py:280
  3.7 0.0 copy-done.9
  3.7 0.0 copy-done.3
  3.7 0.0 copy-done.2
  3.8 0.0 copy-done.6
  3.8 0.0 copy-done.5
  3.8 0.0 copy-done.4
  3.8 1.4 %shard_map.120.near_ref = bf16[176,128]{1,0:T(8,128)(2,1)S(1)} custom-call(s32[4]{0:T(128)S(1)} %copy-done.9, f32[8,128]{1,0:T(8,128)S(1)} %shard_map.119.section_ref, bf16[8,1280]{1,0:T(8,128)(2,1)S(1)} %copy-done.4, bf16[8,256]{1,0:T(8,128)(2,1)S(1)} %copy-done.5, bf16[8,256]{1,0:T(8,128)(2,1)S(1)} %copy-done.6, bf16[4,512,256]{2,1,0:T(8,128)(2,1)S(1)} %copy-done.2, ...), custom_call_target="tpu_custom_call" | custom-call | flops 167772160 | bytes 2097152 | tf_op jit(solution)/shard_map/pallas_call | solution.py:320
  5.2 0.0 copy-done.10
  5.2 0.0 copy-start.7
  5.2 0.1 collective-permute-start.2
  5.3 3.1 %collective-permute-start.4 = (bf16[176,128]{1,0:T(8,128)(2,1)S(1)}, bf16[176,128]{1,0:T(8,128)(2,1)S(1)}, u32[]{:S(2)}, u32[]{:S(2)}) collective-permute-start(bf16[176,128]{1,0:T(8,128)(2,1)S(1)} %shard_map.120.near_ref), channel_id=1, source_target_pairs={{0,8},{4,12},{8,0},{12,4},{1,9},{5,13},{9,1},{13,5},{2,10},{6,14},... | collective-permute-start | bytes 135176 | tf_op jit(solution)/shard_map/ppermute | solution.py:280
  8.4 0.0 collective-permute-done.refs_2_
  8.4 0.2 collective-permute-start.1
  8.5 0.0 collective-permute-done.2.refs_1_
  8.5 0.0 copy-done
  8.6 0.8 %shard_map.121 = (f32[128,256]{1,0:T(8,128)S(1)}, f32[64,128]{1,0:T(8,128)S(1)}) custom-call(bf16[64,1280]{1,0:T(8,128)(2,1)S(1)} %copy-done.10, bf16[64,1280]{1,0:T(8,128)(2,1)S(1)} %collective-permute-done.2.refs_1_, bf16[64,1280]{1,0:T(8,128)(2,1)S(1)} %collective-permute-done.refs_2_, bf16[2,5120,256]{2,1,0:T(8,128)(2,1)S(1)} %copy-done), custom_call_target="tpu_custom_call" | custom-call | flops 68719476736 | bytes 5242880 | tf_op jit(solution)/shard_map/pallas_call | solution.py:332
  9.4 0.4 %collective-permute-done.1.refs_0_ = bf16[64,1280]{1,0:T(8,128)(2,1)S(1)} collective-permute-done((bf16[64,1280]{1,0:T(8,128)(2,1)S(1)}, bf16[64,1280]{1,0:T(8,128)(2,1)S(1)}, u32[]{:S(2)}, u32[]{:S(2)}) %collective-permute-start.1) | collective-permute-done | bytes 163872 | tf_op jit(solution)/shard_map/ppermute | solution.py:280
  9.8 0.0 copy-done.7
  9.8 0.4 %shard_map.122.after.refs_0_ = bf16[128,256]{1,0:T(8,128)(2,1)S(1)} custom-call(bf16[64,1280]{1,0:T(8,128)(2,1)S(1)} %collective-permute-done.1.refs_0_, bf16[2,5120,256]{2,1,0:T(8,128)(2,1)S(1)} %copy-done, f32[128,256]{1,0:T(8,128)S(1)} %get-tuple-element.30.refs_2_, f32[64,128]{1,0:T(8,128)S(1)} %get-tuple-element.31.refs_3_, bf16[2,256]{1,0:T(2,128)(2,1)S(1)} %copy-done.7), custom_call_target="tpu_custom_call" | custom-call | flops 83886080 | bytes 1310720 | tf_op jit(solution)/shard_map/pallas_call | solution.py:340
  10.2 0.0 copy-start.1
  10.2 2.0 %collective-permute-start.3 = (bf16[128,256]{1,0:T(8,128)(2,1)S(1)}, bf16[128,256]{1,0:T(8,128)(2,1)S(1)}, u32[]{:S(2)}, u32[]{:S(2)}) collective-permute-start(bf16[128,256]{1,0:T(8,128)(2,1)S(1)} %shard_map.122.after.refs_0_), channel_id=1, source_target_pairs={{0,8},{4,12},{8,0},{12,4},{1,9},{5,13},{9,1},{13,5},{2,10},{6,14},... | collective-permute-start | bytes 196616 | tf_op jit(solution)/shard_map/ppermute | solution.py:280
  12.2 0.0 collective-permute-done.4.far_ref
  12.2 1.6 %collective-permute-start.6 = (bf16[2,176,128]{2,1,0:T(8,128)(2,1)S(1)}, bf16[2,176,128]{2,1,0:T(8,128)(2,1)S(1)}, u32[]{:S(2)}, u32[]{:S(2)}) collective-permute-start(bf16[2,176,128]{2,1,0:T(8,128)(2,1)S(1)} %shard_map.123.refs_0_), channel_id=1, source_target_pairs={{0,4},{4,0},{8,12},{12,8},{1,5},{5,1},{9,13},{13,9},{2,6},{6,2},{1... | collective-permute-start | bytes 270344 | tf_op jit(solution)/shard_map/ppermute | solution.py:280
  13.8 0.4 %collective-permute-start.7 = (bf16[128,256]{1,0:T(8,128)(2,1)S(1)}, bf16[128,256]{1,0:T(8,128)(2,1)S(1)}, u32[]{:S(2)}, u32[]{:S(2)}) collective-permute-start(bf16[128,256]{1,0:T(8,128)(2,1)S(1)} %shard_map.122.after.refs_0_), channel_id=1, source_target_pairs={{0,4},{4,0},{8,12},{12,8},{1,5},{5,1},{9,13},{13,9},{2,6},{6,2},{1... | collective-permute-start | bytes 196616 | tf_op jit(solution)/shard_map/ppermute | solution.py:280
  14.3 2.5 %collective-permute-done.3.refs_2_ = bf16[128,256]{1,0:T(8,128)(2,1)S(1)} collective-permute-done((bf16[128,256]{1,0:T(8,128)(2,1)S(1)}, bf16[128,256]{1,0:T(8,128)(2,1)S(1)}, u32[]{:S(2)}, u32[]{:S(2)}) %collective-permute-start.3) | collective-permute-done | bytes 65568 | tf_op jit(solution)/shard_map/ppermute | solution.py:280
  16.8 0.6 %collective-permute-start.5 = (bf16[128,256]{1,0:T(8,128)(2,1)S(1)}, bf16[128,256]{1,0:T(8,128)(2,1)S(1)}, u32[]{:S(2)}, u32[]{:S(2)}) collective-permute-start(bf16[128,256]{1,0:T(8,128)(2,1)S(1)} %collective-permute-done.3.refs_2_), channel_id=1, source_target_pairs={{0,4},{4,0},{8,12},{12,8},{1,5},{5,1},{9,13},{13,9},{2,6},{6,2},{1... | collective-permute-start | bytes 196616 | tf_op jit(solution)/shard_map/ppermute | solution.py:280
  17.4 0.8 %collective-permute-done.6.refs_1_ = bf16[2,176,128]{2,1,0:T(8,128)(2,1)S(1)} collective-permute-done((bf16[2,176,128]{2,1,0:T(8,128)(2,1)S(1)}, bf16[2,176,128]{2,1,0:T(8,128)(2,1)S(1)}, u32[]{:S(2)}, u32[]{:S(2)}) %collective-permute-start.6) | collective-permute-done | bytes 90144 | tf_op jit(solution)/shard_map/ppermute | solution.py:280
  18.1 0.0 copy-done.8
  18.1 0.5 %shard_map.124 = (bf16[320,256]{1,0:T(8,128)(2,1)S(1)}, f32[320,192]{1,0:T(8,128)S(1)}, f32[320,64]{1,0:T(8,128)S(1)}, f32[320,128]{1,0:T(8,128)S(1)}, f32[320,128]{1,0:T(8,128)S(1)}) custom-call(bf16[2,176,128]{2,1,0:T(8,128)(2,1)S(1)} %shard_map.123.refs_0_, bf16[2,176,128]{2,1,0:T(8,128)(2,1)S(1)} %collective-permute-done.6.refs_1_, s32[1,256]{1,0:T(1,128)S(1)} %bitcast.1), custom_call_target="tpu_custom_call" | custom-call | flops 1024 | tf_op jit(solution)/shard_map/pallas_call | solution.py:361
  18.6 0.8 %collective-permute-done.7.refs_1_ = bf16[128,256]{1,0:T(8,128)(2,1)S(1)} collective-permute-done((bf16[128,256]{1,0:T(8,128)(2,1)S(1)}, bf16[128,256]{1,0:T(8,128)(2,1)S(1)}, u32[]{:S(2)}, u32[]{:S(2)}) %collective-permute-start.7) | collective-permute-done | bytes 65568 | tf_op jit(solution)/shard_map/ppermute | solution.py:280
  19.4 0.7 %shard_map.125 = (f32[320,128]{1,0:T(8,128)S(1)}, f32[320,128]{1,0:T(8,128)S(1)}) custom-call(bf16[128,256]{1,0:T(8,128)(2,1)S(1)} %shard_map.122.after.refs_0_, bf16[128,256]{1,0:T(8,128)(2,1)S(1)} %collective-permute-done.7.refs_1_, bf16[128,256]{1,0:T(8,128)(2,1)S(1)} %collective-permute-done.3.refs_2_, ...), custom_call_target="tpu_custom_call" | custom-call | flops 62914560 | bytes 163840 | tf_op jit(solution)/shard_map/pallas_call | solution.py:380
  20.2 0.9 %collective-permute-done.5.refs_0_ = bf16[128,256]{1,0:T(8,128)(2,1)S(1)} collective-permute-done((bf16[128,256]{1,0:T(8,128)(2,1)S(1)}, bf16[128,256]{1,0:T(8,128)(2,1)S(1)}, u32[]{:S(2)}, u32[]{:S(2)}) %collective-permute-start.5) | collective-permute-done | bytes 65568 | tf_op jit(solution)/shard_map/ppermute | solution.py:280
  21.1 0.0 copy-done.1
  21.1 1.8 %shard_map.126 = (f32[8,1280]{1,0:T(8,128)S(1)}, bf16[8,1280]{1,0:T(8,128)(2,1)S(1)}, bf16[8,1280]{1,0:T(8,128)(2,1)S(1)}, bf16[8,1280]{1,0:T(8,128)(2,1)S(1)}) custom-call(bf16[128,256]{1,0:T(8,128)(2,1)S(1)} %collective-permute-done.5.refs_0_, bf16[320,256]{1,0:T(8,128)(2,1)S(1)} %get-tuple-element.34.refs_3_.refs_1_, ...), custom_call_target="tpu_custom_call" | custom-call | flops 104857600 | bytes 3276800 | tf_op jit(solution)/shard_map/pallas_call | solution.py:388
  22.8 0.7 %collective-permute-start.8 = (bf16[8,1280]{1,0:T(8,128)(2,1)S(1)}, bf16[8,1280]{1,0:T(8,128)(2,1)S(1)}, u32[]{:S(2)}, u32[]{:S(2)}) collective-permute-start(bf16[8,1280]{1,0:T(8,128)(2,1)S(1)} %get-tuple-element.42), channel_id=1, source_target_pairs={{0,2},{1,3},{2,0},{3,1},{4,6},{5,7},{6,4},{7,5},{8,10},{9,11},{10,... | collective-permute-start | bytes 61448 | tf_op jit(solution)/shard_map/ppermute | solution.py:280
  23.5 0.0 collective-permute-start.9
  23.5 1.6 %collective-permute-start.10 = (bf16[8,1280]{1,0:T(8,128)(2,1)S(1)}, bf16[8,1280]{1,0:T(8,128)(2,1)S(1)}, u32[]{:S(2)}, u32[]{:S(2)}) collective-permute-start(bf16[8,1280]{1,0:T(8,128)(2,1)S(1)} %get-tuple-element.44), channel_id=1, source_target_pairs={{0,1},{1,0},{2,3},{3,2},{4,5},{5,4},{6,7},{7,6},{8,9},{9,8},{10,11... | collective-permute-start | bytes 61448 | tf_op jit(solution)/shard_map/ppermute | solution.py:280
  25.1 1.8 %collective-permute-done.8 = bf16[8,1280]{1,0:T(8,128)(2,1)S(1)} collective-permute-done((bf16[8,1280]{1,0:T(8,128)(2,1)S(1)}, bf16[8,1280]{1,0:T(8,128)(2,1)S(1)}, u32[]{:S(2)}, u32[]{:S(2)}) %collective-permute-start.8) | collective-permute-done | bytes 20512 | tf_op jit(solution)/shard_map/ppermute | solution.py:280
  26.9 0.0 collective-permute-done.9
  26.9 0.0 collective-permute-done.10
  26.9 0.6 %add_convert_fusion = bf16[8,1280]{1,0:T(8,128)(2,1)} fusion(bf16[8,1280]{1,0:T(8,128)(2,1)S(1)} %collective-permute-done.10, bf16[8,1280]{1,0:T(8,128)(2,1)S(1)} %collective-permute-done.9, f32[8,1280]{1,0:T(8,128)S(1)} %get-tuple-element.41, bf16[8,1280]{1,0:T(8,128)(2,1)S(1)} %collective-permute-done.8), kind=kLoop, calls=%fused_computation | loop fusion | flops 71680 | bytes 122880 | tf_op jit(solution)/shard_map/convert_element_type | solution.py:402
  (6 shorter events, 0.0 us)
Async XLA Ops:
  0.0 5.2 %copy-start.10 = (bf16[64,1280]{1,0:T(8,128)(2,1)S(1)}, bf16[64,1280]{1,0:T(8,128)(2,1)}, u32[]{:S(2)}) copy-start(bf16[64,1280]{1,0:T(8,128)(2,1)} %refs_0_) | copy-start | bytes 491524
  0.0 3.7 %copy-start.9 = (s32[4]{0:T(128)S(1)}, s32[4]{0:T(128)}, u32[]{:S(2)}) copy-start(s32[4]{0:T(128)} %lens_ref.1) | copy-start | bytes 52
  0.0 3.7 %copy-start.3 = (bf16[4,512,256]{2,1,0:T(8,128)(2,1)S(1)}, bf16[4,512,256]{2,1,0:T(8,128)(2,1)}, u32[]{:S(2)}) copy-start(bf16[4,512,256]{2,1,0:T(8,128)(2,1)} %cv_ref.1) | copy-start | bytes 3145732
  0.0 3.7 %copy-start.2 = (bf16[4,512,256]{2,1,0:T(8,128)(2,1)S(1)}, bf16[4,512,256]{2,1,0:T(8,128)(2,1)}, u32[]{:S(2)}) copy-start(bf16[4,512,256]{2,1,0:T(8,128)(2,1)} %ck_ref.1) | copy-start | bytes 3145732
  0.0 3.8 %copy-start.6 = (bf16[8,256]{1,0:T(8,128)(2,1)S(1)}, bf16[8,256]{1,0:T(8,128)(2,1)}, u32[]{:S(2)}) copy-start(bf16[8,256]{1,0:T(8,128)(2,1)} %nv_ref.1) | copy-start | bytes 12292
  0.0 3.8 %copy-start.5 = (bf16[8,256]{1,0:T(8,128)(2,1)S(1)}, bf16[8,256]{1,0:T(8,128)(2,1)}, u32[]{:S(2)}) copy-start(bf16[8,256]{1,0:T(8,128)(2,1)} %nk_ref.1) | copy-start | bytes 12292
  0.0 3.8 %copy-start.4 = (bf16[8,1280]{1,0:T(8,128)(2,1)S(1)}, bf16[8,1280]{1,0:T(8,128)(2,1)}, u32[]{:S(2)}) copy-start(bf16[8,1280]{1,0:T(8,128)(2,1)} %q_ref.1) | copy-start | bytes 61444
  0.0 8.5 %copy-start = (bf16[2,5120,256]{2,1,0:T(8,128)(2,1)S(1)}, bf16[2,5120,256]{2,1,0:T(8,128)(2,1)}, u32[]{:S(2)}) copy-start(bf16[2,5120,256]{2,1,0:T(8,128)(2,1)} %refs_1_.1) | copy-start | bytes 15728644
  0.0 8.3 %collective-permute-start = (bf16[64,1280]{1,0:T(8,128)(2,1)}, bf16[64,1280]{1,0:T(8,128)(2,1)S(1)}, u32[]{:S(2)}, u32[]{:S(2)}) collective-permute-start(bf16[64,1280]{1,0:T(8,128)(2,1)} %refs_0_), channel_id=1, source_target_pairs={{0,2},{1,3},{2,0},{3,1},{4,6},{5,7},{6,4},{7,5},{8,10},{9,11},{10,... | collective-permute-start | bytes 491528 | tf_op jit(solution)/shard_map/ppermute | solution.py:280
  5.2 4.6 %copy-start.7 = (bf16[2,256]{1,0:T(2,128)(2,1)S(1)}, bf16[2,256]{1,0:T(2,128)(2,1)}, u32[]{:S(2)}) copy-start(bf16[2,256]{1,0:T(2,128)(2,1)} %refs_4_.1) | copy-start | bytes 3076
  5.2 3.4 %collective-permute-start.2 = (bf16[64,1280]{1,0:T(8,128)(2,1)S(1)}, bf16[64,1280]{1,0:T(8,128)(2,1)S(1)}, u32[]{:S(2)}, u32[]{:S(2)}) collective-permute-start(bf16[64,1280]{1,0:T(8,128)(2,1)S(1)} %copy-done.10), channel_id=1, source_target_pairs={{0,1},{1,0},{2,3},{3,2},{4,5},{5,4},{6,7},{7,6},{8,9},{9,8},{10,11... | collective-permute-start | bytes 491528 | tf_op jit(solution)/shard_map/ppermute | solution.py:280
  5.3 6.9 %collective-permute-start.4 = (bf16[176,128]{1,0:T(8,128)(2,1)S(1)}, bf16[176,128]{1,0:T(8,128)(2,1)S(1)}, u32[]{:S(2)}, u32[]{:S(2)}) collective-permute-start(bf16[176,128]{1,0:T(8,128)(2,1)S(1)} %shard_map.120.near_ref), channel_id=1, source_target_pairs={{0,8},{4,12},{8,0},{12,4},{1,9},{5,13},{9,1},{13,5},{2,10},{6,14},... | collective-permute-start | bytes 135176 | tf_op jit(solution)/shard_map/ppermute | solution.py:280
  8.4 1.4 %collective-permute-start.1 = (bf16[64,1280]{1,0:T(8,128)(2,1)S(1)}, bf16[64,1280]{1,0:T(8,128)(2,1)S(1)}, u32[]{:S(2)}, u32[]{:S(2)}) collective-permute-start(bf16[64,1280]{1,0:T(8,128)(2,1)S(1)} %collective-permute-done.refs_2_), channel_id=1, source_target_pairs={{0,1},{1,0},{2,3},{3,2},{4,5},{5,4},{6,7},{7,6},{8,9},{9,8},{10,11... | collective-permute-start | bytes 491528 | tf_op jit(solution)/shard_map/ppermute | solution.py:280
  10.2 8.0 %copy-start.8 = (s32[256]{0:T(256)S(1)}, s32[256]{0:T(256)}, u32[]{:S(2)}) copy-start(s32[256]{0:T(256)} %param.15) | copy-start | bytes 3076
  10.2 10.9 %copy-start.1 = (bf16[1280,1280]{1,0:T(8,128)(2,1)S(1)}, bf16[1280,1280]{1,0:T(8,128)(2,1)}, u32[]{:S(2)}) copy-start(bf16[1280,1280]{1,0:T(8,128)(2,1)} %refs_5_.1) | copy-start | bytes 9830404
  10.2 6.6 %collective-permute-start.3 = (bf16[128,256]{1,0:T(8,128)(2,1)S(1)}, bf16[128,256]{1,0:T(8,128)(2,1)S(1)}, u32[]{:S(2)}, u32[]{:S(2)}) collective-permute-start(bf16[128,256]{1,0:T(8,128)(2,1)S(1)} %shard_map.122.after.refs_0_), channel_id=1, source_target_pairs={{0,8},{4,12},{8,0},{12,4},{1,9},{5,13},{9,1},{13,5},{2,10},{6,14},... | collective-permute-start | bytes 196616 | tf_op jit(solution)/shard_map/ppermute | solution.py:280
  12.2 6.0 %collective-permute-start.6 = (bf16[2,176,128]{2,1,0:T(8,128)(2,1)S(1)}, bf16[2,176,128]{2,1,0:T(8,128)(2,1)S(1)}, u32[]{:S(2)}, u32[]{:S(2)}) collective-permute-start(bf16[2,176,128]{2,1,0:T(8,128)(2,1)S(1)} %shard_map.123.refs_0_), channel_id=1, source_target_pairs={{0,4},{4,0},{8,12},{12,8},{1,5},{5,1},{9,13},{13,9},{2,6},{6,2},{1... | collective-permute-start | bytes 270344 | tf_op jit(solution)/shard_map/ppermute | solution.py:280
  13.8 5.6 %collective-permute-start.7 = (bf16[128,256]{1,0:T(8,128)(2,1)S(1)}, bf16[128,256]{1,0:T(8,128)(2,1)S(1)}, u32[]{:S(2)}, u32[]{:S(2)}) collective-permute-start(bf16[128,256]{1,0:T(8,128)(2,1)S(1)} %shard_map.122.after.refs_0_), channel_id=1, source_target_pairs={{0,4},{4,0},{8,12},{12,8},{1,5},{5,1},{9,13},{13,9},{2,6},{6,2},{1... | collective-permute-start | bytes 196616 | tf_op jit(solution)/shard_map/ppermute | solution.py:280
  16.8 4.3 %collective-permute-start.5 = (bf16[128,256]{1,0:T(8,128)(2,1)S(1)}, bf16[128,256]{1,0:T(8,128)(2,1)S(1)}, u32[]{:S(2)}, u32[]{:S(2)}) collective-permute-start(bf16[128,256]{1,0:T(8,128)(2,1)S(1)} %collective-permute-done.3.refs_2_), channel_id=1, source_target_pairs={{0,4},{4,0},{8,12},{12,8},{1,5},{5,1},{9,13},{13,9},{2,6},{6,2},{1... | collective-permute-start | bytes 196616 | tf_op jit(solution)/shard_map/ppermute | solution.py:280
  22.8 4.1 %collective-permute-start.8 = (bf16[8,1280]{1,0:T(8,128)(2,1)S(1)}, bf16[8,1280]{1,0:T(8,128)(2,1)S(1)}, u32[]{:S(2)}, u32[]{:S(2)}) collective-permute-start(bf16[8,1280]{1,0:T(8,128)(2,1)S(1)} %get-tuple-element.42), channel_id=1, source_target_pairs={{0,2},{1,3},{2,0},{3,1},{4,6},{5,7},{6,4},{7,5},{8,10},{9,11},{10,... | collective-permute-start | bytes 61448 | tf_op jit(solution)/shard_map/ppermute | solution.py:280
  23.5 3.4 %collective-permute-start.9 = (bf16[8,1280]{1,0:T(8,128)(2,1)S(1)}, bf16[8,1280]{1,0:T(8,128)(2,1)S(1)}, u32[]{:S(2)}, u32[]{:S(2)}) collective-permute-start(bf16[8,1280]{1,0:T(8,128)(2,1)S(1)} %get-tuple-element.43), channel_id=1, source_target_pairs={{0,3},{1,2},{2,1},{3,0},{4,7},{5,6},{6,5},{7,4},{8,11},{9,10},{10,... | collective-permute-start | bytes 61448 | tf_op jit(solution)/shard_map/ppermute | solution.py:280
  23.5 3.4 %collective-permute-start.10 = (bf16[8,1280]{1,0:T(8,128)(2,1)S(1)}, bf16[8,1280]{1,0:T(8,128)(2,1)S(1)}, u32[]{:S(2)}, u32[]{:S(2)}) collective-permute-start(bf16[8,1280]{1,0:T(8,128)(2,1)S(1)} %get-tuple-element.44), channel_id=1, source_target_pairs={{0,1},{1,0},{2,3},{3,2},{4,5},{5,4},{6,7},{7,6},{8,9},{9,8},{10,11... | collective-permute-start | bytes 61448 | tf_op jit(solution)/shard_map/ppermute | solution.py:280

commit v13 on v9

--- a/solution.py
+++ b/solution.py
@@ -162,10 +162,12 @@
     seg = (parts[0].shape[0] - STATS) // 2
     rows = q_ref.shape[0] // groups
     per = rows // heads
-    blocks = [part[0:rows, :].astype(f32) for part in parts]
-    q_ref[...] = jnp.concatenate(
-        [spread([b[j * per : (j + 1) * per, :] for j in range(heads)]) for b in blocks], axis=0
-    ).astype(bf16)
+
+    def by_head(first):
+        blocks = [part[first : first + rows, :].astype(f32) for part in parts]
+        return jnp.concatenate([b[j * per : (j + 1) * per, :] for j in range(heads) for b in blocks], axis=0)
+
+    q_ref[...] = by_head(0).astype(bf16)
     stats = nt(
         eye(rows, HD), jnp.concatenate([part[2 * seg : 2 * seg + STATS, :] for part in parts], axis=0)
     )
@@ -175,12 +177,12 @@
         for k in range(groups):
             c = k * STATS + at
             columns.append(sum([stats[:, c + i : c + i + 1] for i in range(pieces)]))
-        return jnp.concatenate(columns, axis=0)
+        return jnp.concatenate([c[j * per : (j + 1) * per] for j in range(heads) for c in columns], axis=0)
 
     top, total = column(TOP, 3), column(TOTAL, 2)
-    bias_ref[...] = jnp.where(column(SECTION, 1) == section_ref[...].astype(f32), 0.0, masked_score)
-    old = jnp.concatenate([part[seg : seg + rows, :] for part in parts], axis=0).astype(f32)
-    old_ref[...] = old * total
+    own_section = column(SECTION, 1)[0 : groups * per]
+    bias_ref[...] = jnp.where(own_section == section_ref[...].astype(f32), 0.0, masked_score)
+    old_ref[...] = by_head(seg) * total
     lane = lax.broadcasted_iota(jnp.int32, stats_ref.shape, 1)
     stats_ref[...] = jnp.where(lane == 0, top, total)
 
@@ -194,28 +196,32 @@
     heads = kvs[0].shape[1] // HD
     tokens = attended_ref.shape[0] // groups
     per = PER_HEAD * tokens
-    rows = heads * per
     for bits, kv in enumerate(kvs):
         first = pl.multiple_of((me_dp ^ bits) * memory, memory)
         k_ref[pl.ds(first, memory), :] = kv[0:memory, :].astype(k_ref.dtype)
         v_ref[pl.ds(first, memory), :] = kv[memory : 2 * memory, :].astype(v_ref.dtype)
-    s = nt(q_ref[...], k_ref[...].astype(bf16)) * INV + bias_ref[...]
-    old_top, old_total = stats_ref[:, 0:1], stats_ref[:, 1:2]
-    top = jnp.maximum(jnp.max(s, axis=1, keepdims=True), old_top)
-    p = jnp.exp(s - top)
-    shrink = jnp.exp(old_top - top)
-    total = jnp.sum(p, axis=1, keepdims=True) + shrink * old_total
-    acc = nn(p.astype(bf16), v_ref[...].astype(bf16))
-    for k in range(groups):
-        at = pl.multiple_of((me_dp ^ k) * tokens, tokens)
-        for j in range(heads):
-            a = k * rows + j * per
-            block = acc[a : a + per, j * HD : (j + 1) * HD] + old_ref[a : a + per, :] * shrink[a : a + per]
-            block = block / total[a : a + per]
+    some = groups * per
+    sums = None
+    for j in range(heads):
+        at_rows, lanes = slice(j * some, (j + 1) * some), slice(j * HD, (j + 1) * HD)
+        s = nt(q_ref[at_rows, :], k_ref[:, lanes].astype(bf16)) * INV + bias_ref[...]
+        old_top, old_total = stats_ref[at_rows, 0:1], stats_ref[at_rows, 1:2]
+        top = jnp.maximum(jnp.max(s, axis=1, keepdims=True), old_top)
+        p = jnp.exp(s - top)
+        shrink = jnp.exp(old_top - top)
+        total = jnp.sum(p, axis=1, keepdims=True) + shrink * old_total
+        acc = nn(p.astype(bf16), v_ref[:, lanes].astype(bf16))
+        acc = (acc + old_ref[at_rows, :] * shrink) / total
+        for k in range(groups):
+            at = pl.multiple_of((me_dp ^ k) * tokens, tokens)
             for g in range(PER_HEAD):
                 c = (j * PER_HEAD + g) * HD
-                attended_ref[pl.ds(at, tokens), c : c + HD] = block[g * tokens : (g + 1) * tokens, :]
-    sums_ref[...] = nn(attended_ref[...].astype(bf16), w_ref[...])
+                row = k * per + g * tokens
+                attended_ref[pl.ds(at, tokens), c : c + HD] = acc[row : row + tokens, :]
+        width = slice(j * PER_HEAD * HD, (j + 1) * PER_HEAD * HD)
+        term = nn(attended_ref[:, width].astype(bf16), w_ref[width, :])
+        sums = term if sums is None else sums + term
+    sums_ref[...] = sums
     share = sums_ref.shape[0] // shares
     for k, out in enumerate(outs):
         at = pl.multiple_of((me_tp ^ k) * share, share)
@@ -327,12 +333,13 @@
     half = range(1, groups // 2)
     pairs = [pair, *[permute(pair, "dp", bits) for bits in half]]
     kvs = [kv, *[permute(kv, "dp", bits) for bits in half], kv_far, *[permute(kv_on, "dp", bits) for bits in half]]
+    heads = cols // HD
     prepared = call(
-        functools.partial(prepare_kernel, cols // HD),
+        functools.partial(prepare_kernel, heads),
         [VMEM] * (groups // 2 + 1),
         [
-            pltpu.VMEM((groups * rows, cols), bf16),
-            pltpu.VMEM((groups * rows, every), f32),
+            pltpu.VMEM((groups * rows, HD), bf16),
+            pltpu.VMEM((groups * rows // heads, every), f32),
             pltpu.VMEM((groups * rows, HD), f32),
             pltpu.VMEM((groups * rows, HD), f32),
         ],

time: 27.2 us -> 27.1 us (level)
  no operation moved by 1% of the time
where the time goes in v13:
time: 27.1 us; the launch traced here: 26.9 us
  starting transfers between devices  12.9 us (48%)
  waiting for transfers between devices  8.18 us (30%)
  Pallas kernels  4.31 us (16%)
  between operations  0.82 us (3%)
  other arithmetic  0.62 us (2%)
    ppermute x11, starting transfers between devices, permute(): lax.ppermute(x, axis, [(i, i ^ bits) for i in range(lax.axis_size(axis))])  12.9 us
    ppermute x11, waiting for transfers between devices, permute(): lax.ppermute(x, axis, [(i, i ^ bits) for i in range(lax.axis_size(axis))])  8.18 us
    pallas_call x1, Pallas kernels, body(): call(cache_kernel, [SMEM] + [VMEM] * 6, pltpu.VMEM((2 * up(rows, 16) + ST...  1.38 us
    pallas_call x1, Pallas kernels, body(): call(functools.partial(attend_kernel, groups, shares), [VMEM] * (groups +...  1.26 us
    pallas_call x1, Pallas kernels, body(): call(functools.partial(project_kernel, near, True, False), [VMEM] * (len(...  0.82 us
    convert_element_type x1, other arithmetic, body(): return summed.astype(bf16)  0.62 us
  transfers between devices with their start and end apart: 11, of which 7 were waited for; matrix products, arithmetic and copies ran while one was open for 0% of the time, Pallas kernels for 11%

profile of v13, /device:TPU:0, one launch (start us, length us, event | category | flops | bytes accessed | tf_op | source)
XLA Modules:
  0.0 26.9 jit_solution(13046907303099471020)
XLA Ops:
  0.0 0.0 copy-start.10
  0.0 0.0 copy-start.4
  0.0 0.0 copy-start.5
  0.0 0.0 copy-start.6
  0.0 0.0 copy-start.3
  0.0 0.0 copy-start.9
  0.0 0.0 copy-start
  0.0 3.0 %collective-permute-start = (bf16[64,1280]{1,0:T(8,128)(2,1)}, bf16[64,1280]{1,0:T(8,128)(2,1)S(1)}, u32[]{:S(2)}, u32[]{:S(2)}) collective-permute-start(bf16[64,1280]{1,0:T(8,128)(2,1)} %refs_0_), channel_id=1, source_target_pairs={{0,2},{1,3},{2,0},{3,1},{4,6},{5,7},{6,4},{7,5},{8,10},{9,11},{10,... | collective-permute-start | bytes 491528 | tf_op jit(solution)/shard_map/ppermute | solution.py:255
  3.7 0.0 copy-done.4
  3.7 0.0 copy-done.5
  3.7 0.0 copy-done.6
  3.8 0.0 copy-done.2
  3.8 0.0 copy-done.3
  3.8 0.0 copy-done.9
  3.8 1.4 %shard_map.120.near_ref = bf16[176,128]{1,0:T(8,128)(2,1)S(1)} custom-call(s32[4]{0:T(128)S(1)} %copy-done.9, f32[8,128]{1,0:T(8,128)S(1)} %shard_map.119.section_ref, bf16[8,1280]{1,0:T(8,128)(2,1)S(1)} %copy-done.4, bf16[8,256]{1,0:T(8,128)(2,1)S(1)} %copy-done.5, bf16[8,256]{1,0:T(8,128)(2,1)S(1)} %copy-done.6, bf16[4,512,256]{2,1,0:T(8,128)(2,1)S(1)} %copy-done.2, ...), custom_call_target="tpu_custom_call" | custom-call | flops 167772160 | bytes 2097152 | tf_op jit(solution)/shard_map/pallas_call | solution.py:295
  5.2 0.0 copy-done.10
  5.2 0.0 copy-start.7
  5.2 0.1 collective-permute-start.2
  5.3 3.1 %collective-permute-start.5 = (bf16[176,128]{1,0:T(8,128)(2,1)S(1)}, bf16[176,128]{1,0:T(8,128)(2,1)S(1)}, u32[]{:S(2)}, u32[]{:S(2)}) collective-permute-start(bf16[176,128]{1,0:T(8,128)(2,1)S(1)} %shard_map.120.near_ref), channel_id=1, source_target_pairs={{0,8},{4,12},{8,0},{12,4},{1,9},{5,13},{9,1},{13,5},{2,10},{6,14},... | collective-permute-start | bytes 135176 | tf_op jit(solution)/shard_map/ppermute | solution.py:255
  8.4 0.0 collective-permute-done.refs_2_
  8.4 0.2 collective-permute-start.1
  8.5 0.0 collective-permute-done.2.refs_1_
  8.5 0.0 copy-done
  8.6 0.8 %shard_map.121 = (f32[128,256]{1,0:T(8,128)S(1)}, f32[64,128]{1,0:T(8,128)S(1)}) custom-call(bf16[64,1280]{1,0:T(8,128)(2,1)S(1)} %copy-done.10, bf16[64,1280]{1,0:T(8,128)(2,1)S(1)} %collective-permute-done.2.refs_1_, bf16[64,1280]{1,0:T(8,128)(2,1)S(1)} %collective-permute-done.refs_2_, bf16[2,5120,256]{2,1,0:T(8,128)(2,1)S(1)} %copy-done), custom_call_target="tpu_custom_call" | custom-call | flops 68719476736 | bytes 5242880 | tf_op jit(solution)/shard_map/pallas_call | solution.py:307
  9.4 0.4 %collective-permute-done.1.refs_0_ = bf16[64,1280]{1,0:T(8,128)(2,1)S(1)} collective-permute-done((bf16[64,1280]{1,0:T(8,128)(2,1)S(1)}, bf16[64,1280]{1,0:T(8,128)(2,1)S(1)}, u32[]{:S(2)}, u32[]{:S(2)}) %collective-permute-start.1) | collective-permute-done | bytes 163872 | tf_op jit(solution)/shard_map/ppermute | solution.py:255
  9.8 0.0 copy-done.7
  9.8 0.4 %shard_map.122.after.refs_0_ = bf16[128,256]{1,0:T(8,128)(2,1)S(1)} custom-call(bf16[64,1280]{1,0:T(8,128)(2,1)S(1)} %collective-permute-done.1.refs_0_, bf16[2,5120,256]{2,1,0:T(8,128)(2,1)S(1)} %copy-done, f32[128,256]{1,0:T(8,128)S(1)} %get-tuple-element.27.refs_2_, f32[64,128]{1,0:T(8,128)S(1)} %get-tuple-element.28.refs_3_, bf16[2,256]{1,0:T(2,128)(2,1)S(1)} %copy-done.7), custom_call_target="tpu_custom_call" | custom-call | flops 83886080 | bytes 1310720 | tf_op jit(solution)/shard_map/pallas_call | solution.py:315
  10.2 0.0 copy-start.1
  10.2 2.0 %collective-permute-start.4 = (bf16[128,256]{1,0:T(8,128)(2,1)S(1)}, bf16[128,256]{1,0:T(8,128)(2,1)S(1)}, u32[]{:S(2)}, u32[]{:S(2)}) collective-permute-start(bf16[128,256]{1,0:T(8,128)(2,1)S(1)} %shard_map.122.after.refs_0_), channel_id=1, source_target_pairs={{0,8},{4,12},{8,0},{12,4},{1,9},{5,13},{9,1},{13,5},{2,10},{6,14},... | collective-permute-start | bytes 196616 | tf_op jit(solution)/shard_map/ppermute | solution.py:255
  12.2 0.0 collective-permute-done.5.far_ref
  12.2 1.6 %collective-permute-start.7 = (bf16[2,176,128]{2,1,0:T(8,128)(2,1)S(1)}, bf16[2,176,128]{2,1,0:T(8,128)(2,1)S(1)}, u32[]{:S(2)}, u32[]{:S(2)}) collective-permute-start(bf16[2,176,128]{2,1,0:T(8,128)(2,1)S(1)} %shard_map.123.refs_0_), channel_id=1, source_target_pairs={{0,4},{4,0},{8,12},{12,8},{1,5},{5,1},{9,13},{13,9},{2,6},{6,2},{1... | collective-permute-start | bytes 270344 | tf_op jit(solution)/shard_map/ppermute | solution.py:255
  13.8 0.4 %collective-permute-start.3 = (bf16[128,256]{1,0:T(8,128)(2,1)S(1)}, bf16[128,256]{1,0:T(8,128)(2,1)S(1)}, u32[]{:S(2)}, u32[]{:S(2)}) collective-permute-start(bf16[128,256]{1,0:T(8,128)(2,1)S(1)} %shard_map.122.after.refs_0_), channel_id=1, source_target_pairs={{0,4},{4,0},{8,12},{12,8},{1,5},{5,1},{9,13},{13,9},{2,6},{6,2},{1... | collective-permute-start | bytes 196616 | tf_op jit(solution)/shard_map/ppermute | solution.py:255
  14.3 2.5 %collective-permute-done.4.refs_2_ = bf16[128,256]{1,0:T(8,128)(2,1)S(1)} collective-permute-done((bf16[128,256]{1,0:T(8,128)(2,1)S(1)}, bf16[128,256]{1,0:T(8,128)(2,1)S(1)}, u32[]{:S(2)}, u32[]{:S(2)}) %collective-permute-start.4) | collective-permute-done | bytes 65568 | tf_op jit(solution)/shard_map/ppermute | solution.py:255
  16.8 0.6 %collective-permute-start.6 = (bf16[128,256]{1,0:T(8,128)(2,1)S(1)}, bf16[128,256]{1,0:T(8,128)(2,1)S(1)}, u32[]{:S(2)}, u32[]{:S(2)}) collective-permute-start(bf16[128,256]{1,0:T(8,128)(2,1)S(1)} %collective-permute-done.4.refs_2_), channel_id=1, source_target_pairs={{0,4},{4,0},{8,12},{12,8},{1,5},{5,1},{9,13},{13,9},{2,6},{6,2},{1... | collective-permute-start | bytes 196616 | tf_op jit(solution)/shard_map/ppermute | solution.py:255
  17.4 0.8 %collective-permute-done.7.refs_1_ = bf16[2,176,128]{2,1,0:T(8,128)(2,1)S(1)} collective-permute-done((bf16[2,176,128]{2,1,0:T(8,128)(2,1)S(1)}, bf16[2,176,128]{2,1,0:T(8,128)(2,1)S(1)}, u32[]{:S(2)}, u32[]{:S(2)}) %collective-permute-start.7) | collective-permute-done | bytes 90144 | tf_op jit(solution)/shard_map/ppermute | solution.py:255
  18.1 0.0 copy-done.8
  18.1 0.5 %shard_map.124 = (bf16[320,128]{1,0:T(8,128)(2,1)S(1)}, f32[160,256]{1,0:T(8,128)S(1)}, f32[320,128]{1,0:T(8,128)S(1)}, f32[320,128]{1,0:T(8,128)S(1)}) custom-call(bf16[2,176,128]{2,1,0:T(8,128)(2,1)S(1)} %shard_map.123.refs_0_, bf16[2,176,128]{2,1,0:T(8,128)(2,1)S(1)} %collective-permute-done.7.refs_1_, s32[1,256]{1,0:T(1,128)S(1)} %bitcast.1), custom_call_target="tpu_custom_call" | custom-call | flops 1024 | tf_op jit(solution)/shard_map/pallas_call | solution.py:337
  18.6 0.8 %collective-permute-done.3.refs_1_ = bf16[128,256]{1,0:T(8,128)(2,1)S(1)} collective-permute-done((bf16[128,256]{1,0:T(8,128)(2,1)S(1)}, bf16[128,256]{1,0:T(8,128)(2,1)S(1)}, u32[]{:S(2)}, u32[]{:S(2)}) %collective-permute-start.3) | collective-permute-done | bytes 65568 | tf_op jit(solution)/shard_map/ppermute | solution.py:255
  19.4 1.6 %collective-permute-done.6.refs_3_ = bf16[128,256]{1,0:T(8,128)(2,1)S(1)} collective-permute-done((bf16[128,256]{1,0:T(8,128)(2,1)S(1)}, bf16[128,256]{1,0:T(8,128)(2,1)S(1)}, u32[]{:S(2)}, u32[]{:S(2)}) %collective-permute-start.6) | collective-permute-done | bytes 65568 | tf_op jit(solution)/shard_map/ppermute | solution.py:255
  21.1 0.0 copy-done.1
  21.1 1.3 %shard_map.125 = (f32[8,1280]{1,0:T(8,128)S(1)}, bf16[8,1280]{1,0:T(8,128)(2,1)S(1)}, bf16[8,1280]{1,0:T(8,128)(2,1)S(1)}, bf16[8,1280]{1,0:T(8,128)(2,1)S(1)}) custom-call(bf16[128,256]{1,0:T(8,128)(2,1)S(1)} %shard_map.122.after.refs_0_, bf16[128,256]{1,0:T(8,128)(2,1)S(1)} %collective-permute-done.3.refs_1_, ...), custom_call_target="tpu_custom_call" | custom-call | flops 104857600 | bytes 3276800 | tf_op jit(solution)/shard_map/pallas_call | solution.py:354
  22.3 0.1 collective-permute-start.10
  22.4 0.7 %collective-permute-start.8 = (bf16[8,1280]{1,0:T(8,128)(2,1)S(1)}, bf16[8,1280]{1,0:T(8,128)(2,1)S(1)}, u32[]{:S(2)}, u32[]{:S(2)}) collective-permute-start(bf16[8,1280]{1,0:T(8,128)(2,1)S(1)} %get-tuple-element.36), channel_id=1, source_target_pairs={{0,2},{1,3},{2,0},{3,1},{4,6},{5,7},{6,4},{7,5},{8,10},{9,11},{10,... | collective-permute-start | bytes 61448 | tf_op jit(solution)/shard_map/ppermute | solution.py:255
  23.1 1.2 %collective-permute-start.9 = (bf16[8,1280]{1,0:T(8,128)(2,1)S(1)}, bf16[8,1280]{1,0:T(8,128)(2,1)S(1)}, u32[]{:S(2)}, u32[]{:S(2)}) collective-permute-start(bf16[8,1280]{1,0:T(8,128)(2,1)S(1)} %get-tuple-element.37), channel_id=1, source_target_pairs={{0,1},{1,0},{2,3},{3,2},{4,5},{5,4},{6,7},{7,6},{8,9},{9,8},{10,11... | collective-permute-start | bytes 61448 | tf_op jit(solution)/shard_map/ppermute | solution.py:255
  24.3 1.3 %collective-permute-done.10 = bf16[8,1280]{1,0:T(8,128)(2,1)S(1)} collective-permute-done((bf16[8,1280]{1,0:T(8,128)(2,1)S(1)}, bf16[8,1280]{1,0:T(8,128)(2,1)S(1)}, u32[]{:S(2)}, u32[]{:S(2)}) %collective-permute-start.10) | collective-permute-done | bytes 20512 | tf_op jit(solution)/shard_map/ppermute | solution.py:255
  25.6 0.7 %collective-permute-done.8 = bf16[8,1280]{1,0:T(8,128)(2,1)S(1)} collective-permute-done((bf16[8,1280]{1,0:T(8,128)(2,1)S(1)}, bf16[8,1280]{1,0:T(8,128)(2,1)S(1)}, u32[]{:S(2)}, u32[]{:S(2)}) %collective-permute-start.8) | collective-permute-done | bytes 20512 | tf_op jit(solution)/shard_map/ppermute | solution.py:255
  26.3 0.0 collective-permute-done.9
  26.3 0.6 %add_convert_fusion = bf16[8,1280]{1,0:T(8,128)(2,1)} fusion(bf16[8,1280]{1,0:T(8,128)(2,1)S(1)} %collective-permute-done.10, bf16[8,1280]{1,0:T(8,128)(2,1)S(1)} %collective-permute-done.9, f32[8,1280]{1,0:T(8,128)S(1)} %get-tuple-element.35, bf16[8,1280]{1,0:T(8,128)(2,1)S(1)} %collective-permute-done.8), kind=kLoop, calls=%fused_computation | loop fusion | flops 71680 | bytes 122880 | tf_op jit(solution)/shard_map/convert_element_type | solution.py:370
  (5 shorter events, 0.0 us)
Async XLA Ops:
  0.0 5.2 %copy-start.10 = (bf16[64,1280]{1,0:T(8,128)(2,1)S(1)}, bf16[64,1280]{1,0:T(8,128)(2,1)}, u32[]{:S(2)}) copy-start(bf16[64,1280]{1,0:T(8,128)(2,1)} %refs_0_) | copy-start | bytes 491524
  0.0 3.7 %copy-start.4 = (bf16[8,1280]{1,0:T(8,128)(2,1)S(1)}, bf16[8,1280]{1,0:T(8,128)(2,1)}, u32[]{:S(2)}) copy-start(bf16[8,1280]{1,0:T(8,128)(2,1)} %q_ref.1) | copy-start | bytes 61444
  0.0 3.7 %copy-start.5 = (bf16[8,256]{1,0:T(8,128)(2,1)S(1)}, bf16[8,256]{1,0:T(8,128)(2,1)}, u32[]{:S(2)}) copy-start(bf16[8,256]{1,0:T(8,128)(2,1)} %nk_ref.1) | copy-start | bytes 12292
  0.0 3.7 %copy-start.6 = (bf16[8,256]{1,0:T(8,128)(2,1)S(1)}, bf16[8,256]{1,0:T(8,128)(2,1)}, u32[]{:S(2)}) copy-start(bf16[8,256]{1,0:T(8,128)(2,1)} %nv_ref.1) | copy-start | bytes 12292
  0.0 3.8 %copy-start.2 = (bf16[4,512,256]{2,1,0:T(8,128)(2,1)S(1)}, bf16[4,512,256]{2,1,0:T(8,128)(2,1)}, u32[]{:S(2)}) copy-start(bf16[4,512,256]{2,1,0:T(8,128)(2,1)} %ck_ref.1) | copy-start | bytes 3145732
  0.0 3.8 %copy-start.3 = (bf16[4,512,256]{2,1,0:T(8,128)(2,1)S(1)}, bf16[4,512,256]{2,1,0:T(8,128)(2,1)}, u32[]{:S(2)}) copy-start(bf16[4,512,256]{2,1,0:T(8,128)(2,1)} %cv_ref.1) | copy-start | bytes 3145732
  0.0 3.8 %copy-start.9 = (s32[4]{0:T(128)S(1)}, s32[4]{0:T(128)}, u32[]{:S(2)}) copy-start(s32[4]{0:T(128)} %lens_ref.1) | copy-start | bytes 52
  0.0 8.5 %copy-start = (bf16[2,5120,256]{2,1,0:T(8,128)(2,1)S(1)}, bf16[2,5120,256]{2,1,0:T(8,128)(2,1)}, u32[]{:S(2)}) copy-start(bf16[2,5120,256]{2,1,0:T(8,128)(2,1)} %refs_1_.1) | copy-start | bytes 15728644
  0.0 8.3 %collective-permute-start = (bf16[64,1280]{1,0:T(8,128)(2,1)}, bf16[64,1280]{1,0:T(8,128)(2,1)S(1)}, u32[]{:S(2)}, u32[]{:S(2)}) collective-permute-start(bf16[64,1280]{1,0:T(8,128)(2,1)} %refs_0_), channel_id=1, source_target_pairs={{0,2},{1,3},{2,0},{3,1},{4,6},{5,7},{6,4},{7,5},{8,10},{9,11},{10,... | collective-permute-start | bytes 491528 | tf_op jit(solution)/shard_map/ppermute | solution.py:255
  5.2 4.6 %copy-start.7 = (bf16[2,256]{1,0:T(2,128)(2,1)S(1)}, bf16[2,256]{1,0:T(2,128)(2,1)}, u32[]{:S(2)}) copy-start(bf16[2,256]{1,0:T(2,128)(2,1)} %refs_4_.1) | copy-start | bytes 3076
  5.2 3.4 %collective-permute-start.2 = (bf16[64,1280]{1,0:T(8,128)(2,1)S(1)}, bf16[64,1280]{1,0:T(8,128)(2,1)S(1)}, u32[]{:S(2)}, u32[]{:S(2)}) collective-permute-start(bf16[64,1280]{1,0:T(8,128)(2,1)S(1)} %copy-done.10), channel_id=1, source_target_pairs={{0,1},{1,0},{2,3},{3,2},{4,5},{5,4},{6,7},{7,6},{8,9},{9,8},{10,11... | collective-permute-start | bytes 491528 | tf_op jit(solution)/shard_map/ppermute | solution.py:255
  5.3 6.9 %collective-permute-start.5 = (bf16[176,128]{1,0:T(8,128)(2,1)S(1)}, bf16[176,128]{1,0:T(8,128)(2,1)S(1)}, u32[]{:S(2)}, u32[]{:S(2)}) collective-permute-start(bf16[176,128]{1,0:T(8,128)(2,1)S(1)} %shard_map.120.near_ref), channel_id=1, source_target_pairs={{0,8},{4,12},{8,0},{12,4},{1,9},{5,13},{9,1},{13,5},{2,10},{6,14},... | collective-permute-start | bytes 135176 | tf_op jit(solution)/shard_map/ppermute | solution.py:255
  8.4 1.4 %collective-permute-start.1 = (bf16[64,1280]{1,0:T(8,128)(2,1)S(1)}, bf16[64,1280]{1,0:T(8,128)(2,1)S(1)}, u32[]{:S(2)}, u32[]{:S(2)}) collective-permute-start(bf16[64,1280]{1,0:T(8,128)(2,1)S(1)} %collective-permute-done.refs_2_), channel_id=1, source_target_pairs={{0,1},{1,0},{2,3},{3,2},{4,5},{5,4},{6,7},{7,6},{8,9},{9,8},{10,11... | collective-permute-start | bytes 491528 | tf_op jit(solution)/shard_map/ppermute | solution.py:255
  10.2 8.0 %copy-start.8 = (s32[256]{0:T(256)S(1)}, s32[256]{0:T(256)}, u32[]{:S(2)}) copy-start(s32[256]{0:T(256)} %param.15) | copy-start | bytes 3076
  10.2 10.9 %copy-start.1 = (bf16[1280,1280]{1,0:T(8,128)(2,1)S(1)}, bf16[1280,1280]{1,0:T(8,128)(2,1)}, u32[]{:S(2)}) copy-start(bf16[1280,1280]{1,0:T(8,128)(2,1)} %refs_8_.1) | copy-start | bytes 9830404
  10.2 6.6 %collective-permute-start.4 = (bf16[128,256]{1,0:T(8,128)(2,1)S(1)}, bf16[128,256]{1,0:T(8,128)(2,1)S(1)}, u32[]{:S(2)}, u32[]{:S(2)}) collective-permute-start(bf16[128,256]{1,0:T(8,128)(2,1)S(1)} %shard_map.122.after.refs_0_), channel_id=1, source_target_pairs={{0,8},{4,12},{8,0},{12,4},{1,9},{5,13},{9,1},{13,5},{2,10},{6,14},... | collective-permute-start | bytes 196616 | tf_op jit(solution)/shard_map/ppermute | solution.py:255
  12.2 6.0 %collective-permute-start.7 = (bf16[2,176,128]{2,1,0:T(8,128)(2,1)S(1)}, bf16[2,176,128]{2,1,0:T(8,128)(2,1)S(1)}, u32[]{:S(2)}, u32[]{:S(2)}) collective-permute-start(bf16[2,176,128]{2,1,0:T(8,128)(2,1)S(1)} %shard_map.123.refs_0_), channel_id=1, source_target_pairs={{0,4},{4,0},{8,12},{12,8},{1,5},{5,1},{9,13},{13,9},{2,6},{6,2},{1... | collective-permute-start | bytes 270344 | tf_op jit(solution)/shard_map/ppermute | solution.py:255
  13.8 5.6 %collective-permute-start.3 = (bf16[128,256]{1,0:T(8,128)(2,1)S(1)}, bf16[128,256]{1,0:T(8,128)(2,1)S(1)}, u32[]{:S(2)}, u32[]{:S(2)}) collective-permute-start(bf16[128,256]{1,0:T(8,128)(2,1)S(1)} %shard_map.122.after.refs_0_), channel_id=1, source_target_pairs={{0,4},{4,0},{8,12},{12,8},{1,5},{5,1},{9,13},{13,9},{2,6},{6,2},{1... | collective-permute-start | bytes 196616 | tf_op jit(solution)/shard_map/ppermute | solution.py:255
  16.8 4.3 %collective-permute-start.6 = (bf16[128,256]{1,0:T(8,128)(2,1)S(1)}, bf16[128,256]{1,0:T(8,128)(2,1)S(1)}, u32[]{:S(2)}, u32[]{:S(2)}) collective-permute-start(bf16[128,256]{1,0:T(8,128)(2,1)S(1)} %collective-permute-done.4.refs_2_), channel_id=1, source_target_pairs={{0,4},{4,0},{8,12},{12,8},{1,5},{5,1},{9,13},{13,9},{2,6},{6,2},{1... | collective-permute-start | bytes 196616 | tf_op jit(solution)/shard_map/ppermute | solution.py:255
  22.3 3.3 %collective-permute-start.10 = (bf16[8,1280]{1,0:T(8,128)(2,1)S(1)}, bf16[8,1280]{1,0:T(8,128)(2,1)S(1)}, u32[]{:S(2)}, u32[]{:S(2)}) collective-permute-start(bf16[8,1280]{1,0:T(8,128)(2,1)S(1)} %get-tuple-element.38), channel_id=1, source_target_pairs={{0,3},{1,2},{2,1},{3,0},{4,7},{5,6},{6,5},{7,4},{8,11},{9,10},{10,... | collective-permute-start | bytes 61448 | tf_op jit(solution)/shard_map/ppermute | solution.py:255
  22.4 3.8 %collective-permute-start.8 = (bf16[8,1280]{1,0:T(8,128)(2,1)S(1)}, bf16[8,1280]{1,0:T(8,128)(2,1)S(1)}, u32[]{:S(2)}, u32[]{:S(2)}) collective-permute-start(bf16[8,1280]{1,0:T(8,128)(2,1)S(1)} %get-tuple-element.36), channel_id=1, source_target_pairs={{0,2},{1,3},{2,0},{3,1},{4,6},{5,7},{6,4},{7,5},{8,10},{9,11},{10,... | collective-permute-start | bytes 61448 | tf_op jit(solution)/shard_map/ppermute | solution.py:255
  23.1 3.2 %collective-permute-start.9 = (bf16[8,1280]{1,0:T(8,128)(2,1)S(1)}, bf16[8,1280]{1,0:T(8,128)(2,1)S(1)}, u32[]{:S(2)}, u32[]{:S(2)}) collective-permute-start(bf16[8,1280]{1,0:T(8,128)(2,1)S(1)} %get-tuple-element.37), channel_id=1, source_target_pairs={{0,1},{1,0},{2,3},{3,2},{4,5},{5,4},{6,7},{7,6},{8,9},{9,8},{10,11... | collective-permute-start | bytes 61448 | tf_op jit(solution)/shard_map/ppermute | solution.py:255

commit v14 on v13

--- a/solution.py
+++ b/solution.py
@@ -180,37 +180,52 @@
         return jnp.concatenate([c[j * per : (j + 1) * per] for j in range(heads) for c in columns], axis=0)
 
     top, total = column(TOP, 3), column(TOTAL, 2)
+    every = section_ref.shape[1]
+    memory = every // groups
+    sections = jnp.broadcast_to(section_ref[...].astype(f32), (8, every))
+    me = lax.axis_index("dp")
+    held = []
+    for k in range(groups):
+        back = lax.rem(every - (me ^ k) * memory, every)
+        held.append(pltpu.roll(sections, back, 1)[0:1, 0:memory])
     own_section = column(SECTION, 1)[0 : groups * per]
-    bias_ref[...] = jnp.where(own_section == section_ref[...].astype(f32), 0.0, masked_score)
+    bias_ref[...] = jnp.where(own_section == jnp.concatenate(held, axis=1), 0.0, masked_score)
     old_ref[...] = by_head(seg) * total
     lane = lax.broadcasted_iota(jnp.int32, stats_ref.shape, 1)
     stats_ref[...] = jnp.where(lane == 0, top, total)
 
 
+def stack(blocks):
+    if blocks[0].shape[0] % 16:
+        return jnp.concatenate([b.astype(f32) for b in blocks], axis=0).astype(bf16)
+    return jnp.concatenate(blocks, axis=0)
+
+
 def attend_kernel(groups, shares, *refs):
     kvs, (q_ref, bias_ref, old_ref, stats_ref, w_ref) = refs[:groups], refs[groups : groups + 5]
     outs = refs[groups + 5 : groups + 5 + shares]
-    k_ref, v_ref, attended_ref, sums_ref = refs[groups + 5 + shares :]
+    attended_ref, sums_ref = refs[groups + 5 + shares :]
     me_dp, me_tp = lax.axis_index("dp"), lax.axis_index("tp")
     memory = kvs[0].shape[0] // 2
     heads = kvs[0].shape[1] // HD
     tokens = attended_ref.shape[0] // groups
     per = PER_HEAD * tokens
-    for bits, kv in enumerate(kvs):
-        first = pl.multiple_of((me_dp ^ bits) * memory, memory)
-        k_ref[pl.ds(first, memory), :] = kv[0:memory, :].astype(k_ref.dtype)
-        v_ref[pl.ds(first, memory), :] = kv[memory : 2 * memory, :].astype(v_ref.dtype)
     some = groups * per
+    scores = []
+    for j in range(heads):
+        keys = stack([kv[0:memory, j * HD : (j + 1) * HD] for kv in kvs])
+        scores.append(nt(q_ref[j * some : (j + 1) * some, :], keys))
     sums = None
-    for j in range(heads):
-        at_rows, lanes = slice(j * some, (j + 1) * some), slice(j * HD, (j + 1) * HD)
-        s = nt(q_ref[at_rows, :], k_ref[:, lanes].astype(bf16)) * INV + bias_ref[...]
+    for j, s in enumerate(scores):
+        at_rows = slice(j * some, (j + 1) * some)
+        s = s * INV + bias_ref[...]
         old_top, old_total = stats_ref[at_rows, 0:1], stats_ref[at_rows, 1:2]
         top = jnp.maximum(jnp.max(s, axis=1, keepdims=True), old_top)
         p = jnp.exp(s - top)
         shrink = jnp.exp(old_top - top)
         total = jnp.sum(p, axis=1, keepdims=True) + shrink * old_total
-        acc = nn(p.astype(bf16), v_ref[:, lanes].astype(bf16))
+        values = stack([kv[memory : 2 * memory, j * HD : (j + 1) * HD] for kv in kvs])
+        acc = nn(p.astype(bf16), values)
         acc = (acc + old_ref[at_rows, :] * shrink) / total
         for k in range(groups):
             at = pl.multiple_of((me_dp ^ k) * tokens, tokens)
@@ -350,14 +365,11 @@
 
     out_rows, out_cols = groups * tokens, out_weight.shape[1]
     share = out_rows // shares
-    held = bf16 if memory % 16 == 0 else f32
     pieces = call(
         functools.partial(attend_kernel, groups, shares),
         [VMEM] * (groups + 5),
         [pltpu.VMEM((share, out_cols), f32 if k == 0 else bf16) for k in range(shares)],
         [
-            pltpu.VMEM((every, cols), held),
-            pltpu.VMEM((every, cols), held),
             pltpu.VMEM((out_rows, out_weight.shape[0]), f32),
             pltpu.VMEM((out_rows, out_cols), f32),
         ],

time: 27.1 us -> 27 us (level)
  no operation moved by 1% of the time
where the time goes in v14:
time: 27 us; the launch traced here: 26.9 us
  starting transfers between devices  12.9 us (48%)
  waiting for transfers between devices  8.18 us (30%)
  Pallas kernels  4.29 us (16%)
  between operations  0.82 us (3%)
  other arithmetic  0.62 us (2%)
    ppermute x11, starting transfers between devices, permute(): lax.ppermute(x, axis, [(i, i ^ bits) for i in range(lax.axis_size(axis))])  12.9 us
    ppermute x11, waiting for transfers between devices, permute(): lax.ppermute(x, axis, [(i, i ^ bits) for i in range(lax.axis_size(axis))])  8.18 us
    pallas_call x1, Pallas kernels, body(): call(cache_kernel, [SMEM] + [VMEM] * 6, pltpu.VMEM((2 * up(rows, 16) + ST...  1.38 us
    pallas_call x1, Pallas kernels, body(): call(functools.partial(attend_kernel, groups, shares), [VMEM] * (groups +...  1.25 us
    pallas_call x1, Pallas kernels, body(): call(functools.partial(project_kernel, near, True, False), [VMEM] * (len(...  0.82 us
    convert_element_type x1, other arithmetic, body(): return summed.astype(bf16)  0.62 us
  transfers between devices with their start and end apart: 11, of which 7 were waited for; matrix products, arithmetic and copies ran while one was open for 0% of the time, Pallas kernels for 11%

profile of v14, /device:TPU:0, one launch (start us, length us, event | category | flops | bytes accessed | tf_op | source)
XLA Modules:
  0.0 26.9 jit_solution(7421147053159139194)
XLA Ops:
  0.0 0.0 copy-start.4
  0.0 0.0 copy-start.5
  0.0 0.0 copy-start.6
  0.0 0.0 copy-start.2
  0.0 0.0 copy-start.3
  0.0 0.0 copy-start.9
  0.0 0.0 copy-start
  0.0 3.0 %collective-permute-start = (bf16[64,1280]{1,0:T(8,128)(2,1)}, bf16[64,1280]{1,0:T(8,128)(2,1)S(1)}, u32[]{:S(2)}, u32[]{:S(2)}) collective-permute-start(bf16[64,1280]{1,0:T(8,128)(2,1)} %refs_0_), channel_id=1, source_target_pairs={{0,2},{1,3},{2,0},{3,1},{4,6},{5,7},{6,4},{7,5},{8,10},{9,11},{10,... | collective-permute-start | bytes 491528 | tf_op jit(solution)/shard_map/ppermute | solution.py:270
  3.7 0.0 copy-done.4
  3.7 0.0 copy-done.5
  3.7 0.0 copy-done.6
  3.8 0.0 copy-done.2
  3.8 0.0 copy-done.3
  3.8 0.0 copy-done.9
  3.8 1.4 %shard_map.120.near_ref = bf16[176,128]{1,0:T(8,128)(2,1)S(1)} custom-call(s32[4]{0:T(128)S(1)} %copy-done.9, f32[8,128]{1,0:T(8,128)S(1)} %shard_map.119.section_ref, bf16[8,1280]{1,0:T(8,128)(2,1)S(1)} %copy-done.4, bf16[8,256]{1,0:T(8,128)(2,1)S(1)} %copy-done.5, bf16[8,256]{1,0:T(8,128)(2,1)S(1)} %copy-done.6, bf16[4,512,256]{2,1,0:T(8,128)(2,1)S(1)} %copy-done.2, ...), custom_call_target="tpu_custom_call" | custom-call | flops 167772160 | bytes 2097152 | tf_op jit(solution)/shard_map/pallas_call | solution.py:310
  5.2 0.0 copy-done.10
  5.2 0.0 copy-start.7
  5.2 0.1 collective-permute-start.2
  5.3 3.1 %collective-permute-start.5 = (bf16[176,128]{1,0:T(8,128)(2,1)S(1)}, bf16[176,128]{1,0:T(8,128)(2,1)S(1)}, u32[]{:S(2)}, u32[]{:S(2)}) collective-permute-start(bf16[176,128]{1,0:T(8,128)(2,1)S(1)} %shard_map.120.near_ref), channel_id=1, source_target_pairs={{0,8},{4,12},{8,0},{12,4},{1,9},{5,13},{9,1},{13,5},{2,10},{6,14},... | collective-permute-start | bytes 135176 | tf_op jit(solution)/shard_map/ppermute | solution.py:270
  8.4 0.0 collective-permute-done.refs_2_
  8.4 0.2 collective-permute-start.1
  8.5 0.0 collective-permute-done.2.refs_1_
  8.5 0.0 copy-done
  8.6 0.8 %shard_map.121 = (f32[128,256]{1,0:T(8,128)S(1)}, f32[64,128]{1,0:T(8,128)S(1)}) custom-call(bf16[64,1280]{1,0:T(8,128)(2,1)S(1)} %copy-done.10, bf16[64,1280]{1,0:T(8,128)(2,1)S(1)} %collective-permute-done.2.refs_1_, bf16[64,1280]{1,0:T(8,128)(2,1)S(1)} %collective-permute-done.refs_2_, bf16[2,5120,256]{2,1,0:T(8,128)(2,1)S(1)} %copy-done), custom_call_target="tpu_custom_call" | custom-call | flops 68719476736 | bytes 5242880 | tf_op jit(solution)/shard_map/pallas_call | solution.py:322
  9.4 0.4 %collective-permute-done.1.refs_0_ = bf16[64,1280]{1,0:T(8,128)(2,1)S(1)} collective-permute-done((bf16[64,1280]{1,0:T(8,128)(2,1)S(1)}, bf16[64,1280]{1,0:T(8,128)(2,1)S(1)}, u32[]{:S(2)}, u32[]{:S(2)}) %collective-permute-start.1) | collective-permute-done | bytes 163872 | tf_op jit(solution)/shard_map/ppermute | solution.py:270
  9.8 0.0 copy-done.7
  9.8 0.4 %shard_map.122.after.refs_0_ = bf16[128,256]{1,0:T(8,128)(2,1)S(1)} custom-call(bf16[64,1280]{1,0:T(8,128)(2,1)S(1)} %collective-permute-done.1.refs_0_, bf16[2,5120,256]{2,1,0:T(8,128)(2,1)S(1)} %copy-done, f32[128,256]{1,0:T(8,128)S(1)} %get-tuple-element.27.refs_2_, f32[64,128]{1,0:T(8,128)S(1)} %get-tuple-element.28.refs_3_, bf16[2,256]{1,0:T(2,128)(2,1)S(1)} %copy-done.7), custom_call_target="tpu_custom_call" | custom-call | flops 83886080 | bytes 1310720 | tf_op jit(solution)/shard_map/pallas_call | solution.py:330
  10.2 0.0 copy-start.1
  10.2 2.0 %collective-permute-start.4 = (bf16[128,256]{1,0:T(8,128)(2,1)S(1)}, bf16[128,256]{1,0:T(8,128)(2,1)S(1)}, u32[]{:S(2)}, u32[]{:S(2)}) collective-permute-start(bf16[128,256]{1,0:T(8,128)(2,1)S(1)} %shard_map.122.after.refs_0_), channel_id=1, source_target_pairs={{0,8},{4,12},{8,0},{12,4},{1,9},{5,13},{9,1},{13,5},{2,10},{6,14},... | collective-permute-start | bytes 196616 | tf_op jit(solution)/shard_map/ppermute | solution.py:270
  12.2 0.0 collective-permute-done.5.far_ref
  12.2 1.6 %collective-permute-start.7 = (bf16[2,176,128]{2,1,0:T(8,128)(2,1)S(1)}, bf16[2,176,128]{2,1,0:T(8,128)(2,1)S(1)}, u32[]{:S(2)}, u32[]{:S(2)}) collective-permute-start(bf16[2,176,128]{2,1,0:T(8,128)(2,1)S(1)} %shard_map.123.refs_0_), channel_id=1, source_target_pairs={{0,4},{4,0},{8,12},{12,8},{1,5},{5,1},{9,13},{13,9},{2,6},{6,2},{1... | collective-permute-start | bytes 270344 | tf_op jit(solution)/shard_map/ppermute | solution.py:270
  13.8 0.4 %collective-permute-start.3 = (bf16[128,256]{1,0:T(8,128)(2,1)S(1)}, bf16[128,256]{1,0:T(8,128)(2,1)S(1)}, u32[]{:S(2)}, u32[]{:S(2)}) collective-permute-start(bf16[128,256]{1,0:T(8,128)(2,1)S(1)} %shard_map.122.after.refs_0_), channel_id=1, source_target_pairs={{0,4},{4,0},{8,12},{12,8},{1,5},{5,1},{9,13},{13,9},{2,6},{6,2},{1... | collective-permute-start | bytes 196616 | tf_op jit(solution)/shard_map/ppermute | solution.py:270
  14.3 2.5 %collective-permute-done.4.refs_2_ = bf16[128,256]{1,0:T(8,128)(2,1)S(1)} collective-permute-done((bf16[128,256]{1,0:T(8,128)(2,1)S(1)}, bf16[128,256]{1,0:T(8,128)(2,1)S(1)}, u32[]{:S(2)}, u32[]{:S(2)}) %collective-permute-start.4) | collective-permute-done | bytes 65568 | tf_op jit(solution)/shard_map/ppermute | solution.py:270
  16.8 0.6 %collective-permute-start.6 = (bf16[128,256]{1,0:T(8,128)(2,1)S(1)}, bf16[128,256]{1,0:T(8,128)(2,1)S(1)}, u32[]{:S(2)}, u32[]{:S(2)}) collective-permute-start(bf16[128,256]{1,0:T(8,128)(2,1)S(1)} %collective-permute-done.4.refs_2_), channel_id=1, source_target_pairs={{0,4},{4,0},{8,12},{12,8},{1,5},{5,1},{9,13},{13,9},{2,6},{6,2},{1... | collective-permute-start | bytes 196616 | tf_op jit(solution)/shard_map/ppermute | solution.py:270
  17.4 0.8 %collective-permute-done.7.refs_1_ = bf16[2,176,128]{2,1,0:T(8,128)(2,1)S(1)} collective-permute-done((bf16[2,176,128]{2,1,0:T(8,128)(2,1)S(1)}, bf16[2,176,128]{2,1,0:T(8,128)(2,1)S(1)}, u32[]{:S(2)}, u32[]{:S(2)}) %collective-permute-start.7) | collective-permute-done | bytes 90144 | tf_op jit(solution)/shard_map/ppermute | solution.py:270
  18.1 0.0 copy-done.8
  18.1 0.5 %shard_map.124 = (bf16[320,128]{1,0:T(8,128)(2,1)S(1)}, f32[160,256]{1,0:T(8,128)S(1)}, f32[320,128]{1,0:T(8,128)S(1)}, f32[320,128]{1,0:T(8,128)S(1)}) custom-call(bf16[2,176,128]{2,1,0:T(8,128)(2,1)S(1)} %shard_map.123.refs_0_, bf16[2,176,128]{2,1,0:T(8,128)(2,1)S(1)} %collective-permute-done.7.refs_1_, s32[1,256]{1,0:T(1,128)S(1)} %bitcast.1), custom_call_target="tpu_custom_call" | custom-call | flops 1024 | tf_op jit(solution)/shard_map/pallas_call | solution.py:352
  18.6 0.8 %collective-permute-done.3.refs_1_ = bf16[128,256]{1,0:T(8,128)(2,1)S(1)} collective-permute-done((bf16[128,256]{1,0:T(8,128)(2,1)S(1)}, bf16[128,256]{1,0:T(8,128)(2,1)S(1)}, u32[]{:S(2)}, u32[]{:S(2)}) %collective-permute-start.3) | collective-permute-done | bytes 65568 | tf_op jit(solution)/shard_map/ppermute | solution.py:270
  19.4 1.6 %collective-permute-done.6.refs_3_ = bf16[128,256]{1,0:T(8,128)(2,1)S(1)} collective-permute-done((bf16[128,256]{1,0:T(8,128)(2,1)S(1)}, bf16[128,256]{1,0:T(8,128)(2,1)S(1)}, u32[]{:S(2)}, u32[]{:S(2)}) %collective-permute-start.6) | collective-permute-done | bytes 65568 | tf_op jit(solution)/shard_map/ppermute | solution.py:270
  21.1 0.0 copy-done.1
  21.1 1.2 %shard_map.125 = (f32[8,1280]{1,0:T(8,128)S(1)}, bf16[8,1280]{1,0:T(8,128)(2,1)S(1)}, bf16[8,1280]{1,0:T(8,128)(2,1)S(1)}, bf16[8,1280]{1,0:T(8,128)(2,1)S(1)}) custom-call(bf16[128,256]{1,0:T(8,128)(2,1)S(1)} %shard_map.122.after.refs_0_, bf16[128,256]{1,0:T(8,128)(2,1)S(1)} %collective-permute-done.3.refs_1_, ...), custom_call_target="tpu_custom_call" | custom-call | flops 104857600 | bytes 3276800 | tf_op jit(solution)/shard_map/pallas_call | solution.py:368
  22.3 0.1 collective-permute-start.10
  22.4 0.7 %collective-permute-start.8 = (bf16[8,1280]{1,0:T(8,128)(2,1)S(1)}, bf16[8,1280]{1,0:T(8,128)(2,1)S(1)}, u32[]{:S(2)}, u32[]{:S(2)}) collective-permute-start(bf16[8,1280]{1,0:T(8,128)(2,1)S(1)} %get-tuple-element.36), channel_id=1, source_target_pairs={{0,2},{1,3},{2,0},{3,1},{4,6},{5,7},{6,4},{7,5},{8,10},{9,11},{10,... | collective-permute-start | bytes 61448 | tf_op jit(solution)/shard_map/ppermute | solution.py:270
  23.1 1.2 %collective-permute-start.9 = (bf16[8,1280]{1,0:T(8,128)(2,1)S(1)}, bf16[8,1280]{1,0:T(8,128)(2,1)S(1)}, u32[]{:S(2)}, u32[]{:S(2)}) collective-permute-start(bf16[8,1280]{1,0:T(8,128)(2,1)S(1)} %get-tuple-element.37), channel_id=1, source_target_pairs={{0,1},{1,0},{2,3},{3,2},{4,5},{5,4},{6,7},{7,6},{8,9},{9,8},{10,11... | collective-permute-start | bytes 61448 | tf_op jit(solution)/shard_map/ppermute | solution.py:270
  24.3 1.3 %collective-permute-done.10 = bf16[8,1280]{1,0:T(8,128)(2,1)S(1)} collective-permute-done((bf16[8,1280]{1,0:T(8,128)(2,1)S(1)}, bf16[8,1280]{1,0:T(8,128)(2,1)S(1)}, u32[]{:S(2)}, u32[]{:S(2)}) %collective-permute-start.10) | collective-permute-done | bytes 20512 | tf_op jit(solution)/shard_map/ppermute | solution.py:270
  25.6 0.7 %collective-permute-done.8 = bf16[8,1280]{1,0:T(8,128)(2,1)S(1)} collective-permute-done((bf16[8,1280]{1,0:T(8,128)(2,1)S(1)}, bf16[8,1280]{1,0:T(8,128)(2,1)S(1)}, u32[]{:S(2)}, u32[]{:S(2)}) %collective-permute-start.8) | collective-permute-done | bytes 20512 | tf_op jit(solution)/shard_map/ppermute | solution.py:270
  26.3 0.0 collective-permute-done.9
  26.3 0.6 %add_convert_fusion = bf16[8,1280]{1,0:T(8,128)(2,1)} fusion(bf16[8,1280]{1,0:T(8,128)(2,1)S(1)} %collective-permute-done.10, bf16[8,1280]{1,0:T(8,128)(2,1)S(1)} %collective-permute-done.9, f32[8,1280]{1,0:T(8,128)S(1)} %get-tuple-element.35, bf16[8,1280]{1,0:T(8,128)(2,1)S(1)} %collective-permute-done.8), kind=kLoop, calls=%fused_computation | loop fusion | flops 71680 | bytes 122880 | tf_op jit(solution)/shard_map/convert_element_type | solution.py:382
  (5 shorter events, 0.0 us)
Async XLA Ops:
  0.0 5.2 %copy-start.10 = (bf16[64,1280]{1,0:T(8,128)(2,1)S(1)}, bf16[64,1280]{1,0:T(8,128)(2,1)}, u32[]{:S(2)}) copy-start(bf16[64,1280]{1,0:T(8,128)(2,1)} %refs_0_) | copy-start | bytes 491524
  0.0 3.7 %copy-start.4 = (bf16[8,1280]{1,0:T(8,128)(2,1)S(1)}, bf16[8,1280]{1,0:T(8,128)(2,1)}, u32[]{:S(2)}) copy-start(bf16[8,1280]{1,0:T(8,128)(2,1)} %q_ref.1) | copy-start | bytes 61444
  0.0 3.7 %copy-start.5 = (bf16[8,256]{1,0:T(8,128)(2,1)S(1)}, bf16[8,256]{1,0:T(8,128)(2,1)}, u32[]{:S(2)}) copy-start(bf16[8,256]{1,0:T(8,128)(2,1)} %nk_ref.1) | copy-start | bytes 12292
  0.0 3.7 %copy-start.6 = (bf16[8,256]{1,0:T(8,128)(2,1)S(1)}, bf16[8,256]{1,0:T(8,128)(2,1)}, u32[]{:S(2)}) copy-start(bf16[8,256]{1,0:T(8,128)(2,1)} %nv_ref.1) | copy-start | bytes 12292
  0.0 3.8 %copy-start.2 = (bf16[4,512,256]{2,1,0:T(8,128)(2,1)S(1)}, bf16[4,512,256]{2,1,0:T(8,128)(2,1)}, u32[]{:S(2)}) copy-start(bf16[4,512,256]{2,1,0:T(8,128)(2,1)} %ck_ref.1) | copy-start | bytes 3145732
  0.0 3.8 %copy-start.3 = (bf16[4,512,256]{2,1,0:T(8,128)(2,1)S(1)}, bf16[4,512,256]{2,1,0:T(8,128)(2,1)}, u32[]{:S(2)}) copy-start(bf16[4,512,256]{2,1,0:T(8,128)(2,1)} %cv_ref.1) | copy-start | bytes 3145732
  0.0 3.8 %copy-start.9 = (s32[4]{0:T(128)S(1)}, s32[4]{0:T(128)}, u32[]{:S(2)}) copy-start(s32[4]{0:T(128)} %lens_ref.1) | copy-start | bytes 52
  0.0 8.5 %copy-start = (bf16[2,5120,256]{2,1,0:T(8,128)(2,1)S(1)}, bf16[2,5120,256]{2,1,0:T(8,128)(2,1)}, u32[]{:S(2)}) copy-start(bf16[2,5120,256]{2,1,0:T(8,128)(2,1)} %refs_1_.1) | copy-start | bytes 15728644
  0.0 8.3 %collective-permute-start = (bf16[64,1280]{1,0:T(8,128)(2,1)}, bf16[64,1280]{1,0:T(8,128)(2,1)S(1)}, u32[]{:S(2)}, u32[]{:S(2)}) collective-permute-start(bf16[64,1280]{1,0:T(8,128)(2,1)} %refs_0_), channel_id=1, source_target_pairs={{0,2},{1,3},{2,0},{3,1},{4,6},{5,7},{6,4},{7,5},{8,10},{9,11},{10,... | collective-permute-start | bytes 491528 | tf_op jit(solution)/shard_map/ppermute | solution.py:270
  5.2 4.6 %copy-start.7 = (bf16[2,256]{1,0:T(2,128)(2,1)S(1)}, bf16[2,256]{1,0:T(2,128)(2,1)}, u32[]{:S(2)}) copy-start(bf16[2,256]{1,0:T(2,128)(2,1)} %refs_4_.1) | copy-start | bytes 3076
  5.2 3.4 %collective-permute-start.2 = (bf16[64,1280]{1,0:T(8,128)(2,1)S(1)}, bf16[64,1280]{1,0:T(8,128)(2,1)S(1)}, u32[]{:S(2)}, u32[]{:S(2)}) collective-permute-start(bf16[64,1280]{1,0:T(8,128)(2,1)S(1)} %copy-done.10), channel_id=1, source_target_pairs={{0,1},{1,0},{2,3},{3,2},{4,5},{5,4},{6,7},{7,6},{8,9},{9,8},{10,11... | collective-permute-start | bytes 491528 | tf_op jit(solution)/shard_map/ppermute | solution.py:270
  5.3 6.9 %collective-permute-start.5 = (bf16[176,128]{1,0:T(8,128)(2,1)S(1)}, bf16[176,128]{1,0:T(8,128)(2,1)S(1)}, u32[]{:S(2)}, u32[]{:S(2)}) collective-permute-start(bf16[176,128]{1,0:T(8,128)(2,1)S(1)} %shard_map.120.near_ref), channel_id=1, source_target_pairs={{0,8},{4,12},{8,0},{12,4},{1,9},{5,13},{9,1},{13,5},{2,10},{6,14},... | collective-permute-start | bytes 135176 | tf_op jit(solution)/shard_map/ppermute | solution.py:270
  8.4 1.4 %collective-permute-start.1 = (bf16[64,1280]{1,0:T(8,128)(2,1)S(1)}, bf16[64,1280]{1,0:T(8,128)(2,1)S(1)}, u32[]{:S(2)}, u32[]{:S(2)}) collective-permute-start(bf16[64,1280]{1,0:T(8,128)(2,1)S(1)} %collective-permute-done.refs_2_), channel_id=1, source_target_pairs={{0,1},{1,0},{2,3},{3,2},{4,5},{5,4},{6,7},{7,6},{8,9},{9,8},{10,11... | collective-permute-start | bytes 491528 | tf_op jit(solution)/shard_map/ppermute | solution.py:270
  10.2 8.0 %copy-start.8 = (s32[256]{0:T(256)S(1)}, s32[256]{0:T(256)}, u32[]{:S(2)}) copy-start(s32[256]{0:T(256)} %param.15) | copy-start | bytes 3076
  10.2 10.9 %copy-start.1 = (bf16[1280,1280]{1,0:T(8,128)(2,1)S(1)}, bf16[1280,1280]{1,0:T(8,128)(2,1)}, u32[]{:S(2)}) copy-start(bf16[1280,1280]{1,0:T(8,128)(2,1)} %refs_8_.1) | copy-start | bytes 9830404
  10.2 6.6 %collective-permute-start.4 = (bf16[128,256]{1,0:T(8,128)(2,1)S(1)}, bf16[128,256]{1,0:T(8,128)(2,1)S(1)}, u32[]{:S(2)}, u32[]{:S(2)}) collective-permute-start(bf16[128,256]{1,0:T(8,128)(2,1)S(1)} %shard_map.122.after.refs_0_), channel_id=1, source_target_pairs={{0,8},{4,12},{8,0},{12,4},{1,9},{5,13},{9,1},{13,5},{2,10},{6,14},... | collective-permute-start | bytes 196616 | tf_op jit(solution)/shard_map/ppermute | solution.py:270
  12.2 6.0 %collective-permute-start.7 = (bf16[2,176,128]{2,1,0:T(8,128)(2,1)S(1)}, bf16[2,176,128]{2,1,0:T(8,128)(2,1)S(1)}, u32[]{:S(2)}, u32[]{:S(2)}) collective-permute-start(bf16[2,176,128]{2,1,0:T(8,128)(2,1)S(1)} %shard_map.123.refs_0_), channel_id=1, source_target_pairs={{0,4},{4,0},{8,12},{12,8},{1,5},{5,1},{9,13},{13,9},{2,6},{6,2},{1... | collective-permute-start | bytes 270344 | tf_op jit(solution)/shard_map/ppermute | solution.py:270
  13.8 5.6 %collective-permute-start.3 = (bf16[128,256]{1,0:T(8,128)(2,1)S(1)}, bf16[128,256]{1,0:T(8,128)(2,1)S(1)}, u32[]{:S(2)}, u32[]{:S(2)}) collective-permute-start(bf16[128,256]{1,0:T(8,128)(2,1)S(1)} %shard_map.122.after.refs_0_), channel_id=1, source_target_pairs={{0,4},{4,0},{8,12},{12,8},{1,5},{5,1},{9,13},{13,9},{2,6},{6,2},{1... | collective-permute-start | bytes 196616 | tf_op jit(solution)/shard_map/ppermute | solution.py:270
  16.8 4.3 %collective-permute-start.6 = (bf16[128,256]{1,0:T(8,128)(2,1)S(1)}, bf16[128,256]{1,0:T(8,128)(2,1)S(1)}, u32[]{:S(2)}, u32[]{:S(2)}) collective-permute-start(bf16[128,256]{1,0:T(8,128)(2,1)S(1)} %collective-permute-done.4.refs_2_), channel_id=1, source_target_pairs={{0,4},{4,0},{8,12},{12,8},{1,5},{5,1},{9,13},{13,9},{2,6},{6,2},{1... | collective-permute-start | bytes 196616 | tf_op jit(solution)/shard_map/ppermute | solution.py:270
  22.3 3.3 %collective-permute-start.10 = (bf16[8,1280]{1,0:T(8,128)(2,1)S(1)}, bf16[8,1280]{1,0:T(8,128)(2,1)S(1)}, u32[]{:S(2)}, u32[]{:S(2)}) collective-permute-start(bf16[8,1280]{1,0:T(8,128)(2,1)S(1)} %get-tuple-element.38), channel_id=1, source_target_pairs={{0,3},{1,2},{2,1},{3,0},{4,7},{5,6},{6,5},{7,4},{8,11},{9,10},{10,... | collective-permute-start | bytes 61448 | tf_op jit(solution)/shard_map/ppermute | solution.py:270
  22.4 3.8 %collective-permute-start.8 = (bf16[8,1280]{1,0:T(8,128)(2,1)S(1)}, bf16[8,1280]{1,0:T(8,128)(2,1)S(1)}, u32[]{:S(2)}, u32[]{:S(2)}) collective-permute-start(bf16[8,1280]{1,0:T(8,128)(2,1)S(1)} %get-tuple-element.36), channel_id=1, source_target_pairs={{0,2},{1,3},{2,0},{3,1},{4,6},{5,7},{6,4},{7,5},{8,10},{9,11},{10,... | collective-permute-start | bytes 61448 | tf_op jit(solution)/shard_map/ppermute | solution.py:270
  23.1 3.2 %collective-permute-start.9 = (bf16[8,1280]{1,0:T(8,128)(2,1)S(1)}, bf16[8,1280]{1,0:T(8,128)(2,1)S(1)}, u32[]{:S(2)}, u32[]{:S(2)}) collective-permute-start(bf16[8,1280]{1,0:T(8,128)(2,1)S(1)} %get-tuple-element.37), channel_id=1, source_target_pairs={{0,1},{1,0},{2,3},{3,2},{4,5},{5,4},{6,7},{7,6},{8,9},{9,8},{10,11... | collective-permute-start | bytes 61448 | tf_op jit(solution)/shard_map/ppermute | solution.py:270

commit v15 on v13

--- a/solution.py
+++ b/solution.py
@@ -292,12 +292,13 @@
     group, gate = lax.optimization_barrier((group_sections, gate))
     section = call(open_kernel, [SMEM, ANY], pltpu.VMEM((8, HD), f32), [], 1 << 10, 0)(group, gate)
     own, section = lax.optimization_barrier((memory_hidden, section))
+    weight, section = lax.optimization_barrier((kv_weight, section))
     part = call(
         cache_kernel,
         [SMEM] + [VMEM] * 6,
         pltpu.VMEM((2 * up(rows, 16) + STATS, HD), bf16),
         [],
-        4 * rows * slots * cols * requests,
+        COVER,
         4 * requests * slots * cols,
     )(cache_lengths, section, queries, new_keys, new_values, cache_keys, cache_values)
     own_later, part = lax.optimization_barrier((own, part))
@@ -311,7 +312,7 @@
         [],
         COVER,
         4 * D * cols,
-    )(*[hidden[k] for k in near], kv_weight)
+    )(*[hidden[k] for k in near], weight)
     kv = call(
         functools.partial(project_kernel, far, False, True),
         [VMEM] * 5,
@@ -319,7 +320,7 @@
         [],
         4 * memory * D * cols // shares,
         4 * D * cols // shares,
-    )(hidden[far[0]], kv_weight, *partial, kv_bias)
+    )(hidden[far[0]], weight, *partial, kv_bias)
     kv_far = permute(kv, "dp", groups // 2)
     pair = call(
         pair_kernel,

time: 27.1 us -> 26.8 us (0.989)
  no operation moved by 1% of the time
where the time goes in v15:
time: 26.8 us; the launch traced here: 26.7 us
  starting transfers between devices  12.7 us (47%)
  waiting for transfers between devices  7.98 us (30%)
  Pallas kernels  4.31 us (16%)
  between operations  0.98 us (4%)
  other arithmetic  0.62 us (2%)
    ppermute x11, starting transfers between devices, permute(): lax.ppermute(x, axis, [(i, i ^ bits) for i in range(lax.axis_size(axis))])  12.7 us
    ppermute x11, waiting for transfers between devices, permute(): lax.ppermute(x, axis, [(i, i ^ bits) for i in range(lax.axis_size(axis))])  7.98 us
    pallas_call x1, Pallas kernels, body(): call(cache_kernel, [SMEM] + [VMEM] * 6, pltpu.VMEM((2 * up(rows, 16) + ST...  1.38 us
    pallas_call x1, Pallas kernels, body(): call(functools.partial(attend_kernel, groups, shares), [VMEM] * (groups +...  1.26 us
    pallas_call x1, Pallas kernels, body(): call(functools.partial(project_kernel, near, True, False), [VMEM] * (len(...  0.82 us
    convert_element_type x1, other arithmetic, body(): return summed.astype(bf16)  0.62 us
  transfers between devices with their start and end apart: 11, of which 7 were waited for; matrix products, arithmetic and copies ran while one was open for 0% of the time, Pallas kernels for 11%

profile of v15, /device:TPU:0, one launch (start us, length us, event | category | flops | bytes accessed | tf_op | source)
XLA Modules:
  0.0 26.7 jit_solution(15727805657312108498)
XLA Ops:
  0.0 0.0 copy-start.6
  0.0 0.0 copy-start.7
  0.0 0.0 copy-start.8
  0.0 0.0 copy-start.9
  0.0 3.0 %collective-permute-start = (bf16[64,1280]{1,0:T(8,128)(2,1)}, bf16[64,1280]{1,0:T(8,128)(2,1)S(1)}, u32[]{:S(2)}, u32[]{:S(2)}) collective-permute-start(bf16[64,1280]{1,0:T(8,128)(2,1)} %refs_0_), channel_id=1, source_target_pairs={{0,2},{1,3},{2,0},{3,1},{4,6},{5,7},{6,4},{7,5},{8,10},{9,11},{10,... | collective-permute-start | bytes 491528 | tf_op jit(solution)/shard_map/ppermute | solution.py:255
  3.8 0.0 slice-start.1
  3.9 0.0 copy-done.6
  3.9 0.0 copy-done.7
  3.9 0.0 copy-done.8
  3.9 0.0 copy-done.3
  3.9 0.0 copy-done.4
  3.9 0.0 copy-done.9
  3.9 0.0 copy-start.5
  3.9 1.4 %shard_map.120.near_ref = bf16[176,128]{1,0:T(8,128)(2,1)S(1)} custom-call(s32[4]{0:T(128)S(1)} %copy-done.9, f32[8,128]{1,0:T(8,128)S(1)} %shard_map.119.section_ref, bf16[8,1280]{1,0:T(8,128)(2,1)S(1)} %copy-done.6, bf16[8,256]{1,0:T(8,128)(2,1)S(1)} %copy-done.7, bf16[8,256]{1,0:T(8,128)(2,1)S(1)} %copy-done.8, bf16[4,512,256]{2,1,0:T(8,128)(2,1)S(1)} %copy-done.3, ...), custom_call_target="tpu_custom_call" | custom-call | flops 68719476736 | bytes 2097152 | tf_op jit(solution)/shard_map/pallas_call | solution.py:296
  5.3 0.0 copy-done.5
  5.3 0.0 copy-start.1
  5.3 0.1 collective-permute-start.2
  5.4 2.7 %collective-permute-start.5 = (bf16[176,128]{1,0:T(8,128)(2,1)S(1)}, bf16[176,128]{1,0:T(8,128)(2,1)S(1)}, u32[]{:S(2)}, u32[]{:S(2)}) collective-permute-start(bf16[176,128]{1,0:T(8,128)(2,1)S(1)} %shard_map.120.near_ref), channel_id=1, source_target_pairs={{0,8},{4,12},{8,0},{12,4},{1,9},{5,13},{9,1},{13,5},{2,10},{6,14},... | collective-permute-start | bytes 135176 | tf_op jit(solution)/shard_map/ppermute | solution.py:255
  8.1 0.0 collective-permute-done.refs_2_
  8.1 0.2 collective-permute-start.1
  8.3 0.0 collective-permute-done.2.refs_1_
  8.3 0.0 slice-done
  8.3 0.0 slice-done.1
  8.3 0.8 %shard_map.121 = (f32[128,256]{1,0:T(8,128)S(1)}, f32[64,128]{1,0:T(8,128)S(1)}) custom-call(bf16[64,1280]{1,0:T(8,128)(2,1)S(1)} %copy-done.5, bf16[64,1280]{1,0:T(8,128)(2,1)S(1)} %collective-permute-done.2.refs_1_, bf16[64,1280]{1,0:T(8,128)(2,1)S(1)} %collective-permute-done.refs_2_, bf16[2,5120,256]{2,1,0:T(8,128)(2,1)S(1)} %bitcast.2), custom_call_target="tpu_custom_call" | custom-call | flops 68719476736 | bytes 5242880 | tf_op jit(solution)/shard_map/pallas_call | solution.py:308
  9.1 0.4 %collective-permute-done.1.refs_0_ = bf16[64,1280]{1,0:T(8,128)(2,1)S(1)} collective-permute-done((bf16[64,1280]{1,0:T(8,128)(2,1)S(1)}, bf16[64,1280]{1,0:T(8,128)(2,1)S(1)}, u32[]{:S(2)}, u32[]{:S(2)}) %collective-permute-start.1) | collective-permute-done | bytes 163872 | tf_op jit(solution)/shard_map/ppermute | solution.py:255
  9.5 0.0 copy-done.1
  9.5 0.4 %shard_map.122.after.refs_0_ = bf16[128,256]{1,0:T(8,128)(2,1)S(1)} custom-call(bf16[64,1280]{1,0:T(8,128)(2,1)S(1)} %collective-permute-done.1.refs_0_, bf16[2,5120,256]{2,1,0:T(8,128)(2,1)S(1)} %bitcast.2, f32[128,256]{1,0:T(8,128)S(1)} %get-tuple-element.31.refs_2_, f32[64,128]{1,0:T(8,128)S(1)} %get-tuple-element.32.refs_3_, bf16[2,256]{1,0:T(2,128)(2,1)S(1)} %copy-done.1), custom_call_target="tpu_custom_call" | custom-call | flops 83886080 | bytes 1310720 | tf_op jit(solution)/shard_map/pallas_call | solution.py:316
  9.9 0.0 copy-start
  9.9 2.3 %collective-permute-start.4 = (bf16[128,256]{1,0:T(8,128)(2,1)S(1)}, bf16[128,256]{1,0:T(8,128)(2,1)S(1)}, u32[]{:S(2)}, u32[]{:S(2)}) collective-permute-start(bf16[128,256]{1,0:T(8,128)(2,1)S(1)} %shard_map.122.after.refs_0_), channel_id=1, source_target_pairs={{0,8},{4,12},{8,0},{12,4},{1,9},{5,13},{9,1},{13,5},{2,10},{6,14},... | collective-permute-start | bytes 196616 | tf_op jit(solution)/shard_map/ppermute | solution.py:255
  12.2 0.0 collective-permute-done.5.far_ref
  12.2 1.6 %collective-permute-start.7 = (bf16[2,176,128]{2,1,0:T(8,128)(2,1)S(1)}, bf16[2,176,128]{2,1,0:T(8,128)(2,1)S(1)}, u32[]{:S(2)}, u32[]{:S(2)}) collective-permute-start(bf16[2,176,128]{2,1,0:T(8,128)(2,1)S(1)} %shard_map.123.refs_0_), channel_id=1, source_target_pairs={{0,4},{4,0},{8,12},{12,8},{1,5},{5,1},{9,13},{13,9},{2,6},{6,2},{1... | collective-permute-start | bytes 270344 | tf_op jit(solution)/shard_map/ppermute | solution.py:255
  13.8 0.4 %collective-permute-start.3 = (bf16[128,256]{1,0:T(8,128)(2,1)S(1)}, bf16[128,256]{1,0:T(8,128)(2,1)S(1)}, u32[]{:S(2)}, u32[]{:S(2)}) collective-permute-start(bf16[128,256]{1,0:T(8,128)(2,1)S(1)} %shard_map.122.after.refs_0_), channel_id=1, source_target_pairs={{0,4},{4,0},{8,12},{12,8},{1,5},{5,1},{9,13},{13,9},{2,6},{6,2},{1... | collective-permute-start | bytes 196616 | tf_op jit(solution)/shard_map/ppermute | solution.py:255
  14.3 2.3 %collective-permute-done.4.refs_2_ = bf16[128,256]{1,0:T(8,128)(2,1)S(1)} collective-permute-done((bf16[128,256]{1,0:T(8,128)(2,1)S(1)}, bf16[128,256]{1,0:T(8,128)(2,1)S(1)}, u32[]{:S(2)}, u32[]{:S(2)}) %collective-permute-start.4) | collective-permute-done | bytes 65568 | tf_op jit(solution)/shard_map/ppermute | solution.py:255
  16.5 0.5 %collective-permute-start.6 = (bf16[128,256]{1,0:T(8,128)(2,1)S(1)}, bf16[128,256]{1,0:T(8,128)(2,1)S(1)}, u32[]{:S(2)}, u32[]{:S(2)}) collective-permute-start(bf16[128,256]{1,0:T(8,128)(2,1)S(1)} %collective-permute-done.4.refs_2_), channel_id=1, source_target_pairs={{0,4},{4,0},{8,12},{12,8},{1,5},{5,1},{9,13},{13,9},{2,6},{6,2},{1... | collective-permute-start | bytes 196616 | tf_op jit(solution)/shard_map/ppermute | solution.py:255
  17.1 0.9 %collective-permute-done.7.refs_1_ = bf16[2,176,128]{2,1,0:T(8,128)(2,1)S(1)} collective-permute-done((bf16[2,176,128]{2,1,0:T(8,128)(2,1)S(1)}, bf16[2,176,128]{2,1,0:T(8,128)(2,1)S(1)}, u32[]{:S(2)}, u32[]{:S(2)}) %collective-permute-start.7) | collective-permute-done | bytes 90144 | tf_op jit(solution)/shard_map/ppermute | solution.py:255
  18.0 0.0 copy-done.2
  18.0 0.5 %shard_map.124 = (bf16[320,128]{1,0:T(8,128)(2,1)S(1)}, f32[160,256]{1,0:T(8,128)S(1)}, f32[320,128]{1,0:T(8,128)S(1)}, f32[320,128]{1,0:T(8,128)S(1)}) custom-call(bf16[2,176,128]{2,1,0:T(8,128)(2,1)S(1)} %shard_map.123.refs_0_, bf16[2,176,128]{2,1,0:T(8,128)(2,1)S(1)} %collective-permute-done.7.refs_1_, s32[1,256]{1,0:T(1,128)S(1)} %bitcast.3), custom_call_target="tpu_custom_call" | custom-call | flops 1024 | tf_op jit(solution)/shard_map/pallas_call | solution.py:338
  18.4 0.8 %collective-permute-done.3.refs_1_ = bf16[128,256]{1,0:T(8,128)(2,1)S(1)} collective-permute-done((bf16[128,256]{1,0:T(8,128)(2,1)S(1)}, bf16[128,256]{1,0:T(8,128)(2,1)S(1)}, u32[]{:S(2)}, u32[]{:S(2)}) %collective-permute-start.3) | collective-permute-done | bytes 65568 | tf_op jit(solution)/shard_map/ppermute | solution.py:255
  19.3 1.5 %collective-permute-done.6.refs_3_ = bf16[128,256]{1,0:T(8,128)(2,1)S(1)} collective-permute-done((bf16[128,256]{1,0:T(8,128)(2,1)S(1)}, bf16[128,256]{1,0:T(8,128)(2,1)S(1)}, u32[]{:S(2)}, u32[]{:S(2)}) %collective-permute-start.6) | collective-permute-done | bytes 65568 | tf_op jit(solution)/shard_map/ppermute | solution.py:255
  20.8 0.0 copy-done
  20.8 1.3 %shard_map.125 = (f32[8,1280]{1,0:T(8,128)S(1)}, bf16[8,1280]{1,0:T(8,128)(2,1)S(1)}, bf16[8,1280]{1,0:T(8,128)(2,1)S(1)}, bf16[8,1280]{1,0:T(8,128)(2,1)S(1)}) custom-call(bf16[128,256]{1,0:T(8,128)(2,1)S(1)} %shard_map.122.after.refs_0_, bf16[128,256]{1,0:T(8,128)(2,1)S(1)} %collective-permute-done.3.refs_1_, ...), custom_call_target="tpu_custom_call" | custom-call | flops 104857600 | bytes 3276800 | tf_op jit(solution)/shard_map/pallas_call | solution.py:355
  22.1 0.1 collective-permute-start.10
  22.1 0.9 %collective-permute-start.8 = (bf16[8,1280]{1,0:T(8,128)(2,1)S(1)}, bf16[8,1280]{1,0:T(8,128)(2,1)S(1)}, u32[]{:S(2)}, u32[]{:S(2)}) collective-permute-start(bf16[8,1280]{1,0:T(8,128)(2,1)S(1)} %get-tuple-element.40), channel_id=1, source_target_pairs={{0,2},{1,3},{2,0},{3,1},{4,6},{5,7},{6,4},{7,5},{8,10},{9,11},{10,... | collective-permute-start | bytes 61448 | tf_op jit(solution)/shard_map/ppermute | solution.py:255
  23.0 1.0 %collective-permute-start.9 = (bf16[8,1280]{1,0:T(8,128)(2,1)S(1)}, bf16[8,1280]{1,0:T(8,128)(2,1)S(1)}, u32[]{:S(2)}, u32[]{:S(2)}) collective-permute-start(bf16[8,1280]{1,0:T(8,128)(2,1)S(1)} %get-tuple-element.41), channel_id=1, source_target_pairs={{0,1},{1,0},{2,3},{3,2},{4,5},{5,4},{6,7},{7,6},{8,9},{9,8},{10,11... | collective-permute-start | bytes 61448 | tf_op jit(solution)/shard_map/ppermute | solution.py:255
  24.0 1.3 %collective-permute-done.10 = bf16[8,1280]{1,0:T(8,128)(2,1)S(1)} collective-permute-done((bf16[8,1280]{1,0:T(8,128)(2,1)S(1)}, bf16[8,1280]{1,0:T(8,128)(2,1)S(1)}, u32[]{:S(2)}, u32[]{:S(2)}) %collective-permute-start.10) | collective-permute-done | bytes 20512 | tf_op jit(solution)/shard_map/ppermute | solution.py:255
  25.3 0.7 %collective-permute-done.8 = bf16[8,1280]{1,0:T(8,128)(2,1)S(1)} collective-permute-done((bf16[8,1280]{1,0:T(8,128)(2,1)S(1)}, bf16[8,1280]{1,0:T(8,128)(2,1)S(1)}, u32[]{:S(2)}, u32[]{:S(2)}) %collective-permute-start.8) | collective-permute-done | bytes 20512 | tf_op jit(solution)/shard_map/ppermute | solution.py:255
  26.1 0.0 collective-permute-done.9
  26.1 0.6 %add_convert_fusion = bf16[8,1280]{1,0:T(8,128)(2,1)} fusion(bf16[8,1280]{1,0:T(8,128)(2,1)S(1)} %collective-permute-done.10, bf16[8,1280]{1,0:T(8,128)(2,1)S(1)} %collective-permute-done.9, f32[8,1280]{1,0:T(8,128)S(1)} %get-tuple-element.39, bf16[8,1280]{1,0:T(8,128)(2,1)S(1)} %collective-permute-done.8), kind=kLoop, calls=%fused_computation | loop fusion | flops 71680 | bytes 122880 | tf_op jit(solution)/shard_map/convert_element_type | solution.py:371
  (8 shorter events, 0.0 us)
Async XLA Ops:
  0.0 3.9 %copy-start.6 = (bf16[8,1280]{1,0:T(8,128)(2,1)S(1)}, bf16[8,1280]{1,0:T(8,128)(2,1)}, u32[]{:S(2)}) copy-start(bf16[8,1280]{1,0:T(8,128)(2,1)} %q_ref.1) | copy-start | bytes 61444
  0.0 3.9 %copy-start.7 = (bf16[8,256]{1,0:T(8,128)(2,1)S(1)}, bf16[8,256]{1,0:T(8,128)(2,1)}, u32[]{:S(2)}) copy-start(bf16[8,256]{1,0:T(8,128)(2,1)} %nk_ref.1) | copy-start | bytes 12292
  0.0 3.9 %copy-start.8 = (bf16[8,256]{1,0:T(8,128)(2,1)S(1)}, bf16[8,256]{1,0:T(8,128)(2,1)}, u32[]{:S(2)}) copy-start(bf16[8,256]{1,0:T(8,128)(2,1)} %nv_ref.1) | copy-start | bytes 12292
  0.0 3.9 %copy-start.3 = (bf16[4,512,256]{2,1,0:T(8,128)(2,1)S(1)}, bf16[4,512,256]{2,1,0:T(8,128)(2,1)}, u32[]{:S(2)}) copy-start(bf16[4,512,256]{2,1,0:T(8,128)(2,1)} %ck_ref.1) | copy-start | bytes 3145732
  0.0 3.9 %copy-start.4 = (bf16[4,512,256]{2,1,0:T(8,128)(2,1)S(1)}, bf16[4,512,256]{2,1,0:T(8,128)(2,1)}, u32[]{:S(2)}) copy-start(bf16[4,512,256]{2,1,0:T(8,128)(2,1)} %cv_ref.1) | copy-start | bytes 3145732
  0.0 3.9 %copy-start.9 = (s32[4]{0:T(128)S(1)}, s32[4]{0:T(128)}, u32[]{:S(2)}) copy-start(s32[4]{0:T(128)} %lens_ref.1) | copy-start | bytes 52
  0.0 8.1 %collective-permute-start = (bf16[64,1280]{1,0:T(8,128)(2,1)}, bf16[64,1280]{1,0:T(8,128)(2,1)S(1)}, u32[]{:S(2)}, u32[]{:S(2)}) collective-permute-start(bf16[64,1280]{1,0:T(8,128)(2,1)} %refs_0_), channel_id=1, source_target_pairs={{0,2},{1,3},{2,0},{3,1},{4,6},{5,7},{6,4},{7,5},{8,10},{9,11},{10,... | collective-permute-start | bytes 491528 | tf_op jit(solution)/shard_map/ppermute | solution.py:255
  3.0 5.2 %slice-start = ((s8[5242880]{0:T(1024)(128)(4,1)}), s8[4194304]{0:T(1024)(128)(4,1)S(1)}, s32[]{:S(2)}) async-start(s8[5242880]{0:T(1024)(128)(4,1)} %bitcast.1), calls=%async_computation | async-start | bytes 8388608
  3.8 4.4 %slice-start.1 = ((s8[5242880]{0:T(1024)(128)(4,1)}), s8[1048576]{0:T(1024)(128)(4,1)S(1)}, s32[]{:S(2)}) async-start(s8[5242880]{0:T(1024)(128)(4,1)} %bitcast.1), calls=%async_computation.1 | async-start | bytes 2097152
  3.9 1.4 %copy-start.5 = (bf16[64,1280]{1,0:T(8,128)(2,1)S(1)}, bf16[64,1280]{1,0:T(8,128)(2,1)}, u32[]{:S(2)}) copy-start(bf16[64,1280]{1,0:T(8,128)(2,1)} %refs_0_) | copy-start | bytes 491524
  5.3 4.1 %copy-start.1 = (bf16[2,256]{1,0:T(2,128)(2,1)S(1)}, bf16[2,256]{1,0:T(2,128)(2,1)}, u32[]{:S(2)}) copy-start(bf16[2,256]{1,0:T(2,128)(2,1)} %refs_4_.1) | copy-start | bytes 3076
  5.3 2.9 %collective-permute-start.2 = (bf16[64,1280]{1,0:T(8,128)(2,1)S(1)}, bf16[64,1280]{1,0:T(8,128)(2,1)S(1)}, u32[]{:S(2)}, u32[]{:S(2)}) collective-permute-start(bf16[64,1280]{1,0:T(8,128)(2,1)S(1)} %copy-done.5), channel_id=1, source_target_pairs={{0,1},{1,0},{2,3},{3,2},{4,5},{5,4},{6,7},{7,6},{8,9},{9,8},{10,11... | collective-permute-start | bytes 491528 | tf_op jit(solution)/shard_map/ppermute | solution.py:255
  5.4 6.7 %collective-permute-start.5 = (bf16[176,128]{1,0:T(8,128)(2,1)S(1)}, bf16[176,128]{1,0:T(8,128)(2,1)S(1)}, u32[]{:S(2)}, u32[]{:S(2)}) collective-permute-start(bf16[176,128]{1,0:T(8,128)(2,1)S(1)} %shard_map.120.near_ref), channel_id=1, source_target_pairs={{0,8},{4,12},{8,0},{12,4},{1,9},{5,13},{9,1},{13,5},{2,10},{6,14},... | collective-permute-start | bytes 135176 | tf_op jit(solution)/shard_map/ppermute | solution.py:255
  8.1 1.4 %collective-permute-start.1 = (bf16[64,1280]{1,0:T(8,128)(2,1)S(1)}, bf16[64,1280]{1,0:T(8,128)(2,1)S(1)}, u32[]{:S(2)}, u32[]{:S(2)}) collective-permute-start(bf16[64,1280]{1,0:T(8,128)(2,1)S(1)} %collective-permute-done.refs_2_), channel_id=1, source_target_pairs={{0,1},{1,0},{2,3},{3,2},{4,5},{5,4},{6,7},{7,6},{8,9},{9,8},{10,11... | collective-permute-start | bytes 491528 | tf_op jit(solution)/shard_map/ppermute | solution.py:255
  9.9 8.1 %copy-start.2 = (s32[256]{0:T(256)S(1)}, s32[256]{0:T(256)}, u32[]{:S(2)}) copy-start(s32[256]{0:T(256)} %param.15) | copy-start | bytes 3076
  9.9 10.9 %copy-start = (bf16[1280,1280]{1,0:T(8,128)(2,1)S(1)}, bf16[1280,1280]{1,0:T(8,128)(2,1)}, u32[]{:S(2)}) copy-start(bf16[1280,1280]{1,0:T(8,128)(2,1)} %refs_8_.1) | copy-start | bytes 9830404
  9.9 6.6 %collective-permute-start.4 = (bf16[128,256]{1,0:T(8,128)(2,1)S(1)}, bf16[128,256]{1,0:T(8,128)(2,1)S(1)}, u32[]{:S(2)}, u32[]{:S(2)}) collective-permute-start(bf16[128,256]{1,0:T(8,128)(2,1)S(1)} %shard_map.122.after.refs_0_), channel_id=1, source_target_pairs={{0,8},{4,12},{8,0},{12,4},{1,9},{5,13},{9,1},{13,5},{2,10},{6,14},... | collective-permute-start | bytes 196616 | tf_op jit(solution)/shard_map/ppermute | solution.py:255
  12.2 5.8 %collective-permute-start.7 = (bf16[2,176,128]{2,1,0:T(8,128)(2,1)S(1)}, bf16[2,176,128]{2,1,0:T(8,128)(2,1)S(1)}, u32[]{:S(2)}, u32[]{:S(2)}) collective-permute-start(bf16[2,176,128]{2,1,0:T(8,128)(2,1)S(1)} %shard_map.123.refs_0_), channel_id=1, source_target_pairs={{0,4},{4,0},{8,12},{12,8},{1,5},{5,1},{9,13},{13,9},{2,6},{6,2},{1... | collective-permute-start | bytes 270344 | tf_op jit(solution)/shard_map/ppermute | solution.py:255
  13.8 5.4 %collective-permute-start.3 = (bf16[128,256]{1,0:T(8,128)(2,1)S(1)}, bf16[128,256]{1,0:T(8,128)(2,1)S(1)}, u32[]{:S(2)}, u32[]{:S(2)}) collective-permute-start(bf16[128,256]{1,0:T(8,128)(2,1)S(1)} %shard_map.122.after.refs_0_), channel_id=1, source_target_pairs={{0,4},{4,0},{8,12},{12,8},{1,5},{5,1},{9,13},{13,9},{2,6},{6,2},{1... | collective-permute-start | bytes 196616 | tf_op jit(solution)/shard_map/ppermute | solution.py:255
  16.5 4.3 %collective-permute-start.6 = (bf16[128,256]{1,0:T(8,128)(2,1)S(1)}, bf16[128,256]{1,0:T(8,128)(2,1)S(1)}, u32[]{:S(2)}, u32[]{:S(2)}) collective-permute-start(bf16[128,256]{1,0:T(8,128)(2,1)S(1)} %collective-permute-done.4.refs_2_), channel_id=1, source_target_pairs={{0,4},{4,0},{8,12},{12,8},{1,5},{5,1},{9,13},{13,9},{2,6},{6,2},{1... | collective-permute-start | bytes 196616 | tf_op jit(solution)/shard_map/ppermute | solution.py:255
  22.1 3.3 %collective-permute-start.10 = (bf16[8,1280]{1,0:T(8,128)(2,1)S(1)}, bf16[8,1280]{1,0:T(8,128)(2,1)S(1)}, u32[]{:S(2)}, u32[]{:S(2)}) collective-permute-start(bf16[8,1280]{1,0:T(8,128)(2,1)S(1)} %get-tuple-element.42), channel_id=1, source_target_pairs={{0,3},{1,2},{2,1},{3,0},{4,7},{5,6},{6,5},{7,4},{8,11},{9,10},{10,... | collective-permute-start | bytes 61448 | tf_op jit(solution)/shard_map/ppermute | solution.py:255
  22.1 3.9 %collective-permute-start.8 = (bf16[8,1280]{1,0:T(8,128)(2,1)S(1)}, bf16[8,1280]{1,0:T(8,128)(2,1)S(1)}, u32[]{:S(2)}, u32[]{:S(2)}) collective-permute-start(bf16[8,1280]{1,0:T(8,128)(2,1)S(1)} %get-tuple-element.40), channel_id=1, source_target_pairs={{0,2},{1,3},{2,0},{3,1},{4,6},{5,7},{6,4},{7,5},{8,10},{9,11},{10,... | collective-permute-start | bytes 61448 | tf_op jit(solution)/shard_map/ppermute | solution.py:255
  23.0 3.1 %collective-permute-start.9 = (bf16[8,1280]{1,0:T(8,128)(2,1)S(1)}, bf16[8,1280]{1,0:T(8,128)(2,1)S(1)}, u32[]{:S(2)}, u32[]{:S(2)}) collective-permute-start(bf16[8,1280]{1,0:T(8,128)(2,1)S(1)} %get-tuple-element.41), channel_id=1, source_target_pairs={{0,1},{1,0},{2,3},{3,2},{4,5},{5,4},{6,7},{7,6},{8,9},{9,8},{10,11... | collective-permute-start | bytes 61448 | tf_op jit(solution)/shard_map/ppermute | solution.py:255

commit v16 on v14

--- a/solution.py
+++ b/solution.py
@@ -307,12 +307,13 @@
     group, gate = lax.optimization_barrier((group_sections, gate))
     section = call(open_kernel, [SMEM, ANY], pltpu.VMEM((8, HD), f32), [], 1 << 10, 0)(group, gate)
     own, section = lax.optimization_barrier((memory_hidden, section))
+    weight, section = lax.optimization_barrier((kv_weight, section))
     part = call(
         cache_kernel,
         [SMEM] + [VMEM] * 6,
         pltpu.VMEM((2 * up(rows, 16) + STATS, HD), bf16),
         [],
-        4 * rows * slots * cols * requests,
+        COVER,
         4 * requests * slots * cols,
     )(cache_lengths, section, queries, new_keys, new_values, cache_keys, cache_values)
     own_later, part = lax.optimization_barrier((own, part))
@@ -326,7 +327,7 @@
         [],
         COVER,
         4 * D * cols,
-    )(*[hidden[k] for k in near], kv_weight)
+    )(*[hidden[k] for k in near], weight)
     kv = call(
         functools.partial(project_kernel, far, False, True),
         [VMEM] * 5,
@@ -334,7 +335,7 @@
         [],
         4 * memory * D * cols // shares,
         4 * D * cols // shares,
-    )(hidden[far[0]], kv_weight, *partial, kv_bias)
+    )(hidden[far[0]], weight, *partial, kv_bias)
     kv_far = permute(kv, "dp", groups // 2)
     pair = call(
         pair_kernel,

time: 27 us -> 26.8 us (level)
  no operation moved by 1% of the time
where the time goes in v16:
time: 26.8 us; the launch traced here: 26.7 us
  starting transfers between devices  12.7 us (47%)
  waiting for transfers between devices  7.98 us (30%)
  Pallas kernels  4.3 us (16%)
  between operations  0.98 us (4%)
  other arithmetic  0.62 us (2%)
    ppermute x11, starting transfers between devices, permute(): lax.ppermute(x, axis, [(i, i ^ bits) for i in range(lax.axis_size(axis))])  12.7 us
    ppermute x11, waiting for transfers between devices, permute(): lax.ppermute(x, axis, [(i, i ^ bits) for i in range(lax.axis_size(axis))])  7.98 us
    pallas_call x1, Pallas kernels, body(): call(cache_kernel, [SMEM] + [VMEM] * 6, pltpu.VMEM((2 * up(rows, 16) + ST...  1.38 us
    pallas_call x1, Pallas kernels, body(): call(functools.partial(attend_kernel, groups, shares), [VMEM] * (groups +...  1.25 us
    pallas_call x1, Pallas kernels, body(): call(functools.partial(project_kernel, near, True, False), [VMEM] * (len(...  0.82 us
    convert_element_type x1, other arithmetic, body(): return summed.astype(bf16)  0.62 us
  transfers between devices with their start and end apart: 11, of which 7 were waited for; matrix products, arithmetic and copies ran while one was open for 0% of the time, Pallas kernels for 11%

profile of v16, /device:TPU:0, one launch (start us, length us, event | category | flops | bytes accessed | tf_op | source)
XLA Modules:
  0.0 26.7 jit_solution(13855053329093513782)
XLA Ops:
  0.0 0.0 copy-start.6
  0.0 0.0 copy-start.7
  0.0 0.0 copy-start.8
  0.0 0.0 copy-start.9
  0.0 3.0 %collective-permute-start = (bf16[64,1280]{1,0:T(8,128)(2,1)}, bf16[64,1280]{1,0:T(8,128)(2,1)S(1)}, u32[]{:S(2)}, u32[]{:S(2)}) collective-permute-start(bf16[64,1280]{1,0:T(8,128)(2,1)} %refs_0_), channel_id=1, source_target_pairs={{0,2},{1,3},{2,0},{3,1},{4,6},{5,7},{6,4},{7,5},{8,10},{9,11},{10,... | collective-permute-start | bytes 491528 | tf_op jit(solution)/shard_map/ppermute | solution.py:270
  3.8 0.0 slice-start.1
  3.9 0.0 copy-done.6
  3.9 0.0 copy-done.7
  3.9 0.0 copy-done.8
  3.9 0.0 copy-done.3
  3.9 0.0 copy-done.4
  3.9 0.0 copy-done.9
  3.9 0.0 copy-start.5
  3.9 1.4 %shard_map.120.near_ref = bf16[176,128]{1,0:T(8,128)(2,1)S(1)} custom-call(s32[4]{0:T(128)S(1)} %copy-done.9, f32[8,128]{1,0:T(8,128)S(1)} %shard_map.119.section_ref, bf16[8,1280]{1,0:T(8,128)(2,1)S(1)} %copy-done.6, bf16[8,256]{1,0:T(8,128)(2,1)S(1)} %copy-done.7, bf16[8,256]{1,0:T(8,128)(2,1)S(1)} %copy-done.8, bf16[4,512,256]{2,1,0:T(8,128)(2,1)S(1)} %copy-done.3, ...), custom_call_target="tpu_custom_call" | custom-call | flops 68719476736 | bytes 2097152 | tf_op jit(solution)/shard_map/pallas_call | solution.py:311
  5.3 0.0 copy-done.5
  5.3 0.0 copy-start.1
  5.3 0.1 collective-permute-start.2
  5.4 2.7 %collective-permute-start.5 = (bf16[176,128]{1,0:T(8,128)(2,1)S(1)}, bf16[176,128]{1,0:T(8,128)(2,1)S(1)}, u32[]{:S(2)}, u32[]{:S(2)}) collective-permute-start(bf16[176,128]{1,0:T(8,128)(2,1)S(1)} %shard_map.120.near_ref), channel_id=1, source_target_pairs={{0,8},{4,12},{8,0},{12,4},{1,9},{5,13},{9,1},{13,5},{2,10},{6,14},... | collective-permute-start | bytes 135176 | tf_op jit(solution)/shard_map/ppermute | solution.py:270
  8.1 0.0 collective-permute-done.refs_2_
  8.1 0.2 collective-permute-start.1
  8.3 0.0 collective-permute-done.2.refs_1_
  8.3 0.0 slice-done
  8.3 0.0 slice-done.1
  8.3 0.8 %shard_map.121 = (f32[128,256]{1,0:T(8,128)S(1)}, f32[64,128]{1,0:T(8,128)S(1)}) custom-call(bf16[64,1280]{1,0:T(8,128)(2,1)S(1)} %copy-done.5, bf16[64,1280]{1,0:T(8,128)(2,1)S(1)} %collective-permute-done.2.refs_1_, bf16[64,1280]{1,0:T(8,128)(2,1)S(1)} %collective-permute-done.refs_2_, bf16[2,5120,256]{2,1,0:T(8,128)(2,1)S(1)} %bitcast.2), custom_call_target="tpu_custom_call" | custom-call | flops 68719476736 | bytes 5242880 | tf_op jit(solution)/shard_map/pallas_call | solution.py:323
  9.1 0.4 %collective-permute-done.1.refs_0_ = bf16[64,1280]{1,0:T(8,128)(2,1)S(1)} collective-permute-done((bf16[64,1280]{1,0:T(8,128)(2,1)S(1)}, bf16[64,1280]{1,0:T(8,128)(2,1)S(1)}, u32[]{:S(2)}, u32[]{:S(2)}) %collective-permute-start.1) | collective-permute-done | bytes 163872 | tf_op jit(solution)/shard_map/ppermute | solution.py:270
  9.5 0.0 copy-done.1
  9.5 0.4 %shard_map.122.after.refs_0_ = bf16[128,256]{1,0:T(8,128)(2,1)S(1)} custom-call(bf16[64,1280]{1,0:T(8,128)(2,1)S(1)} %collective-permute-done.1.refs_0_, bf16[2,5120,256]{2,1,0:T(8,128)(2,1)S(1)} %bitcast.2, f32[128,256]{1,0:T(8,128)S(1)} %get-tuple-element.31.refs_2_, f32[64,128]{1,0:T(8,128)S(1)} %get-tuple-element.32.refs_3_, bf16[2,256]{1,0:T(2,128)(2,1)S(1)} %copy-done.1), custom_call_target="tpu_custom_call" | custom-call | flops 83886080 | bytes 1310720 | tf_op jit(solution)/shard_map/pallas_call | solution.py:331
  9.9 0.0 copy-start
  9.9 2.3 %collective-permute-start.4 = (bf16[128,256]{1,0:T(8,128)(2,1)S(1)}, bf16[128,256]{1,0:T(8,128)(2,1)S(1)}, u32[]{:S(2)}, u32[]{:S(2)}) collective-permute-start(bf16[128,256]{1,0:T(8,128)(2,1)S(1)} %shard_map.122.after.refs_0_), channel_id=1, source_target_pairs={{0,8},{4,12},{8,0},{12,4},{1,9},{5,13},{9,1},{13,5},{2,10},{6,14},... | collective-permute-start | bytes 196616 | tf_op jit(solution)/shard_map/ppermute | solution.py:270
  12.2 0.0 collective-permute-done.5.far_ref
  12.2 1.6 %collective-permute-start.7 = (bf16[2,176,128]{2,1,0:T(8,128)(2,1)S(1)}, bf16[2,176,128]{2,1,0:T(8,128)(2,1)S(1)}, u32[]{:S(2)}, u32[]{:S(2)}) collective-permute-start(bf16[2,176,128]{2,1,0:T(8,128)(2,1)S(1)} %shard_map.123.refs_0_), channel_id=1, source_target_pairs={{0,4},{4,0},{8,12},{12,8},{1,5},{5,1},{9,13},{13,9},{2,6},{6,2},{1... | collective-permute-start | bytes 270344 | tf_op jit(solution)/shard_map/ppermute | solution.py:270
  13.8 0.4 %collective-permute-start.3 = (bf16[128,256]{1,0:T(8,128)(2,1)S(1)}, bf16[128,256]{1,0:T(8,128)(2,1)S(1)}, u32[]{:S(2)}, u32[]{:S(2)}) collective-permute-start(bf16[128,256]{1,0:T(8,128)(2,1)S(1)} %shard_map.122.after.refs_0_), channel_id=1, source_target_pairs={{0,4},{4,0},{8,12},{12,8},{1,5},{5,1},{9,13},{13,9},{2,6},{6,2},{1... | collective-permute-start | bytes 196616 | tf_op jit(solution)/shard_map/ppermute | solution.py:270
  14.3 2.3 %collective-permute-done.4.refs_2_ = bf16[128,256]{1,0:T(8,128)(2,1)S(1)} collective-permute-done((bf16[128,256]{1,0:T(8,128)(2,1)S(1)}, bf16[128,256]{1,0:T(8,128)(2,1)S(1)}, u32[]{:S(2)}, u32[]{:S(2)}) %collective-permute-start.4) | collective-permute-done | bytes 65568 | tf_op jit(solution)/shard_map/ppermute | solution.py:270
  16.5 0.5 %collective-permute-start.6 = (bf16[128,256]{1,0:T(8,128)(2,1)S(1)}, bf16[128,256]{1,0:T(8,128)(2,1)S(1)}, u32[]{:S(2)}, u32[]{:S(2)}) collective-permute-start(bf16[128,256]{1,0:T(8,128)(2,1)S(1)} %collective-permute-done.4.refs_2_), channel_id=1, source_target_pairs={{0,4},{4,0},{8,12},{12,8},{1,5},{5,1},{9,13},{13,9},{2,6},{6,2},{1... | collective-permute-start | bytes 196616 | tf_op jit(solution)/shard_map/ppermute | solution.py:270
  17.1 0.9 %collective-permute-done.7.refs_1_ = bf16[2,176,128]{2,1,0:T(8,128)(2,1)S(1)} collective-permute-done((bf16[2,176,128]{2,1,0:T(8,128)(2,1)S(1)}, bf16[2,176,128]{2,1,0:T(8,128)(2,1)S(1)}, u32[]{:S(2)}, u32[]{:S(2)}) %collective-permute-start.7) | collective-permute-done | bytes 90144 | tf_op jit(solution)/shard_map/ppermute | solution.py:270
  18.0 0.0 copy-done.2
  18.0 0.5 %shard_map.124 = (bf16[320,128]{1,0:T(8,128)(2,1)S(1)}, f32[160,256]{1,0:T(8,128)S(1)}, f32[320,128]{1,0:T(8,128)S(1)}, f32[320,128]{1,0:T(8,128)S(1)}) custom-call(bf16[2,176,128]{2,1,0:T(8,128)(2,1)S(1)} %shard_map.123.refs_0_, bf16[2,176,128]{2,1,0:T(8,128)(2,1)S(1)} %collective-permute-done.7.refs_1_, s32[1,256]{1,0:T(1,128)S(1)} %bitcast.3), custom_call_target="tpu_custom_call" | custom-call | flops 1024 | tf_op jit(solution)/shard_map/pallas_call | solution.py:353
  18.4 0.8 %collective-permute-done.3.refs_1_ = bf16[128,256]{1,0:T(8,128)(2,1)S(1)} collective-permute-done((bf16[128,256]{1,0:T(8,128)(2,1)S(1)}, bf16[128,256]{1,0:T(8,128)(2,1)S(1)}, u32[]{:S(2)}, u32[]{:S(2)}) %collective-permute-start.3) | collective-permute-done | bytes 65568 | tf_op jit(solution)/shard_map/ppermute | solution.py:270
  19.3 1.5 %collective-permute-done.6.refs_3_ = bf16[128,256]{1,0:T(8,128)(2,1)S(1)} collective-permute-done((bf16[128,256]{1,0:T(8,128)(2,1)S(1)}, bf16[128,256]{1,0:T(8,128)(2,1)S(1)}, u32[]{:S(2)}, u32[]{:S(2)}) %collective-permute-start.6) | collective-permute-done | bytes 65568 | tf_op jit(solution)/shard_map/ppermute | solution.py:270
  20.8 0.0 copy-done
  20.8 1.2 %shard_map.125 = (f32[8,1280]{1,0:T(8,128)S(1)}, bf16[8,1280]{1,0:T(8,128)(2,1)S(1)}, bf16[8,1280]{1,0:T(8,128)(2,1)S(1)}, bf16[8,1280]{1,0:T(8,128)(2,1)S(1)}) custom-call(bf16[128,256]{1,0:T(8,128)(2,1)S(1)} %shard_map.122.after.refs_0_, bf16[128,256]{1,0:T(8,128)(2,1)S(1)} %collective-permute-done.3.refs_1_, ...), custom_call_target="tpu_custom_call" | custom-call | flops 104857600 | bytes 3276800 | tf_op jit(solution)/shard_map/pallas_call | solution.py:369
  22.0 0.1 collective-permute-start.10
  22.1 0.9 %collective-permute-start.8 = (bf16[8,1280]{1,0:T(8,128)(2,1)S(1)}, bf16[8,1280]{1,0:T(8,128)(2,1)S(1)}, u32[]{:S(2)}, u32[]{:S(2)}) collective-permute-start(bf16[8,1280]{1,0:T(8,128)(2,1)S(1)} %get-tuple-element.40), channel_id=1, source_target_pairs={{0,2},{1,3},{2,0},{3,1},{4,6},{5,7},{6,4},{7,5},{8,10},{9,11},{10,... | collective-permute-start | bytes 61448 | tf_op jit(solution)/shard_map/ppermute | solution.py:270
  23.0 1.0 %collective-permute-start.9 = (bf16[8,1280]{1,0:T(8,128)(2,1)S(1)}, bf16[8,1280]{1,0:T(8,128)(2,1)S(1)}, u32[]{:S(2)}, u32[]{:S(2)}) collective-permute-start(bf16[8,1280]{1,0:T(8,128)(2,1)S(1)} %get-tuple-element.41), channel_id=1, source_target_pairs={{0,1},{1,0},{2,3},{3,2},{4,5},{5,4},{6,7},{7,6},{8,9},{9,8},{10,11... | collective-permute-start | bytes 61448 | tf_op jit(solution)/shard_map/ppermute | solution.py:270
  24.0 1.3 %collective-permute-done.10 = bf16[8,1280]{1,0:T(8,128)(2,1)S(1)} collective-permute-done((bf16[8,1280]{1,0:T(8,128)(2,1)S(1)}, bf16[8,1280]{1,0:T(8,128)(2,1)S(1)}, u32[]{:S(2)}, u32[]{:S(2)}) %collective-permute-start.10) | collective-permute-done | bytes 20512 | tf_op jit(solution)/shard_map/ppermute | solution.py:270
  25.3 0.7 %collective-permute-done.8 = bf16[8,1280]{1,0:T(8,128)(2,1)S(1)} collective-permute-done((bf16[8,1280]{1,0:T(8,128)(2,1)S(1)}, bf16[8,1280]{1,0:T(8,128)(2,1)S(1)}, u32[]{:S(2)}, u32[]{:S(2)}) %collective-permute-start.8) | collective-permute-done | bytes 20512 | tf_op jit(solution)/shard_map/ppermute | solution.py:270
  26.0 0.0 collective-permute-done.9
  26.1 0.6 %add_convert_fusion = bf16[8,1280]{1,0:T(8,128)(2,1)} fusion(bf16[8,1280]{1,0:T(8,128)(2,1)S(1)} %collective-permute-done.10, bf16[8,1280]{1,0:T(8,128)(2,1)S(1)} %collective-permute-done.9, f32[8,1280]{1,0:T(8,128)S(1)} %get-tuple-element.39, bf16[8,1280]{1,0:T(8,128)(2,1)S(1)} %collective-permute-done.8), kind=kLoop, calls=%fused_computation | loop fusion | flops 71680 | bytes 122880 | tf_op jit(solution)/shard_map/convert_element_type | solution.py:383
  (8 shorter events, 0.0 us)
Async XLA Ops:
  0.0 3.9 %copy-start.6 = (bf16[8,1280]{1,0:T(8,128)(2,1)S(1)}, bf16[8,1280]{1,0:T(8,128)(2,1)}, u32[]{:S(2)}) copy-start(bf16[8,1280]{1,0:T(8,128)(2,1)} %q_ref.1) | copy-start | bytes 61444
  0.0 3.9 %copy-start.7 = (bf16[8,256]{1,0:T(8,128)(2,1)S(1)}, bf16[8,256]{1,0:T(8,128)(2,1)}, u32[]{:S(2)}) copy-start(bf16[8,256]{1,0:T(8,128)(2,1)} %nk_ref.1) | copy-start | bytes 12292
  0.0 3.9 %copy-start.8 = (bf16[8,256]{1,0:T(8,128)(2,1)S(1)}, bf16[8,256]{1,0:T(8,128)(2,1)}, u32[]{:S(2)}) copy-start(bf16[8,256]{1,0:T(8,128)(2,1)} %nv_ref.1) | copy-start | bytes 12292
  0.0 3.9 %copy-start.3 = (bf16[4,512,256]{2,1,0:T(8,128)(2,1)S(1)}, bf16[4,512,256]{2,1,0:T(8,128)(2,1)}, u32[]{:S(2)}) copy-start(bf16[4,512,256]{2,1,0:T(8,128)(2,1)} %ck_ref.1) | copy-start | bytes 3145732
  0.0 3.9 %copy-start.4 = (bf16[4,512,256]{2,1,0:T(8,128)(2,1)S(1)}, bf16[4,512,256]{2,1,0:T(8,128)(2,1)}, u32[]{:S(2)}) copy-start(bf16[4,512,256]{2,1,0:T(8,128)(2,1)} %cv_ref.1) | copy-start | bytes 3145732
  0.0 3.9 %copy-start.9 = (s32[4]{0:T(128)S(1)}, s32[4]{0:T(128)}, u32[]{:S(2)}) copy-start(s32[4]{0:T(128)} %lens_ref.1) | copy-start | bytes 52
  0.0 8.1 %collective-permute-start = (bf16[64,1280]{1,0:T(8,128)(2,1)}, bf16[64,1280]{1,0:T(8,128)(2,1)S(1)}, u32[]{:S(2)}, u32[]{:S(2)}) collective-permute-start(bf16[64,1280]{1,0:T(8,128)(2,1)} %refs_0_), channel_id=1, source_target_pairs={{0,2},{1,3},{2,0},{3,1},{4,6},{5,7},{6,4},{7,5},{8,10},{9,11},{10,... | collective-permute-start | bytes 491528 | tf_op jit(solution)/shard_map/ppermute | solution.py:270
  3.0 5.2 %slice-start = ((s8[5242880]{0:T(1024)(128)(4,1)}), s8[4194304]{0:T(1024)(128)(4,1)S(1)}, s32[]{:S(2)}) async-start(s8[5242880]{0:T(1024)(128)(4,1)} %bitcast.1), calls=%async_computation | async-start | bytes 8388608
  3.8 4.4 %slice-start.1 = ((s8[5242880]{0:T(1024)(128)(4,1)}), s8[1048576]{0:T(1024)(128)(4,1)S(1)}, s32[]{:S(2)}) async-start(s8[5242880]{0:T(1024)(128)(4,1)} %bitcast.1), calls=%async_computation.1 | async-start | bytes 2097152
  3.9 1.4 %copy-start.5 = (bf16[64,1280]{1,0:T(8,128)(2,1)S(1)}, bf16[64,1280]{1,0:T(8,128)(2,1)}, u32[]{:S(2)}) copy-start(bf16[64,1280]{1,0:T(8,128)(2,1)} %refs_0_) | copy-start | bytes 491524
  5.3 4.1 %copy-start.1 = (bf16[2,256]{1,0:T(2,128)(2,1)S(1)}, bf16[2,256]{1,0:T(2,128)(2,1)}, u32[]{:S(2)}) copy-start(bf16[2,256]{1,0:T(2,128)(2,1)} %refs_4_.1) | copy-start | bytes 3076
  5.3 2.9 %collective-permute-start.2 = (bf16[64,1280]{1,0:T(8,128)(2,1)S(1)}, bf16[64,1280]{1,0:T(8,128)(2,1)S(1)}, u32[]{:S(2)}, u32[]{:S(2)}) collective-permute-start(bf16[64,1280]{1,0:T(8,128)(2,1)S(1)} %copy-done.5), channel_id=1, source_target_pairs={{0,1},{1,0},{2,3},{3,2},{4,5},{5,4},{6,7},{7,6},{8,9},{9,8},{10,11... | collective-permute-start | bytes 491528 | tf_op jit(solution)/shard_map/ppermute | solution.py:270
  5.4 6.7 %collective-permute-start.5 = (bf16[176,128]{1,0:T(8,128)(2,1)S(1)}, bf16[176,128]{1,0:T(8,128)(2,1)S(1)}, u32[]{:S(2)}, u32[]{:S(2)}) collective-permute-start(bf16[176,128]{1,0:T(8,128)(2,1)S(1)} %shard_map.120.near_ref), channel_id=1, source_target_pairs={{0,8},{4,12},{8,0},{12,4},{1,9},{5,13},{9,1},{13,5},{2,10},{6,14},... | collective-permute-start | bytes 135176 | tf_op jit(solution)/shard_map/ppermute | solution.py:270
  8.1 1.4 %collective-permute-start.1 = (bf16[64,1280]{1,0:T(8,128)(2,1)S(1)}, bf16[64,1280]{1,0:T(8,128)(2,1)S(1)}, u32[]{:S(2)}, u32[]{:S(2)}) collective-permute-start(bf16[64,1280]{1,0:T(8,128)(2,1)S(1)} %collective-permute-done.refs_2_), channel_id=1, source_target_pairs={{0,1},{1,0},{2,3},{3,2},{4,5},{5,4},{6,7},{7,6},{8,9},{9,8},{10,11... | collective-permute-start | bytes 491528 | tf_op jit(solution)/shard_map/ppermute | solution.py:270
  9.9 8.1 %copy-start.2 = (s32[256]{0:T(256)S(1)}, s32[256]{0:T(256)}, u32[]{:S(2)}) copy-start(s32[256]{0:T(256)} %param.15) | copy-start | bytes 3076
  9.9 10.9 %copy-start = (bf16[1280,1280]{1,0:T(8,128)(2,1)S(1)}, bf16[1280,1280]{1,0:T(8,128)(2,1)}, u32[]{:S(2)}) copy-start(bf16[1280,1280]{1,0:T(8,128)(2,1)} %refs_8_.1) | copy-start | bytes 9830404
  9.9 6.6 %collective-permute-start.4 = (bf16[128,256]{1,0:T(8,128)(2,1)S(1)}, bf16[128,256]{1,0:T(8,128)(2,1)S(1)}, u32[]{:S(2)}, u32[]{:S(2)}) collective-permute-start(bf16[128,256]{1,0:T(8,128)(2,1)S(1)} %shard_map.122.after.refs_0_), channel_id=1, source_target_pairs={{0,8},{4,12},{8,0},{12,4},{1,9},{5,13},{9,1},{13,5},{2,10},{6,14},... | collective-permute-start | bytes 196616 | tf_op jit(solution)/shard_map/ppermute | solution.py:270
  12.2 5.8 %collective-permute-start.7 = (bf16[2,176,128]{2,1,0:T(8,128)(2,1)S(1)}, bf16[2,176,128]{2,1,0:T(8,128)(2,1)S(1)}, u32[]{:S(2)}, u32[]{:S(2)}) collective-permute-start(bf16[2,176,128]{2,1,0:T(8,128)(2,1)S(1)} %shard_map.123.refs_0_), channel_id=1, source_target_pairs={{0,4},{4,0},{8,12},{12,8},{1,5},{5,1},{9,13},{13,9},{2,6},{6,2},{1... | collective-permute-start | bytes 270344 | tf_op jit(solution)/shard_map/ppermute | solution.py:270
  13.8 5.4 %collective-permute-start.3 = (bf16[128,256]{1,0:T(8,128)(2,1)S(1)}, bf16[128,256]{1,0:T(8,128)(2,1)S(1)}, u32[]{:S(2)}, u32[]{:S(2)}) collective-permute-start(bf16[128,256]{1,0:T(8,128)(2,1)S(1)} %shard_map.122.after.refs_0_), channel_id=1, source_target_pairs={{0,4},{4,0},{8,12},{12,8},{1,5},{5,1},{9,13},{13,9},{2,6},{6,2},{1... | collective-permute-start | bytes 196616 | tf_op jit(solution)/shard_map/ppermute | solution.py:270
  16.5 4.3 %collective-permute-start.6 = (bf16[128,256]{1,0:T(8,128)(2,1)S(1)}, bf16[128,256]{1,0:T(8,128)(2,1)S(1)}, u32[]{:S(2)}, u32[]{:S(2)}) collective-permute-start(bf16[128,256]{1,0:T(8,128)(2,1)S(1)} %collective-permute-done.4.refs_2_), channel_id=1, source_target_pairs={{0,4},{4,0},{8,12},{12,8},{1,5},{5,1},{9,13},{13,9},{2,6},{6,2},{1... | collective-permute-start | bytes 196616 | tf_op jit(solution)/shard_map/ppermute | solution.py:270
  22.0 3.3 %collective-permute-start.10 = (bf16[8,1280]{1,0:T(8,128)(2,1)S(1)}, bf16[8,1280]{1,0:T(8,128)(2,1)S(1)}, u32[]{:S(2)}, u32[]{:S(2)}) collective-permute-start(bf16[8,1280]{1,0:T(8,128)(2,1)S(1)} %get-tuple-element.42), channel_id=1, source_target_pairs={{0,3},{1,2},{2,1},{3,0},{4,7},{5,6},{6,5},{7,4},{8,11},{9,10},{10,... | collective-permute-start | bytes 61448 | tf_op jit(solution)/shard_map/ppermute | solution.py:270
  22.1 3.9 %collective-permute-start.8 = (bf16[8,1280]{1,0:T(8,128)(2,1)S(1)}, bf16[8,1280]{1,0:T(8,128)(2,1)S(1)}, u32[]{:S(2)}, u32[]{:S(2)}) collective-permute-start(bf16[8,1280]{1,0:T(8,128)(2,1)S(1)} %get-tuple-element.40), channel_id=1, source_target_pairs={{0,2},{1,3},{2,0},{3,1},{4,6},{5,7},{6,4},{7,5},{8,10},{9,11},{10,... | collective-permute-start | bytes 61448 | tf_op jit(solution)/shard_map/ppermute | solution.py:270
  23.0 3.1 %collective-permute-start.9 = (bf16[8,1280]{1,0:T(8,128)(2,1)S(1)}, bf16[8,1280]{1,0:T(8,128)(2,1)S(1)}, u32[]{:S(2)}, u32[]{:S(2)}) collective-permute-start(bf16[8,1280]{1,0:T(8,128)(2,1)S(1)} %get-tuple-element.41), channel_id=1, source_target_pairs={{0,1},{1,0},{2,3},{3,2},{4,5},{5,4},{6,7},{7,6},{8,9},{9,8},{10,11... | collective-permute-start | bytes 61448 | tf_op jit(solution)/shard_map/ppermute | solution.py:270

commit v17 on v16

--- a/solution.py
+++ b/solution.py
@@ -243,6 +243,13 @@
         out[...] = sums_ref[pl.ds(at, share), :].astype(out.dtype)
 
 
+def sum_kernel(own_ref, *refs):
+    total = own_ref[...]
+    for ref in refs[:-1]:
+        total = total + ref[...].astype(f32)
+    refs[-1][...] = total.astype(bf16)
+
+
 SMEM = pl.BlockSpec(memory_space=pltpu.SMEM)
 VMEM = pl.BlockSpec(memory_space=pltpu.VMEM)
 ANY = pl.BlockSpec(memory_space=pl.ANY)
@@ -377,10 +384,16 @@
         2 * out_rows * out_weight.size,
         2 * out_weight.size,
     )(*kvs, *prepared, out_weight)
-    summed = pieces[0]
-    for bits in [*range(shares - 2, 0, -1), shares - 1]:
-        summed = summed + permute(pieces[bits], "tp", bits).astype(f32)
-    return summed.astype(bf16)
+    order = [*range(shares - 2, 0, -1), shares - 1]
+    arrived = [permute(pieces[bits], "tp", bits) for bits in order]
+    return call(
+        sum_kernel,
+        [VMEM] * shares,
+        jax.ShapeDtypeStruct((share, out_cols), bf16),
+        [],
+        shares * share * out_cols,
+        2 * shares * share * out_cols,
+    )(pieces[0], *arrived)
 
 
 def solution(mesh):

time: 26.8 us -> 26.8 us (level)
  Pallas kernels: 4.3 us -> 4.92 us
  other arithmetic: 0.62 us -> 0.01 us
    convert_element_type x1 -> x0, other arithmetic: 0.62 us -> none  [body(): return summed.astype(bf16)]
    pallas_call x0 -> x1, Pallas kernels: none -> 0.62 us  [body(): call(sum_kernel, [VMEM] * shares, jax.ShapeDtypeStruct((share, out_cols),...]
where the time goes in v17:
time: 26.8 us; the launch traced here: 26.7 us
  starting transfers between devices  12.7 us (47%)
  waiting for transfers between devices  7.98 us (30%)
  Pallas kernels  4.92 us (18%)
  between operations  0.98 us (4%)
    ppermute x11, starting transfers between devices, permute(): lax.ppermute(x, axis, [(i, i ^ bits) for i in range(lax.axis_size(axis))])  12.7 us
    ppermute x11, waiting for transfers between devices, permute(): lax.ppermute(x, axis, [(i, i ^ bits) for i in range(lax.axis_size(axis))])  7.98 us
    pallas_call x1, Pallas kernels, body(): call(cache_kernel, [SMEM] + [VMEM] * 6, pltpu.VMEM((2 * up(rows, 16) + ST...  1.38 us
    pallas_call x1, Pallas kernels, body(): call(functools.partial(attend_kernel, groups, shares), [VMEM] * (groups +...  1.25 us
    pallas_call x1, Pallas kernels, body(): call(functools.partial(project_kernel, near, True, False), [VMEM] * (len(...  0.82 us
    pallas_call x1, Pallas kernels, body(): call(sum_kernel, [VMEM] * shares, jax.ShapeDtypeStruct((share, out_cols),...  0.62 us
  transfers between devices with their start and end apart: 11, of which 7 were waited for; matrix products, arithmetic and copies ran while one was open for 0% of the time, Pallas kernels for 11%

profile of v17, /device:TPU:0, one launch (start us, length us, event | category | flops | bytes accessed | tf_op | source)
XLA Modules:
  0.0 26.7 jit_solution(7971719823058617426)
XLA Ops:
  0.0 0.0 copy-start.6
  0.0 0.0 copy-start.7
  0.0 0.0 copy-start.8
  0.0 0.0 copy-start.9
  0.0 3.0 %collective-permute-start = (bf16[64,1280]{1,0:T(8,128)(2,1)}, bf16[64,1280]{1,0:T(8,128)(2,1)S(1)}, u32[]{:S(2)}, u32[]{:S(2)}) collective-permute-start(bf16[64,1280]{1,0:T(8,128)(2,1)} %refs_0_), channel_id=1, source_target_pairs={{0,2},{1,3},{2,0},{3,1},{4,6},{5,7},{6,4},{7,5},{8,10},{9,11},{10,... | collective-permute-start | bytes 491528 | tf_op jit(solution)/shard_map/ppermute | solution.py:277
  3.8 0.0 slice-start.1
  3.9 0.0 copy-done.6
  3.9 0.0 copy-done.7
  3.9 0.0 copy-done.8
  3.9 0.0 copy-done.3
  3.9 0.0 copy-done.4
  3.9 0.0 copy-done.9
  3.9 0.0 copy-start.5
  3.9 1.4 %shard_map.120.near_ref = bf16[176,128]{1,0:T(8,128)(2,1)S(1)} custom-call(s32[4]{0:T(128)S(1)} %copy-done.9, f32[8,128]{1,0:T(8,128)S(1)} %shard_map.119.section_ref, bf16[8,1280]{1,0:T(8,128)(2,1)S(1)} %copy-done.6, bf16[8,256]{1,0:T(8,128)(2,1)S(1)} %copy-done.7, bf16[8,256]{1,0:T(8,128)(2,1)S(1)} %copy-done.8, bf16[4,512,256]{2,1,0:T(8,128)(2,1)S(1)} %copy-done.3, ...), custom_call_target="tpu_custom_call" | custom-call | flops 68719476736 | bytes 2097152 | tf_op jit(solution)/shard_map/pallas_call | solution.py:318
  5.3 0.0 copy-done.5
  5.3 0.0 copy-start.1
  5.3 0.1 collective-permute-start.2
  5.4 2.7 %collective-permute-start.5 = (bf16[176,128]{1,0:T(8,128)(2,1)S(1)}, bf16[176,128]{1,0:T(8,128)(2,1)S(1)}, u32[]{:S(2)}, u32[]{:S(2)}) collective-permute-start(bf16[176,128]{1,0:T(8,128)(2,1)S(1)} %shard_map.120.near_ref), channel_id=1, source_target_pairs={{0,8},{4,12},{8,0},{12,4},{1,9},{5,13},{9,1},{13,5},{2,10},{6,14},... | collective-permute-start | bytes 135176 | tf_op jit(solution)/shard_map/ppermute | solution.py:277
  8.1 0.0 collective-permute-done.refs_2_
  8.1 0.2 collective-permute-start.1
  8.3 0.0 collective-permute-done.2.refs_1_
  8.3 0.0 slice-done
  8.3 0.0 slice-done.1
  8.3 0.8 %shard_map.121 = (f32[128,256]{1,0:T(8,128)S(1)}, f32[64,128]{1,0:T(8,128)S(1)}) custom-call(bf16[64,1280]{1,0:T(8,128)(2,1)S(1)} %copy-done.5, bf16[64,1280]{1,0:T(8,128)(2,1)S(1)} %collective-permute-done.2.refs_1_, bf16[64,1280]{1,0:T(8,128)(2,1)S(1)} %collective-permute-done.refs_2_, bf16[2,5120,256]{2,1,0:T(8,128)(2,1)S(1)} %bitcast.2), custom_call_target="tpu_custom_call" | custom-call | flops 68719476736 | bytes 5242880 | tf_op jit(solution)/shard_map/pallas_call | solution.py:330
  9.1 0.4 %collective-permute-done.1.refs_0_ = bf16[64,1280]{1,0:T(8,128)(2,1)S(1)} collective-permute-done((bf16[64,1280]{1,0:T(8,128)(2,1)S(1)}, bf16[64,1280]{1,0:T(8,128)(2,1)S(1)}, u32[]{:S(2)}, u32[]{:S(2)}) %collective-permute-start.1) | collective-permute-done | bytes 163872 | tf_op jit(solution)/shard_map/ppermute | solution.py:277
  9.5 0.0 copy-done.1
  9.5 0.4 %shard_map.122.after.refs_0_ = bf16[128,256]{1,0:T(8,128)(2,1)S(1)} custom-call(bf16[64,1280]{1,0:T(8,128)(2,1)S(1)} %collective-permute-done.1.refs_0_, bf16[2,5120,256]{2,1,0:T(8,128)(2,1)S(1)} %bitcast.2, f32[128,256]{1,0:T(8,128)S(1)} %get-tuple-element.31.refs_2_, f32[64,128]{1,0:T(8,128)S(1)} %get-tuple-element.32.refs_3_, bf16[2,256]{1,0:T(2,128)(2,1)S(1)} %copy-done.1), custom_call_target="tpu_custom_call" | custom-call | flops 83886080 | bytes 1310720 | tf_op jit(solution)/shard_map/pallas_call | solution.py:338
  9.9 0.0 copy-start
  9.9 2.3 %collective-permute-start.4 = (bf16[128,256]{1,0:T(8,128)(2,1)S(1)}, bf16[128,256]{1,0:T(8,128)(2,1)S(1)}, u32[]{:S(2)}, u32[]{:S(2)}) collective-permute-start(bf16[128,256]{1,0:T(8,128)(2,1)S(1)} %shard_map.122.after.refs_0_), channel_id=1, source_target_pairs={{0,8},{4,12},{8,0},{12,4},{1,9},{5,13},{9,1},{13,5},{2,10},{6,14},... | collective-permute-start | bytes 196616 | tf_op jit(solution)/shard_map/ppermute | solution.py:277
  12.2 0.0 collective-permute-done.5.far_ref
  12.2 1.6 %collective-permute-start.7 = (bf16[2,176,128]{2,1,0:T(8,128)(2,1)S(1)}, bf16[2,176,128]{2,1,0:T(8,128)(2,1)S(1)}, u32[]{:S(2)}, u32[]{:S(2)}) collective-permute-start(bf16[2,176,128]{2,1,0:T(8,128)(2,1)S(1)} %shard_map.123.refs_0_), channel_id=1, source_target_pairs={{0,4},{4,0},{8,12},{12,8},{1,5},{5,1},{9,13},{13,9},{2,6},{6,2},{1... | collective-permute-start | bytes 270344 | tf_op jit(solution)/shard_map/ppermute | solution.py:277
  13.8 0.4 %collective-permute-start.3 = (bf16[128,256]{1,0:T(8,128)(2,1)S(1)}, bf16[128,256]{1,0:T(8,128)(2,1)S(1)}, u32[]{:S(2)}, u32[]{:S(2)}) collective-permute-start(bf16[128,256]{1,0:T(8,128)(2,1)S(1)} %shard_map.122.after.refs_0_), channel_id=1, source_target_pairs={{0,4},{4,0},{8,12},{12,8},{1,5},{5,1},{9,13},{13,9},{2,6},{6,2},{1... | collective-permute-start | bytes 196616 | tf_op jit(solution)/shard_map/ppermute | solution.py:277
  14.3 2.3 %collective-permute-done.4.refs_2_ = bf16[128,256]{1,0:T(8,128)(2,1)S(1)} collective-permute-done((bf16[128,256]{1,0:T(8,128)(2,1)S(1)}, bf16[128,256]{1,0:T(8,128)(2,1)S(1)}, u32[]{:S(2)}, u32[]{:S(2)}) %collective-permute-start.4) | collective-permute-done | bytes 65568 | tf_op jit(solution)/shard_map/ppermute | solution.py:277
  16.5 0.5 %collective-permute-start.6 = (bf16[128,256]{1,0:T(8,128)(2,1)S(1)}, bf16[128,256]{1,0:T(8,128)(2,1)S(1)}, u32[]{:S(2)}, u32[]{:S(2)}) collective-permute-start(bf16[128,256]{1,0:T(8,128)(2,1)S(1)} %collective-permute-done.4.refs_2_), channel_id=1, source_target_pairs={{0,4},{4,0},{8,12},{12,8},{1,5},{5,1},{9,13},{13,9},{2,6},{6,2},{1... | collective-permute-start | bytes 196616 | tf_op jit(solution)/shard_map/ppermute | solution.py:277
  17.1 0.9 %collective-permute-done.7.refs_1_ = bf16[2,176,128]{2,1,0:T(8,128)(2,1)S(1)} collective-permute-done((bf16[2,176,128]{2,1,0:T(8,128)(2,1)S(1)}, bf16[2,176,128]{2,1,0:T(8,128)(2,1)S(1)}, u32[]{:S(2)}, u32[]{:S(2)}) %collective-permute-start.7) | collective-permute-done | bytes 90144 | tf_op jit(solution)/shard_map/ppermute | solution.py:277
  18.0 0.0 copy-done.2
  18.0 0.5 %shard_map.124 = (bf16[320,128]{1,0:T(8,128)(2,1)S(1)}, f32[160,256]{1,0:T(8,128)S(1)}, f32[320,128]{1,0:T(8,128)S(1)}, f32[320,128]{1,0:T(8,128)S(1)}) custom-call(bf16[2,176,128]{2,1,0:T(8,128)(2,1)S(1)} %shard_map.123.refs_0_, bf16[2,176,128]{2,1,0:T(8,128)(2,1)S(1)} %collective-permute-done.7.refs_1_, s32[1,256]{1,0:T(1,128)S(1)} %bitcast.3), custom_call_target="tpu_custom_call" | custom-call | flops 1024 | tf_op jit(solution)/shard_map/pallas_call | solution.py:360
  18.4 0.8 %collective-permute-done.3.refs_1_ = bf16[128,256]{1,0:T(8,128)(2,1)S(1)} collective-permute-done((bf16[128,256]{1,0:T(8,128)(2,1)S(1)}, bf16[128,256]{1,0:T(8,128)(2,1)S(1)}, u32[]{:S(2)}, u32[]{:S(2)}) %collective-permute-start.3) | collective-permute-done | bytes 65568 | tf_op jit(solution)/shard_map/ppermute | solution.py:277
  19.3 1.5 %collective-permute-done.6.refs_3_ = bf16[128,256]{1,0:T(8,128)(2,1)S(1)} collective-permute-done((bf16[128,256]{1,0:T(8,128)(2,1)S(1)}, bf16[128,256]{1,0:T(8,128)(2,1)S(1)}, u32[]{:S(2)}, u32[]{:S(2)}) %collective-permute-start.6) | collective-permute-done | bytes 65568 | tf_op jit(solution)/shard_map/ppermute | solution.py:277
  20.8 0.0 copy-done
  20.8 1.2 %shard_map.125 = (f32[8,1280]{1,0:T(8,128)S(1)}, bf16[8,1280]{1,0:T(8,128)(2,1)S(1)}, bf16[8,1280]{1,0:T(8,128)(2,1)S(1)}, bf16[8,1280]{1,0:T(8,128)(2,1)S(1)}) custom-call(bf16[128,256]{1,0:T(8,128)(2,1)S(1)} %shard_map.122.after.refs_0_, bf16[128,256]{1,0:T(8,128)(2,1)S(1)} %collective-permute-done.3.refs_1_, ...), custom_call_target="tpu_custom_call" | custom-call | flops 104857600 | bytes 3276800 | tf_op jit(solution)/shard_map/pallas_call | solution.py:376
  22.0 0.1 collective-permute-start.10
  22.1 0.9 %collective-permute-start.8 = (bf16[8,1280]{1,0:T(8,128)(2,1)S(1)}, bf16[8,1280]{1,0:T(8,128)(2,1)S(1)}, u32[]{:S(2)}, u32[]{:S(2)}) collective-permute-start(bf16[8,1280]{1,0:T(8,128)(2,1)S(1)} %get-tuple-element.40), channel_id=1, source_target_pairs={{0,2},{1,3},{2,0},{3,1},{4,6},{5,7},{6,4},{7,5},{8,10},{9,11},{10,... | collective-permute-start | bytes 61448 | tf_op jit(solution)/shard_map/ppermute | solution.py:277
  23.0 1.0 %collective-permute-start.9 = (bf16[8,1280]{1,0:T(8,128)(2,1)S(1)}, bf16[8,1280]{1,0:T(8,128)(2,1)S(1)}, u32[]{:S(2)}, u32[]{:S(2)}) collective-permute-start(bf16[8,1280]{1,0:T(8,128)(2,1)S(1)} %get-tuple-element.41), channel_id=1, source_target_pairs={{0,1},{1,0},{2,3},{3,2},{4,5},{5,4},{6,7},{7,6},{8,9},{9,8},{10,11... | collective-permute-start | bytes 61448 | tf_op jit(solution)/shard_map/ppermute | solution.py:277
  24.0 1.3 %collective-permute-done.10.refs_2_ = bf16[8,1280]{1,0:T(8,128)(2,1)S(1)} collective-permute-done((bf16[8,1280]{1,0:T(8,128)(2,1)S(1)}, bf16[8,1280]{1,0:T(8,128)(2,1)S(1)}, u32[]{:S(2)}, u32[]{:S(2)}) %collective-permute-start.10) | collective-permute-done | bytes 20512 | tf_op jit(solution)/shard_map/ppermute | solution.py:277
  25.3 0.7 %collective-permute-done.8.refs_0_ = bf16[8,1280]{1,0:T(8,128)(2,1)S(1)} collective-permute-done((bf16[8,1280]{1,0:T(8,128)(2,1)S(1)}, bf16[8,1280]{1,0:T(8,128)(2,1)S(1)}, u32[]{:S(2)}, u32[]{:S(2)}) %collective-permute-start.8) | collective-permute-done | bytes 20512 | tf_op jit(solution)/shard_map/ppermute | solution.py:277
  26.0 0.0 collective-permute-done.9.refs_1_
  26.1 0.6 %shard_map.126 = bf16[8,1280]{1,0:T(8,128)(2,1)} custom-call(f32[8,1280]{1,0:T(8,128)S(1)} %get-tuple-element.39.own_ref, bf16[8,1280]{1,0:T(8,128)(2,1)S(1)} %collective-permute-done.8.refs_0_, bf16[8,1280]{1,0:T(8,128)(2,1)S(1)} %collective-permute-done.9.refs_1_, bf16[8,1280]{1,0:T(8,128)(2,1)S(1)} %collective-permute-done.10.refs_2_), custom_call_target="tpu_custom_call" | custom-call | flops 40960 | bytes 81920 | tf_op jit(solution)/shard_map/pallas_call | solution.py:389
  (8 shorter events, 0.0 us)
Async XLA Ops:
  0.0 3.9 %copy-start.6 = (bf16[8,1280]{1,0:T(8,128)(2,1)S(1)}, bf16[8,1280]{1,0:T(8,128)(2,1)}, u32[]{:S(2)}) copy-start(bf16[8,1280]{1,0:T(8,128)(2,1)} %q_ref.1) | copy-start | bytes 61444
  0.0 3.9 %copy-start.7 = (bf16[8,256]{1,0:T(8,128)(2,1)S(1)}, bf16[8,256]{1,0:T(8,128)(2,1)}, u32[]{:S(2)}) copy-start(bf16[8,256]{1,0:T(8,128)(2,1)} %nk_ref.1) | copy-start | bytes 12292
  0.0 3.9 %copy-start.8 = (bf16[8,256]{1,0:T(8,128)(2,1)S(1)}, bf16[8,256]{1,0:T(8,128)(2,1)}, u32[]{:S(2)}) copy-start(bf16[8,256]{1,0:T(8,128)(2,1)} %nv_ref.1) | copy-start | bytes 12292
  0.0 3.9 %copy-start.3 = (bf16[4,512,256]{2,1,0:T(8,128)(2,1)S(1)}, bf16[4,512,256]{2,1,0:T(8,128)(2,1)}, u32[]{:S(2)}) copy-start(bf16[4,512,256]{2,1,0:T(8,128)(2,1)} %ck_ref.1) | copy-start | bytes 3145732
  0.0 3.9 %copy-start.4 = (bf16[4,512,256]{2,1,0:T(8,128)(2,1)S(1)}, bf16[4,512,256]{2,1,0:T(8,128)(2,1)}, u32[]{:S(2)}) copy-start(bf16[4,512,256]{2,1,0:T(8,128)(2,1)} %cv_ref.1) | copy-start | bytes 3145732
  0.0 3.9 %copy-start.9 = (s32[4]{0:T(128)S(1)}, s32[4]{0:T(128)}, u32[]{:S(2)}) copy-start(s32[4]{0:T(128)} %lens_ref.1) | copy-start | bytes 52
  0.0 8.1 %collective-permute-start = (bf16[64,1280]{1,0:T(8,128)(2,1)}, bf16[64,1280]{1,0:T(8,128)(2,1)S(1)}, u32[]{:S(2)}, u32[]{:S(2)}) collective-permute-start(bf16[64,1280]{1,0:T(8,128)(2,1)} %refs_0_), channel_id=1, source_target_pairs={{0,2},{1,3},{2,0},{3,1},{4,6},{5,7},{6,4},{7,5},{8,10},{9,11},{10,... | collective-permute-start | bytes 491528 | tf_op jit(solution)/shard_map/ppermute | solution.py:277
  3.0 5.2 %slice-start = ((s8[5242880]{0:T(1024)(128)(4,1)}), s8[4194304]{0:T(1024)(128)(4,1)S(1)}, s32[]{:S(2)}) async-start(s8[5242880]{0:T(1024)(128)(4,1)} %bitcast.1), calls=%async_computation | async-start | bytes 8388608
  3.8 4.4 %slice-start.1 = ((s8[5242880]{0:T(1024)(128)(4,1)}), s8[1048576]{0:T(1024)(128)(4,1)S(1)}, s32[]{:S(2)}) async-start(s8[5242880]{0:T(1024)(128)(4,1)} %bitcast.1), calls=%async_computation.1 | async-start | bytes 2097152
  3.9 1.4 %copy-start.5 = (bf16[64,1280]{1,0:T(8,128)(2,1)S(1)}, bf16[64,1280]{1,0:T(8,128)(2,1)}, u32[]{:S(2)}) copy-start(bf16[64,1280]{1,0:T(8,128)(2,1)} %refs_0_) | copy-start | bytes 491524
  5.3 4.1 %copy-start.1 = (bf16[2,256]{1,0:T(2,128)(2,1)S(1)}, bf16[2,256]{1,0:T(2,128)(2,1)}, u32[]{:S(2)}) copy-start(bf16[2,256]{1,0:T(2,128)(2,1)} %refs_4_.1) | copy-start | bytes 3076
  5.3 2.9 %collective-permute-start.2 = (bf16[64,1280]{1,0:T(8,128)(2,1)S(1)}, bf16[64,1280]{1,0:T(8,128)(2,1)S(1)}, u32[]{:S(2)}, u32[]{:S(2)}) collective-permute-start(bf16[64,1280]{1,0:T(8,128)(2,1)S(1)} %copy-done.5), channel_id=1, source_target_pairs={{0,1},{1,0},{2,3},{3,2},{4,5},{5,4},{6,7},{7,6},{8,9},{9,8},{10,11... | collective-permute-start | bytes 491528 | tf_op jit(solution)/shard_map/ppermute | solution.py:277
  5.4 6.7 %collective-permute-start.5 = (bf16[176,128]{1,0:T(8,128)(2,1)S(1)}, bf16[176,128]{1,0:T(8,128)(2,1)S(1)}, u32[]{:S(2)}, u32[]{:S(2)}) collective-permute-start(bf16[176,128]{1,0:T(8,128)(2,1)S(1)} %shard_map.120.near_ref), channel_id=1, source_target_pairs={{0,8},{4,12},{8,0},{12,4},{1,9},{5,13},{9,1},{13,5},{2,10},{6,14},... | collective-permute-start | bytes 135176 | tf_op jit(solution)/shard_map/ppermute | solution.py:277
  8.1 1.4 %collective-permute-start.1 = (bf16[64,1280]{1,0:T(8,128)(2,1)S(1)}, bf16[64,1280]{1,0:T(8,128)(2,1)S(1)}, u32[]{:S(2)}, u32[]{:S(2)}) collective-permute-start(bf16[64,1280]{1,0:T(8,128)(2,1)S(1)} %collective-permute-done.refs_2_), channel_id=1, source_target_pairs={{0,1},{1,0},{2,3},{3,2},{4,5},{5,4},{6,7},{7,6},{8,9},{9,8},{10,11... | collective-permute-start | bytes 491528 | tf_op jit(solution)/shard_map/ppermute | solution.py:277
  9.9 8.1 %copy-start.2 = (s32[256]{0:T(256)S(1)}, s32[256]{0:T(256)}, u32[]{:S(2)}) copy-start(s32[256]{0:T(256)} %param.15) | copy-start | bytes 3076
  9.9 10.9 %copy-start = (bf16[1280,1280]{1,0:T(8,128)(2,1)S(1)}, bf16[1280,1280]{1,0:T(8,128)(2,1)}, u32[]{:S(2)}) copy-start(bf16[1280,1280]{1,0:T(8,128)(2,1)} %refs_8_.1) | copy-start | bytes 9830404
  9.9 6.6 %collective-permute-start.4 = (bf16[128,256]{1,0:T(8,128)(2,1)S(1)}, bf16[128,256]{1,0:T(8,128)(2,1)S(1)}, u32[]{:S(2)}, u32[]{:S(2)}) collective-permute-start(bf16[128,256]{1,0:T(8,128)(2,1)S(1)} %shard_map.122.after.refs_0_), channel_id=1, source_target_pairs={{0,8},{4,12},{8,0},{12,4},{1,9},{5,13},{9,1},{13,5},{2,10},{6,14},... | collective-permute-start | bytes 196616 | tf_op jit(solution)/shard_map/ppermute | solution.py:277
  12.2 5.8 %collective-permute-start.7 = (bf16[2,176,128]{2,1,0:T(8,128)(2,1)S(1)}, bf16[2,176,128]{2,1,0:T(8,128)(2,1)S(1)}, u32[]{:S(2)}, u32[]{:S(2)}) collective-permute-start(bf16[2,176,128]{2,1,0:T(8,128)(2,1)S(1)} %shard_map.123.refs_0_), channel_id=1, source_target_pairs={{0,4},{4,0},{8,12},{12,8},{1,5},{5,1},{9,13},{13,9},{2,6},{6,2},{1... | collective-permute-start | bytes 270344 | tf_op jit(solution)/shard_map/ppermute | solution.py:277
  13.8 5.4 %collective-permute-start.3 = (bf16[128,256]{1,0:T(8,128)(2,1)S(1)}, bf16[128,256]{1,0:T(8,128)(2,1)S(1)}, u32[]{:S(2)}, u32[]{:S(2)}) collective-permute-start(bf16[128,256]{1,0:T(8,128)(2,1)S(1)} %shard_map.122.after.refs_0_), channel_id=1, source_target_pairs={{0,4},{4,0},{8,12},{12,8},{1,5},{5,1},{9,13},{13,9},{2,6},{6,2},{1... | collective-permute-start | bytes 196616 | tf_op jit(solution)/shard_map/ppermute | solution.py:277
  16.5 4.3 %collective-permute-start.6 = (bf16[128,256]{1,0:T(8,128)(2,1)S(1)}, bf16[128,256]{1,0:T(8,128)(2,1)S(1)}, u32[]{:S(2)}, u32[]{:S(2)}) collective-permute-start(bf16[128,256]{1,0:T(8,128)(2,1)S(1)} %collective-permute-done.4.refs_2_), channel_id=1, source_target_pairs={{0,4},{4,0},{8,12},{12,8},{1,5},{5,1},{9,13},{13,9},{2,6},{6,2},{1... | collective-permute-start | bytes 196616 | tf_op jit(solution)/shard_map/ppermute | solution.py:277
  22.0 3.3 %collective-permute-start.10 = (bf16[8,1280]{1,0:T(8,128)(2,1)S(1)}, bf16[8,1280]{1,0:T(8,128)(2,1)S(1)}, u32[]{:S(2)}, u32[]{:S(2)}) collective-permute-start(bf16[8,1280]{1,0:T(8,128)(2,1)S(1)} %get-tuple-element.42), channel_id=1, source_target_pairs={{0,3},{1,2},{2,1},{3,0},{4,7},{5,6},{6,5},{7,4},{8,11},{9,10},{10,... | collective-permute-start | bytes 61448 | tf_op jit(solution)/shard_map/ppermute | solution.py:277
  22.1 3.9 %collective-permute-start.8 = (bf16[8,1280]{1,0:T(8,128)(2,1)S(1)}, bf16[8,1280]{1,0:T(8,128)(2,1)S(1)}, u32[]{:S(2)}, u32[]{:S(2)}) collective-permute-start(bf16[8,1280]{1,0:T(8,128)(2,1)S(1)} %get-tuple-element.40), channel_id=1, source_target_pairs={{0,2},{1,3},{2,0},{3,1},{4,6},{5,7},{6,4},{7,5},{8,10},{9,11},{10,... | collective-permute-start | bytes 61448 | tf_op jit(solution)/shard_map/ppermute | solution.py:277
  23.0 3.1 %collective-permute-start.9 = (bf16[8,1280]{1,0:T(8,128)(2,1)S(1)}, bf16[8,1280]{1,0:T(8,128)(2,1)S(1)}, u32[]{:S(2)}, u32[]{:S(2)}) collective-permute-start(bf16[8,1280]{1,0:T(8,128)(2,1)S(1)} %get-tuple-element.41), channel_id=1, source_target_pairs={{0,1},{1,0},{2,3},{3,2},{4,5},{5,4},{6,7},{7,6},{8,9},{9,8},{10,11... | collective-permute-start | bytes 61448 | tf_op jit(solution)/shard_map/ppermute | solution.py:277
